TPU v7x, 32 devices: a whole 2x2x4 slice. The times are simulated.
32 devices in a mesh: pipe: 4 (over y, x), rows: 8 (over z, core).
Axes of the slice: x: 2, y: 2, z: 4, core: 2. Of those that a mesh axis runs over, the one named last changes fastest.
Arguments:
- features: bfloat16 [128, 65536], P('pipe', 'rows'), may hold values from 0 to 16
- weights: bfloat16 [8, 1024, 64, 256], P('pipe', 'rows'), may hold values from -0.5 to 0.5
- bias: bfloat16 [8, 65536], P('pipe', 'rows'), may hold values from -2 to 2
- layout: int32 [8, 4096], P('pipe'), may hold values from 0 to 1023, as said below
Outputs:
- activations: bfloat16 [128, 65536], P('pipe', 'rows')
Inputs may be any that keep to these rules, and one draw needn't show every extreme that they name: `layout`: for every layer and every index of rows, the 512 slots of that index's 128 output blocks read blocks held by exactly 8 distinct indices of rows (index = block // 128), exactly 64 slots from each of them.
All inputs are finite; a program needn't handle non-finite values.
Results may differ from a plain program's by a relative error of at most 0.013.
Values may be sent and summed in bfloat16 or wider, within the bound.
No kernel may reach another device: no remote copies, remote signals or barrier semaphores. Data moves between devices by JAX's collectives and lax.ppermute only.
A program may use at most 192 MiB of HBM per device.

v0:
```python
import jax
import jax.numpy as jnp
from jax import lax
from jax.sharding import PartitionSpec as P

BLOCK = 64
K = 4


clamp_top = 32.0


def make_tables(layout_row, my_row, row_devs, blocks_dev, capacity):
    slot_count = layout_row.shape[0] // row_devs
    layout_grid = layout_row.reshape(row_devs, slot_count)
    owners = layout_grid // blocks_dev
    local_idx = layout_grid % blocks_dev
    before = jnp.arange(slot_count)[None, :] < jnp.arange(slot_count)[:, None]
    same_owner = owners[:, :, None] == owners[:, None, :]
    slot_rank = jnp.sum(same_owner & before[None, :, :], axis=2)
    is_mine = owners == my_row
    rank_onehot = (slot_rank[:, :, None] == jnp.arange(capacity)[None, None, :]) & is_mine[
        :, :, None
    ]
    local_onehot = local_idx[:, :, None] == jnp.arange(blocks_dev)[None, None, :]
    chooser = jnp.einsum(
        "dic,dib->dcb", rank_onehot.astype(jnp.float32), local_onehot.astype(jnp.float32)
    ).astype(jnp.bfloat16)
    own_owner = lax.dynamic_index_in_dim(owners, my_row, 0, keepdims=False)
    own_rank = lax.dynamic_index_in_dim(slot_rank, my_row, 0, keepdims=False)
    flat_idx = own_owner * capacity + own_rank
    picker = (flat_idx[:, None] == jnp.arange(row_devs * capacity)[None, :]).astype(jnp.bfloat16)
    return (chooser, picker)


def apply_layer(features_now, chooser, picker, weight_now, bias_now, row_devs, capacity):
    rows_now = features_now.shape[0]
    blocks_dev = chooser.shape[2]
    block_len = weight_now.shape[1]
    blocks = features_now.reshape(rows_now, blocks_dev, block_len)
    outgoing = jnp.einsum("dcb,mbf->dcmf", chooser, blocks, preferred_element_type=jnp.float32)
    outgoing = outgoing.astype(jnp.bfloat16).reshape(row_devs, capacity * rows_now * block_len)
    arrived = lax.all_to_all(outgoing, "rows", split_axis=0, concat_axis=0, tiled=True)
    arrived = arrived.reshape(row_devs * capacity, rows_now * block_len)
    gathered = jnp.dot(picker, arrived, preferred_element_type=jnp.float32).astype(jnp.bfloat16)
    gathered = gathered.reshape(blocks_dev, K, rows_now, block_len)
    weight_four = weight_now.reshape(blocks_dev, block_len, K, block_len)
    summed = jnp.einsum("bkmf,bfkg->mbg", gathered, weight_four, preferred_element_type=jnp.float32)
    summed = summed.reshape(rows_now, blocks_dev * block_len)
    summed = summed + bias_now.astype(jnp.float32)[None, :]
    return jnp.clip(jax.nn.relu(summed), 0.0, clamp_top).astype(jnp.bfloat16)


def on_device(features, weights, bias, layout):
    row_devs = lax.axis_size("rows")
    my_row = lax.axis_index("rows")
    blocks_dev = features.shape[1] // BLOCK
    slot_count = weights.shape[1] * K
    groups_used = min(row_devs, slot_count // 2)
    capacity = slot_count // groups_used
    all_weights, all_bias = (
        lax.all_gather(weights, "pipe", axis=0, tiled=True),
        lax.all_gather(bias, "pipe", axis=0, tiled=True),
    )
    all_layout = lax.all_gather(layout, "pipe", axis=0, tiled=True)
    current = features
    for layer_idx in range(all_weights.shape[0]):
        chooser, picker = make_tables(all_layout[layer_idx], my_row, row_devs, blocks_dev, capacity)
        current = apply_layer(
            current,
            chooser,
            picker,
            all_weights[layer_idx],
            all_bias[layer_idx],
            row_devs,
            capacity,
        )
    return current


def solution(mesh):
    in_specs = (
        P("pipe", "rows"),
        P("pipe", "rows", None, None),
        P("pipe", "rows"),
        P("pipe", None),
    )
    out_specs = P("pipe", "rows")
    return jax.shard_map(
        on_device, mesh=mesh, in_specs=in_specs, out_specs=out_specs, check_vma=False
    )
```

profile of v0, /device:TPU:0, one launch (start us, length us, event | category | flops | bytes accessed | tf_op | source)
XLA Modules:
  0.0 1224.5 jit_solution(9440437914124511572)
XLA Ops:
  7.3 9.9 all-gather
  20.3 15.5 %convert_reduce_fusion.7 = (s32[8,512]{1,0:T(8,128)}, s32[8,512]{1,0:T(8,128)}, s32[8,512]{1,0:T(8,128)}, s32[8,512]{1,0:T(8,128)S(1)}, s32[8,512]{1,0:T(8,128)S...) fusion(s32[8,512]{1,0:T(8,128)S(1)} %get-tuple-element.59, ...), kind=kLoop, calls=%fused_computation.7 | loop fusion | flops 67076096 | bytes 524288 | tf_op jit(solution)/shard_map/reduce_sum | solution.py:20
  39.5 6.9 copy.74
  46.4 7.5 all_to_all.64
  54.4 12.9 %reduce.68 = bf16[8,131072]{1,0:T(8,128)(2,1)S(1)} reduce(bf16[8,1,131072]{2,1,0:T(2,128)(2,1)} %all_to_all.64, bf16[]{:T(256)} %broadcast.998), dimensions={1}, to_apply=%all_to_all.64.reduce_sub_computation | reduce | bytes 4194306 | tf_op jit(solution)/shard_map/all_to_all | solution.py:43
  75.4 9.7 all-gather.1
  86.3 38.1 %all-to-all-done = bf16[8,2,65536]{2,1,0:T(2,128)(2,1)S(1)} async-done(((bf16[8,2,65536]{2,1,0:T(2,128)(2,1)}), bf16[8,2,65536]{2,1,0:T(2,128)(2,1)S(1)}, u32[]{:S(2)}, u32[]{:S(2)}) %all-to-all-start) | async-done | bytes 2097184 | tf_op jit(solution)/shard_map/all_to_all | solution.py:43
  128.8 12.5 %reduce.8 = bf16[8,131072]{1,0:T(8,128)(2,1)S(1)} reduce(bf16[8,1,131072]{2,1,0:T(2,128)(2,1)} %reshape.1112, bf16[]{:T(256)} %constant.178), dimensions={1}, to_apply=%all_to_all.49.reduce_sub_computation | reduce | bytes 4194306 | tf_op jit(solution)/shard_map/all_to_all | solution.py:43
  151.8 158.4 %all-gather.4.cloned.1.call-done = bf16[8,128,64,256]{3,2,1,0:T(8,128)(2,1)} async-done(((bf16[2,128,64,256]{3,2,1,0:T(8,128)(2,1)}), bf16[8,128,64,256]{3,2,1,0:T(8,128)(2,1)}) %all-gather.4.cloned.1.call-update) | async-done | bytes 33554448 | tf_op jit(solution)/shard_map/all_gather | solution.py:62
  310.2 24.9 %fusion.172 = (bf16[1,128,64,256]{3,2,1,0:T(8,128)(2,1)}, bf16[1,128,64,256]{3,2,1,0:T(8,128)(2,1)}, bf16[1,128,64,256]{3,2,1,0:T(8,128)(2,1)}, bf16[1,128,64,25...) fusion(bf16[8,128,64,256]{3,2,1,0:T(8,128)(2,1)} %all-gather.4., ...), kind=kLoop, calls=%fused_computation.278 | loop fusion | bytes 67108864 | tf_op jit(solution)/shard_map/slice | solution.py:73
  335.1 6.8 copy.132
  341.9 13.0 %copy.77 = bf16[128,64,4,64]{3,1,2,0:T(8,128)(2,1)} copy(bf16[128,64,4,64]{0,3,2,1:T(8,128)(2,1)} %bitcast.213) | data formatting | bytes 8388608 | tf_op jit(solution)/shard_map/reshape;squeeze | solution.py:47
  366.2 6.8 copy.79
  373.0 7.5 all_to_all.65
  380.5 12.9 %reduce.69 = bf16[8,131072]{1,0:T(8,128)(2,1)S(1)} reduce(bf16[8,1,131072]{2,1,0:T(2,128)(2,1)} %all_to_all.65, bf16[]{:T(256)} %broadcast.998), dimensions={1}, to_apply=%all_to_all.65.reduce_sub_computation | reduce | bytes 4194306 | tf_op jit(solution)/shard_map/all_to_all | solution.py:43
  401.6 6.8 copy.133
  408.4 13.0 %copy.82 = bf16[128,64,4,64]{3,1,2,0:T(8,128)(2,1)} copy(bf16[128,64,4,64]{0,3,2,1:T(8,128)(2,1)} %bitcast.214) | data formatting | bytes 8388608 | tf_op jit(solution)/shard_map/reshape;squeeze | solution.py:47
  421.4 29.1 %all-to-all-done.1 = bf16[8,2,65536]{2,1,0:T(2,128)(2,1)S(1)} async-done(((bf16[8,2,65536]{2,1,0:T(2,128)(2,1)}), bf16[8,2,65536]{2,1,0:T(2,128)(2,1)S(1)}, u32[]{:S(2)}, u32[]{:S(2)}) %all-to-all-start.1) | async-done | bytes 2097184 | tf_op jit(solution)/shard_map/all_to_all | solution.py:43
  454.9 12.4 %reduce.10 = bf16[8,131072]{1,0:T(8,128)(2,1)S(1)} reduce(bf16[8,1,131072]{2,1,0:T(2,128)(2,1)} %reshape.1114, bf16[]{:T(256)} %constant.178), dimensions={1}, to_apply=%all_to_all.51.reduce_sub_computation | reduce | bytes 4194306 | tf_op jit(solution)/shard_map/all_to_all | solution.py:43
  488.9 6.8 copy.84
  495.7 7.5 all_to_all.66
  503.2 12.9 %reduce.70 = bf16[8,131072]{1,0:T(8,128)(2,1)S(1)} reduce(bf16[8,1,131072]{2,1,0:T(2,128)(2,1)} %all_to_all.66, bf16[]{:T(256)} %broadcast.998), dimensions={1}, to_apply=%all_to_all.66.reduce_sub_computation | reduce | bytes 4194306 | tf_op jit(solution)/shard_map/all_to_all | solution.py:43
  523.3 6.8 copy.134
  530.1 13.0 %copy.87 = bf16[128,64,4,64]{3,1,2,0:T(8,128)(2,1)} copy(bf16[128,64,4,64]{0,3,2,1:T(8,128)(2,1)} %bitcast.215) | data formatting | bytes 8388608 | tf_op jit(solution)/shard_map/reshape;squeeze | solution.py:47
  543.1 29.0 %all-to-all-done.2 = bf16[8,2,65536]{2,1,0:T(2,128)(2,1)S(1)} async-done(((bf16[8,2,65536]{2,1,0:T(2,128)(2,1)}), bf16[8,2,65536]{2,1,0:T(2,128)(2,1)S(1)}, u32[]{:S(2)}, u32[]{:S(2)}) %all-to-all-start.2) | async-done | bytes 2097184 | tf_op jit(solution)/shard_map/all_to_all | solution.py:43
  576.6 12.4 %reduce.12 = bf16[8,131072]{1,0:T(8,128)(2,1)S(1)} reduce(bf16[8,1,131072]{2,1,0:T(2,128)(2,1)} %reshape.1116, bf16[]{:T(256)} %constant.178), dimensions={1}, to_apply=%all_to_all.53.reduce_sub_computation | reduce | bytes 4194306 | tf_op jit(solution)/shard_map/all_to_all | solution.py:43
  610.8 6.8 copy.89
  617.7 7.5 all_to_all.67
  625.1 12.9 %reduce.71 = bf16[8,131072]{1,0:T(8,128)(2,1)S(1)} reduce(bf16[8,1,131072]{2,1,0:T(2,128)(2,1)} %all_to_all.67, bf16[]{:T(256)} %broadcast.998), dimensions={1}, to_apply=%all_to_all.67.reduce_sub_computation | reduce | bytes 4194306 | tf_op jit(solution)/shard_map/all_to_all | solution.py:43
  645.2 6.8 copy.135
  652.0 13.0 %copy.92 = bf16[128,64,4,64]{3,1,2,0:T(8,128)(2,1)} copy(bf16[128,64,4,64]{0,3,2,1:T(8,128)(2,1)} %bitcast.216) | data formatting | bytes 8388608 | tf_op jit(solution)/shard_map/reshape;squeeze | solution.py:47
  665.0 29.0 %all-to-all-done.3 = bf16[8,2,65536]{2,1,0:T(2,128)(2,1)S(1)} async-done(((bf16[8,2,65536]{2,1,0:T(2,128)(2,1)}), bf16[8,2,65536]{2,1,0:T(2,128)(2,1)S(1)}, u32[]{:S(2)}, u32[]{:S(2)}) %all-to-all-start.3) | async-done | bytes 2097184 | tf_op jit(solution)/shard_map/all_to_all | solution.py:43
  698.5 12.4 %reduce.14 = bf16[8,131072]{1,0:T(8,128)(2,1)S(1)} reduce(bf16[8,1,131072]{2,1,0:T(2,128)(2,1)} %reshape.1118, bf16[]{:T(256)} %constant.178), dimensions={1}, to_apply=%all_to_all.55.reduce_sub_computation | reduce | bytes 4194306 | tf_op jit(solution)/shard_map/all_to_all | solution.py:43
  732.4 6.8 copy.94
  739.3 7.5 all_to_all.68
  746.8 12.9 %reduce.72 = bf16[8,131072]{1,0:T(8,128)(2,1)S(1)} reduce(bf16[8,1,131072]{2,1,0:T(2,128)(2,1)} %all_to_all.68, bf16[]{:T(256)} %broadcast.998), dimensions={1}, to_apply=%all_to_all.68.reduce_sub_computation | reduce | bytes 4194306 | tf_op jit(solution)/shard_map/all_to_all | solution.py:43
  767.6 6.8 copy.136
  774.4 13.0 %copy.97 = bf16[128,64,4,64]{3,1,2,0:T(8,128)(2,1)} copy(bf16[128,64,4,64]{0,3,2,1:T(8,128)(2,1)} %bitcast.217) | data formatting | bytes 8388608 | tf_op jit(solution)/shard_map/reshape;squeeze | solution.py:47
  787.4 28.3 %all-to-all-done.4 = bf16[8,2,65536]{2,1,0:T(2,128)(2,1)S(1)} async-done(((bf16[8,2,65536]{2,1,0:T(2,128)(2,1)}), bf16[8,2,65536]{2,1,0:T(2,128)(2,1)S(1)}, u32[]{:S(2)}, u32[]{:S(2)}) %all-to-all-start.4) | async-done | bytes 2097184 | tf_op jit(solution)/shard_map/all_to_all | solution.py:43
  820.2 12.4 %reduce.16 = bf16[8,131072]{1,0:T(8,128)(2,1)S(1)} reduce(bf16[8,1,131072]{2,1,0:T(2,128)(2,1)} %reshape.1120, bf16[]{:T(256)} %constant.178), dimensions={1}, to_apply=%all_to_all.57.reduce_sub_computation | reduce | bytes 4194306 | tf_op jit(solution)/shard_map/all_to_all | solution.py:43
  843.1 6.1 fusion.26
  854.4 6.8 copy.99
  861.3 7.5 all_to_all.69
  868.7 12.9 %reduce.73 = bf16[8,131072]{1,0:T(8,128)(2,1)S(1)} reduce(bf16[8,1,131072]{2,1,0:T(2,128)(2,1)} %all_to_all.69, bf16[]{:T(256)} %broadcast.998), dimensions={1}, to_apply=%all_to_all.69.reduce_sub_computation | reduce | bytes 4194306 | tf_op jit(solution)/shard_map/all_to_all | solution.py:43
  889.5 6.8 copy.137
  896.3 13.0 %copy.102 = bf16[128,64,4,64]{3,1,2,0:T(8,128)(2,1)} copy(bf16[128,64,4,64]{0,3,2,1:T(8,128)(2,1)} %bitcast.218) | data formatting | bytes 8388608 | tf_op jit(solution)/shard_map/reshape;squeeze | solution.py:47
  909.3 28.3 %all-to-all-done.5 = bf16[8,2,65536]{2,1,0:T(2,128)(2,1)S(1)} async-done(((bf16[8,2,65536]{2,1,0:T(2,128)(2,1)}), bf16[8,2,65536]{2,1,0:T(2,128)(2,1)S(1)}, u32[]{:S(2)}, u32[]{:S(2)}) %all-to-all-start.5) | async-done | bytes 2097184 | tf_op jit(solution)/shard_map/all_to_all | solution.py:43
  942.1 12.4 %reduce.18 = bf16[8,131072]{1,0:T(8,128)(2,1)S(1)} reduce(bf16[8,1,131072]{2,1,0:T(2,128)(2,1)} %reshape.1122, bf16[]{:T(256)} %constant.178), dimensions={1}, to_apply=%all_to_all.59.reduce_sub_computation | reduce | bytes 4194306 | tf_op jit(solution)/shard_map/all_to_all | solution.py:43
  965.0 6.1 fusion.27
  976.1 6.8 copy.104
  982.9 7.5 all_to_all.70
  990.4 12.9 %reduce.74 = bf16[8,131072]{1,0:T(8,128)(2,1)S(1)} reduce(bf16[8,1,131072]{2,1,0:T(2,128)(2,1)} %all_to_all.70, bf16[]{:T(256)} %broadcast.998), dimensions={1}, to_apply=%all_to_all.70.reduce_sub_computation | reduce | bytes 4194306 | tf_op jit(solution)/shard_map/all_to_all | solution.py:43
  1011.3 6.8 copy.138
  1018.1 13.0 %copy.107 = bf16[128,64,4,64]{3,1,2,0:T(8,128)(2,1)} copy(bf16[128,64,4,64]{0,3,2,1:T(8,128)(2,1)} %bitcast.219) | data formatting | bytes 8388608 | tf_op jit(solution)/shard_map/reshape;squeeze | solution.py:47
  1031.1 28.3 %all-to-all-done.6 = bf16[8,2,65536]{2,1,0:T(2,128)(2,1)S(1)} async-done(((bf16[8,2,65536]{2,1,0:T(2,128)(2,1)}), bf16[8,2,65536]{2,1,0:T(2,128)(2,1)S(1)}, u32[]{:S(2)}, u32[]{:S(2)}) %all-to-all-start.6) | async-done | bytes 2097184 | tf_op jit(solution)/shard_map/all_to_all | solution.py:43
  1063.8 12.4 %reduce.20 = bf16[8,131072]{1,0:T(8,128)(2,1)S(1)} reduce(bf16[8,1,131072]{2,1,0:T(2,128)(2,1)} %reshape.1124, bf16[]{:T(256)} %constant.178), dimensions={1}, to_apply=%all_to_all.61.reduce_sub_computation | reduce | bytes 4194306 | tf_op jit(solution)/shard_map/all_to_all | solution.py:43
  1086.7 6.1 fusion.28
  1098.1 6.8 copy.109
  1104.9 7.5 all_to_all.71
  1112.4 12.9 %reduce.75 = bf16[8,131072]{1,0:T(8,128)(2,1)S(1)} reduce(bf16[8,1,131072]{2,1,0:T(2,128)(2,1)} %all_to_all.71, bf16[]{:T(256)} %broadcast.998), dimensions={1}, to_apply=%all_to_all.71.reduce_sub_computation | reduce | bytes 4194306 | tf_op jit(solution)/shard_map/all_to_all | solution.py:43
  1134.0 6.8 copy.139
  1140.8 13.0 %copy.112 = bf16[128,64,4,64]{3,1,2,0:T(8,128)(2,1)} copy(bf16[128,64,4,64]{0,3,2,1:T(8,128)(2,1)} %bitcast.220) | data formatting | bytes 8388608 | tf_op jit(solution)/shard_map/reshape;squeeze | solution.py:47
  1153.8 27.5 %all-to-all-done.7 = bf16[8,2,65536]{2,1,0:T(2,128)(2,1)S(1)} async-done(((bf16[8,2,65536]{2,1,0:T(2,128)(2,1)}), bf16[8,2,65536]{2,1,0:T(2,128)(2,1)S(1)}, u32[]{:S(2)}, u32[]{:S(2)}) %all-to-all-start.7) | async-done | bytes 2097184 | tf_op jit(solution)/shard_map/all_to_all | solution.py:43
  1185.7 12.4 %reduce.22 = bf16[8,131072]{1,0:T(8,128)(2,1)S(1)} reduce(bf16[8,1,131072]{2,1,0:T(2,128)(2,1)} %reshape.1126, bf16[]{:T(256)} %constant.178), dimensions={1}, to_apply=%all_to_all.63.reduce_sub_computation | reduce | bytes 4194306 | tf_op jit(solution)/shard_map/all_to_all | solution.py:43
  (160 shorter events, 260.3 us)
Async XLA Ops:
  6.5 0.8 copy-start.17
  6.5 11.2 copy-start.1
  6.5 303.7 %all-gather.4.cloned.1.call-start = ((), (), s32[]{:S(2)}) async-start(), calls=%async_computation.8 | async-start | bytes 41943040 | tf_op jit(solution)/shard_map/all_gather | solution.py:62
  17.6 28.7 %copy-start.6 = (s32[8,512]{1,0:T(8,128)}, s32[8,512]{1,0:T(8,128)S(1)}, u32[]{:S(2)}) copy-start(s32[8,512]{1,0:T(8,128)S(1)} %reshape_squeeze.48) | copy-start | bytes 49156
  17.7 28.7 %copy-start.8 = (s32[8,512]{1,0:T(8,128)}, s32[8,512]{1,0:T(8,128)S(1)}, u32[]{:S(2)}) copy-start(s32[8,512]{1,0:T(8,128)S(1)} %reshape_squeeze.49) | copy-start | bytes 49156
  17.7 28.7 %copy-start.10 = (s32[8,512]{1,0:T(8,128)}, s32[8,512]{1,0:T(8,128)S(1)}, u32[]{:S(2)}) copy-start(s32[8,512]{1,0:T(8,128)S(1)} %reshape_squeeze.50) | copy-start | bytes 49156
  19.7 16.2 %copy-start.2 = (s32[8,512]{1,0:T(8,128)}, s32[8,512]{1,0:T(8,128)S(1)}, u32[]{:S(2)}) copy-start(s32[8,512]{1,0:T(8,128)S(1)} %get-tuple-element.59) | copy-start | bytes 49156
  19.7 16.2 %copy-start.3 = (s32[8,512]{1,0:T(8,128)}, s32[8,512]{1,0:T(8,128)S(1)}, u32[]{:S(2)}) copy-start(s32[8,512]{1,0:T(8,128)S(1)} %get-tuple-element.31) | copy-start | bytes 49156
  20.3 15.5 %copy-start.4 = (s32[8,512]{1,0:T(8,128)}, s32[8,512]{1,0:T(8,128)S(1)}, u32[]{:S(2)}) copy-start(s32[8,512]{1,0:T(8,128)S(1)} %get-tuple-element.57) | copy-start | bytes 49156
  20.3 15.5 %copy-start.5 = (s32[8,512]{1,0:T(8,128)}, s32[8,512]{1,0:T(8,128)S(1)}, u32[]{:S(2)}) copy-start(s32[8,512]{1,0:T(8,128)S(1)} %get-tuple-element.35) | copy-start | bytes 49156
  67.3 8.1 copy-start.18
  70.5 53.9 %all-to-all-start = ((bf16[8,2,65536]{2,1,0:T(2,128)(2,1)}), bf16[8,2,65536]{2,1,0:T(2,128)(2,1)S(1)}, u32[]{:S(2)}, u32[]{:S(2)}) async-start(bf16[8,2,65536]{2,1,0:T(2,128)(2,1)} %reshape.1111), calls=%async_computation | async-start | bytes 4194304 | tf_op jit(solution)/shard_map/all_to_all | solution.py:43
  85.1 56.2 %copy-start = (bf16[8,8192]{1,0:T(8,128)(2,1)}, bf16[8,8192]{1,0:T(8,128)(2,1)S(1)}, u32[]{:S(2)}) copy-start(bf16[8,8192]{1,0:T(8,128)(2,1)S(1)} %reshape.999) | copy-start | bytes 393220
  396.6 53.8 %all-to-all-start.1 = ((bf16[8,2,65536]{2,1,0:T(2,128)(2,1)}), bf16[8,2,65536]{2,1,0:T(2,128)(2,1)S(1)}, u32[]{:S(2)}, u32[]{:S(2)}) async-start(bf16[8,2,65536]{2,1,0:T(2,128)(2,1)} %reshape.1113), calls=%async_computation.1 | async-start | bytes 4194304 | tf_op jit(solution)/shard_map/all_to_all | solution.py:43
  519.3 52.8 %all-to-all-start.2 = ((bf16[8,2,65536]{2,1,0:T(2,128)(2,1)}), bf16[8,2,65536]{2,1,0:T(2,128)(2,1)S(1)}, u32[]{:S(2)}, u32[]{:S(2)}) async-start(bf16[8,2,65536]{2,1,0:T(2,128)(2,1)} %reshape.1115), calls=%async_computation.2 | async-start | bytes 4194304 | tf_op jit(solution)/shard_map/all_to_all | solution.py:43
  641.3 52.8 %all-to-all-start.3 = ((bf16[8,2,65536]{2,1,0:T(2,128)(2,1)}), bf16[8,2,65536]{2,1,0:T(2,128)(2,1)S(1)}, u32[]{:S(2)}, u32[]{:S(2)}) async-start(bf16[8,2,65536]{2,1,0:T(2,128)(2,1)} %reshape.1117), calls=%async_computation.3 | async-start | bytes 4194304 | tf_op jit(solution)/shard_map/all_to_all | solution.py:43
  759.7 7.9 copy-start.11
  762.9 52.8 %all-to-all-start.4 = ((bf16[8,2,65536]{2,1,0:T(2,128)(2,1)}), bf16[8,2,65536]{2,1,0:T(2,128)(2,1)S(1)}, u32[]{:S(2)}, u32[]{:S(2)}) async-start(bf16[8,2,65536]{2,1,0:T(2,128)(2,1)} %reshape.1119), calls=%async_computation.4 | async-start | bytes 4194304 | tf_op jit(solution)/shard_map/all_to_all | solution.py:43
  843.1 7.2 copy-start.16
  843.1 7.3 copy-start.21
  881.6 7.0 copy-start.13
  881.7 7.8 copy-start.9
  884.9 52.8 %all-to-all-start.5 = ((bf16[8,2,65536]{2,1,0:T(2,128)(2,1)}), bf16[8,2,65536]{2,1,0:T(2,128)(2,1)S(1)}, u32[]{:S(2)}, u32[]{:S(2)}) async-start(bf16[8,2,65536]{2,1,0:T(2,128)(2,1)} %reshape.1121), calls=%async_computation.5 | async-start | bytes 4194304 | tf_op jit(solution)/shard_map/all_to_all | solution.py:43
  965.0 7.2 copy-start.15
  965.0 7.3 copy-start.20
  1003.3 7.1 copy-start.12
  1003.3 7.9 copy-start.7
  1006.6 52.8 %all-to-all-start.6 = ((bf16[8,2,65536]{2,1,0:T(2,128)(2,1)}), bf16[8,2,65536]{2,1,0:T(2,128)(2,1)S(1)}, u32[]{:S(2)}, u32[]{:S(2)}) async-start(bf16[8,2,65536]{2,1,0:T(2,128)(2,1)} %reshape.1123), calls=%async_computation.6 | async-start | bytes 4194304 | tf_op jit(solution)/shard_map/all_to_all | solution.py:43
  1086.7 7.2 copy-start.14
  1086.7 7.3 copy-start.19
  1128.5 52.8 %all-to-all-start.7 = ((bf16[8,2,65536]{2,1,0:T(2,128)(2,1)}), bf16[8,2,65536]{2,1,0:T(2,128)(2,1)S(1)}, u32[]{:S(2)}, u32[]{:S(2)}) async-start(bf16[8,2,65536]{2,1,0:T(2,128)(2,1)} %reshape.1125), calls=%async_computation.7 | async-start | bytes 4194304 | tf_op jit(solution)/shard_map/all_to_all | solution.py:43
Sparse Core Ops, SparseCore 0:
  9.2 300.9 all-gather.3
where the time goes:
time: 1240 us; the launch traced here: 1220 us
  local copies, waits for them, and re-layouts  433 us (35%)
  waiting for transfers between devices  397 us (32%)
  other arithmetic  225 us (18%)
  matrix products  103 us (8%)
  starting transfers between devices  32.6 us (3%)
  blocking collectives  19.6 us (2%)
  between operations  14.4 us (1%)
    all_to_all x8, waiting for transfers between devices, apply_layer(): lax.all_to_all(outgoing, 'rows', split_axis=0, concat_axis=0, tiled=True)  238 us
    all_to_all x16, other arithmetic, apply_layer(): lax.all_to_all(outgoing, 'rows', split_axis=0, concat_axis=0, tiled=True)  202 us
    all_gather x1, waiting for transfers between devices, on_device(): lax.all_gather(weights, 'pipe', axis=0, tiled=True)  158 us
    unnamed x70, local copies, waits for them, and re-layouts  116 us
    another operation x8, local copies, waits for them, and re-layouts, apply_layer(): weight_four = weight_now.reshape(blocks_dev, block_len, K, block_len)  104 us
    all_to_all x9, local copies, waits for them, and re-layouts, apply_layer(): lax.all_to_all(outgoing, 'rows', split_axis=0, concat_axis=0, tiled=True)  60.3 us
    convert_element_type x8, local copies, waits for them, and re-layouts, apply_layer(): outgoing.astype(jnp.bfloat16)  54.7 us
    dot_general x8, matrix products, apply_layer(): jnp.einsum('bkmf,bfkg->mbg', gathered, weight_four, preferred_element_typ...  48.9 us
  transfers between devices with their start and end apart: 9, of which 9 were waited for; matrix products, arithmetic and copies ran while one was open for 18% of the time, Pallas kernels for 0%

commit v1 on v0

v1 whole, which is shorter than its diff:
```python
import functools

import jax
import jax.numpy as jnp
import numpy as np
from jax import lax
from jax.experimental import pallas as pl
from jax.experimental.pallas import tpu as pltpu
from jax.sharding import PartitionSpec as P

BLOCK = 64
K = 4
LANES = 128
CORES = 2
WEIGHT_PARTS = 4

clamp_top = 32.0


def layer_kernel(act_plan, weight_plan, unroll, codes, place, *refs):
    n_acts = 1 + max(p[0] for p in act_plan)
    n_weights = 1 + max(p[0] for p in weight_plan)
    acts, weights = refs[:n_acts], refs[n_acts : n_acts + n_weights]
    bias, out, held, wheld, masks, act_sem, w_sem = refs[n_acts + n_weights :]
    rows = out.shape[0]
    blocks = wheld.shape[0]
    pairs = held.shape[2] // LANES

    def start(copy, want):
        if want is None:
            copy.start()
        else:
            pl.when(place[want[0]] == want[1])(copy.start)

    def act_copy(operand, slot, slots):
        src = acts[operand] if slots == 1 else acts[operand].at[:]
        dst = held.at[slot] if slots == 1 else held.at[pl.ds(slot, slots)]
        return pltpu.make_async_copy(src, dst, act_sem.at[slot])

    def weight_copy(operand, first, count, index):
        src = weights[operand] if index is None else weights[operand].at[index]
        part = wheld.at[pl.ds(first, count)]
        return pltpu.make_async_copy(src, part, w_sem.at[first])

    for operand, slot, slots, want in act_plan:
        start(act_copy(operand, slot, slots), want)
    for operand, first, count, index, want in weight_plan:
        start(weight_copy(operand, first, count, index), want)

    low = lax.broadcasted_iota(jnp.int32, (rows, LANES), 1) < BLOCK
    masks[0] = jnp.where(low, 1.0, 0.0).astype(jnp.bfloat16)
    masks[1] = jnp.where(low, 0.0, 1.0).astype(jnp.bfloat16)

    waited = set()
    for operand, slot, slots, _ in act_plan:
        if slot not in waited:
            waited.add(slot)
            act_copy(operand, slot, slots).wait()

    def products(block):
        parts = []
        for k in range(K):
            code = codes[block * K + k]
            pair = lax.rem(code // 2, pairs)
            columns = pl.ds(pl.multiple_of(pair * LANES, LANES), LANES)
            parts.append(held[code // (2 * pairs), :, columns] * masks[lax.rem(code, 2)])
        left = jnp.concatenate(
            [
                jnp.concatenate([parts[0], parts[2]], axis=1),
                jnp.concatenate([parts[1], parts[3]], axis=1),
            ],
            axis=0,
        )
        w = wheld[block]
        first, second = w[:, :LANES], w[:, LANES:]
        right = jnp.concatenate([first, first, second, second], axis=0)
        return jnp.dot(left, right, preferred_element_type=jnp.float32)

    def two_blocks(q, _):
        a, b = products(2 * q), products(2 * q + 1)
        even = a[:rows] + pltpu.roll(a[rows:], BLOCK, 1)
        odd = b[rows:] + pltpu.roll(b[:rows], BLOCK, 1)
        columns = pl.ds(pl.multiple_of(q * LANES, LANES), LANES)
        total = jnp.where(low, even, odd) + bias[:, columns].astype(jnp.float32)
        out[:, columns] = jnp.clip(total, 0.0, clamp_top).astype(jnp.bfloat16)
        return 0

    parts = sorted({(first, count) for _, first, count, _, _ in weight_plan})
    for first, count in parts:
        entry = next(p for p in weight_plan if p[1] == first)
        weight_copy(*entry[:4]).wait()
        steps = count // 2
        lax.fori_loop(first // 2, first // 2 + steps, two_blocks, 0, unroll=min(unroll, steps))


def apply_layer(codes, place, acts, act_plan, weights, weight_plan, bias):
    slots = sum(
        count for slot, count in {(slot, count) for _, slot, count, _ in act_plan}
    )
    rows, neurons = acts[0].shape[-2:]
    blocks = neurons // BLOCK
    held = (slots, rows, neurons)
    wheld = (blocks, BLOCK, K * BLOCK)
    smem = pl.BlockSpec(memory_space=pltpu.SMEM)
    anywhere = pl.BlockSpec(memory_space=pl.ANY)
    vmem = pl.BlockSpec(memory_space=pltpu.VMEM)
    kernel = functools.partial(layer_kernel, act_plan, weight_plan, 8)
    return pl.pallas_call(
        kernel,
        out_shape=jax.ShapeDtypeStruct((rows, neurons), jnp.bfloat16),
        in_specs=[smem, smem] + [anywhere] * (len(acts) + len(weights)) + [vmem],
        out_specs=vmem,
        scratch_shapes=[
            pltpu.VMEM(held, jnp.bfloat16),
            pltpu.VMEM(wheld, jnp.bfloat16),
            pltpu.VMEM((2, rows, LANES), jnp.bfloat16),
            pltpu.SemaphoreType.DMA((slots,)),
            pltpu.SemaphoreType.DMA((blocks,)),
        ],
        compiler_params=pltpu.CompilerParams(vmem_limit_bytes=32 * 2**20),
    )(codes, place, *acts, *weights, bias)


def along_line(x, pairs):
    moves = [(a * CORES + c, b * CORES + c) for a, b in pairs for c in range(CORES)]
    return lax.ppermute(x, "rows", moves)


def to_other_core(x, chips):
    moves = [(z * CORES + c, z * CORES + 1 - c) for z in chips for c in range(CORES)]
    return lax.ppermute(x, "rows", moves)


def gather_line(x):
    ends, middle, every = (0, 3), (1, 2), (0, 1, 2, 3)
    near = along_line(x, [(0, 1), (1, 0), (2, 3), (3, 2)])
    inner = along_line(x, [(1, 2), (2, 1)])
    far = along_line(near, [(1, 2), (2, 1)])
    outer = along_line(inner, [(2, 3), (1, 0)])
    last = along_line(far, [(2, 3), (1, 0)])
    own_side = [x, near, inner, far, outer, last]
    other_side = [
        to_other_core(buf, chips)
        for buf, chips in zip(own_side, (every, every, middle, middle, ends, ends))
    ]
    return own_side + other_side


def line_plan():
    plan = []
    for side in range(CORES):
        for buf, (slot, want) in enumerate(
            [(0, None), (1, None), (2, (0, 1)), (3, (0, 1)), (2, (0, 0)), (3, (0, 0))]
        ):
            plan.append((side * 6 + buf, side * 4 + slot, 1, want))
    return plan


def line_slots(row_devs):
    table = np.zeros((row_devs, row_devs), np.int32)
    chips = row_devs // CORES
    for me in range(row_devs):
        for owner in range(row_devs):
            z, c = divmod(me, CORES)
            oz, oc = divmod(owner, CORES)
            far = [chip for chip in range(chips) if chip // 2 != z // 2]
            if oz // 2 == z // 2:
                slot = 0 if oz == z else 1
            else:
                nearest = min(far, key=lambda chip: abs(chip - z))
                slot = 2 if oz == nearest else 3
            table[me, owner] = (c != oc) * chips + slot
    return table


def on_device(features, weights, bias, layout):
    row_devs = lax.axis_size("rows")
    my_row = lax.axis_index("rows")
    neurons = features.shape[1]
    blocks = neurons // BLOCK
    slot_count = blocks * K
    pairs = neurons // LANES
    is_line = row_devs == 4 * CORES

    mine = lax.dynamic_slice_in_dim(layout, my_row * slot_count, slot_count, axis=1)
    owners, local = mine // blocks, mine % blocks
    table = line_slots(row_devs) if is_line else np.tile(np.arange(row_devs, dtype=np.int32), (row_devs, 1))
    my_slots = lax.dynamic_index_in_dim(jnp.asarray(table), my_row, 0, keepdims=False)
    hit = owners[:, :, None] == jnp.arange(row_devs)[None, None, :]
    slots = jnp.sum(jnp.where(hit, my_slots[None, None, :], 0), axis=2)
    codes = (slots * pairs + local // 2) * 2 + local % 2

    all_codes = lax.all_gather(codes, "pipe", axis=0, tiled=True)
    all_bias = lax.all_gather(bias, "pipe", axis=0, tiled=True)
    all_weights = lax.all_gather(weights, "pipe", axis=0, tiled=True)
    z = my_row // CORES
    is_middle = (z > 0) & (z < row_devs // CORES - 1)
    place = jnp.stack([is_middle.astype(jnp.int32)])

    current = features
    parts = min(WEIGHT_PARTS, blocks // 2)
    each = blocks // parts
    for layer in range(all_weights.shape[0]):
        if is_line:
            acts, act_plan = gather_line(current), line_plan()
        else:
            acts = [lax.all_gather(current, "rows", axis=0, tiled=False)]
            act_plan = [(0, 0, row_devs, None)]
        weight_plan = [
            (0, i * each, each, (layer, pl.ds(i * each, each)), None) for i in range(parts)
        ]
        current = apply_layer(
            all_codes[layer], place, acts, act_plan, [all_weights], weight_plan, all_bias[layer][None]
        )
    return current


def solution(mesh):
    in_specs = (
        P("pipe", "rows"),
        P("pipe", "rows", None, None),
        P("pipe", "rows"),
        P("pipe", None),
    )
    out_specs = P("pipe", "rows")
    return jax.shard_map(
        on_device, mesh=mesh, in_specs=in_specs, out_specs=out_specs, check_vma=False
    )
```

time: 1240 us -> 738 us (0.60)
  local copies, waits for them, and re-layouts: 433 us -> 2.07 us
  other arithmetic: 225 us -> 1.51 us
  waiting for transfers between devices: 397 us -> 524 us
  matrix products: 103 us -> 0 us
  Pallas kernels: 0 us -> 86.1 us
  starting transfers between devices: 32.6 us -> 83.8 us
    ppermute x0 -> x88, waiting for transfers between devices: none -> 285 us  [the longest x40 272 us: along_line(): return lax.ppermute(x, 'rows', moves)]
    all_to_all x8 -> x0, waiting for transfers between devices: 238 us -> none  [apply_layer(): lax.all_to_all(outgoing, 'rows', split_axis=0, concat_axis=0, tiled=True)]
    all_to_all x16 -> x0, other arithmetic: 202 us -> none  [apply_layer(): lax.all_to_all(outgoing, 'rows', split_axis=0, concat_axis=0, tiled=True)]
    unnamed x70 -> x4, local copies, waits for them, and re-layouts: 116 us -> 1.11 us
    another operation x16 -> x0, local copies, waits for them, and re-layouts: 104 us -> none  [the longest x8 104 us: apply_layer(): weight_four = weight_now.reshape(blocks_dev, block_len, K, block_len)]
    dot_general x24 -> x0, matrix products: 103 us -> none  [the longest x8 48.9 us: apply_layer(): jnp.einsum('bkmf,bfkg->mbg', gathered, weight_four, preferred_element_typ...]
    pallas_call x0 -> x8, Pallas kernels: none -> 86.1 us  [apply_layer(): pl.pallas_call(kernel, out_shape=jax.ShapeDtypeStruct((rows, neurons), jn...]
    ppermute x0 -> x88, starting transfers between devices: none -> 83.8 us  [the longest x48 47.7 us: to_other_core(): return lax.ppermute(x, 'rows', moves)]
  transfers between devices with their start and end apart: 9 -> 89, of which waited for: 9 -> 32; matrix products, arithmetic and copies ran while one was open for 18% -> 0% of each run, Pallas kernels for 0% -> 0%
where the time goes in v1:
time: 738 us; the launch traced here: 729 us
  waiting for transfers between devices  524 us (71%)
  Pallas kernels  86.1 us (12%)
  starting transfers between devices  83.8 us (11%)
  blocking collectives  16.6 us (2%)
  between operations  15 us (2%)
    ppermute x40, waiting for transfers between devices, along_line(): return lax.ppermute(x, 'rows', moves)  272 us
    all_gather x1, waiting for transfers between devices, on_device(): all_weights = lax.all_gather(weights, 'pipe', axis=0, tiled=True)  238 us
    pallas_call x8, Pallas kernels, apply_layer(): pl.pallas_call(kernel, out_shape=jax.ShapeDtypeStruct((rows, neurons), jn...  86.1 us
    ppermute x48, starting transfers between devices, to_other_core(): return lax.ppermute(x, 'rows', moves)  47.7 us
    ppermute x40, starting transfers between devices, along_line(): return lax.ppermute(x, 'rows', moves)  36.1 us
  transfers between devices with their start and end apart: 89, of which 32 were waited for; matrix products, arithmetic and copies ran while one was open for 0% of the time, Pallas kernels for 0%

profile of v1, /device:TPU:0, one launch (start us, length us, event | category | flops | bytes accessed | tf_op | source)
XLA Modules:
  0.0 728.6 jit_solution(16706105768505559230)
XLA Ops:
  7.3 3.1 collective-permute-start
  11.0 11.4 %collective-permute-done.refs_1_ = bf16[32,8192]{1,0:T(8,128)(2,1)S(1)} collective-permute-done((bf16[32,8192]{1,0:T(8,128)(2,1)}, bf16[32,8192]{1,0:T(8,128)(2,1)S(1)}, u32[]{:S(2)}, u32[]{:S(2)}) %collective-permute-start) | collective-permute-done | bytes 524320 | tf_op jit(solution)/shard_map/ppermute | solution.py:126
  23.3 9.3 %all-gather.1 = bf16[4,2,8192]{2,1,0:T(2,128)(2,1)S(1)} all-gather(bf16[1,2,8192]{2,1,0:T(2,128)(2,1)} %bitcast.22), channel_id=1, replica_groups=mesh['pipe'=4,'rows'=8] {'pipe'}, dimensions={0}, use_global_device_ids=true | all-gather | bytes 163840 | tf_op jit(solution)/shard_map/all_gather | solution.py:194
  36.9 1.5 collective-permute-start.7
  38.4 1.5 collective-permute-start.8
  39.9 11.7 %collective-permute-done.3.refs_4_ = bf16[32,8192]{1,0:T(8,128)(2,1)S(1)} collective-permute-done((bf16[32,8192]{1,0:T(8,128)(2,1)S(1)}, bf16[32,8192]{1,0:T(8,128)(2,1)S(1)}, u32[]{:S(2)}, u32[]{:S(2)}) %collective-permute-start.3) | collective-permute-done | bytes 524320 | tf_op jit(solution)/shard_map/ppermute | solution.py:126
  51.6 1.9 collective-permute-start.9
  53.5 8.4 %collective-permute-done.4.refs_5_ = bf16[32,8192]{1,0:T(8,128)(2,1)S(1)} collective-permute-done((bf16[32,8192]{1,0:T(8,128)(2,1)S(1)}, bf16[32,8192]{1,0:T(8,128)(2,1)S(1)}, u32[]{:S(2)}, u32[]{:S(2)}) %collective-permute-start.4) | collective-permute-done | bytes 524320 | tf_op jit(solution)/shard_map/ppermute | solution.py:126
  61.9 1.9 collective-permute-start.10
  64.7 7.3 %all-gather = s32[4,2,512]{2,1,0:T(2,128)S(1)} all-gather(s32[1,2,512]{2,1,0:T(2,128)S(1)} %fusion.2), channel_id=1, replica_groups=mesh['pipe'=4,'rows'=8] {'pipe'}, dimensions={0}, use_global_device_ids=true | all-gather | bytes 20480 | tf_op jit(solution)/shard_map/all_gather | solution.py:193
  72.1 237.6 %all-gather.4.cloned.1.call-done.refs_12_ = bf16[8,128,64,256]{3,2,1,0:T(8,128)(2,1)} async-done(((bf16[2,128,64,256]{3,2,1,0:T(8,128)(2,1)}), bf16[8,128,64,256]{3,2,1,0:T(8,128)(2,1)}) %all-gather.4.cloned.1.call-update) | async-done | bytes 33554448 | tf_op jit(solution)/shard_map/all_gather | solution.py:195
  310.7 11.4 %shard_map.55.refs_0_ = bf16[32,8192]{1,0:T(8,128)(2,1)S(1)} custom-call(s32[512]{0:T(512)S(1)} %bitcast.21, s32[1]{0:T(128)} %bitcast.3.place, bf16[32,8192]{1,0:T(8,128)(2,1)S(1)} %copy-done, bf16[32,8192]{1,0:T(8,128)(2,1)S(1)} %collective-permute-done.refs_1_, bf16[32,8192]{1,0:T(8,128)(2,1)S(1)} %collective-permute-done.1.refs_2_, ...), custom_call_target="tpu_custom_call" | custom-call | tf_op jit(solution)/shard_map/pallas_call | solution.py:108
  323.7 12.1 %collective-permute-done.11.refs_1_ = bf16[32,8192]{1,0:T(8,128)(2,1)S(1)} collective-permute-done((bf16[32,8192]{1,0:T(8,128)(2,1)S(1)}, bf16[32,8192]{1,0:T(8,128)(2,1)S(1)}, u32[]{:S(2)}, u32[]{:S(2)}) %collective-permute-start.11) | collective-permute-done | bytes 524320 | tf_op jit(solution)/shard_map/ppermute | solution.py:126
  337.9 1.3 collective-permute-start.15
  341.2 13.4 %collective-permute-done.14.refs_4_ = bf16[32,8192]{1,0:T(8,128)(2,1)S(1)} collective-permute-done((bf16[32,8192]{1,0:T(8,128)(2,1)S(1)}, bf16[32,8192]{1,0:T(8,128)(2,1)S(1)}, u32[]{:S(2)}, u32[]{:S(2)}) %collective-permute-start.14) | collective-permute-done | bytes 524320 | tf_op jit(solution)/shard_map/ppermute | solution.py:126
  354.6 1.9 collective-permute-start.20
  356.5 9.1 %collective-permute-done.15.refs_5_ = bf16[32,8192]{1,0:T(8,128)(2,1)S(1)} collective-permute-done((bf16[32,8192]{1,0:T(8,128)(2,1)S(1)}, bf16[32,8192]{1,0:T(8,128)(2,1)S(1)}, u32[]{:S(2)}, u32[]{:S(2)}) %collective-permute-start.15) | collective-permute-done | bytes 524320 | tf_op jit(solution)/shard_map/ppermute | solution.py:126
  365.6 1.9 collective-permute-start.21
  367.6 1.8 collective-permute-done.21.refs_11_
  369.4 10.5 %shard_map.56.refs_0_ = bf16[32,8192]{1,0:T(8,128)(2,1)S(1)} custom-call(s32[512]{0:T(512)S(1)} %bitcast.20, s32[1]{0:T(128)} %bitcast.3.place, bf16[32,8192]{1,0:T(8,128)(2,1)S(1)} %shard_map.55.refs_0_, bf16[32,8192]{1,0:T(8,128)(2,1)S(1)} %collective-permute-done.11.refs_1_, bf16[32,8192]{1,0:T(8,128)(2,1)S(1)} %collective-permute-done.12.refs_2_, ...), custom_call_target="tpu_custom_call" | custom-call | tf_op jit(solution)/shard_map/pallas_call | solution.py:108
  380.7 13.2 %collective-permute-done.22.refs_1_ = bf16[32,8192]{1,0:T(8,128)(2,1)S(1)} collective-permute-done((bf16[32,8192]{1,0:T(8,128)(2,1)S(1)}, bf16[32,8192]{1,0:T(8,128)(2,1)S(1)}, u32[]{:S(2)}, u32[]{:S(2)}) %collective-permute-start.22) | collective-permute-done | bytes 524320 | tf_op jit(solution)/shard_map/ppermute | solution.py:126
  394.7 1.3 collective-permute-start.25
  399.5 11.9 %collective-permute-done.25.refs_4_ = bf16[32,8192]{1,0:T(8,128)(2,1)S(1)} collective-permute-done((bf16[32,8192]{1,0:T(8,128)(2,1)S(1)}, bf16[32,8192]{1,0:T(8,128)(2,1)S(1)}, u32[]{:S(2)}, u32[]{:S(2)}) %collective-permute-start.25) | collective-permute-done | bytes 524320 | tf_op jit(solution)/shard_map/ppermute | solution.py:126
  411.4 1.9 collective-permute-start.31
  413.3 8.9 %collective-permute-done.26.refs_5_ = bf16[32,8192]{1,0:T(8,128)(2,1)S(1)} collective-permute-done((bf16[32,8192]{1,0:T(8,128)(2,1)S(1)}, bf16[32,8192]{1,0:T(8,128)(2,1)S(1)}, u32[]{:S(2)}, u32[]{:S(2)}) %collective-permute-start.26) | collective-permute-done | bytes 524320 | tf_op jit(solution)/shard_map/ppermute | solution.py:126
  422.2 1.9 collective-permute-start.32
  424.1 1.8 collective-permute-done.32.refs_11_
  426.0 10.5 %shard_map.57.refs_0_ = bf16[32,8192]{1,0:T(8,128)(2,1)S(1)} custom-call(s32[512]{0:T(512)S(1)} %bitcast.19, s32[1]{0:T(128)} %bitcast.3.place, bf16[32,8192]{1,0:T(8,128)(2,1)S(1)} %shard_map.56.refs_0_, bf16[32,8192]{1,0:T(8,128)(2,1)S(1)} %collective-permute-done.22.refs_1_, bf16[32,8192]{1,0:T(8,128)(2,1)S(1)} %collective-permute-done.23.refs_2_, ...), custom_call_target="tpu_custom_call" | custom-call | tf_op jit(solution)/shard_map/pallas_call | solution.py:108
  437.3 13.2 %collective-permute-done.33.refs_1_ = bf16[32,8192]{1,0:T(8,128)(2,1)S(1)} collective-permute-done((bf16[32,8192]{1,0:T(8,128)(2,1)S(1)}, bf16[32,8192]{1,0:T(8,128)(2,1)S(1)}, u32[]{:S(2)}, u32[]{:S(2)}) %collective-permute-start.33) | collective-permute-done | bytes 524320 | tf_op jit(solution)/shard_map/ppermute | solution.py:126
  455.8 12.2 %collective-permute-done.36.refs_4_ = bf16[32,8192]{1,0:T(8,128)(2,1)S(1)} collective-permute-done((bf16[32,8192]{1,0:T(8,128)(2,1)S(1)}, bf16[32,8192]{1,0:T(8,128)(2,1)S(1)}, u32[]{:S(2)}, u32[]{:S(2)}) %collective-permute-start.36) | collective-permute-done | bytes 524320 | tf_op jit(solution)/shard_map/ppermute | solution.py:126
  468.1 1.9 collective-permute-start.42
  470.0 9.0 %collective-permute-done.37.refs_5_ = bf16[32,8192]{1,0:T(8,128)(2,1)S(1)} collective-permute-done((bf16[32,8192]{1,0:T(8,128)(2,1)S(1)}, bf16[32,8192]{1,0:T(8,128)(2,1)S(1)}, u32[]{:S(2)}, u32[]{:S(2)}) %collective-permute-start.37) | collective-permute-done | bytes 524320 | tf_op jit(solution)/shard_map/ppermute | solution.py:126
  479.0 1.9 collective-permute-start.43
  481.0 1.8 collective-permute-done.43.refs_11_
  482.8 10.5 %shard_map.58.refs_0_ = bf16[32,8192]{1,0:T(8,128)(2,1)S(1)} custom-call(s32[512]{0:T(512)S(1)} %bitcast.18, s32[1]{0:T(128)} %bitcast.3.place, bf16[32,8192]{1,0:T(8,128)(2,1)S(1)} %shard_map.57.refs_0_, bf16[32,8192]{1,0:T(8,128)(2,1)S(1)} %collective-permute-done.33.refs_1_, bf16[32,8192]{1,0:T(8,128)(2,1)S(1)} %collective-permute-done.34.refs_2_, ...), custom_call_target="tpu_custom_call" | custom-call | tf_op jit(solution)/shard_map/pallas_call | solution.py:108
  494.1 13.3 %collective-permute-done.44.refs_1_ = bf16[32,8192]{1,0:T(8,128)(2,1)S(1)} collective-permute-done((bf16[32,8192]{1,0:T(8,128)(2,1)S(1)}, bf16[32,8192]{1,0:T(8,128)(2,1)S(1)}, u32[]{:S(2)}, u32[]{:S(2)}) %collective-permute-start.44) | collective-permute-done | bytes 524320 | tf_op jit(solution)/shard_map/ppermute | solution.py:126
  512.7 12.1 %collective-permute-done.47.refs_4_ = bf16[32,8192]{1,0:T(8,128)(2,1)S(1)} collective-permute-done((bf16[32,8192]{1,0:T(8,128)(2,1)S(1)}, bf16[32,8192]{1,0:T(8,128)(2,1)S(1)}, u32[]{:S(2)}, u32[]{:S(2)}) %collective-permute-start.47) | collective-permute-done | bytes 524320 | tf_op jit(solution)/shard_map/ppermute | solution.py:126
  524.8 1.9 collective-permute-start.53
  526.7 8.9 %collective-permute-done.48.refs_5_ = bf16[32,8192]{1,0:T(8,128)(2,1)S(1)} collective-permute-done((bf16[32,8192]{1,0:T(8,128)(2,1)S(1)}, bf16[32,8192]{1,0:T(8,128)(2,1)S(1)}, u32[]{:S(2)}, u32[]{:S(2)}) %collective-permute-start.48) | collective-permute-done | bytes 524320 | tf_op jit(solution)/shard_map/ppermute | solution.py:126
  535.6 1.9 collective-permute-start.54
  537.5 1.8 collective-permute-done.54.refs_11_
  539.4 10.7 %shard_map.59.refs_0_ = bf16[32,8192]{1,0:T(8,128)(2,1)S(1)} custom-call(s32[512]{0:T(512)S(1)} %bitcast.17, s32[1]{0:T(128)} %bitcast.3.place, bf16[32,8192]{1,0:T(8,128)(2,1)S(1)} %shard_map.58.refs_0_, bf16[32,8192]{1,0:T(8,128)(2,1)S(1)} %collective-permute-done.44.refs_1_, bf16[32,8192]{1,0:T(8,128)(2,1)S(1)} %collective-permute-done.45.refs_2_, ...), custom_call_target="tpu_custom_call" | custom-call | tf_op jit(solution)/shard_map/pallas_call | solution.py:108
  550.9 13.2 %collective-permute-done.55.refs_1_ = bf16[32,8192]{1,0:T(8,128)(2,1)S(1)} collective-permute-done((bf16[32,8192]{1,0:T(8,128)(2,1)S(1)}, bf16[32,8192]{1,0:T(8,128)(2,1)S(1)}, u32[]{:S(2)}, u32[]{:S(2)}) %collective-permute-start.55) | collective-permute-done | bytes 524320 | tf_op jit(solution)/shard_map/ppermute | solution.py:126
  564.9 1.3 collective-permute-start.58
  569.4 12.2 %collective-permute-done.58.refs_4_ = bf16[32,8192]{1,0:T(8,128)(2,1)S(1)} collective-permute-done((bf16[32,8192]{1,0:T(8,128)(2,1)S(1)}, bf16[32,8192]{1,0:T(8,128)(2,1)S(1)}, u32[]{:S(2)}, u32[]{:S(2)}) %collective-permute-start.58) | collective-permute-done | bytes 524320 | tf_op jit(solution)/shard_map/ppermute | solution.py:126
  581.7 1.9 collective-permute-start.64
  583.6 9.0 %collective-permute-done.59.refs_5_ = bf16[32,8192]{1,0:T(8,128)(2,1)S(1)} collective-permute-done((bf16[32,8192]{1,0:T(8,128)(2,1)S(1)}, bf16[32,8192]{1,0:T(8,128)(2,1)S(1)}, u32[]{:S(2)}, u32[]{:S(2)}) %collective-permute-start.59) | collective-permute-done | bytes 524320 | tf_op jit(solution)/shard_map/ppermute | solution.py:126
  592.6 1.9 collective-permute-start.65
  594.6 1.8 collective-permute-done.65.refs_11_
  596.4 10.5 %shard_map.60.refs_0_ = bf16[32,8192]{1,0:T(8,128)(2,1)S(1)} custom-call(s32[512]{0:T(512)S(1)} %bitcast.16, s32[1]{0:T(128)} %bitcast.3.place, bf16[32,8192]{1,0:T(8,128)(2,1)S(1)} %shard_map.59.refs_0_, bf16[32,8192]{1,0:T(8,128)(2,1)S(1)} %collective-permute-done.55.refs_1_, bf16[32,8192]{1,0:T(8,128)(2,1)S(1)} %collective-permute-done.56.refs_2_, ...), custom_call_target="tpu_custom_call" | custom-call | tf_op jit(solution)/shard_map/pallas_call | solution.py:108
  607.7 13.2 %collective-permute-done.66.refs_1_ = bf16[32,8192]{1,0:T(8,128)(2,1)S(1)} collective-permute-done((bf16[32,8192]{1,0:T(8,128)(2,1)S(1)}, bf16[32,8192]{1,0:T(8,128)(2,1)S(1)}, u32[]{:S(2)}, u32[]{:S(2)}) %collective-permute-start.66) | collective-permute-done | bytes 524320 | tf_op jit(solution)/shard_map/ppermute | solution.py:126
  626.3 12.1 %collective-permute-done.69.refs_4_ = bf16[32,8192]{1,0:T(8,128)(2,1)S(1)} collective-permute-done((bf16[32,8192]{1,0:T(8,128)(2,1)S(1)}, bf16[32,8192]{1,0:T(8,128)(2,1)S(1)}, u32[]{:S(2)}, u32[]{:S(2)}) %collective-permute-start.69) | collective-permute-done | bytes 524320 | tf_op jit(solution)/shard_map/ppermute | solution.py:126
  638.4 1.9 collective-permute-start.75
  640.3 8.9 %collective-permute-done.70.refs_5_ = bf16[32,8192]{1,0:T(8,128)(2,1)S(1)} collective-permute-done((bf16[32,8192]{1,0:T(8,128)(2,1)S(1)}, bf16[32,8192]{1,0:T(8,128)(2,1)S(1)}, u32[]{:S(2)}, u32[]{:S(2)}) %collective-permute-start.70) | collective-permute-done | bytes 524320 | tf_op jit(solution)/shard_map/ppermute | solution.py:126
  649.2 1.9 collective-permute-start.76
  651.1 1.8 collective-permute-done.76.refs_11_
  653.0 10.7 %shard_map.61.refs_0_ = bf16[32,8192]{1,0:T(8,128)(2,1)S(1)} custom-call(s32[512]{0:T(512)S(1)} %bitcast.15, s32[1]{0:T(128)} %bitcast.3.place, bf16[32,8192]{1,0:T(8,128)(2,1)S(1)} %shard_map.60.refs_0_, bf16[32,8192]{1,0:T(8,128)(2,1)S(1)} %collective-permute-done.66.refs_1_, bf16[32,8192]{1,0:T(8,128)(2,1)S(1)} %collective-permute-done.67.refs_2_, ...), custom_call_target="tpu_custom_call" | custom-call | tf_op jit(solution)/shard_map/pallas_call | solution.py:108
  664.5 13.2 %collective-permute-done.77.refs_1_ = bf16[32,8192]{1,0:T(8,128)(2,1)S(1)} collective-permute-done((bf16[32,8192]{1,0:T(8,128)(2,1)S(1)}, bf16[32,8192]{1,0:T(8,128)(2,1)S(1)}, u32[]{:S(2)}, u32[]{:S(2)}) %collective-permute-start.77) | collective-permute-done | bytes 524320 | tf_op jit(solution)/shard_map/ppermute | solution.py:126
  683.1 12.2 %collective-permute-done.80.refs_4_ = bf16[32,8192]{1,0:T(8,128)(2,1)S(1)} collective-permute-done((bf16[32,8192]{1,0:T(8,128)(2,1)S(1)}, bf16[32,8192]{1,0:T(8,128)(2,1)S(1)}, u32[]{:S(2)}, u32[]{:S(2)}) %collective-permute-start.80) | collective-permute-done | bytes 524320 | tf_op jit(solution)/shard_map/ppermute | solution.py:126
  695.3 1.9 collective-permute-start.86
  697.2 9.0 %collective-permute-done.81.refs_5_ = bf16[32,8192]{1,0:T(8,128)(2,1)S(1)} collective-permute-done((bf16[32,8192]{1,0:T(8,128)(2,1)S(1)}, bf16[32,8192]{1,0:T(8,128)(2,1)S(1)}, u32[]{:S(2)}, u32[]{:S(2)}) %collective-permute-start.81) | collective-permute-done | bytes 524320 | tf_op jit(solution)/shard_map/ppermute | solution.py:126
  706.3 1.9 collective-permute-start.87
  708.2 1.8 collective-permute-done.87.refs_11_
  710.1 11.3 %shard_map.62 = bf16[32,8192]{1,0:T(8,128)(2,1)} custom-call(s32[512]{0:T(512)S(1)} %bitcast.14, s32[1]{0:T(128)} %bitcast.3.place, bf16[32,8192]{1,0:T(8,128)(2,1)S(1)} %shard_map.61.refs_0_, bf16[32,8192]{1,0:T(8,128)(2,1)S(1)} %collective-permute-done.77.refs_1_, bf16[32,8192]{1,0:T(8,128)(2,1)S(1)} %collective-permute-done.78.refs_2_, ...), custom_call_target="tpu_custom_call" | custom-call | tf_op jit(solution)/shard_map/pallas_call | solution.py:108
  (135 shorter events, 47.8 us)
Async XLA Ops:
  6.5 303.1 %all-gather.4.cloned.1.call-start = ((), (), s32[]{:S(2)}) async-start(), calls=%async_computation | async-start | bytes 41943040 | tf_op jit(solution)/shard_map/all_gather | solution.py:195
  7.3 15.2 %collective-permute-start = (bf16[32,8192]{1,0:T(8,128)(2,1)}, bf16[32,8192]{1,0:T(8,128)(2,1)S(1)}, u32[]{:S(2)}, u32[]{:S(2)}) collective-permute-start(bf16[32,8192]{1,0:T(8,128)(2,1)} %refs_0_.1), channel_id=1, source_target_pairs={{0,2},{1,3},{2,0},{3,1},{4,6},{5,7},{6,4},{7,5},{8,10},{9,11},{10,... | collective-permute-start | bytes 1572872 | tf_op jit(solution)/shard_map/ppermute | solution.py:126
  10.3 22.3 %collective-permute-start.1 = (bf16[32,8192]{1,0:T(8,128)(2,1)}, bf16[32,8192]{1,0:T(8,128)(2,1)S(1)}, u32[]{:S(2)}, u32[]{:S(2)}) collective-permute-start(bf16[32,8192]{1,0:T(8,128)(2,1)} %refs_0_.1), channel_id=1, source_target_pairs={{2,4},{3,5},{4,2},{5,3},{10,12},{11,13},{12,10},{13,11},{18,20},{1... | collective-permute-start | bytes 1572872 | tf_op jit(solution)/shard_map/ppermute | solution.py:126
  23.2 15.2 %collective-permute-start.5 = (bf16[32,8192]{1,0:T(8,128)(2,1)}, bf16[32,8192]{1,0:T(8,128)(2,1)S(1)}, u32[]{:S(2)}, u32[]{:S(2)}) collective-permute-start(bf16[32,8192]{1,0:T(8,128)(2,1)} %refs_0_.1), channel_id=1, source_target_pairs={{0,1},{1,0},{2,3},{3,2},{4,5},{5,4},{6,7},{7,6},{8,9},{9,8},{10,11... | collective-permute-start | bytes 1572872 | tf_op jit(solution)/shard_map/ppermute | solution.py:131
  32.6 19.0 %collective-permute-start.3 = (bf16[32,8192]{1,0:T(8,128)(2,1)S(1)}, bf16[32,8192]{1,0:T(8,128)(2,1)S(1)}, u32[]{:S(2)}, u32[]{:S(2)}) collective-permute-start(bf16[32,8192]{1,0:T(8,128)(2,1)S(1)} %collective-permute-done.1.refs_2_), channel_id=1, source_target_pairs={{4,6},{5,7},{2,0},{3,1},{12,14},{13,15},{10,8},{11,9},{20,22},{21,... | collective-permute-start | bytes 1572872 | tf_op jit(solution)/shard_map/ppermute | solution.py:126
  33.9 28.0 %collective-permute-start.4 = (bf16[32,8192]{1,0:T(8,128)(2,1)S(1)}, bf16[32,8192]{1,0:T(8,128)(2,1)S(1)}, u32[]{:S(2)}, u32[]{:S(2)}) collective-permute-start(bf16[32,8192]{1,0:T(8,128)(2,1)S(1)} %collective-permute-done.2.refs_3_), channel_id=1, source_target_pairs={{4,6},{5,7},{2,0},{3,1},{12,14},{13,15},{10,8},{11,9},{20,22},{21,... | collective-permute-start | bytes 1572872 | tf_op jit(solution)/shard_map/ppermute | solution.py:126
  36.9 35.1 %collective-permute-start.7 = (bf16[32,8192]{1,0:T(8,128)(2,1)S(1)}, bf16[32,8192]{1,0:T(8,128)(2,1)}, u32[]{:S(2)}, u32[]{:S(2)}) collective-permute-start(bf16[32,8192]{1,0:T(8,128)(2,1)S(1)} %collective-permute-done.1.refs_2_), channel_id=1, source_target_pairs={{2,3},{3,2},{4,5},{5,4},{10,11},{11,10},{12,13},{13,12},{18,19},{1... | collective-permute-start | bytes 1572872 | tf_op jit(solution)/shard_map/ppermute | solution.py:131
  38.4 33.6 %collective-permute-start.6 = (bf16[32,8192]{1,0:T(8,128)(2,1)S(1)}, bf16[32,8192]{1,0:T(8,128)(2,1)}, u32[]{:S(2)}, u32[]{:S(2)}) collective-permute-start(bf16[32,8192]{1,0:T(8,128)(2,1)S(1)} %collective-permute-done.refs_1_), channel_id=1, source_target_pairs={{0,1},{1,0},{2,3},{3,2},{4,5},{5,4},{6,7},{7,6},{8,9},{9,8},{10,11... | collective-permute-start | bytes 1572872 | tf_op jit(solution)/shard_map/ppermute | solution.py:131
  38.4 33.6 %collective-permute-start.8 = (bf16[32,8192]{1,0:T(8,128)(2,1)S(1)}, bf16[32,8192]{1,0:T(8,128)(2,1)}, u32[]{:S(2)}, u32[]{:S(2)}) collective-permute-start(bf16[32,8192]{1,0:T(8,128)(2,1)S(1)} %collective-permute-done.2.refs_3_), channel_id=1, source_target_pairs={{2,3},{3,2},{4,5},{5,4},{10,11},{11,10},{12,13},{13,12},{18,19},{1... | collective-permute-start | bytes 1572872 | tf_op jit(solution)/shard_map/ppermute | solution.py:131
  51.6 20.4 %collective-permute-start.9 = (bf16[32,8192]{1,0:T(8,128)(2,1)S(1)}, bf16[32,8192]{1,0:T(8,128)(2,1)}, u32[]{:S(2)}, u32[]{:S(2)}) collective-permute-start(bf16[32,8192]{1,0:T(8,128)(2,1)S(1)} %collective-permute-done.3.refs_4_), channel_id=1, source_target_pairs={{0,1},{1,0},{6,7},{7,6},{8,9},{9,8},{14,15},{15,14},{16,17},{17,16... | collective-permute-start | bytes 1572872 | tf_op jit(solution)/shard_map/ppermute | solution.py:131
  322.1 13.7 %collective-permute-start.11 = (bf16[32,8192]{1,0:T(8,128)(2,1)S(1)}, bf16[32,8192]{1,0:T(8,128)(2,1)S(1)}, u32[]{:S(2)}, u32[]{:S(2)}) collective-permute-start(bf16[32,8192]{1,0:T(8,128)(2,1)S(1)} %shard_map.55.refs_0_), channel_id=1, source_target_pairs={{0,2},{1,3},{2,0},{3,1},{4,6},{5,7},{6,4},{7,5},{8,10},{9,11},{10,... | collective-permute-start | bytes 1572872 | tf_op jit(solution)/shard_map/ppermute | solution.py:126
  323.0 13.6 %collective-permute-start.12 = (bf16[32,8192]{1,0:T(8,128)(2,1)S(1)}, bf16[32,8192]{1,0:T(8,128)(2,1)S(1)}, u32[]{:S(2)}, u32[]{:S(2)}) collective-permute-start(bf16[32,8192]{1,0:T(8,128)(2,1)S(1)} %shard_map.55.refs_0_), channel_id=1, source_target_pairs={{2,4},{3,5},{4,2},{5,3},{10,12},{11,13},{12,10},{13,11},{18,20},{1... | collective-permute-start | bytes 1572872 | tf_op jit(solution)/shard_map/ppermute | solution.py:126
  336.6 18.0 %collective-permute-start.14 = (bf16[32,8192]{1,0:T(8,128)(2,1)S(1)}, bf16[32,8192]{1,0:T(8,128)(2,1)S(1)}, u32[]{:S(2)}, u32[]{:S(2)}) collective-permute-start(bf16[32,8192]{1,0:T(8,128)(2,1)S(1)} %collective-permute-done.12.refs_2_), channel_id=1, source_target_pairs={{4,6},{5,7},{2,0},{3,1},{12,14},{13,15},{10,8},{11,9},{20,22},{21,... | collective-permute-start | bytes 1572872 | tf_op jit(solution)/shard_map/ppermute | solution.py:126
  337.9 27.7 %collective-permute-start.15 = (bf16[32,8192]{1,0:T(8,128)(2,1)S(1)}, bf16[32,8192]{1,0:T(8,128)(2,1)S(1)}, u32[]{:S(2)}, u32[]{:S(2)}) collective-permute-start(bf16[32,8192]{1,0:T(8,128)(2,1)S(1)} %collective-permute-done.13.refs_3_), channel_id=1, source_target_pairs={{4,6},{5,7},{2,0},{3,1},{12,14},{13,15},{10,8},{11,9},{20,22},{21,... | collective-permute-start | bytes 1572872 | tf_op jit(solution)/shard_map/ppermute | solution.py:126
  339.2 28.3 %collective-permute-start.18 = (bf16[32,8192]{1,0:T(8,128)(2,1)S(1)}, bf16[32,8192]{1,0:T(8,128)(2,1)S(1)}, u32[]{:S(2)}, u32[]{:S(2)}) collective-permute-start(bf16[32,8192]{1,0:T(8,128)(2,1)S(1)} %collective-permute-done.12.refs_2_), channel_id=1, source_target_pairs={{2,3},{3,2},{4,5},{5,4},{10,11},{11,10},{12,13},{13,12},{18,19},{1... | collective-permute-start | bytes 1572872 | tf_op jit(solution)/shard_map/ppermute | solution.py:131
  339.9 27.6 %collective-permute-start.17 = (bf16[32,8192]{1,0:T(8,128)(2,1)S(1)}, bf16[32,8192]{1,0:T(8,128)(2,1)S(1)}, u32[]{:S(2)}, u32[]{:S(2)}) collective-permute-start(bf16[32,8192]{1,0:T(8,128)(2,1)S(1)} %collective-permute-done.11.refs_1_), channel_id=1, source_target_pairs={{0,1},{1,0},{2,3},{3,2},{4,5},{5,4},{6,7},{7,6},{8,9},{9,8},{10,11... | collective-permute-start | bytes 1572872 | tf_op jit(solution)/shard_map/ppermute | solution.py:131
  340.5 27.1 %collective-permute-start.19 = (bf16[32,8192]{1,0:T(8,128)(2,1)S(1)}, bf16[32,8192]{1,0:T(8,128)(2,1)S(1)}, u32[]{:S(2)}, u32[]{:S(2)}) collective-permute-start(bf16[32,8192]{1,0:T(8,128)(2,1)S(1)} %collective-permute-done.13.refs_3_), channel_id=1, source_target_pairs={{2,3},{3,2},{4,5},{5,4},{10,11},{11,10},{12,13},{13,12},{18,19},{1... | collective-permute-start | bytes 1572872 | tf_op jit(solution)/shard_map/ppermute | solution.py:131
  354.6 13.0 %collective-permute-start.20 = (bf16[32,8192]{1,0:T(8,128)(2,1)S(1)}, bf16[32,8192]{1,0:T(8,128)(2,1)S(1)}, u32[]{:S(2)}, u32[]{:S(2)}) collective-permute-start(bf16[32,8192]{1,0:T(8,128)(2,1)S(1)} %collective-permute-done.14.refs_4_), channel_id=1, source_target_pairs={{0,1},{1,0},{6,7},{7,6},{8,9},{9,8},{14,15},{15,14},{16,17},{17,16... | collective-permute-start | bytes 1572872 | tf_op jit(solution)/shard_map/ppermute | solution.py:131
  379.9 14.0 %collective-permute-start.22 = (bf16[32,8192]{1,0:T(8,128)(2,1)S(1)}, bf16[32,8192]{1,0:T(8,128)(2,1)S(1)}, u32[]{:S(2)}, u32[]{:S(2)}) collective-permute-start(bf16[32,8192]{1,0:T(8,128)(2,1)S(1)} %shard_map.56.refs_0_), channel_id=1, source_target_pairs={{0,2},{1,3},{2,0},{3,1},{4,6},{5,7},{6,4},{7,5},{8,10},{9,11},{10,... | collective-permute-start | bytes 1572872 | tf_op jit(solution)/shard_map/ppermute | solution.py:126
  380.0 14.7 %collective-permute-start.23 = (bf16[32,8192]{1,0:T(8,128)(2,1)S(1)}, bf16[32,8192]{1,0:T(8,128)(2,1)S(1)}, u32[]{:S(2)}, u32[]{:S(2)}) collective-permute-start(bf16[32,8192]{1,0:T(8,128)(2,1)S(1)} %shard_map.56.refs_0_), channel_id=1, source_target_pairs={{2,4},{3,5},{4,2},{5,3},{10,12},{11,13},{12,10},{13,11},{18,20},{1... | collective-permute-start | bytes 1572872 | tf_op jit(solution)/shard_map/ppermute | solution.py:126
  394.7 16.6 %collective-permute-start.25 = (bf16[32,8192]{1,0:T(8,128)(2,1)S(1)}, bf16[32,8192]{1,0:T(8,128)(2,1)S(1)}, u32[]{:S(2)}, u32[]{:S(2)}) collective-permute-start(bf16[32,8192]{1,0:T(8,128)(2,1)S(1)} %collective-permute-done.23.refs_2_), channel_id=1, source_target_pairs={{4,6},{5,7},{2,0},{3,1},{12,14},{13,15},{10,8},{11,9},{20,22},{21,... | collective-permute-start | bytes 1572872 | tf_op jit(solution)/shard_map/ppermute | solution.py:126
  396.1 26.1 %collective-permute-start.26 = (bf16[32,8192]{1,0:T(8,128)(2,1)S(1)}, bf16[32,8192]{1,0:T(8,128)(2,1)S(1)}, u32[]{:S(2)}, u32[]{:S(2)}) collective-permute-start(bf16[32,8192]{1,0:T(8,128)(2,1)S(1)} %collective-permute-done.24.refs_3_), channel_id=1, source_target_pairs={{4,6},{5,7},{2,0},{3,1},{12,14},{13,15},{10,8},{11,9},{20,22},{21,... | collective-permute-start | bytes 1572872 | tf_op jit(solution)/shard_map/ppermute | solution.py:126
  397.4 26.7 %collective-permute-start.29 = (bf16[32,8192]{1,0:T(8,128)(2,1)S(1)}, bf16[32,8192]{1,0:T(8,128)(2,1)S(1)}, u32[]{:S(2)}, u32[]{:S(2)}) collective-permute-start(bf16[32,8192]{1,0:T(8,128)(2,1)S(1)} %collective-permute-done.23.refs_2_), channel_id=1, source_target_pairs={{2,3},{3,2},{4,5},{5,4},{10,11},{11,10},{12,13},{13,12},{18,19},{1... | collective-permute-start | bytes 1572872 | tf_op jit(solution)/shard_map/ppermute | solution.py:131
  398.2 25.9 %collective-permute-start.28 = (bf16[32,8192]{1,0:T(8,128)(2,1)S(1)}, bf16[32,8192]{1,0:T(8,128)(2,1)S(1)}, u32[]{:S(2)}, u32[]{:S(2)}) collective-permute-start(bf16[32,8192]{1,0:T(8,128)(2,1)S(1)} %collective-permute-done.22.refs_1_), channel_id=1, source_target_pairs={{0,1},{1,0},{2,3},{3,2},{4,5},{5,4},{6,7},{7,6},{8,9},{9,8},{10,11... | collective-permute-start | bytes 1572872 | tf_op jit(solution)/shard_map/ppermute | solution.py:131
  398.8 25.4 %collective-permute-start.30 = (bf16[32,8192]{1,0:T(8,128)(2,1)S(1)}, bf16[32,8192]{1,0:T(8,128)(2,1)S(1)}, u32[]{:S(2)}, u32[]{:S(2)}) collective-permute-start(bf16[32,8192]{1,0:T(8,128)(2,1)S(1)} %collective-permute-done.24.refs_3_), channel_id=1, source_target_pairs={{2,3},{3,2},{4,5},{5,4},{10,11},{11,10},{12,13},{13,12},{18,19},{1... | collective-permute-start | bytes 1572872 | tf_op jit(solution)/shard_map/ppermute | solution.py:131
  411.4 12.7 %collective-permute-start.31 = (bf16[32,8192]{1,0:T(8,128)(2,1)S(1)}, bf16[32,8192]{1,0:T(8,128)(2,1)S(1)}, u32[]{:S(2)}, u32[]{:S(2)}) collective-permute-start(bf16[32,8192]{1,0:T(8,128)(2,1)S(1)} %collective-permute-done.25.refs_4_), channel_id=1, source_target_pairs={{0,1},{1,0},{6,7},{7,6},{8,9},{9,8},{14,15},{15,14},{16,17},{17,16... | collective-permute-start | bytes 1572872 | tf_op jit(solution)/shard_map/ppermute | solution.py:131
  436.5 14.0 %collective-permute-start.33 = (bf16[32,8192]{1,0:T(8,128)(2,1)S(1)}, bf16[32,8192]{1,0:T(8,128)(2,1)S(1)}, u32[]{:S(2)}, u32[]{:S(2)}) collective-permute-start(bf16[32,8192]{1,0:T(8,128)(2,1)S(1)} %shard_map.57.refs_0_), channel_id=1, source_target_pairs={{0,2},{1,3},{2,0},{3,1},{4,6},{5,7},{6,4},{7,5},{8,10},{9,11},{10,... | collective-permute-start | bytes 1572872 | tf_op jit(solution)/shard_map/ppermute | solution.py:126
  436.6 14.7 %collective-permute-start.34 = (bf16[32,8192]{1,0:T(8,128)(2,1)S(1)}, bf16[32,8192]{1,0:T(8,128)(2,1)S(1)}, u32[]{:S(2)}, u32[]{:S(2)}) collective-permute-start(bf16[32,8192]{1,0:T(8,128)(2,1)S(1)} %shard_map.57.refs_0_), channel_id=1, source_target_pairs={{2,4},{3,5},{4,2},{5,3},{10,12},{11,13},{12,10},{13,11},{18,20},{1... | collective-permute-start | bytes 1572872 | tf_op jit(solution)/shard_map/ppermute | solution.py:126
  451.3 16.8 %collective-permute-start.36 = (bf16[32,8192]{1,0:T(8,128)(2,1)S(1)}, bf16[32,8192]{1,0:T(8,128)(2,1)S(1)}, u32[]{:S(2)}, u32[]{:S(2)}) collective-permute-start(bf16[32,8192]{1,0:T(8,128)(2,1)S(1)} %collective-permute-done.34.refs_2_), channel_id=1, source_target_pairs={{4,6},{5,7},{2,0},{3,1},{12,14},{13,15},{10,8},{11,9},{20,22},{21,... | collective-permute-start | bytes 1572872 | tf_op jit(solution)/shard_map/ppermute | solution.py:126
  452.6 26.4 %collective-permute-start.37 = (bf16[32,8192]{1,0:T(8,128)(2,1)S(1)}, bf16[32,8192]{1,0:T(8,128)(2,1)S(1)}, u32[]{:S(2)}, u32[]{:S(2)}) collective-permute-start(bf16[32,8192]{1,0:T(8,128)(2,1)S(1)} %collective-permute-done.35.refs_3_), channel_id=1, source_target_pairs={{4,6},{5,7},{2,0},{3,1},{12,14},{13,15},{10,8},{11,9},{20,22},{21,... | collective-permute-start | bytes 1572872 | tf_op jit(solution)/shard_map/ppermute | solution.py:126
  453.9 27.0 %collective-permute-start.40 = (bf16[32,8192]{1,0:T(8,128)(2,1)S(1)}, bf16[32,8192]{1,0:T(8,128)(2,1)S(1)}, u32[]{:S(2)}, u32[]{:S(2)}) collective-permute-start(bf16[32,8192]{1,0:T(8,128)(2,1)S(1)} %collective-permute-done.34.refs_2_), channel_id=1, source_target_pairs={{2,3},{3,2},{4,5},{5,4},{10,11},{11,10},{12,13},{13,12},{18,19},{1... | collective-permute-start | bytes 1572872 | tf_op jit(solution)/shard_map/ppermute | solution.py:131
  454.6 26.4 %collective-permute-start.39 = (bf16[32,8192]{1,0:T(8,128)(2,1)S(1)}, bf16[32,8192]{1,0:T(8,128)(2,1)S(1)}, u32[]{:S(2)}, u32[]{:S(2)}) collective-permute-start(bf16[32,8192]{1,0:T(8,128)(2,1)S(1)} %collective-permute-done.33.refs_1_), channel_id=1, source_target_pairs={{0,1},{1,0},{2,3},{3,2},{4,5},{5,4},{6,7},{7,6},{8,9},{9,8},{10,11... | collective-permute-start | bytes 1572872 | tf_op jit(solution)/shard_map/ppermute | solution.py:131
  455.1 25.8 %collective-permute-start.41 = (bf16[32,8192]{1,0:T(8,128)(2,1)S(1)}, bf16[32,8192]{1,0:T(8,128)(2,1)S(1)}, u32[]{:S(2)}, u32[]{:S(2)}) collective-permute-start(bf16[32,8192]{1,0:T(8,128)(2,1)S(1)} %collective-permute-done.35.refs_3_), channel_id=1, source_target_pairs={{2,3},{3,2},{4,5},{5,4},{10,11},{11,10},{12,13},{13,12},{18,19},{1... | collective-permute-start | bytes 1572872 | tf_op jit(solution)/shard_map/ppermute | solution.py:131
  468.1 12.9 %collective-permute-start.42 = (bf16[32,8192]{1,0:T(8,128)(2,1)S(1)}, bf16[32,8192]{1,0:T(8,128)(2,1)S(1)}, u32[]{:S(2)}, u32[]{:S(2)}) collective-permute-start(bf16[32,8192]{1,0:T(8,128)(2,1)S(1)} %collective-permute-done.36.refs_4_), channel_id=1, source_target_pairs={{0,1},{1,0},{6,7},{7,6},{8,9},{9,8},{14,15},{15,14},{16,17},{17,16... | collective-permute-start | bytes 1572872 | tf_op jit(solution)/shard_map/ppermute | solution.py:131
  493.3 14.0 %collective-permute-start.44 = (bf16[32,8192]{1,0:T(8,128)(2,1)S(1)}, bf16[32,8192]{1,0:T(8,128)(2,1)S(1)}, u32[]{:S(2)}, u32[]{:S(2)}) collective-permute-start(bf16[32,8192]{1,0:T(8,128)(2,1)S(1)} %shard_map.58.refs_0_), channel_id=1, source_target_pairs={{0,2},{1,3},{2,0},{3,1},{4,6},{5,7},{6,4},{7,5},{8,10},{9,11},{10,... | collective-permute-start | bytes 1572872 | tf_op jit(solution)/shard_map/ppermute | solution.py:126
  493.4 14.7 %collective-permute-start.45 = (bf16[32,8192]{1,0:T(8,128)(2,1)S(1)}, bf16[32,8192]{1,0:T(8,128)(2,1)S(1)}, u32[]{:S(2)}, u32[]{:S(2)}) collective-permute-start(bf16[32,8192]{1,0:T(8,128)(2,1)S(1)} %shard_map.58.refs_0_), channel_id=1, source_target_pairs={{2,4},{3,5},{4,2},{5,3},{10,12},{11,13},{12,10},{13,11},{18,20},{1... | collective-permute-start | bytes 1572872 | tf_op jit(solution)/shard_map/ppermute | solution.py:126
  508.1 16.7 %collective-permute-start.47 = (bf16[32,8192]{1,0:T(8,128)(2,1)S(1)}, bf16[32,8192]{1,0:T(8,128)(2,1)S(1)}, u32[]{:S(2)}, u32[]{:S(2)}) collective-permute-start(bf16[32,8192]{1,0:T(8,128)(2,1)S(1)} %collective-permute-done.45.refs_2_), channel_id=1, source_target_pairs={{4,6},{5,7},{2,0},{3,1},{12,14},{13,15},{10,8},{11,9},{20,22},{21,... | collective-permute-start | bytes 1572872 | tf_op jit(solution)/shard_map/ppermute | solution.py:126
  509.4 26.1 %collective-permute-start.48 = (bf16[32,8192]{1,0:T(8,128)(2,1)S(1)}, bf16[32,8192]{1,0:T(8,128)(2,1)S(1)}, u32[]{:S(2)}, u32[]{:S(2)}) collective-permute-start(bf16[32,8192]{1,0:T(8,128)(2,1)S(1)} %collective-permute-done.46.refs_3_), channel_id=1, source_target_pairs={{4,6},{5,7},{2,0},{3,1},{12,14},{13,15},{10,8},{11,9},{20,22},{21,... | collective-permute-start | bytes 1572872 | tf_op jit(solution)/shard_map/ppermute | solution.py:126
  510.7 26.7 %collective-permute-start.51 = (bf16[32,8192]{1,0:T(8,128)(2,1)S(1)}, bf16[32,8192]{1,0:T(8,128)(2,1)S(1)}, u32[]{:S(2)}, u32[]{:S(2)}) collective-permute-start(bf16[32,8192]{1,0:T(8,128)(2,1)S(1)} %collective-permute-done.45.refs_2_), channel_id=1, source_target_pairs={{2,3},{3,2},{4,5},{5,4},{10,11},{11,10},{12,13},{13,12},{18,19},{1... | collective-permute-start | bytes 1572872 | tf_op jit(solution)/shard_map/ppermute | solution.py:131
  511.4 26.1 %collective-permute-start.50 = (bf16[32,8192]{1,0:T(8,128)(2,1)S(1)}, bf16[32,8192]{1,0:T(8,128)(2,1)S(1)}, u32[]{:S(2)}, u32[]{:S(2)}) collective-permute-start(bf16[32,8192]{1,0:T(8,128)(2,1)S(1)} %collective-permute-done.44.refs_1_), channel_id=1, source_target_pairs={{0,1},{1,0},{2,3},{3,2},{4,5},{5,4},{6,7},{7,6},{8,9},{9,8},{10,11... | collective-permute-start | bytes 1572872 | tf_op jit(solution)/shard_map/ppermute | solution.py:131
  512.0 25.5 %collective-permute-start.52 = (bf16[32,8192]{1,0:T(8,128)(2,1)S(1)}, bf16[32,8192]{1,0:T(8,128)(2,1)S(1)}, u32[]{:S(2)}, u32[]{:S(2)}) collective-permute-start(bf16[32,8192]{1,0:T(8,128)(2,1)S(1)} %collective-permute-done.46.refs_3_), channel_id=1, source_target_pairs={{2,3},{3,2},{4,5},{5,4},{10,11},{11,10},{12,13},{13,12},{18,19},{1... | collective-permute-start | bytes 1572872 | tf_op jit(solution)/shard_map/ppermute | solution.py:131
  550.1 14.0 %collective-permute-start.55 = (bf16[32,8192]{1,0:T(8,128)(2,1)S(1)}, bf16[32,8192]{1,0:T(8,128)(2,1)S(1)}, u32[]{:S(2)}, u32[]{:S(2)}) collective-permute-start(bf16[32,8192]{1,0:T(8,128)(2,1)S(1)} %shard_map.59.refs_0_), channel_id=1, source_target_pairs={{0,2},{1,3},{2,0},{3,1},{4,6},{5,7},{6,4},{7,5},{8,10},{9,11},{10,... | collective-permute-start | bytes 1572872 | tf_op jit(solution)/shard_map/ppermute | solution.py:126
  550.2 14.7 %collective-permute-start.56 = (bf16[32,8192]{1,0:T(8,128)(2,1)S(1)}, bf16[32,8192]{1,0:T(8,128)(2,1)S(1)}, u32[]{:S(2)}, u32[]{:S(2)}) collective-permute-start(bf16[32,8192]{1,0:T(8,128)(2,1)S(1)} %shard_map.59.refs_0_), channel_id=1, source_target_pairs={{2,4},{3,5},{4,2},{5,3},{10,12},{11,13},{12,10},{13,11},{18,20},{1... | collective-permute-start | bytes 1572872 | tf_op jit(solution)/shard_map/ppermute | solution.py:126
  564.9 16.8 %collective-permute-start.58 = (bf16[32,8192]{1,0:T(8,128)(2,1)S(1)}, bf16[32,8192]{1,0:T(8,128)(2,1)S(1)}, u32[]{:S(2)}, u32[]{:S(2)}) collective-permute-start(bf16[32,8192]{1,0:T(8,128)(2,1)S(1)} %collective-permute-done.56.refs_2_), channel_id=1, source_target_pairs={{4,6},{5,7},{2,0},{3,1},{12,14},{13,15},{10,8},{11,9},{20,22},{21,... | collective-permute-start | bytes 1572872 | tf_op jit(solution)/shard_map/ppermute | solution.py:126
  566.2 26.4 %collective-permute-start.59 = (bf16[32,8192]{1,0:T(8,128)(2,1)S(1)}, bf16[32,8192]{1,0:T(8,128)(2,1)S(1)}, u32[]{:S(2)}, u32[]{:S(2)}) collective-permute-start(bf16[32,8192]{1,0:T(8,128)(2,1)S(1)} %collective-permute-done.57.refs_3_), channel_id=1, source_target_pairs={{4,6},{5,7},{2,0},{3,1},{12,14},{13,15},{10,8},{11,9},{20,22},{21,... | collective-permute-start | bytes 1572872 | tf_op jit(solution)/shard_map/ppermute | solution.py:126
  567.5 27.0 %collective-permute-start.62 = (bf16[32,8192]{1,0:T(8,128)(2,1)S(1)}, bf16[32,8192]{1,0:T(8,128)(2,1)S(1)}, u32[]{:S(2)}, u32[]{:S(2)}) collective-permute-start(bf16[32,8192]{1,0:T(8,128)(2,1)S(1)} %collective-permute-done.56.refs_2_), channel_id=1, source_target_pairs={{2,3},{3,2},{4,5},{5,4},{10,11},{11,10},{12,13},{13,12},{18,19},{1... | collective-permute-start | bytes 1572872 | tf_op jit(solution)/shard_map/ppermute | solution.py:131
  568.2 26.4 %collective-permute-start.61 = (bf16[32,8192]{1,0:T(8,128)(2,1)S(1)}, bf16[32,8192]{1,0:T(8,128)(2,1)S(1)}, u32[]{:S(2)}, u32[]{:S(2)}) collective-permute-start(bf16[32,8192]{1,0:T(8,128)(2,1)S(1)} %collective-permute-done.55.refs_1_), channel_id=1, source_target_pairs={{0,1},{1,0},{2,3},{3,2},{4,5},{5,4},{6,7},{7,6},{8,9},{9,8},{10,11... | collective-permute-start | bytes 1572872 | tf_op jit(solution)/shard_map/ppermute | solution.py:131
  568.7 25.8 %collective-permute-start.63 = (bf16[32,8192]{1,0:T(8,128)(2,1)S(1)}, bf16[32,8192]{1,0:T(8,128)(2,1)S(1)}, u32[]{:S(2)}, u32[]{:S(2)}) collective-permute-start(bf16[32,8192]{1,0:T(8,128)(2,1)S(1)} %collective-permute-done.57.refs_3_), channel_id=1, source_target_pairs={{2,3},{3,2},{4,5},{5,4},{10,11},{11,10},{12,13},{13,12},{18,19},{1... | collective-permute-start | bytes 1572872 | tf_op jit(solution)/shard_map/ppermute | solution.py:131
  581.7 12.9 %collective-permute-start.64 = (bf16[32,8192]{1,0:T(8,128)(2,1)S(1)}, bf16[32,8192]{1,0:T(8,128)(2,1)S(1)}, u32[]{:S(2)}, u32[]{:S(2)}) collective-permute-start(bf16[32,8192]{1,0:T(8,128)(2,1)S(1)} %collective-permute-done.58.refs_4_), channel_id=1, source_target_pairs={{0,1},{1,0},{6,7},{7,6},{8,9},{9,8},{14,15},{15,14},{16,17},{17,16... | collective-permute-start | bytes 1572872 | tf_op jit(solution)/shard_map/ppermute | solution.py:131
  606.9 14.0 %collective-permute-start.66 = (bf16[32,8192]{1,0:T(8,128)(2,1)S(1)}, bf16[32,8192]{1,0:T(8,128)(2,1)S(1)}, u32[]{:S(2)}, u32[]{:S(2)}) collective-permute-start(bf16[32,8192]{1,0:T(8,128)(2,1)S(1)} %shard_map.60.refs_0_), channel_id=1, source_target_pairs={{0,2},{1,3},{2,0},{3,1},{4,6},{5,7},{6,4},{7,5},{8,10},{9,11},{10,... | collective-permute-start | bytes 1572872 | tf_op jit(solution)/shard_map/ppermute | solution.py:126
  607.0 14.7 %collective-permute-start.67 = (bf16[32,8192]{1,0:T(8,128)(2,1)S(1)}, bf16[32,8192]{1,0:T(8,128)(2,1)S(1)}, u32[]{:S(2)}, u32[]{:S(2)}) collective-permute-start(bf16[32,8192]{1,0:T(8,128)(2,1)S(1)} %shard_map.60.refs_0_), channel_id=1, source_target_pairs={{2,4},{3,5},{4,2},{5,3},{10,12},{11,13},{12,10},{13,11},{18,20},{1... | collective-permute-start | bytes 1572872 | tf_op jit(solution)/shard_map/ppermute | solution.py:126
  621.7 16.7 %collective-permute-start.69 = (bf16[32,8192]{1,0:T(8,128)(2,1)S(1)}, bf16[32,8192]{1,0:T(8,128)(2,1)S(1)}, u32[]{:S(2)}, u32[]{:S(2)}) collective-permute-start(bf16[32,8192]{1,0:T(8,128)(2,1)S(1)} %collective-permute-done.67.refs_2_), channel_id=1, source_target_pairs={{4,6},{5,7},{2,0},{3,1},{12,14},{13,15},{10,8},{11,9},{20,22},{21,... | collective-permute-start | bytes 1572872 | tf_op jit(solution)/shard_map/ppermute | solution.py:126
  623.0 26.1 %collective-permute-start.70 = (bf16[32,8192]{1,0:T(8,128)(2,1)S(1)}, bf16[32,8192]{1,0:T(8,128)(2,1)S(1)}, u32[]{:S(2)}, u32[]{:S(2)}) collective-permute-start(bf16[32,8192]{1,0:T(8,128)(2,1)S(1)} %collective-permute-done.68.refs_3_), channel_id=1, source_target_pairs={{4,6},{5,7},{2,0},{3,1},{12,14},{13,15},{10,8},{11,9},{20,22},{21,... | collective-permute-start | bytes 1572872 | tf_op jit(solution)/shard_map/ppermute | solution.py:126
  624.3 26.8 %collective-permute-start.73 = (bf16[32,8192]{1,0:T(8,128)(2,1)S(1)}, bf16[32,8192]{1,0:T(8,128)(2,1)S(1)}, u32[]{:S(2)}, u32[]{:S(2)}) collective-permute-start(bf16[32,8192]{1,0:T(8,128)(2,1)S(1)} %collective-permute-done.67.refs_2_), channel_id=1, source_target_pairs={{2,3},{3,2},{4,5},{5,4},{10,11},{11,10},{12,13},{13,12},{18,19},{1... | collective-permute-start | bytes 1572872 | tf_op jit(solution)/shard_map/ppermute | solution.py:131
  625.0 26.1 %collective-permute-start.72 = (bf16[32,8192]{1,0:T(8,128)(2,1)S(1)}, bf16[32,8192]{1,0:T(8,128)(2,1)S(1)}, u32[]{:S(2)}, u32[]{:S(2)}) collective-permute-start(bf16[32,8192]{1,0:T(8,128)(2,1)S(1)} %collective-permute-done.66.refs_1_), channel_id=1, source_target_pairs={{0,1},{1,0},{2,3},{3,2},{4,5},{5,4},{6,7},{7,6},{8,9},{9,8},{10,11... | collective-permute-start | bytes 1572872 | tf_op jit(solution)/shard_map/ppermute | solution.py:131
  625.6 25.5 %collective-permute-start.74 = (bf16[32,8192]{1,0:T(8,128)(2,1)S(1)}, bf16[32,8192]{1,0:T(8,128)(2,1)S(1)}, u32[]{:S(2)}, u32[]{:S(2)}) collective-permute-start(bf16[32,8192]{1,0:T(8,128)(2,1)S(1)} %collective-permute-done.68.refs_3_), channel_id=1, source_target_pairs={{2,3},{3,2},{4,5},{5,4},{10,11},{11,10},{12,13},{13,12},{18,19},{1... | collective-permute-start | bytes 1572872 | tf_op jit(solution)/shard_map/ppermute | solution.py:131
  663.7 14.0 %collective-permute-start.77 = (bf16[32,8192]{1,0:T(8,128)(2,1)S(1)}, bf16[32,8192]{1,0:T(8,128)(2,1)S(1)}, u32[]{:S(2)}, u32[]{:S(2)}) collective-permute-start(bf16[32,8192]{1,0:T(8,128)(2,1)S(1)} %shard_map.61.refs_0_), channel_id=1, source_target_pairs={{0,2},{1,3},{2,0},{3,1},{4,6},{5,7},{6,4},{7,5},{8,10},{9,11},{10,... | collective-permute-start | bytes 1572872 | tf_op jit(solution)/shard_map/ppermute | solution.py:126
  663.8 14.7 %collective-permute-start.78 = (bf16[32,8192]{1,0:T(8,128)(2,1)S(1)}, bf16[32,8192]{1,0:T(8,128)(2,1)S(1)}, u32[]{:S(2)}, u32[]{:S(2)}) collective-permute-start(bf16[32,8192]{1,0:T(8,128)(2,1)S(1)} %shard_map.61.refs_0_), channel_id=1, source_target_pairs={{2,4},{3,5},{4,2},{5,3},{10,12},{11,13},{12,10},{13,11},{18,20},{1... | collective-permute-start | bytes 1572872 | tf_op jit(solution)/shard_map/ppermute | solution.py:126
  678.5 16.8 %collective-permute-start.80 = (bf16[32,8192]{1,0:T(8,128)(2,1)S(1)}, bf16[32,8192]{1,0:T(8,128)(2,1)S(1)}, u32[]{:S(2)}, u32[]{:S(2)}) collective-permute-start(bf16[32,8192]{1,0:T(8,128)(2,1)S(1)} %collective-permute-done.78.refs_2_), channel_id=1, source_target_pairs={{4,6},{5,7},{2,0},{3,1},{12,14},{13,15},{10,8},{11,9},{20,22},{21,... | collective-permute-start | bytes 1572872 | tf_op jit(solution)/shard_map/ppermute | solution.py:126
  679.8 26.4 %collective-permute-start.81 = (bf16[32,8192]{1,0:T(8,128)(2,1)S(1)}, bf16[32,8192]{1,0:T(8,128)(2,1)S(1)}, u32[]{:S(2)}, u32[]{:S(2)}) collective-permute-start(bf16[32,8192]{1,0:T(8,128)(2,1)S(1)} %collective-permute-done.79.refs_3_), channel_id=1, source_target_pairs={{4,6},{5,7},{2,0},{3,1},{12,14},{13,15},{10,8},{11,9},{20,22},{21,... | collective-permute-start | bytes 1572872 | tf_op jit(solution)/shard_map/ppermute | solution.py:126
  681.1 27.0 %collective-permute-start.84 = (bf16[32,8192]{1,0:T(8,128)(2,1)S(1)}, bf16[32,8192]{1,0:T(8,128)(2,1)S(1)}, u32[]{:S(2)}, u32[]{:S(2)}) collective-permute-start(bf16[32,8192]{1,0:T(8,128)(2,1)S(1)} %collective-permute-done.78.refs_2_), channel_id=1, source_target_pairs={{2,3},{3,2},{4,5},{5,4},{10,11},{11,10},{12,13},{13,12},{18,19},{1... | collective-permute-start | bytes 1572872 | tf_op jit(solution)/shard_map/ppermute | solution.py:131
  681.8 26.4 %collective-permute-start.83 = (bf16[32,8192]{1,0:T(8,128)(2,1)S(1)}, bf16[32,8192]{1,0:T(8,128)(2,1)S(1)}, u32[]{:S(2)}, u32[]{:S(2)}) collective-permute-start(bf16[32,8192]{1,0:T(8,128)(2,1)S(1)} %collective-permute-done.77.refs_1_), channel_id=1, source_target_pairs={{0,1},{1,0},{2,3},{3,2},{4,5},{5,4},{6,7},{7,6},{8,9},{9,8},{10,11... | collective-permute-start | bytes 1572872 | tf_op jit(solution)/shard_map/ppermute | solution.py:131
  682.4 25.8 %collective-permute-start.85 = (bf16[32,8192]{1,0:T(8,128)(2,1)S(1)}, bf16[32,8192]{1,0:T(8,128)(2,1)S(1)}, u32[]{:S(2)}, u32[]{:S(2)}) collective-permute-start(bf16[32,8192]{1,0:T(8,128)(2,1)S(1)} %collective-permute-done.79.refs_3_), channel_id=1, source_target_pairs={{2,3},{3,2},{4,5},{5,4},{10,11},{11,10},{12,13},{13,12},{18,19},{1... | collective-permute-start | bytes 1572872 | tf_op jit(solution)/shard_map/ppermute | solution.py:131
  695.3 12.9 %collective-permute-start.86 = (bf16[32,8192]{1,0:T(8,128)(2,1)S(1)}, bf16[32,8192]{1,0:T(8,128)(2,1)S(1)}, u32[]{:S(2)}, u32[]{:S(2)}) collective-permute-start(bf16[32,8192]{1,0:T(8,128)(2,1)S(1)} %collective-permute-done.80.refs_4_), channel_id=1, source_target_pairs={{0,1},{1,0},{6,7},{7,6},{8,9},{9,8},{14,15},{15,14},{16,17},{17,16... | collective-permute-start | bytes 1572872 | tf_op jit(solution)/shard_map/ppermute | solution.py:131
  (26 other events, 117.0 us)
Sparse Core Ops, SparseCore 0:
  9.2 300.3 all-gather.3

commit v2 on v1

v2 whole, which is shorter than its diff:
```python
import functools
import random

import jax
import jax.numpy as jnp
import numpy as np
from jax import lax
from jax.experimental import pallas as pl
from jax.experimental.pallas import tpu as pltpu
from jax.sharding import PartitionSpec as P

BLOCK = 64
K = 4
LANES = 128
CORES = 2
WEIGHT_PARTS = 4
STREAM_SEED = 486
LAYER_VMEM = 10 * 2**20
SMALL_VMEM = 2 * 2**20

clamp_top = 32.0


def bits_for(count):
    return (count - 1).bit_length()


def start_if(copy, place, want):
    if want is None:
        copy.start()
    else:
        pl.when(place[want[0]] == want[1])(copy.start)


def layer_kernel(act_plan, unroll, codes, place, *refs):
    n_acts = 1 + max(p[0] for p in act_plan)
    acts = refs[:n_acts]
    weights, bias, out, held, masks, act_sem = refs[n_acts:]
    rows = out.shape[0]
    blocks = weights.shape[0]
    pair_bits = bits_for(held.shape[2] // LANES)

    def act_copy(operand, slot, slots):
        src = acts[operand] if slots == 1 else acts[operand].at[:]
        dst = held.at[slot] if slots == 1 else held.at[pl.ds(slot, slots)]
        return pltpu.make_async_copy(src, dst, act_sem.at[slot])

    for operand, slot, slots, want in act_plan:
        start_if(act_copy(operand, slot, slots), place, want)

    low = lax.broadcasted_iota(jnp.int32, (rows, LANES), 1) < BLOCK
    masks[0] = jnp.where(low, 1.0, 0.0).astype(jnp.bfloat16)
    masks[1] = jnp.where(low, 0.0, 1.0).astype(jnp.bfloat16)

    waited = set()
    for operand, slot, slots, _ in act_plan:
        if slot not in waited:
            waited.add(slot)
            act_copy(operand, slot, slots).wait()

    def products(block):
        parts = []
        for k in range(K):
            code = codes[block * K + k]
            pair = (code >> 1) & (2**pair_bits - 1)
            columns = pl.ds(pl.multiple_of(pair * LANES, LANES), LANES)
            parts.append(held[code >> (1 + pair_bits), :, columns] * masks[code & 1])
        left = jnp.concatenate(
            [
                jnp.concatenate([parts[0], parts[2]], axis=1),
                jnp.concatenate([parts[1], parts[3]], axis=1),
            ],
            axis=0,
        )
        w = weights[block]
        first, second = w[:, :LANES], w[:, LANES:]
        right = jnp.concatenate([first, first, second, second], axis=0)
        return jnp.dot(left, right, preferred_element_type=jnp.float32)

    def two_blocks(q, _):
        a, b = products(2 * q), products(2 * q + 1)
        even = a[:rows] + pltpu.roll(a[rows:], BLOCK, 1)
        odd = b[rows:] + pltpu.roll(b[:rows], BLOCK, 1)
        columns = pl.ds(pl.multiple_of(q * LANES, LANES), LANES)
        total = jnp.where(low, even, odd) + bias[:, columns].astype(jnp.float32)
        out[:, columns] = jnp.clip(total, 0.0, clamp_top).astype(jnp.bfloat16)
        return 0

    lax.fori_loop(0, blocks // 2, two_blocks, 0, unroll=min(unroll, blocks // 2))


def gather_weights_kernel(plan, place, *refs):
    sources, out, sem = refs[:-2], refs[-2], refs[-1]

    def copy(operand, first, count, index):
        source = sources[operand] if index is None else sources[operand].at[index]
        return pltpu.make_async_copy(source, out.at[pl.ds(first, count)], sem.at[first])

    for operand, first, count, index, want in plan:
        start_if(copy(operand, first, count, index), place, want)
    for first, (operand, count, index) in {p[1]: (p[0], p[2], p[3]) for p in plan}.items():
        copy(operand, first, count, index).wait()


def gather_weights(place, weights, plan, shape):
    smem = pl.BlockSpec(memory_space=pltpu.SMEM)
    return pl.pallas_call(
        functools.partial(gather_weights_kernel, plan),
        out_shape=pltpu.VMEM(shape, jnp.bfloat16),
        in_specs=[smem] + [pl.BlockSpec(memory_space=pl.ANY)] * len(weights),
        out_specs=pl.BlockSpec(memory_space=pltpu.VMEM),
        scratch_shapes=[pltpu.SemaphoreType.DMA((shape[0],))],
        compiler_params=pltpu.CompilerParams(vmem_limit_bytes=SMALL_VMEM),
    )(place, *weights)


def apply_layer(codes, place, acts, act_plan, weights, bias):
    slots = sum(
        count for slot, count in {(slot, count) for _, slot, count, _ in act_plan}
    )
    rows, neurons = acts[0].shape[-2:]
    held = (slots, rows, neurons)
    smem = pl.BlockSpec(memory_space=pltpu.SMEM)
    anywhere = pl.BlockSpec(memory_space=pl.ANY)
    vmem = pl.BlockSpec(memory_space=pltpu.VMEM)
    kernel = functools.partial(layer_kernel, act_plan, 16)
    return pl.pallas_call(
        kernel,
        out_shape=jax.ShapeDtypeStruct((rows, neurons), jnp.bfloat16),
        in_specs=[smem, smem] + [anywhere] * len(acts) + [vmem, vmem],
        out_specs=vmem,
        scratch_shapes=[
            pltpu.VMEM(held, jnp.bfloat16),
            pltpu.VMEM((2, rows, LANES), jnp.bfloat16),
            pltpu.SemaphoreType.DMA((slots,)),
        ],
        compiler_params=pltpu.CompilerParams(vmem_limit_bytes=LAYER_VMEM),
    )(codes, place, *acts, weights, bias)


def along_line(x, pairs):
    moves = [(a * CORES + c, b * CORES + c) for a, b in pairs for c in range(CORES)]
    return lax.ppermute(x, "rows", moves)


def to_other_core(x):
    return lax.ppermute(x, "rows", [(i, i ^ 1) for i in range(lax.axis_size("rows"))])


def gather_line(x, pause):
    near = along_line(x, [(0, 1), (1, 0), (2, 3), (3, 2)])
    cross = along_line(x, [(1, 2), (2, 1), (0, 3), (3, 0)])
    x_swapped = to_other_core(x)
    near, cross = pause(x_swapped, [near, cross])
    far = along_line(near, [(1, 2), (2, 1)])
    outer = along_line(cross, [(2, 3), (1, 0)])
    near_swapped = to_other_core(near)
    far, outer = pause(near_swapped, [far, outer])
    rest = [cross, far, outer]
    return [x, near] + rest + [x_swapped, near_swapped] + [to_other_core(buf) for buf in rest]


def line_plan():
    plan = []
    for side in range(CORES):
        for buf, (slot, want) in enumerate([(0, None), (1, None), (2, None), (3, (0, 1)), (3, (0, 0))]):
            plan.append((side * 5 + buf, side * 4 + slot, 1, want))
    return plan


def line_slots(row_devs):
    table = np.zeros((row_devs, row_devs), np.int32)
    chips = row_devs // CORES
    for me in range(row_devs):
        for owner in range(row_devs):
            z, c = divmod(me, CORES)
            oz, oc = divmod(owner, CORES)
            if oz // 2 == z // 2:
                slot = 0 if oz == z else 1
            else:
                across = chips - 1 - z
                slot = 2 if oz == across else 3
            table[me, owner] = (c != oc) * chips + slot
    return table


def stream_order(seed, layers, parts, square):
    draw = random.Random(seed)
    each = layers // square
    links = [(u, u ^ 1) for u in range(square)] + [(u, u ^ 2) for u in range(square)]
    pieces = [(layer, q) for layer in range(layers) for q in range(parts)]
    have = {(p, piece): 0 for p in range(square) for piece in pieces if piece[0] // each == p}
    noise, direct, spread = draw.choice([0, 0.3, 1, 2]), draw.choice([0, 1, 2]), draw.choice([0, 0.5, 1, 2])
    slots = []
    while len(have) < square * len(pieces):
        now, sends = len(slots), []
        taken = set()
        order = links[:]
        draw.shuffle(order)
        if now == 0:
            sends = [(u, v, (u * each, 0 if u ^ v == 1 else 1)) for u, v in links]
            order = []
        for u, v in order:
            best = None
            for piece in pieces:
                if (v, piece) in have or (v, piece) in taken or have.get((u, piece), now + 1) > now:
                    continue
                w = v ^ 1 if u == v ^ 2 else v ^ 2
                holders = sum((p, piece) in have or (p, piece) in taken for p in range(square))
                also = have.get((w, piece), now + 1) <= now
                key = piece[0] * 4 + direct * also + spread * holders + noise * draw.random()
                if best is None or key < best[0]:
                    best = (key, piece)
            if best is not None:
                taken.add((v, best[1]))
                sends.append((u, v, best[1]))
        for u, v, piece in sends:
            have[v, piece] = now + 1
        slots.append(sends)
    ready = [max(have[p, (layer, q)] for p in range(square) for q in range(parts)) for layer in range(layers)]
    return slots, ready


def pick_kernel(choices, count, place, *refs):
    sources, outs, sems = refs[:-count - 1], refs[-count - 1 : -1], refs[-1]

    def copy_for(p):
        copies = []
        for n, per_device in enumerate(choices):
            operand, index = per_device[p]
            source = sources[operand] if index is None else sources[operand].at[index]
            copies.append(pltpu.make_async_copy(source, outs[n], sems.at[n]))
        for copy in copies:
            copy.start()
        for copy in copies:
            copy.wait()

    for p in range(len(choices[0])):
        pl.when(place[1] == p)(functools.partial(copy_for, p))


def pick(place, operands, choices, shape):
    smem = pl.BlockSpec(memory_space=pltpu.SMEM)
    return pl.pallas_call(
        functools.partial(pick_kernel, choices, len(choices)),
        out_shape=[pltpu.VMEM(shape, jnp.bfloat16)] * len(choices),
        in_specs=[smem] + [pl.BlockSpec(memory_space=pl.ANY)] * len(operands),
        out_specs=[pl.BlockSpec(memory_space=pltpu.VMEM)] * len(choices),
        scratch_shapes=[pltpu.SemaphoreType.DMA((len(choices),))],
        compiler_params=pltpu.CompilerParams(vmem_limit_bytes=SMALL_VMEM),
    )(place, *operands)


class WeightStream:
    def __init__(self, weights, place, square, parts):
        self.weights, self.place = weights, place
        self.sections, self.parts = weights.shape[0], parts
        self.each = weights.shape[1] // parts
        self.slots, self.ready = stream_order(STREAM_SEED, square * self.sections, parts, square)
        self.square = square
        self.arrays = {}
        self.where = {}
        self.flying = []
        self.started = 0
        self.gathered = {}

    def source(self, p, piece):
        if piece is None:
            piece = (p * self.sections, 0)
        if (p, piece) in self.where:
            return self.where[p, piece], None
        return "own", (piece[0] % self.sections, pl.ds(piece[1] * self.each, self.each))

    def array(self, name):
        return self.weights if name == "own" else self.arrays[name]

    def advance(self, after=(), through=(), layer=None):
        sends = self.slots[self.started] if self.started < len(self.slots) else []
        sides = {}
        for u, v, piece in sends:
            sides.setdefault(u ^ v, {})[u] = piece
        chosen = {side: [self.source(p, by.get(p)) for p in range(self.square)] for side, by in sorted(sides.items())}
        names = sorted({name for items in chosen.values() for name, _ in items}, key=str)
        keys = self.flying + [n for n in names if n != "own" and n not in self.flying]
        _, held = lax.optimization_barrier((list(after), [self.arrays[k] for k in keys]))
        for key, value in zip(keys, held):
            self.arrays[key] = value
        self.flying = []
        made = []
        if layer is not None and self.started >= self.ready[layer]:
            self.gathered[layer] = self.gather(layer)
            made = [self.gathered[layer]]
        if not sends:
            return lax.optimization_barrier((list(through), made))[0]
        choices = [[(names.index(name), index) for name, index in items] for items in chosen.values()]
        shape = (self.each,) + self.weights.shape[2:]
        if self.started == 0:
            picked = [self.weights[0, q * self.each : (q + 1) * self.each] for q in range(2)]
        else:
            picked = pick(self.place, [self.array(n) for n in names], choices, shape)
        for side, array in zip(chosen, picked):
            key = ("got", self.started, side)
            self.arrays[key] = lax.ppermute(array, "pipe", [(p, p ^ side) for p in range(self.square)])
            self.flying.append(key)
        for u, v, piece in sends:
            self.where[v, piece] = ("got", self.started, u ^ v)
        self.started += 1
        return lax.optimization_barrier((list(through), made + list(picked)))[0]

    def gather(self, layer):
        if layer in self.gathered:
            return self.gathered[layer]
        names, plan = [], []
        for q in range(self.parts):
            for p in range(self.square):
                name, index = self.source(p, (layer, q))
                if name not in names:
                    names.append(name)
                plan.append((names.index(name), q * self.each, self.each, index, (1, p)))
        shape = self.weights.shape[1:]
        return gather_weights(self.place, [self.array(name) for name in names], plan, shape)


def gather_square(x):
    mine = lax.axis_index("pipe")
    got = [x] + [lax.ppermute(x, "pipe", [(p, p ^ side) for p in range(4)]) for side in (1, 2, 3)]
    got = jnp.stack(got)
    return jnp.concatenate([lax.dynamic_index_in_dim(got, p ^ mine, 0, keepdims=False) for p in range(4)])


def on_device(features, weights, bias, layout):
    row_devs = lax.axis_size("rows")
    my_row = lax.axis_index("rows")
    neurons = features.shape[1]
    blocks = neurons // BLOCK
    slot_count = blocks * K
    pairs = neurons // LANES
    is_line = row_devs == 4 * CORES and lax.axis_size("pipe") == 4

    mine = lax.dynamic_slice_in_dim(layout, my_row * slot_count, slot_count, axis=1)
    owners, local = mine // blocks, mine % blocks
    table = line_slots(row_devs) if is_line else np.tile(np.arange(row_devs, dtype=np.int32), (row_devs, 1))
    my_slots = lax.dynamic_index_in_dim(jnp.asarray(table), my_row, 0, keepdims=False)
    hit = owners[:, :, None] == jnp.arange(row_devs)[None, None, :]
    slots = jnp.sum(jnp.where(hit, my_slots[None, None, :], 0), axis=2)
    codes = (((slots << bits_for(pairs)) | (local // 2)) << 1) | (local % 2)

    if is_line:
        all_codes, all_bias = gather_square(codes), gather_square(bias)
    else:
        all_codes = lax.all_gather(codes, "pipe", axis=0, tiled=True)
        all_bias = lax.all_gather(bias, "pipe", axis=0, tiled=True)
    z = my_row // CORES
    is_middle = (z > 0) & (z < row_devs // CORES - 1)
    place = jnp.stack([is_middle.astype(jnp.int32), lax.axis_index("pipe").astype(jnp.int32)])
    layers = weights.shape[0] * lax.axis_size("pipe")

    current = features
    if is_line:
        stream = WeightStream(weights, place, 4, WEIGHT_PARTS)
        stream.advance()
        for layer in range(layers):
            step = 0

            def pause(arrived, through):
                nonlocal step, all_codes, all_bias
                step += 1
                if layer == 0 and step == 1:
                    arrived, all_codes, all_bias = lax.optimization_barrier((arrived, all_codes, all_bias))
                return stream.advance([arrived], through, layer if step == 2 else None)

            acts = gather_line(current, pause)
            while stream.started < stream.ready[layer] + (layer == 0):
                stream.advance()
            current = apply_layer(
                all_codes[layer], place, acts, line_plan(), stream.gather(layer), all_bias[layer][None]
            )
        return current

    all_weights = lax.all_gather(weights, "pipe", axis=0, tiled=True)
    for layer in range(layers):
        acts = [lax.all_gather(current, "rows", axis=0, tiled=False)]
        act_plan = [(0, 0, row_devs, None)]
        current = apply_layer(
            all_codes[layer], place, acts, act_plan, all_weights[layer], all_bias[layer][None]
        )
    return current


def solution(mesh):
    in_specs = (
        P("pipe", "rows"),
        P("pipe", "rows", None, None),
        P("pipe", "rows"),
        P("pipe", None),
    )
    out_specs = P("pipe", "rows")
    return jax.shard_map(
        on_device, mesh=mesh, in_specs=in_specs, out_specs=out_specs, check_vma=False
    )
```

time: 738 us -> 487 us (0.66); the launches traced: 729 us -> 486 us
  waiting for transfers between devices: 524 us -> 330 us
  Pallas kernels: 86.1 us -> 60.7 us
  blocking collectives: 16.6 us -> 0 us
  between operations: 15 us -> 0.89 us
  local copies, waits for them, and re-layouts: 2.07 us -> 10.5 us
    all_gather x1 -> x0, waiting for transfers between devices: 238 us -> none  [on_device(): all_weights = lax.all_gather(weights, 'pipe', axis=0, tiled=True)]
    ppermute x48 -> x70, waiting for transfers between devices: 12.9 us -> 166 us  [the longest x24 138 us: advance(): lax.ppermute(array, 'pipe', [(p, p ^ side) for p in range(self.square)])]
    ppermute x40 -> x32, waiting for transfers between devices: 272 us -> 164 us  [along_line(): return lax.ppermute(x, 'rows', moves)]
    pallas_call x8, Pallas kernels: 86.1 us -> 33.2 us  [apply_layer(): pl.pallas_call(kernel, out_shape=jax.ShapeDtypeStruct((rows, neurons), jn...]
    pallas_call x0 -> x19, Pallas kernels: none -> 27.5 us  [the longest x8 17.9 us: gather_weights(): pl.pallas_call(functools.partial(gather_weights_kernel, plan), out_shape=...]
    all_gather x2 -> x0, blocking collectives: 16.6 us -> none  [the longest x1 9.31 us: on_device(): all_bias = lax.all_gather(bias, 'pipe', axis=0, tiled=True)]
    ppermute x48 -> x70, starting transfers between devices: 47.7 us -> 44.5 us  [the longest x24 28.8 us: advance(): lax.ppermute(array, 'pipe', [(p, p ^ side) for p in range(self.square)])]
    ppermute x40 -> x32, starting transfers between devices: 36.1 us -> 37.4 us  [along_line(): return lax.ppermute(x, 'rows', moves)]
  transfers between devices with their start and end apart: 89 -> 102, of which waited for: 32 -> 48; matrix products, arithmetic and copies ran while one was open for 0% -> 1% of each run, Pallas kernels for 0% -> 10%
where the time goes in v2:
time: 487 us; the launch traced here: 486 us
  waiting for transfers between devices  330 us (68%)
  starting transfers between devices  81.8 us (17%)
  Pallas kernels  60.7 us (12%)
  local copies, waits for them, and re-layouts  10.5 us (2%)
    ppermute x32, waiting for transfers between devices, along_line(): return lax.ppermute(x, 'rows', moves)  164 us
    ppermute x24, waiting for transfers between devices, advance(): lax.ppermute(array, 'pipe', [(p, p ^ side) for p in range(self.square)])  138 us
    ppermute x32, starting transfers between devices, along_line(): return lax.ppermute(x, 'rows', moves)  37.4 us
    pallas_call x8, Pallas kernels, apply_layer(): pl.pallas_call(kernel, out_shape=jax.ShapeDtypeStruct((rows, neurons), jn...  33.2 us
    ppermute x24, starting transfers between devices, advance(): lax.ppermute(array, 'pipe', [(p, p ^ side) for p in range(self.square)])  28.8 us
    ppermute x6, waiting for transfers between devices, gather_square(): lax.ppermute(x, 'pipe', [(p, p ^ side) for p in range(4)])  19.2 us
    pallas_call x8, Pallas kernels, gather_weights(): pl.pallas_call(functools.partial(gather_weights_kernel, plan), out_shape=...  17.9 us
  transfers between devices with their start and end apart: 102, of which 48 were waited for; matrix products, arithmetic and copies ran while one was open for 1% of the time, Pallas kernels for 10%

profile of v2, /device:TPU:0, one launch (start us, length us, event | category | flops | bytes accessed | tf_op | source)
XLA Modules:
  0.0 486.1 jit_solution(7882803722799954424)
XLA Ops:
  0.0 2.7 slice_bitcast_fusion
  2.7 2.9 collective-permute-start.9
  7.2 1.6 collective-permute-start.7
  8.7 2.5 collective-permute-start.8
  11.3 17.7 %collective-permute-done.9.refs_0_.refs_1_.refs_3_.refs_2_ = bf16[32,64,256]{2,1,0:T(8,128)(2,1)S(1)} collective-permute-done((bf16[32,64,256]{2,1,0:T(8,128)(2,1)}, bf16[32,64,256]{2,1,0:T(8,128)(2,1)S(1)}, u32[]{:S(2)}, u32[]{:S(2)}) %collective-permute-start.9) | collective-permute-done | bytes 1048608 | tf_op jit(solution)/shard_map/ppermute | solution.py:303
  30.3 3.4 copy-done
  33.6 2.1 shard_map.55
  36.3 1.6 collective-permute-start.15
  43.2 17.7 %collective-permute-done.3 = s32[2,512]{1,0:T(2,128)S(1)} collective-permute-done((s32[2,512]{1,0:T(2,128)S(1)}, s32[2,512]{1,0:T(2,128)S(1)}, u32[]{:S(2)}, u32[]{:S(2)}) %collective-permute-start.3) | collective-permute-done | bytes 4128 | tf_op jit(solution)/shard_map/ppermute | solution.py:326
  65.9 3.4 copy-done.1
  70.0 2.7 collective-permute-start.19
  74.5 17.9 %collective-permute-done.19.refs_2_.refs_7_ = bf16[32,64,256]{2,1,0:T(8,128)(2,1)S(1)} collective-permute-done((bf16[32,64,256]{2,1,0:T(8,128)(2,1)S(1)}, bf16[32,64,256]{2,1,0:T(8,128)(2,1)S(1)}, u32[]{:S(2)}, u32[]{:S(2)}) %collective-permute-start.19) | collective-permute-done | bytes 1048608 | tf_op jit(solution)/shard_map/ppermute | solution.py:303
  92.5 2.2 collective-permute-done.20.refs_0_.refs_4_.refs_2_
  95.8 1.9 collective-permute-start.22
  100.0 11.4 %collective-permute-done.12.refs_4_ = bf16[32,8192]{1,0:T(8,128)(2,1)S(1)} collective-permute-done((bf16[32,8192]{1,0:T(8,128)(2,1)}, bf16[32,8192]{1,0:T(8,128)(2,1)S(1)}, u32[]{:S(2)}, u32[]{:S(2)}) %collective-permute-start.12) | collective-permute-done | bytes 524320 | tf_op jit(solution)/shard_map/ppermute | solution.py:143
  112.0 2.6 collective-permute-done.21.refs_7_.refs_0_.refs_3_.refs_1_
  117.5 2.5 collective-permute-start.27
  120.2 2.1 shard_map.58.refs_10_
  122.3 5.1 %shard_map.59.refs_0_ = bf16[32,8192]{1,0:T(8,128)(2,1)S(1)} custom-call(s32[512]{0:T(512)S(1)} %bitcast.47, s32[2]{0:T(128)S(1)} %pad_add_fusion.2.place, bf16[32,8192]{1,0:T(8,128)(2,1)} %refs_0_.4, bf16[32,8192]{1,0:T(8,128)(2,1)} %collective-permute-done.7.refs_1_, bf16[32,8192]{1,0:T(8,128)(2,1)} %collective-permute-done.8.refs_2_, ...), custom_call_target="tpu_custom_call" | custom-call | tf_op jit(solution)/shard_map/pallas_call | solution.py:127
  127.5 2.8 collective-permute-start.23
  130.3 2.5 collective-permute-start.24
  132.8 5.9 %collective-permute-done.26.refs_2_.refs_7_.refs_8_.refs_4_ = bf16[32,64,256]{2,1,0:T(8,128)(2,1)S(1)} collective-permute-done((bf16[32,64,256]{2,1,0:T(8,128)(2,1)S(1)}, bf16[32,64,256]{2,1,0:T(8,128)(2,1)S(1)}, u32[]{:S(2)}, u32[]{:S(2)}) %collective-permute-start.26) | collective-permute-done | bytes 1048608 | tf_op jit(solution)/shard_map/ppermute | solution.py:303
  141.2 2.1 collective-permute-start.32
  143.3 13.1 %collective-permute-done.24.refs_2_ = bf16[32,8192]{1,0:T(8,128)(2,1)S(1)} collective-permute-done((bf16[32,8192]{1,0:T(8,128)(2,1)S(1)}, bf16[32,8192]{1,0:T(8,128)(2,1)S(1)}, u32[]{:S(2)}, u32[]{:S(2)}) %collective-permute-start.24) | collective-permute-done | bytes 524320 | tf_op jit(solution)/shard_map/ppermute | solution.py:143
  161.2 2.1 shard_map.62.refs_10_
  164.0 10.2 %collective-permute-done.29.refs_4_ = bf16[32,8192]{1,0:T(8,128)(2,1)S(1)} collective-permute-done((bf16[32,8192]{1,0:T(8,128)(2,1)S(1)}, bf16[32,8192]{1,0:T(8,128)(2,1)S(1)}, u32[]{:S(2)}, u32[]{:S(2)}) %collective-permute-start.29) | collective-permute-done | bytes 524320 | tf_op jit(solution)/shard_map/ppermute | solution.py:143
  174.7 2.2 collective-permute-start.39
  177.0 3.9 shard_map.64.refs_0_
  181.1 1.6 collective-permute-start.37
  182.9 17.4 %collective-permute-done.39.refs_2_.refs_3_.refs_8_.refs_5_ = bf16[32,64,256]{2,1,0:T(8,128)(2,1)S(1)} collective-permute-done((bf16[32,64,256]{2,1,0:T(8,128)(2,1)S(1)}, bf16[32,64,256]{2,1,0:T(8,128)(2,1)S(1)}, u32[]{:S(2)}, u32[]{:S(2)}) %collective-permute-start.39) | collective-permute-done | bytes 1048608 | tf_op jit(solution)/shard_map/ppermute | solution.py:303
  203.1 3.4 collective-permute-done.36.refs_1_
  209.1 17.3 %collective-permute-done.44.refs_1_.refs_5_.refs_7_.refs_4_ = bf16[32,64,256]{2,1,0:T(8,128)(2,1)S(1)} collective-permute-done((bf16[32,64,256]{2,1,0:T(8,128)(2,1)S(1)}, bf16[32,64,256]{2,1,0:T(8,128)(2,1)S(1)}, u32[]{:S(2)}, u32[]{:S(2)}) %collective-permute-start.44) | collective-permute-done | bytes 1048608 | tf_op jit(solution)/shard_map/ppermute | solution.py:303
  226.8 3.2 shard_map.66.refs_10_
  233.5 3.9 shard_map.68.refs_0_
  237.6 1.6 collective-permute-start.50
  239.2 17.2 %collective-permute-done.52.refs_4_.refs_2_.refs_1_.refs_10_ = bf16[32,64,256]{2,1,0:T(8,128)(2,1)S(1)} collective-permute-done((bf16[32,64,256]{2,1,0:T(8,128)(2,1)S(1)}, bf16[32,64,256]{2,1,0:T(8,128)(2,1)S(1)}, u32[]{:S(2)}, u32[]{:S(2)}) %collective-permute-start.52) | collective-permute-done | bytes 1048608 | tf_op jit(solution)/shard_map/ppermute | solution.py:303
  257.4 1.8 collective-permute-start.57
  259.7 3.4 collective-permute-done.49.refs_1_
  265.0 2.1 shard_map.70.refs_10_
  267.7 14.1 %collective-permute-done.57.refs_1_.refs_6_.refs_8_.refs_7_ = bf16[32,64,256]{2,1,0:T(8,128)(2,1)S(1)} collective-permute-done((bf16[32,64,256]{2,1,0:T(8,128)(2,1)S(1)}, bf16[32,64,256]{2,1,0:T(8,128)(2,1)S(1)}, u32[]{:S(2)}, u32[]{:S(2)}) %collective-permute-start.57) | collective-permute-done | bytes 1048608 | tf_op jit(solution)/shard_map/ppermute | solution.py:303
  286.4 3.9 shard_map.72.refs_0_
  290.5 1.6 collective-permute-start.63
  292.2 17.2 %collective-permute-done.65.refs_0_.refs_5_.refs_2_ = bf16[32,64,256]{2,1,0:T(8,128)(2,1)S(1)} collective-permute-done((bf16[32,64,256]{2,1,0:T(8,128)(2,1)S(1)}, bf16[32,64,256]{2,1,0:T(8,128)(2,1)S(1)}, u32[]{:S(2)}, u32[]{:S(2)}) %collective-permute-start.65) | collective-permute-done | bytes 1048608 | tf_op jit(solution)/shard_map/ppermute | solution.py:303
  310.5 5.5 %collective-permute-done.62.refs_1_ = bf16[32,8192]{1,0:T(8,128)(2,1)S(1)} collective-permute-done((bf16[32,8192]{1,0:T(8,128)(2,1)S(1)}, bf16[32,8192]{1,0:T(8,128)(2,1)S(1)}, u32[]{:S(2)}, u32[]{:S(2)}) %collective-permute-start.62) | collective-permute-done | bytes 524320 | tf_op jit(solution)/shard_map/ppermute | solution.py:143
  317.9 2.1 shard_map.74.refs_10_
  320.6 11.6 %collective-permute-done.68.refs_4_ = bf16[32,8192]{1,0:T(8,128)(2,1)S(1)} collective-permute-done((bf16[32,8192]{1,0:T(8,128)(2,1)S(1)}, bf16[32,8192]{1,0:T(8,128)(2,1)S(1)}, u32[]{:S(2)}, u32[]{:S(2)}) %collective-permute-start.68) | collective-permute-done | bytes 524320 | tf_op jit(solution)/shard_map/ppermute | solution.py:143
  334.9 3.9 shard_map.75.refs_0_
  339.3 2.3 collective-permute-start.74
  341.5 11.3 %collective-permute-done.73.refs_1_ = bf16[32,8192]{1,0:T(8,128)(2,1)S(1)} collective-permute-done((bf16[32,8192]{1,0:T(8,128)(2,1)S(1)}, bf16[32,8192]{1,0:T(8,128)(2,1)S(1)}, u32[]{:S(2)}, u32[]{:S(2)}) %collective-permute-start.73) | collective-permute-done | bytes 524320 | tf_op jit(solution)/shard_map/ppermute | solution.py:143
  352.8 12.2 %collective-permute-done.74.refs_2_ = bf16[32,8192]{1,0:T(8,128)(2,1)S(1)} collective-permute-done((bf16[32,8192]{1,0:T(8,128)(2,1)S(1)}, bf16[32,8192]{1,0:T(8,128)(2,1)S(1)}, u32[]{:S(2)}, u32[]{:S(2)}) %collective-permute-start.74) | collective-permute-done | bytes 524320 | tf_op jit(solution)/shard_map/ppermute | solution.py:143
  367.0 2.1 shard_map.76.refs_10_
  369.8 11.7 %collective-permute-done.76.refs_4_ = bf16[32,8192]{1,0:T(8,128)(2,1)S(1)} collective-permute-done((bf16[32,8192]{1,0:T(8,128)(2,1)S(1)}, bf16[32,8192]{1,0:T(8,128)(2,1)S(1)}, u32[]{:S(2)}, u32[]{:S(2)}) %collective-permute-start.76) | collective-permute-done | bytes 524320 | tf_op jit(solution)/shard_map/ppermute | solution.py:143
  384.1 3.9 shard_map.77.refs_0_
  388.1 1.6 collective-permute-start.85
  389.7 23.6 %collective-permute-done.84.refs_1_ = bf16[32,8192]{1,0:T(8,128)(2,1)S(1)} collective-permute-done((bf16[32,8192]{1,0:T(8,128)(2,1)S(1)}, bf16[32,8192]{1,0:T(8,128)(2,1)S(1)}, u32[]{:S(2)}, u32[]{:S(2)}) %collective-permute-start.84) | collective-permute-done | bytes 524320 | tf_op jit(solution)/shard_map/ppermute | solution.py:143
  415.3 2.1 shard_map.78.refs_10_
  418.1 11.3 %collective-permute-done.87.refs_4_ = bf16[32,8192]{1,0:T(8,128)(2,1)S(1)} collective-permute-done((bf16[32,8192]{1,0:T(8,128)(2,1)S(1)}, bf16[32,8192]{1,0:T(8,128)(2,1)S(1)}, u32[]{:S(2)}, u32[]{:S(2)}) %collective-permute-start.87) | collective-permute-done | bytes 524320 | tf_op jit(solution)/shard_map/ppermute | solution.py:143
  432.0 3.9 shard_map.79.refs_0_
  436.4 2.3 collective-permute-start.94
  438.7 11.3 %collective-permute-done.93.refs_1_ = bf16[32,8192]{1,0:T(8,128)(2,1)S(1)} collective-permute-done((bf16[32,8192]{1,0:T(8,128)(2,1)S(1)}, bf16[32,8192]{1,0:T(8,128)(2,1)S(1)}, u32[]{:S(2)}, u32[]{:S(2)}) %collective-permute-start.93) | collective-permute-done | bytes 524320 | tf_op jit(solution)/shard_map/ppermute | solution.py:143
  449.9 12.2 %collective-permute-done.94.refs_2_ = bf16[32,8192]{1,0:T(8,128)(2,1)S(1)} collective-permute-done((bf16[32,8192]{1,0:T(8,128)(2,1)S(1)}, bf16[32,8192]{1,0:T(8,128)(2,1)S(1)}, u32[]{:S(2)}, u32[]{:S(2)}) %collective-permute-start.94) | collective-permute-done | bytes 524320 | tf_op jit(solution)/shard_map/ppermute | solution.py:143
  464.2 2.1 shard_map.80.refs_10_
  466.9 11.7 %collective-permute-done.96.refs_4_ = bf16[32,8192]{1,0:T(8,128)(2,1)S(1)} collective-permute-done((bf16[32,8192]{1,0:T(8,128)(2,1)S(1)}, bf16[32,8192]{1,0:T(8,128)(2,1)S(1)}, u32[]{:S(2)}, u32[]{:S(2)}) %collective-permute-start.96) | collective-permute-done | bytes 524320 | tf_op jit(solution)/shard_map/ppermute | solution.py:143
  481.3 4.7 shard_map.81
  (189 shorter events, 73.5 us)
Async XLA Ops:
  2.7 26.3 %collective-permute-start.9 = (bf16[32,64,256]{2,1,0:T(8,128)(2,1)}, bf16[32,64,256]{2,1,0:T(8,128)(2,1)S(1)}, u32[]{:S(2)}, u32[]{:S(2)}) collective-permute-start(bf16[32,64,256]{2,1,0:T(8,128)(2,1)} %get-tuple-element.192), channel_id=1, source_target_pairs={{0,8},{8,0},{16,24},{24,16},{1,9},{9,1},{17,25},{25,17},{2,10},{10... | collective-permute-start | bytes 3145736 | tf_op jit(solution)/shard_map/ppermute | solution.py:303
  5.6 24.6 %collective-permute-start.10 = (bf16[32,64,256]{2,1,0:T(8,128)(2,1)S(1)}, bf16[32,64,256]{2,1,0:T(8,128)(2,1)S(1)}, u32[]{:S(2)}, u32[]{:S(2)}) collective-permute-start(bf16[32,64,256]{2,1,0:T(8,128)(2,1)S(1)} %get-tuple-element.191), channel_id=1, source_target_pairs={{0,16},{8,24},{16,0},{24,8},{1,17},{9,25},{17,1},{25,9},{2,18},{10... | collective-permute-start | bytes 3145736 | tf_op jit(solution)/shard_map/ppermute | solution.py:303
  7.2 31.4 %collective-permute-start.7 = (bf16[32,8192]{1,0:T(8,128)(2,1)}, bf16[32,8192]{1,0:T(8,128)(2,1)}, u32[]{:S(2)}, u32[]{:S(2)}) collective-permute-start(bf16[32,8192]{1,0:T(8,128)(2,1)} %refs_0_.4), channel_id=1, source_target_pairs={{0,2},{1,3},{2,0},{3,1},{4,6},{5,7},{6,4},{7,5},{8,10},{9,11},{10,... | collective-permute-start | bytes 1572872 | tf_op jit(solution)/shard_map/ppermute | solution.py:143
  8.7 29.8 %collective-permute-start.8 = (bf16[32,8192]{1,0:T(8,128)(2,1)}, bf16[32,8192]{1,0:T(8,128)(2,1)}, u32[]{:S(2)}, u32[]{:S(2)}) collective-permute-start(bf16[32,8192]{1,0:T(8,128)(2,1)} %refs_0_.4), channel_id=1, source_target_pairs={{2,4},{3,5},{4,2},{5,3},{0,6},{1,7},{6,0},{7,1},{10,12},{11,13},{1... | collective-permute-start | bytes 1572872 | tf_op jit(solution)/shard_map/ppermute | solution.py:143
  35.7 30.2 %collective-permute-start.14 = (bf16[32,64,256]{2,1,0:T(8,128)(2,1)}, bf16[32,64,256]{2,1,0:T(8,128)(2,1)}, u32[]{:S(2)}, u32[]{:S(2)}) collective-permute-start(bf16[32,64,256]{2,1,0:T(8,128)(2,1)} %get-tuple-element.101), channel_id=1, source_target_pairs={{0,8},{8,0},{16,24},{24,16},{1,9},{9,1},{17,25},{25,17},{2,10},{10... | collective-permute-start | bytes 3145736 | tf_op jit(solution)/shard_map/ppermute | solution.py:303
  36.3 29.6 %collective-permute-start.15 = (bf16[32,64,256]{2,1,0:T(8,128)(2,1)}, bf16[32,64,256]{2,1,0:T(8,128)(2,1)S(1)}, u32[]{:S(2)}, u32[]{:S(2)}) collective-permute-start(bf16[32,64,256]{2,1,0:T(8,128)(2,1)} %get-tuple-element.102), channel_id=1, source_target_pairs={{0,16},{8,24},{16,0},{24,8},{1,17},{9,25},{17,1},{25,9},{2,18},{10... | collective-permute-start | bytes 3145736 | tf_op jit(solution)/shard_map/ppermute | solution.py:303
  38.6 26.5 %collective-permute-start.13 = (bf16[32,8192]{1,0:T(8,128)(2,1)}, bf16[32,8192]{1,0:T(8,128)(2,1)}, u32[]{:S(2)}, u32[]{:S(2)}) collective-permute-start(bf16[32,8192]{1,0:T(8,128)(2,1)} %collective-permute-done.7.refs_1_), channel_id=1, source_target_pairs={{0,1},{1,0},{2,3},{3,2},{4,5},{5,4},{6,7},{7,6},{8,9},{9,8},{10,11... | collective-permute-start | bytes 1572872 | tf_op jit(solution)/shard_map/ppermute | solution.py:147
  40.2 20.7 %collective-permute-start.3 = (s32[2,512]{1,0:T(2,128)S(1)}, s32[2,512]{1,0:T(2,128)S(1)}, u32[]{:S(2)}, u32[]{:S(2)}) collective-permute-start(s32[2,512]{1,0:T(2,128)S(1)} %fusion.1), channel_id=1, source_target_pairs={{0,24},{8,16},{16,8},{24,0},{1,25},{9,17},{17,9},{25,1},{2,26},{10... | collective-permute-start | bytes 12296 | tf_op jit(solution)/shard_map/ppermute | solution.py:326
  41.7 20.1 %collective-permute-start.2 = (s32[2,512]{1,0:T(2,128)S(1)}, s32[2,512]{1,0:T(2,128)S(1)}, u32[]{:S(2)}, u32[]{:S(2)}) collective-permute-start(s32[2,512]{1,0:T(2,128)S(1)} %fusion.1), channel_id=1, source_target_pairs={{0,16},{8,24},{16,0},{24,8},{1,17},{9,25},{17,1},{25,9},{2,18},{10... | collective-permute-start | bytes 12296 | tf_op jit(solution)/shard_map/ppermute | solution.py:326
  70.0 22.4 %collective-permute-start.19 = (bf16[32,64,256]{2,1,0:T(8,128)(2,1)S(1)}, bf16[32,64,256]{2,1,0:T(8,128)(2,1)S(1)}, u32[]{:S(2)}, u32[]{:S(2)}) collective-permute-start(bf16[32,64,256]{2,1,0:T(8,128)(2,1)S(1)} %get-tuple-element.107), channel_id=1, source_target_pairs={{0,8},{8,0},{16,24},{24,16},{1,9},{9,1},{17,25},{25,17},{2,10},{10... | collective-permute-start | bytes 3145736 | tf_op jit(solution)/shard_map/ppermute | solution.py:303
  72.7 22.0 %collective-permute-start.20 = (bf16[32,64,256]{2,1,0:T(8,128)(2,1)S(1)}, bf16[32,64,256]{2,1,0:T(8,128)(2,1)S(1)}, u32[]{:S(2)}, u32[]{:S(2)}) collective-permute-start(bf16[32,64,256]{2,1,0:T(8,128)(2,1)S(1)} %get-tuple-element.108), channel_id=1, source_target_pairs={{0,16},{8,24},{16,0},{24,8},{1,17},{9,25},{17,1},{25,9},{2,18},{10... | collective-permute-start | bytes 3145736 | tf_op jit(solution)/shard_map/ppermute | solution.py:303
  74.2 25.7 %collective-permute-start = (bf16[32,8192]{1,0:T(8,128)(2,1)}, bf16[32,8192]{1,0:T(8,128)(2,1)S(1)}, u32[]{:S(2)}, u32[]{:S(2)}) collective-permute-start(bf16[32,8192]{1,0:T(8,128)(2,1)} %refs_0_.4), channel_id=1, source_target_pairs={{0,1},{1,0},{2,3},{3,2},{4,5},{5,4},{6,7},{7,6},{8,9},{9,8},{10,11... | collective-permute-start | bytes 1572872 | tf_op jit(solution)/shard_map/ppermute | solution.py:147
  95.4 19.1 %collective-permute-start.21 = (bf16[32,64,256]{2,1,0:T(8,128)(2,1)S(1)}, bf16[32,64,256]{2,1,0:T(8,128)(2,1)S(1)}, u32[]{:S(2)}, u32[]{:S(2)}) collective-permute-start(bf16[32,64,256]{2,1,0:T(8,128)(2,1)S(1)} %get-tuple-element.113), channel_id=1, source_target_pairs={{0,8},{8,0},{16,24},{24,16},{1,9},{9,1},{17,25},{25,17},{2,10},{10... | collective-permute-start | bytes 3145736 | tf_op jit(solution)/shard_map/ppermute | solution.py:303
  95.8 20.2 %collective-permute-start.22 = (bf16[32,64,256]{2,1,0:T(8,128)(2,1)S(1)}, bf16[32,64,256]{2,1,0:T(8,128)(2,1)S(1)}, u32[]{:S(2)}, u32[]{:S(2)}) collective-permute-start(bf16[32,64,256]{2,1,0:T(8,128)(2,1)S(1)} %get-tuple-element.114), channel_id=1, source_target_pairs={{0,16},{8,24},{16,0},{24,8},{1,17},{9,25},{17,1},{25,9},{2,18},{10... | collective-permute-start | bytes 3145736 | tf_op jit(solution)/shard_map/ppermute | solution.py:303
  98.4 13.0 %collective-permute-start.12 = (bf16[32,8192]{1,0:T(8,128)(2,1)}, bf16[32,8192]{1,0:T(8,128)(2,1)S(1)}, u32[]{:S(2)}, u32[]{:S(2)}) collective-permute-start(bf16[32,8192]{1,0:T(8,128)(2,1)} %collective-permute-done.8.refs_2_), channel_id=1, source_target_pairs={{4,6},{5,7},{2,0},{3,1},{12,14},{13,15},{10,8},{11,9},{20,22},{21,... | collective-permute-start | bytes 1572872 | tf_op jit(solution)/shard_map/ppermute | solution.py:143
  99.9 22.4 %collective-permute-start.16 = (bf16[32,8192]{1,0:T(8,128)(2,1)}, bf16[32,8192]{1,0:T(8,128)(2,1)S(1)}, u32[]{:S(2)}, u32[]{:S(2)}) collective-permute-start(bf16[32,8192]{1,0:T(8,128)(2,1)} %collective-permute-done.8.refs_2_), channel_id=1, source_target_pairs={{0,1},{1,0},{2,3},{3,2},{4,5},{5,4},{6,7},{7,6},{8,9},{9,8},{10,11... | collective-permute-start | bytes 1572872 | tf_op jit(solution)/shard_map/ppermute | solution.py:147
  116.7 22.0 %collective-permute-start.26 = (bf16[32,64,256]{2,1,0:T(8,128)(2,1)S(1)}, bf16[32,64,256]{2,1,0:T(8,128)(2,1)S(1)}, u32[]{:S(2)}, u32[]{:S(2)}) collective-permute-start(bf16[32,64,256]{2,1,0:T(8,128)(2,1)S(1)} %get-tuple-element.118), channel_id=1, source_target_pairs={{0,8},{8,0},{16,24},{24,16},{1,9},{9,1},{17,25},{25,17},{2,10},{10... | collective-permute-start | bytes 3145736 | tf_op jit(solution)/shard_map/ppermute | solution.py:303
  117.5 21.5 %collective-permute-start.27 = (bf16[32,64,256]{2,1,0:T(8,128)(2,1)S(1)}, bf16[32,64,256]{2,1,0:T(8,128)(2,1)S(1)}, u32[]{:S(2)}, u32[]{:S(2)}) collective-permute-start(bf16[32,64,256]{2,1,0:T(8,128)(2,1)S(1)} %get-tuple-element.119), channel_id=1, source_target_pairs={{0,16},{8,24},{16,0},{24,8},{1,17},{9,25},{17,1},{25,9},{2,18},{10... | collective-permute-start | bytes 3145736 | tf_op jit(solution)/shard_map/ppermute | solution.py:303
  127.5 15.7 %collective-permute-start.23 = (bf16[32,8192]{1,0:T(8,128)(2,1)S(1)}, bf16[32,8192]{1,0:T(8,128)(2,1)S(1)}, u32[]{:S(2)}, u32[]{:S(2)}) collective-permute-start(bf16[32,8192]{1,0:T(8,128)(2,1)S(1)} %shard_map.59.refs_0_), channel_id=1, source_target_pairs={{0,2},{1,3},{2,0},{3,1},{4,6},{5,7},{6,4},{7,5},{8,10},{9,11},{10,... | collective-permute-start | bytes 1572872 | tf_op jit(solution)/shard_map/ppermute | solution.py:143
  130.3 26.1 %collective-permute-start.24 = (bf16[32,8192]{1,0:T(8,128)(2,1)S(1)}, bf16[32,8192]{1,0:T(8,128)(2,1)S(1)}, u32[]{:S(2)}, u32[]{:S(2)}) collective-permute-start(bf16[32,8192]{1,0:T(8,128)(2,1)S(1)} %shard_map.59.refs_0_), channel_id=1, source_target_pairs={{2,4},{3,5},{4,2},{5,3},{0,6},{1,7},{6,0},{7,1},{10,12},{11,13},{1... | collective-permute-start | bytes 1572872 | tf_op jit(solution)/shard_map/ppermute | solution.py:143
  139.7 20.6 %collective-permute-start.31 = (bf16[32,64,256]{2,1,0:T(8,128)(2,1)S(1)}, bf16[32,64,256]{2,1,0:T(8,128)(2,1)S(1)}, u32[]{:S(2)}, u32[]{:S(2)}) collective-permute-start(bf16[32,64,256]{2,1,0:T(8,128)(2,1)S(1)} %get-tuple-element.124), channel_id=1, source_target_pairs={{0,8},{8,0},{16,24},{24,16},{1,9},{9,1},{17,25},{25,17},{2,10},{10... | collective-permute-start | bytes 3145736 | tf_op jit(solution)/shard_map/ppermute | solution.py:303
  141.2 20.0 %collective-permute-start.32 = (bf16[32,64,256]{2,1,0:T(8,128)(2,1)S(1)}, bf16[32,64,256]{2,1,0:T(8,128)(2,1)S(1)}, u32[]{:S(2)}, u32[]{:S(2)}) collective-permute-start(bf16[32,64,256]{2,1,0:T(8,128)(2,1)S(1)} %get-tuple-element.125), channel_id=1, source_target_pairs={{0,16},{8,24},{16,0},{24,8},{1,17},{9,25},{17,1},{25,9},{2,18},{10... | collective-permute-start | bytes 3145736 | tf_op jit(solution)/shard_map/ppermute | solution.py:303
  157.1 17.1 %collective-permute-start.29 = (bf16[32,8192]{1,0:T(8,128)(2,1)S(1)}, bf16[32,8192]{1,0:T(8,128)(2,1)S(1)}, u32[]{:S(2)}, u32[]{:S(2)}) collective-permute-start(bf16[32,8192]{1,0:T(8,128)(2,1)S(1)} %collective-permute-done.24.refs_2_), channel_id=1, source_target_pairs={{4,6},{5,7},{2,0},{3,1},{12,14},{13,15},{10,8},{11,9},{20,22},{21,... | collective-permute-start | bytes 1572872 | tf_op jit(solution)/shard_map/ppermute | solution.py:143
  158.4 18.6 %collective-permute-start.33 = (bf16[32,8192]{1,0:T(8,128)(2,1)S(1)}, bf16[32,8192]{1,0:T(8,128)(2,1)S(1)}, u32[]{:S(2)}, u32[]{:S(2)}) collective-permute-start(bf16[32,8192]{1,0:T(8,128)(2,1)S(1)} %collective-permute-done.24.refs_2_), channel_id=1, source_target_pairs={{0,1},{1,0},{2,3},{3,2},{4,5},{5,4},{6,7},{7,6},{8,9},{9,8},{10,11... | collective-permute-start | bytes 1572872 | tf_op jit(solution)/shard_map/ppermute | solution.py:147
  174.7 25.6 %collective-permute-start.39 = (bf16[32,64,256]{2,1,0:T(8,128)(2,1)S(1)}, bf16[32,64,256]{2,1,0:T(8,128)(2,1)S(1)}, u32[]{:S(2)}, u32[]{:S(2)}) collective-permute-start(bf16[32,64,256]{2,1,0:T(8,128)(2,1)S(1)} %get-tuple-element.132), channel_id=1, source_target_pairs={{0,8},{8,0},{16,24},{24,16},{1,9},{9,1},{17,25},{25,17},{2,10},{10... | collective-permute-start | bytes 3145736 | tf_op jit(solution)/shard_map/ppermute | solution.py:303
  177.0 24.8 %collective-permute-start.40 = (bf16[32,64,256]{2,1,0:T(8,128)(2,1)S(1)}, bf16[32,64,256]{2,1,0:T(8,128)(2,1)S(1)}, u32[]{:S(2)}, u32[]{:S(2)}) collective-permute-start(bf16[32,64,256]{2,1,0:T(8,128)(2,1)S(1)} %get-tuple-element.133), channel_id=1, source_target_pairs={{0,16},{8,24},{16,0},{24,8},{1,17},{9,25},{17,1},{25,9},{2,18},{10... | collective-permute-start | bytes 3145736 | tf_op jit(solution)/shard_map/ppermute | solution.py:303
  181.0 25.6 %collective-permute-start.36 = (bf16[32,8192]{1,0:T(8,128)(2,1)S(1)}, bf16[32,8192]{1,0:T(8,128)(2,1)S(1)}, u32[]{:S(2)}, u32[]{:S(2)}) collective-permute-start(bf16[32,8192]{1,0:T(8,128)(2,1)S(1)} %shard_map.64.refs_0_), channel_id=1, source_target_pairs={{0,2},{1,3},{2,0},{3,1},{4,6},{5,7},{6,4},{7,5},{8,10},{9,11},{10,... | collective-permute-start | bytes 1572872 | tf_op jit(solution)/shard_map/ppermute | solution.py:143
  181.1 25.5 %collective-permute-start.37 = (bf16[32,8192]{1,0:T(8,128)(2,1)S(1)}, bf16[32,8192]{1,0:T(8,128)(2,1)S(1)}, u32[]{:S(2)}, u32[]{:S(2)}) collective-permute-start(bf16[32,8192]{1,0:T(8,128)(2,1)S(1)} %shard_map.64.refs_0_), channel_id=1, source_target_pairs={{2,4},{3,5},{4,2},{5,3},{0,6},{1,7},{6,0},{7,1},{10,12},{11,13},{1... | collective-permute-start | bytes 1572872 | tf_op jit(solution)/shard_map/ppermute | solution.py:143
  202.5 24.0 %collective-permute-start.44 = (bf16[32,64,256]{2,1,0:T(8,128)(2,1)S(1)}, bf16[32,64,256]{2,1,0:T(8,128)(2,1)S(1)}, u32[]{:S(2)}, u32[]{:S(2)}) collective-permute-start(bf16[32,64,256]{2,1,0:T(8,128)(2,1)S(1)} %get-tuple-element.140), channel_id=1, source_target_pairs={{0,8},{8,0},{16,24},{24,16},{1,9},{9,1},{17,25},{25,17},{2,10},{10... | collective-permute-start | bytes 3145736 | tf_op jit(solution)/shard_map/ppermute | solution.py:303
  202.9 23.9 %collective-permute-start.45 = (bf16[32,64,256]{2,1,0:T(8,128)(2,1)S(1)}, bf16[32,64,256]{2,1,0:T(8,128)(2,1)S(1)}, u32[]{:S(2)}, u32[]{:S(2)}) collective-permute-start(bf16[32,64,256]{2,1,0:T(8,128)(2,1)S(1)} %get-tuple-element.141), channel_id=1, source_target_pairs={{0,16},{8,24},{16,0},{24,8},{1,17},{9,25},{17,1},{25,9},{2,18},{10... | collective-permute-start | bytes 3145736 | tf_op jit(solution)/shard_map/ppermute | solution.py:303
  206.6 24.2 %collective-permute-start.41 = (bf16[32,8192]{1,0:T(8,128)(2,1)S(1)}, bf16[32,8192]{1,0:T(8,128)(2,1)S(1)}, u32[]{:S(2)}, u32[]{:S(2)}) collective-permute-start(bf16[32,8192]{1,0:T(8,128)(2,1)S(1)} %collective-permute-done.36.refs_1_), channel_id=1, source_target_pairs={{2,4},{3,5},{4,2},{5,3},{10,12},{11,13},{12,10},{13,11},{18,20},{1... | collective-permute-start | bytes 1572872 | tf_op jit(solution)/shard_map/ppermute | solution.py:143
  207.3 23.5 %collective-permute-start.42 = (bf16[32,8192]{1,0:T(8,128)(2,1)S(1)}, bf16[32,8192]{1,0:T(8,128)(2,1)S(1)}, u32[]{:S(2)}, u32[]{:S(2)}) collective-permute-start(bf16[32,8192]{1,0:T(8,128)(2,1)S(1)} %collective-permute-done.37.refs_2_), channel_id=1, source_target_pairs={{4,6},{5,7},{2,0},{3,1},{12,14},{13,15},{10,8},{11,9},{20,22},{21,... | collective-permute-start | bytes 1572872 | tf_op jit(solution)/shard_map/ppermute | solution.py:143
  208.6 23.7 %collective-permute-start.46 = (bf16[32,8192]{1,0:T(8,128)(2,1)S(1)}, bf16[32,8192]{1,0:T(8,128)(2,1)S(1)}, u32[]{:S(2)}, u32[]{:S(2)}) collective-permute-start(bf16[32,8192]{1,0:T(8,128)(2,1)S(1)} %collective-permute-done.37.refs_2_), channel_id=1, source_target_pairs={{0,1},{1,0},{2,3},{3,2},{4,5},{5,4},{6,7},{7,6},{8,9},{9,8},{10,11... | collective-permute-start | bytes 1572872 | tf_op jit(solution)/shard_map/ppermute | solution.py:147
  231.3 25.1 %collective-permute-start.52 = (bf16[32,64,256]{2,1,0:T(8,128)(2,1)S(1)}, bf16[32,64,256]{2,1,0:T(8,128)(2,1)S(1)}, u32[]{:S(2)}, u32[]{:S(2)}) collective-permute-start(bf16[32,64,256]{2,1,0:T(8,128)(2,1)S(1)} %get-tuple-element.147), channel_id=1, source_target_pairs={{0,8},{8,0},{16,24},{24,16},{1,9},{9,1},{17,25},{25,17},{2,10},{10... | collective-permute-start | bytes 3145736 | tf_op jit(solution)/shard_map/ppermute | solution.py:303
  231.6 24.9 %collective-permute-start.53 = (bf16[32,64,256]{2,1,0:T(8,128)(2,1)S(1)}, bf16[32,64,256]{2,1,0:T(8,128)(2,1)S(1)}, u32[]{:S(2)}, u32[]{:S(2)}) collective-permute-start(bf16[32,64,256]{2,1,0:T(8,128)(2,1)S(1)} %get-tuple-element.148), channel_id=1, source_target_pairs={{0,16},{8,24},{16,0},{24,8},{1,17},{9,25},{17,1},{25,9},{2,18},{10... | collective-permute-start | bytes 3145736 | tf_op jit(solution)/shard_map/ppermute | solution.py:303
  237.4 19.1 %collective-permute-start.51 = (bf16[32,8192]{1,0:T(8,128)(2,1)S(1)}, bf16[32,8192]{1,0:T(8,128)(2,1)S(1)}, u32[]{:S(2)}, u32[]{:S(2)}) collective-permute-start(bf16[32,8192]{1,0:T(8,128)(2,1)S(1)} %shard_map.68.refs_0_), channel_id=1, source_target_pairs={{0,1},{1,0},{2,3},{3,2},{4,5},{5,4},{6,7},{7,6},{8,9},{9,8},{10,11... | collective-permute-start | bytes 1572872 | tf_op jit(solution)/shard_map/ppermute | solution.py:147
  237.6 25.4 %collective-permute-start.49 = (bf16[32,8192]{1,0:T(8,128)(2,1)S(1)}, bf16[32,8192]{1,0:T(8,128)(2,1)S(1)}, u32[]{:S(2)}, u32[]{:S(2)}) collective-permute-start(bf16[32,8192]{1,0:T(8,128)(2,1)S(1)} %shard_map.68.refs_0_), channel_id=1, source_target_pairs={{0,2},{1,3},{2,0},{3,1},{4,6},{5,7},{6,4},{7,5},{8,10},{9,11},{10,... | collective-permute-start | bytes 1572872 | tf_op jit(solution)/shard_map/ppermute | solution.py:143
  237.6 25.4 %collective-permute-start.50 = (bf16[32,8192]{1,0:T(8,128)(2,1)S(1)}, bf16[32,8192]{1,0:T(8,128)(2,1)S(1)}, u32[]{:S(2)}, u32[]{:S(2)}) collective-permute-start(bf16[32,8192]{1,0:T(8,128)(2,1)S(1)} %shard_map.68.refs_0_), channel_id=1, source_target_pairs={{2,4},{3,5},{4,2},{5,3},{0,6},{1,7},{6,0},{7,1},{10,12},{11,13},{1... | collective-permute-start | bytes 1572872 | tf_op jit(solution)/shard_map/ppermute | solution.py:143
  257.4 24.4 %collective-permute-start.57 = (bf16[32,64,256]{2,1,0:T(8,128)(2,1)S(1)}, bf16[32,64,256]{2,1,0:T(8,128)(2,1)S(1)}, u32[]{:S(2)}, u32[]{:S(2)}) collective-permute-start(bf16[32,64,256]{2,1,0:T(8,128)(2,1)S(1)} %get-tuple-element.156), channel_id=1, source_target_pairs={{0,8},{8,0},{16,24},{24,16},{1,9},{9,1},{17,25},{25,17},{2,10},{10... | collective-permute-start | bytes 3145736 | tf_op jit(solution)/shard_map/ppermute | solution.py:303
  259.2 23.7 %collective-permute-start.58 = (bf16[32,64,256]{2,1,0:T(8,128)(2,1)S(1)}, bf16[32,64,256]{2,1,0:T(8,128)(2,1)S(1)}, u32[]{:S(2)}, u32[]{:S(2)}) collective-permute-start(bf16[32,64,256]{2,1,0:T(8,128)(2,1)S(1)} %get-tuple-element.157), channel_id=1, source_target_pairs={{0,16},{8,24},{16,0},{24,8},{1,17},{9,25},{17,1},{25,9},{2,18},{10... | collective-permute-start | bytes 3145736 | tf_op jit(solution)/shard_map/ppermute | solution.py:303
  263.0 20.6 %collective-permute-start.54 = (bf16[32,8192]{1,0:T(8,128)(2,1)S(1)}, bf16[32,8192]{1,0:T(8,128)(2,1)S(1)}, u32[]{:S(2)}, u32[]{:S(2)}) collective-permute-start(bf16[32,8192]{1,0:T(8,128)(2,1)S(1)} %collective-permute-done.49.refs_1_), channel_id=1, source_target_pairs={{2,4},{3,5},{4,2},{5,3},{10,12},{11,13},{12,10},{13,11},{18,20},{1... | collective-permute-start | bytes 1572872 | tf_op jit(solution)/shard_map/ppermute | solution.py:143
  263.7 19.9 %collective-permute-start.55 = (bf16[32,8192]{1,0:T(8,128)(2,1)S(1)}, bf16[32,8192]{1,0:T(8,128)(2,1)S(1)}, u32[]{:S(2)}, u32[]{:S(2)}) collective-permute-start(bf16[32,8192]{1,0:T(8,128)(2,1)S(1)} %collective-permute-done.50.refs_2_), channel_id=1, source_target_pairs={{4,6},{5,7},{2,0},{3,1},{12,14},{13,15},{10,8},{11,9},{20,22},{21,... | collective-permute-start | bytes 1572872 | tf_op jit(solution)/shard_map/ppermute | solution.py:143
  267.2 18.1 %collective-permute-start.59 = (bf16[32,8192]{1,0:T(8,128)(2,1)S(1)}, bf16[32,8192]{1,0:T(8,128)(2,1)S(1)}, u32[]{:S(2)}, u32[]{:S(2)}) collective-permute-start(bf16[32,8192]{1,0:T(8,128)(2,1)S(1)} %collective-permute-done.50.refs_2_), channel_id=1, source_target_pairs={{0,1},{1,0},{2,3},{3,2},{4,5},{5,4},{6,7},{7,6},{8,9},{9,8},{10,11... | collective-permute-start | bytes 1572872 | tf_op jit(solution)/shard_map/ppermute | solution.py:147
  284.3 25.1 %collective-permute-start.65 = (bf16[32,64,256]{2,1,0:T(8,128)(2,1)S(1)}, bf16[32,64,256]{2,1,0:T(8,128)(2,1)S(1)}, u32[]{:S(2)}, u32[]{:S(2)}) collective-permute-start(bf16[32,64,256]{2,1,0:T(8,128)(2,1)S(1)} %get-tuple-element.164), channel_id=1, source_target_pairs={{0,8},{8,0},{16,24},{24,16},{1,9},{9,1},{17,25},{25,17},{2,10},{10... | collective-permute-start | bytes 3145736 | tf_op jit(solution)/shard_map/ppermute | solution.py:303
  284.9 24.9 %collective-permute-start.66 = (bf16[32,64,256]{2,1,0:T(8,128)(2,1)S(1)}, bf16[32,64,256]{2,1,0:T(8,128)(2,1)S(1)}, u32[]{:S(2)}, u32[]{:S(2)}) collective-permute-start(bf16[32,64,256]{2,1,0:T(8,128)(2,1)S(1)} %get-tuple-element.165), channel_id=1, source_target_pairs={{0,16},{8,24},{16,0},{24,8},{1,17},{9,25},{17,1},{25,9},{2,18},{10... | collective-permute-start | bytes 3145736 | tf_op jit(solution)/shard_map/ppermute | solution.py:303
  290.3 19.4 %collective-permute-start.64 = (bf16[32,8192]{1,0:T(8,128)(2,1)S(1)}, bf16[32,8192]{1,0:T(8,128)(2,1)S(1)}, u32[]{:S(2)}, u32[]{:S(2)}) collective-permute-start(bf16[32,8192]{1,0:T(8,128)(2,1)S(1)} %shard_map.72.refs_0_), channel_id=1, source_target_pairs={{0,1},{1,0},{2,3},{3,2},{4,5},{5,4},{6,7},{7,6},{8,9},{9,8},{10,11... | collective-permute-start | bytes 1572872 | tf_op jit(solution)/shard_map/ppermute | solution.py:147
  290.5 25.4 %collective-permute-start.62 = (bf16[32,8192]{1,0:T(8,128)(2,1)S(1)}, bf16[32,8192]{1,0:T(8,128)(2,1)S(1)}, u32[]{:S(2)}, u32[]{:S(2)}) collective-permute-start(bf16[32,8192]{1,0:T(8,128)(2,1)S(1)} %shard_map.72.refs_0_), channel_id=1, source_target_pairs={{0,2},{1,3},{2,0},{3,1},{4,6},{5,7},{6,4},{7,5},{8,10},{9,11},{10,... | collective-permute-start | bytes 1572872 | tf_op jit(solution)/shard_map/ppermute | solution.py:143
  290.5 25.4 %collective-permute-start.63 = (bf16[32,8192]{1,0:T(8,128)(2,1)S(1)}, bf16[32,8192]{1,0:T(8,128)(2,1)S(1)}, u32[]{:S(2)}, u32[]{:S(2)}) collective-permute-start(bf16[32,8192]{1,0:T(8,128)(2,1)S(1)} %shard_map.72.refs_0_), channel_id=1, source_target_pairs={{2,4},{3,5},{4,2},{5,3},{0,6},{1,7},{6,0},{7,1},{10,12},{11,13},{1... | collective-permute-start | bytes 1572872 | tf_op jit(solution)/shard_map/ppermute | solution.py:143
  316.6 15.6 %collective-permute-start.68 = (bf16[32,8192]{1,0:T(8,128)(2,1)S(1)}, bf16[32,8192]{1,0:T(8,128)(2,1)S(1)}, u32[]{:S(2)}, u32[]{:S(2)}) collective-permute-start(bf16[32,8192]{1,0:T(8,128)(2,1)S(1)} %collective-permute-done.63.refs_2_), channel_id=1, source_target_pairs={{4,6},{5,7},{2,0},{3,1},{12,14},{13,15},{10,8},{11,9},{20,22},{21,... | collective-permute-start | bytes 1572872 | tf_op jit(solution)/shard_map/ppermute | solution.py:143
  320.1 13.3 %collective-permute-start.69 = (bf16[32,8192]{1,0:T(8,128)(2,1)S(1)}, bf16[32,8192]{1,0:T(8,128)(2,1)S(1)}, u32[]{:S(2)}, u32[]{:S(2)}) collective-permute-start(bf16[32,8192]{1,0:T(8,128)(2,1)S(1)} %collective-permute-done.62.refs_1_), channel_id=1, source_target_pairs={{0,1},{1,0},{2,3},{3,2},{4,5},{5,4},{6,7},{7,6},{8,9},{9,8},{10,11... | collective-permute-start | bytes 1572872 | tf_op jit(solution)/shard_map/ppermute | solution.py:147
  320.1 14.6 %collective-permute-start.70 = (bf16[32,8192]{1,0:T(8,128)(2,1)S(1)}, bf16[32,8192]{1,0:T(8,128)(2,1)S(1)}, u32[]{:S(2)}, u32[]{:S(2)}) collective-permute-start(bf16[32,8192]{1,0:T(8,128)(2,1)S(1)} %collective-permute-done.63.refs_2_), channel_id=1, source_target_pairs={{0,1},{1,0},{2,3},{3,2},{4,5},{5,4},{6,7},{7,6},{8,9},{9,8},{10,11... | collective-permute-start | bytes 1572872 | tf_op jit(solution)/shard_map/ppermute | solution.py:147
  332.7 34.3 %collective-permute-start.77 = (bf16[32,64,256]{2,1,0:T(8,128)(2,1)S(1)}, bf16[32,64,256]{2,1,0:T(8,128)(2,1)S(1)}, u32[]{:S(2)}, u32[]{:S(2)}) collective-permute-start(bf16[32,64,256]{2,1,0:T(8,128)(2,1)S(1)} %get-tuple-element.171), channel_id=1, source_target_pairs={{0,8},{8,0},{16,24},{24,16},{1,9},{9,1},{17,25},{25,17},{2,10},{10... | collective-permute-start | bytes 3145736 | tf_op jit(solution)/shard_map/ppermute | solution.py:303
  333.3 33.7 %collective-permute-start.78 = (bf16[32,64,256]{2,1,0:T(8,128)(2,1)S(1)}, bf16[32,64,256]{2,1,0:T(8,128)(2,1)S(1)}, u32[]{:S(2)}, u32[]{:S(2)}) collective-permute-start(bf16[32,64,256]{2,1,0:T(8,128)(2,1)S(1)} %get-tuple-element.172), channel_id=1, source_target_pairs={{0,16},{8,24},{16,0},{24,8},{1,17},{9,25},{17,1},{25,9},{2,18},{10... | collective-permute-start | bytes 3145736 | tf_op jit(solution)/shard_map/ppermute | solution.py:303
  338.8 14.0 %collective-permute-start.73 = (bf16[32,8192]{1,0:T(8,128)(2,1)S(1)}, bf16[32,8192]{1,0:T(8,128)(2,1)S(1)}, u32[]{:S(2)}, u32[]{:S(2)}) collective-permute-start(bf16[32,8192]{1,0:T(8,128)(2,1)S(1)} %shard_map.75.refs_0_), channel_id=1, source_target_pairs={{0,2},{1,3},{2,0},{3,1},{4,6},{5,7},{6,4},{7,5},{8,10},{9,11},{10,... | collective-permute-start | bytes 1572872 | tf_op jit(solution)/shard_map/ppermute | solution.py:143
  339.3 25.8 %collective-permute-start.74 = (bf16[32,8192]{1,0:T(8,128)(2,1)S(1)}, bf16[32,8192]{1,0:T(8,128)(2,1)S(1)}, u32[]{:S(2)}, u32[]{:S(2)}) collective-permute-start(bf16[32,8192]{1,0:T(8,128)(2,1)S(1)} %shard_map.75.refs_0_), channel_id=1, source_target_pairs={{2,4},{3,5},{4,2},{5,3},{0,6},{1,7},{6,0},{7,1},{10,12},{11,13},{1... | collective-permute-start | bytes 1572872 | tf_op jit(solution)/shard_map/ppermute | solution.py:143
  365.7 15.8 %collective-permute-start.76 = (bf16[32,8192]{1,0:T(8,128)(2,1)S(1)}, bf16[32,8192]{1,0:T(8,128)(2,1)S(1)}, u32[]{:S(2)}, u32[]{:S(2)}) collective-permute-start(bf16[32,8192]{1,0:T(8,128)(2,1)S(1)} %collective-permute-done.74.refs_2_), channel_id=1, source_target_pairs={{4,6},{5,7},{2,0},{3,1},{12,14},{13,15},{10,8},{11,9},{20,22},{21,... | collective-permute-start | bytes 1572872 | tf_op jit(solution)/shard_map/ppermute | solution.py:143
  369.2 12.8 %collective-permute-start.79 = (bf16[32,8192]{1,0:T(8,128)(2,1)S(1)}, bf16[32,8192]{1,0:T(8,128)(2,1)S(1)}, u32[]{:S(2)}, u32[]{:S(2)}) collective-permute-start(bf16[32,8192]{1,0:T(8,128)(2,1)S(1)} %shard_map.75.refs_0_), channel_id=1, source_target_pairs={{0,1},{1,0},{2,3},{3,2},{4,5},{5,4},{6,7},{7,6},{8,9},{9,8},{10,11... | collective-permute-start | bytes 1572872 | tf_op jit(solution)/shard_map/ppermute | solution.py:147
  388.0 25.3 %collective-permute-start.84 = (bf16[32,8192]{1,0:T(8,128)(2,1)S(1)}, bf16[32,8192]{1,0:T(8,128)(2,1)S(1)}, u32[]{:S(2)}, u32[]{:S(2)}) collective-permute-start(bf16[32,8192]{1,0:T(8,128)(2,1)S(1)} %shard_map.77.refs_0_), channel_id=1, source_target_pairs={{0,2},{1,3},{2,0},{3,1},{4,6},{5,7},{6,4},{7,5},{8,10},{9,11},{10,... | collective-permute-start | bytes 1572872 | tf_op jit(solution)/shard_map/ppermute | solution.py:143
  388.1 25.2 %collective-permute-start.85 = (bf16[32,8192]{1,0:T(8,128)(2,1)S(1)}, bf16[32,8192]{1,0:T(8,128)(2,1)S(1)}, u32[]{:S(2)}, u32[]{:S(2)}) collective-permute-start(bf16[32,8192]{1,0:T(8,128)(2,1)S(1)} %shard_map.77.refs_0_), channel_id=1, source_target_pairs={{2,4},{3,5},{4,2},{5,3},{0,6},{1,7},{6,0},{7,1},{10,12},{11,13},{1... | collective-permute-start | bytes 1572872 | tf_op jit(solution)/shard_map/ppermute | solution.py:143
  414.0 15.3 %collective-permute-start.87 = (bf16[32,8192]{1,0:T(8,128)(2,1)S(1)}, bf16[32,8192]{1,0:T(8,128)(2,1)S(1)}, u32[]{:S(2)}, u32[]{:S(2)}) collective-permute-start(bf16[32,8192]{1,0:T(8,128)(2,1)S(1)} %collective-permute-done.85.refs_2_), channel_id=1, source_target_pairs={{4,6},{5,7},{2,0},{3,1},{12,14},{13,15},{10,8},{11,9},{20,22},{21,... | collective-permute-start | bytes 1572872 | tf_op jit(solution)/shard_map/ppermute | solution.py:143
  435.9 14.0 %collective-permute-start.93 = (bf16[32,8192]{1,0:T(8,128)(2,1)S(1)}, bf16[32,8192]{1,0:T(8,128)(2,1)S(1)}, u32[]{:S(2)}, u32[]{:S(2)}) collective-permute-start(bf16[32,8192]{1,0:T(8,128)(2,1)S(1)} %shard_map.79.refs_0_), channel_id=1, source_target_pairs={{0,2},{1,3},{2,0},{3,1},{4,6},{5,7},{6,4},{7,5},{8,10},{9,11},{10,... | collective-permute-start | bytes 1572872 | tf_op jit(solution)/shard_map/ppermute | solution.py:143
  436.4 25.8 %collective-permute-start.94 = (bf16[32,8192]{1,0:T(8,128)(2,1)S(1)}, bf16[32,8192]{1,0:T(8,128)(2,1)S(1)}, u32[]{:S(2)}, u32[]{:S(2)}) collective-permute-start(bf16[32,8192]{1,0:T(8,128)(2,1)S(1)} %shard_map.79.refs_0_), channel_id=1, source_target_pairs={{2,4},{3,5},{4,2},{5,3},{0,6},{1,7},{6,0},{7,1},{10,12},{11,13},{1... | collective-permute-start | bytes 1572872 | tf_op jit(solution)/shard_map/ppermute | solution.py:143
  462.9 15.8 %collective-permute-start.96 = (bf16[32,8192]{1,0:T(8,128)(2,1)S(1)}, bf16[32,8192]{1,0:T(8,128)(2,1)S(1)}, u32[]{:S(2)}, u32[]{:S(2)}) collective-permute-start(bf16[32,8192]{1,0:T(8,128)(2,1)S(1)} %collective-permute-done.94.refs_2_), channel_id=1, source_target_pairs={{4,6},{5,7},{2,0},{3,1},{12,14},{13,15},{10,8},{11,9},{20,22},{21,... | collective-permute-start | bytes 1572872 | tf_op jit(solution)/shard_map/ppermute | solution.py:143
  466.3 12.9 %collective-permute-start.97 = (bf16[32,8192]{1,0:T(8,128)(2,1)S(1)}, bf16[32,8192]{1,0:T(8,128)(2,1)S(1)}, u32[]{:S(2)}, u32[]{:S(2)}) collective-permute-start(bf16[32,8192]{1,0:T(8,128)(2,1)S(1)} %shard_map.79.refs_0_), channel_id=1, source_target_pairs={{0,1},{1,0},{2,3},{3,2},{4,5},{5,4},{6,7},{7,6},{8,9},{9,8},{10,11... | collective-permute-start | bytes 1572872 | tf_op jit(solution)/shard_map/ppermute | solution.py:147
  (42 other events, 281.8 us)

commit v3 on v2

--- a/solution.py
+++ b/solution.py
@@ -102,7 +102,11 @@
         copy(operand, first, count, index).wait()
 
 
-def gather_weights(place, weights, plan, shape):
+def pinned(operands, in_hbm):
+    return [pltpu.with_memory_space_constraint(x, pltpu.HBM) if n in in_hbm else x for n, x in enumerate(operands)]
+
+
+def gather_weights(place, weights, in_hbm, plan, shape):
     smem = pl.BlockSpec(memory_space=pltpu.SMEM)
     return pl.pallas_call(
         functools.partial(gather_weights_kernel, plan),
@@ -111,7 +115,7 @@
         out_specs=pl.BlockSpec(memory_space=pltpu.VMEM),
         scratch_shapes=[pltpu.SemaphoreType.DMA((shape[0],))],
         compiler_params=pltpu.CompilerParams(vmem_limit_bytes=SMALL_VMEM),
-    )(place, *weights)
+    )(place, *pinned(weights, in_hbm))
 
 
 def apply_layer(codes, place, acts, act_plan, weights, bias):
@@ -147,25 +151,34 @@
     return lax.ppermute(x, "rows", [(i, i ^ 1) for i in range(lax.axis_size("rows"))])
 
 
-def gather_line(x, pause):
+def after_all(x, *arrived):
+    return lax.optimization_barrier((x, *arrived))[0]
+
+
+def gather_line(x, pause, split):
+    inside, ends = [(1, 2), (2, 1)], [(0, 3), (3, 0)]
     near = along_line(x, [(0, 1), (1, 0), (2, 3), (3, 2)])
-    cross = along_line(x, [(1, 2), (2, 1), (0, 3), (3, 0)])
+    cross = along_line(x, inside if split else inside + ends)
+    trade = [along_line(x, ends)] if split else []
     x_swapped = to_other_core(x)
     near, cross = pause(x_swapped, [near, cross])
-    far = along_line(near, [(1, 2), (2, 1)])
+    far = along_line(near, inside)
     outer = along_line(cross, [(2, 3), (1, 0)])
     near_swapped = to_other_core(near)
-    far, outer = pause(near_swapped, [far, outer])
-    rest = [cross, far, outer]
+    (outer,) = pause(near_swapped, [outer])
+    rest = [cross, far, outer] + trade
     return [x, near] + rest + [x_swapped, near_swapped] + [to_other_core(buf) for buf in rest]
 
 
-def line_plan():
-    plan = []
-    for side in range(CORES):
-        for buf, (slot, want) in enumerate([(0, None), (1, None), (2, None), (3, (0, 1)), (3, (0, 0))]):
-            plan.append((side * 5 + buf, side * 4 + slot, 1, want))
-    return plan
+def line_plan(split):
+    middle, ends = (0, 1), (0, 0)
+    where = [(0, None), (1, None), (2, middle if split else None), (3, middle), (3, ends), (2, ends)]
+    where = where[: 6 if split else 5]
+    return [
+        (side * len(where) + buf, side * 4 + slot, 1, want)
+        for side in range(CORES)
+        for buf, (slot, want) in enumerate(where)
+    ]
 
 
 def line_slots(row_devs):
@@ -239,7 +252,7 @@
         pl.when(place[1] == p)(functools.partial(copy_for, p))
 
 
-def pick(place, operands, choices, shape):
+def pick(place, operands, in_hbm, choices, shape):
     smem = pl.BlockSpec(memory_space=pltpu.SMEM)
     return pl.pallas_call(
         functools.partial(pick_kernel, choices, len(choices)),
@@ -248,7 +261,24 @@
         out_specs=[pl.BlockSpec(memory_space=pltpu.VMEM)] * len(choices),
         scratch_shapes=[pltpu.SemaphoreType.DMA((len(choices),))],
         compiler_params=pltpu.CompilerParams(vmem_limit_bytes=SMALL_VMEM),
-    )(place, *operands)
+    )(place, *pinned(operands, in_hbm))
+
+
+def load_kernel(source, out, sem):
+    copy = pltpu.make_async_copy(source, out, sem)
+    copy.start()
+    copy.wait()
+
+
+def load(x):
+    return pl.pallas_call(
+        load_kernel,
+        out_shape=pltpu.VMEM(x.shape, x.dtype),
+        in_specs=[pl.BlockSpec(memory_space=pl.ANY)],
+        out_specs=pl.BlockSpec(memory_space=pltpu.VMEM),
+        scratch_shapes=[pltpu.SemaphoreType.DMA],
+        compiler_params=pltpu.CompilerParams(vmem_limit_bytes=SMALL_VMEM),
+    )(pltpu.with_memory_space_constraint(x, pltpu.HBM))
 
 
 class WeightStream:
@@ -261,6 +291,7 @@
         self.arrays = {}
         self.where = {}
         self.flying = []
+        self.loaded = False
         self.started = 0
         self.gathered = {}
 
@@ -274,7 +305,7 @@
     def array(self, name):
         return self.weights if name == "own" else self.arrays[name]
 
-    def advance(self, after=(), through=(), layer=None):
+    def advance(self, after=(), through=()):
         sends = self.slots[self.started] if self.started < len(self.slots) else []
         sides = {}
         for u, v, piece in sends:
@@ -286,18 +317,12 @@
         for key, value in zip(keys, held):
             self.arrays[key] = value
         self.flying = []
-        made = []
-        if layer is not None and self.started >= self.ready[layer]:
-            self.gathered[layer] = self.gather(layer)
-            made = [self.gathered[layer]]
         if not sends:
-            return lax.optimization_barrier((list(through), made))[0]
+            return list(through)
         choices = [[(names.index(name), index) for name, index in items] for items in chosen.values()]
         shape = (self.each,) + self.weights.shape[2:]
-        if self.started == 0:
-            picked = [self.weights[0, q * self.each : (q + 1) * self.each] for q in range(2)]
-        else:
-            picked = pick(self.place, [self.array(n) for n in names], choices, shape)
+        in_hbm = [n for n, name in enumerate(names) if name == "own" and not self.loaded]
+        picked = pick(self.place, [self.array(n) for n in names], in_hbm, choices, shape)
         for side, array in zip(chosen, picked):
             key = ("got", self.started, side)
             self.arrays[key] = lax.ppermute(array, "pipe", [(p, p ^ side) for p in range(self.square)])
@@ -305,7 +330,7 @@
         for u, v, piece in sends:
             self.where[v, piece] = ("got", self.started, u ^ v)
         self.started += 1
-        return lax.optimization_barrier((list(through), made + list(picked)))[0]
+        return lax.optimization_barrier((list(through), picked))[0]
 
     def gather(self, layer):
         if layer in self.gathered:
@@ -317,8 +342,10 @@
                 if name not in names:
                     names.append(name)
                 plan.append((names.index(name), q * self.each, self.each, index, (1, p)))
-        shape = self.weights.shape[1:]
-        return gather_weights(self.place, [self.array(name) for name in names], plan, shape)
+        in_hbm = [n for n, name in enumerate(names) if name == "own" and not self.loaded]
+        arrays = [self.array(name) for name in names]
+        self.gathered[layer] = gather_weights(self.place, arrays, in_hbm, plan, self.weights.shape[1:])
+        return self.gathered[layer]
 
 
 def gather_square(x):
@@ -363,17 +390,25 @@
             step = 0
 
             def pause(arrived, through):
-                nonlocal step, all_codes, all_bias
+                nonlocal step
                 step += 1
                 if layer == 0 and step == 1:
-                    arrived, all_codes, all_bias = lax.optimization_barrier((arrived, all_codes, all_bias))
-                return stream.advance([arrived], through, layer if step == 2 else None)
-
-            acts = gather_line(current, pause)
+                    stream.weights = load(after_all(weights, arrived))
+                    stream.loaded = True
+                if step == 1:
+                    through = stream.advance([arrived] + ([all_codes, all_bias] if layer == 0 else []), through)
+                else:
+                    through = stream.advance([arrived], through)
+                if step == 2 and stream.started >= stream.ready[layer]:
+                    through, _ = lax.optimization_barrier((through, stream.gather(layer)))
+                return through
+
+            split = stream.started == len(stream.slots)
+            acts = gather_line(current, pause, split)
             while stream.started < stream.ready[layer] + (layer == 0):
                 stream.advance()
             current = apply_layer(
-                all_codes[layer], place, acts, line_plan(), stream.gather(layer), all_bias[layer][None]
+                all_codes[layer], place, acts, line_plan(split), stream.gather(layer), all_bias[layer][None]
             )
         return current
 

time: 487 us -> 476 us (0.977)
  waiting for transfers between devices: 330 us -> 304 us
  starting transfers between devices: 81.8 us -> 97.7 us
  local copies, waits for them, and re-layouts: 10.5 us -> 5.18 us
    ppermute x32 -> x35, waiting for transfers between devices: 164 us -> 137 us  [along_line(): return lax.ppermute(x, 'rows', moves)]
    ppermute x6, waiting for transfers between devices: 19.2 us -> 0.02 us  [gather_square(): lax.ppermute(x, 'pipe', [(p, p ^ side) for p in range(4)])]
    ppermute x24, waiting for transfers between devices: 138 us -> 155 us  [advance(): lax.ppermute(array, 'pipe', [(p, p ^ side) for p in range(self.square)])]
    ppermute x32 -> x35, starting transfers between devices: 37.4 us -> 52.7 us  [along_line(): return lax.ppermute(x, 'rows', moves)]
    ppermute x40 -> x43, waiting for transfers between devices: 9.15 us -> 12.7 us  [to_other_core(): lax.ppermute(x, 'rows', [(i, i ^ 1) for i in range(lax.axis_size('rows'))])]
    pallas_call x11 -> x12, Pallas kernels: 9.6 us -> 11.6 us  [pick(): pl.pallas_call(functools.partial(pick_kernel, choices, len(choices)), out...]
  transfers between devices with their start and end apart: 102 -> 108, of which waited for: 48 -> 49; matrix products, arithmetic and copies ran while one was open for 1% -> 1% of each run, Pallas kernels for 10% -> 10%
where the time goes in v3:
time: 476 us; the launch traced here: 475 us
  waiting for transfers between devices  304 us (64%)
  starting transfers between devices  97.7 us (21%)
  Pallas kernels  65.1 us (14%)
  local copies, waits for them, and re-layouts  5.18 us (1%)
    ppermute x24, waiting for transfers between devices, advance(): lax.ppermute(array, 'pipe', [(p, p ^ side) for p in range(self.square)])  155 us
    ppermute x35, waiting for transfers between devices, along_line(): return lax.ppermute(x, 'rows', moves)  137 us
    ppermute x35, starting transfers between devices, along_line(): return lax.ppermute(x, 'rows', moves)  52.7 us
    pallas_call x8, Pallas kernels, apply_layer(): pl.pallas_call(kernel, out_shape=jax.ShapeDtypeStruct((rows, neurons), jn...  32.1 us
    ppermute x24, starting transfers between devices, advance(): lax.ppermute(array, 'pipe', [(p, p ^ side) for p in range(self.square)])  29.6 us
    pallas_call x8, Pallas kernels, gather_weights(): pl.pallas_call(functools.partial(gather_weights_kernel, plan), out_shape=...  17.8 us
    ppermute x43, waiting for transfers between devices, to_other_core(): lax.ppermute(x, 'rows', [(i, i ^ 1) for i in range(lax.axis_size('rows'))])  12.7 us
    pallas_call x12, Pallas kernels, pick(): pl.pallas_call(functools.partial(pick_kernel, choices, len(choices)), out...  11.6 us
  transfers between devices with their start and end apart: 108, of which 49 were waited for; matrix products, arithmetic and copies ran while one was open for 1% of the time, Pallas kernels for 10%

profile of v3, /device:TPU:0, one launch (start us, length us, event | category | flops | bytes accessed | tf_op | source)
XLA Modules:
  0.0 474.9 jit_solution(15985372915137491267)
XLA Ops:
  0.1 2.1 shard_map.55
  2.2 3.0 collective-permute-start.6
  8.3 2.5 collective-permute-start.4
  10.8 3.6 shard_map.56.refs_2_.refs_1_.refs_0_.refs_4_.refs_3_.refs_5_
  14.4 14.0 %collective-permute-done.6.refs_0_.refs_1_.refs_3_.refs_2_ = bf16[32,64,256]{2,1,0:T(8,128)(2,1)S(1)} collective-permute-done((bf16[32,64,256]{2,1,0:T(8,128)(2,1)S(1)}, bf16[32,64,256]{2,1,0:T(8,128)(2,1)S(1)}, u32[]{:S(2)}, u32[]{:S(2)}) %collective-permute-start.6) | collective-permute-done | bytes 1048608 | tf_op jit(solution)/shard_map/ppermute | solution.py:328
  31.0 1.7 collective-permute-start.12
  32.7 1.7 collective-permute-done.4.refs_2_
  34.4 1.9 collective-permute-done.10.refs_6_
  37.2 17.2 %collective-permute-done.11.refs_0_.refs_6_.refs_5_ = bf16[32,64,256]{2,1,0:T(8,128)(2,1)S(1)} collective-permute-done((bf16[32,64,256]{2,1,0:T(8,128)(2,1)S(1)}, bf16[32,64,256]{2,1,0:T(8,128)(2,1)S(1)}, u32[]{:S(2)}, u32[]{:S(2)}) %collective-permute-start.11) | collective-permute-done | bytes 1048608 | tf_op jit(solution)/shard_map/ppermute | solution.py:328
  54.7 2.0 shard_map.58
  65.5 14.7 %collective-permute-done.16.refs_2_.refs_7_ = bf16[32,64,256]{2,1,0:T(8,128)(2,1)} collective-permute-done((bf16[32,64,256]{2,1,0:T(8,128)(2,1)}, bf16[32,64,256]{2,1,0:T(8,128)(2,1)}, u32[]{:S(2)}, u32[]{:S(2)}) %collective-permute-start.16) | collective-permute-done | bytes 1048608 | tf_op jit(solution)/shard_map/ppermute | solution.py:328
  80.2 2.3 collective-permute-start.22
  83.0 3.4 copy-done.1
  93.7 10.6 %collective-permute-done.9.refs_4_ = bf16[32,8192]{1,0:T(8,128)(2,1)S(1)} collective-permute-done((bf16[32,8192]{1,0:T(8,128)(2,1)S(1)}, bf16[32,8192]{1,0:T(8,128)(2,1)S(1)}, u32[]{:S(2)}, u32[]{:S(2)}) %collective-permute-start.9) | collective-permute-done | bytes 524320 | tf_op jit(solution)/shard_map/ppermute | solution.py:147
  104.3 5.7 %collective-permute-done.18.refs_7_.refs_0_.refs_1_.refs_3_ = bf16[32,64,256]{2,1,0:T(8,128)(2,1)S(1)} collective-permute-done((bf16[32,64,256]{2,1,0:T(8,128)(2,1)S(1)}, bf16[32,64,256]{2,1,0:T(8,128)(2,1)S(1)}, u32[]{:S(2)}, u32[]{:S(2)}) %collective-permute-start.18) | collective-permute-done | bytes 1048608 | tf_op jit(solution)/shard_map/ppermute | solution.py:328
  111.8 2.2 collective-permute-start.27
  114.3 2.1 shard_map.60.refs_10_
  116.5 3.9 shard_map.61.refs_0_
  122.1 2.5 collective-permute-start.24
  124.6 8.7 %collective-permute-done.26.refs_2_.refs_7_.refs_8_.refs_4_ = bf16[32,64,256]{2,1,0:T(8,128)(2,1)S(1)} collective-permute-done((bf16[32,64,256]{2,1,0:T(8,128)(2,1)S(1)}, bf16[32,64,256]{2,1,0:T(8,128)(2,1)S(1)}, u32[]{:S(2)}, u32[]{:S(2)}) %collective-permute-start.26) | collective-permute-done | bytes 1048608 | tf_op jit(solution)/shard_map/ppermute | solution.py:328
  135.2 2.2 collective-permute-start.32
  137.4 10.8 %collective-permute-done.24.refs_2_ = bf16[32,8192]{1,0:T(8,128)(2,1)S(1)} collective-permute-done((bf16[32,8192]{1,0:T(8,128)(2,1)S(1)}, bf16[32,8192]{1,0:T(8,128)(2,1)S(1)}, u32[]{:S(2)}, u32[]{:S(2)}) %collective-permute-start.24) | collective-permute-done | bytes 524320 | tf_op jit(solution)/shard_map/ppermute | solution.py:147
  151.0 3.1 collective-permute-done.31.refs_4_.refs_2_.refs_0_.refs_10_
  154.9 11.4 %collective-permute-done.29.refs_4_ = bf16[32,8192]{1,0:T(8,128)(2,1)S(1)} collective-permute-done((bf16[32,8192]{1,0:T(8,128)(2,1)S(1)}, bf16[32,8192]{1,0:T(8,128)(2,1)S(1)}, u32[]{:S(2)}, u32[]{:S(2)}) %collective-permute-start.29) | collective-permute-done | bytes 524320 | tf_op jit(solution)/shard_map/ppermute | solution.py:147
  166.3 2.1 shard_map.65.refs_10_
  168.5 2.2 collective-permute-start.39
  171.3 3.9 shard_map.66.refs_0_
  177.1 17.3 %collective-permute-done.39.refs_2_.refs_3_.refs_8_.refs_5_ = bf16[32,64,256]{2,1,0:T(8,128)(2,1)S(1)} collective-permute-done((bf16[32,64,256]{2,1,0:T(8,128)(2,1)S(1)}, bf16[32,64,256]{2,1,0:T(8,128)(2,1)S(1)}, u32[]{:S(2)}, u32[]{:S(2)}) %collective-permute-start.39) | collective-permute-done | bytes 1048608 | tf_op jit(solution)/shard_map/ppermute | solution.py:328
  198.1 2.8 collective-permute-done.36.refs_1_
  203.6 17.5 %collective-permute-done.44.refs_1_.refs_5_.refs_7_.refs_4_ = bf16[32,64,256]{2,1,0:T(8,128)(2,1)S(1)} collective-permute-done((bf16[32,64,256]{2,1,0:T(8,128)(2,1)S(1)}, bf16[32,64,256]{2,1,0:T(8,128)(2,1)S(1)}, u32[]{:S(2)}, u32[]{:S(2)}) %collective-permute-start.44) | collective-permute-done | bytes 1048608 | tf_op jit(solution)/shard_map/ppermute | solution.py:328
  221.4 3.1 shard_map.69.refs_10_
  227.3 3.9 shard_map.70.refs_0_
  232.8 18.2 %collective-permute-done.52.refs_4_.refs_2_.refs_1_.refs_10_ = bf16[32,64,256]{2,1,0:T(8,128)(2,1)S(1)} collective-permute-done((bf16[32,64,256]{2,1,0:T(8,128)(2,1)S(1)}, bf16[32,64,256]{2,1,0:T(8,128)(2,1)S(1)}, u32[]{:S(2)}, u32[]{:S(2)}) %collective-permute-start.52) | collective-permute-done | bytes 1048608 | tf_op jit(solution)/shard_map/ppermute | solution.py:328
  252.0 1.7 collective-permute-start.57
  254.0 2.8 collective-permute-done.49.refs_1_
  258.9 2.1 shard_map.73.refs_10_
  261.7 15.0 %collective-permute-done.57.refs_1_.refs_6_.refs_8_.refs_7_ = bf16[32,64,256]{2,1,0:T(8,128)(2,1)S(1)} collective-permute-done((bf16[32,64,256]{2,1,0:T(8,128)(2,1)S(1)}, bf16[32,64,256]{2,1,0:T(8,128)(2,1)S(1)}, u32[]{:S(2)}, u32[]{:S(2)}) %collective-permute-start.57) | collective-permute-done | bytes 1048608 | tf_op jit(solution)/shard_map/ppermute | solution.py:328
  280.6 3.9 shard_map.74.refs_0_
  286.1 18.2 %collective-permute-done.65.refs_0_.refs_5_.refs_2_ = bf16[32,64,256]{2,1,0:T(8,128)(2,1)S(1)} collective-permute-done((bf16[32,64,256]{2,1,0:T(8,128)(2,1)S(1)}, bf16[32,64,256]{2,1,0:T(8,128)(2,1)S(1)}, u32[]{:S(2)}, u32[]{:S(2)}) %collective-permute-start.65) | collective-permute-done | bytes 1048608 | tf_op jit(solution)/shard_map/ppermute | solution.py:328
  305.3 4.8 %collective-permute-done.62.refs_1_ = bf16[32,8192]{1,0:T(8,128)(2,1)S(1)} collective-permute-done((bf16[32,8192]{1,0:T(8,128)(2,1)S(1)}, bf16[32,8192]{1,0:T(8,128)(2,1)S(1)}, u32[]{:S(2)}, u32[]{:S(2)}) %collective-permute-start.62) | collective-permute-done | bytes 524320 | tf_op jit(solution)/shard_map/ppermute | solution.py:147
  312.1 2.1 shard_map.76.refs_10_
  314.8 10.1 %collective-permute-done.68.refs_4_ = bf16[32,8192]{1,0:T(8,128)(2,1)S(1)} collective-permute-done((bf16[32,8192]{1,0:T(8,128)(2,1)S(1)}, bf16[32,8192]{1,0:T(8,128)(2,1)S(1)}, u32[]{:S(2)}, u32[]{:S(2)}) %collective-permute-start.68) | collective-permute-done | bytes 524320 | tf_op jit(solution)/shard_map/ppermute | solution.py:147
  327.8 3.9 shard_map.77.refs_0_
  332.4 6.8 %collective-permute-start.73 = (bf16[32,8192]{1,0:T(8,128)(2,1)S(1)}, bf16[32,8192]{1,0:T(8,128)(2,1)S(1)}, u32[]{:S(2)}, u32[]{:S(2)}) collective-permute-start(bf16[32,8192]{1,0:T(8,128)(2,1)S(1)} %shard_map.77.refs_0_), channel_id=1, source_target_pairs={{0,2},{1,3},{2,0},{3,1},{4,6},{5,7},{6,4},{7,5},{8,10},{9,11},{10,... | collective-permute-start | bytes 1572872 | tf_op jit(solution)/shard_map/ppermute | solution.py:147
  339.2 3.1 collective-permute-start.79
  343.6 8.0 %collective-permute-done.73.refs_1_ = bf16[32,8192]{1,0:T(8,128)(2,1)S(1)} collective-permute-done((bf16[32,8192]{1,0:T(8,128)(2,1)S(1)}, bf16[32,8192]{1,0:T(8,128)(2,1)S(1)}, u32[]{:S(2)}, u32[]{:S(2)}) %collective-permute-start.73) | collective-permute-done | bytes 524320 | tf_op jit(solution)/shard_map/ppermute | solution.py:147
  352.4 2.1 shard_map.78.refs_12_
  355.0 8.3 %collective-permute-done.79.refs_5_ = bf16[32,8192]{1,0:T(8,128)(2,1)S(1)} collective-permute-done((bf16[32,8192]{1,0:T(8,128)(2,1)S(1)}, bf16[32,8192]{1,0:T(8,128)(2,1)S(1)}, u32[]{:S(2)}, u32[]{:S(2)}) %collective-permute-start.79) | collective-permute-done | bytes 524320 | tf_op jit(solution)/shard_map/ppermute | solution.py:147
  363.3 10.7 %collective-permute-done.76.refs_4_ = bf16[32,8192]{1,0:T(8,128)(2,1)S(1)} collective-permute-done((bf16[32,8192]{1,0:T(8,128)(2,1)S(1)}, bf16[32,8192]{1,0:T(8,128)(2,1)S(1)}, u32[]{:S(2)}, u32[]{:S(2)}) %collective-permute-start.76) | collective-permute-done | bytes 524320 | tf_op jit(solution)/shard_map/ppermute | solution.py:147
  377.4 3.9 shard_map.79.refs_0_
  382.0 3.2 collective-permute-start.86
  385.3 3.1 collective-permute-start.90
  389.7 7.9 %collective-permute-done.86.refs_1_ = bf16[32,8192]{1,0:T(8,128)(2,1)S(1)} collective-permute-done((bf16[32,8192]{1,0:T(8,128)(2,1)S(1)}, bf16[32,8192]{1,0:T(8,128)(2,1)S(1)}, u32[]{:S(2)}, u32[]{:S(2)}) %collective-permute-start.86) | collective-permute-done | bytes 524320 | tf_op jit(solution)/shard_map/ppermute | solution.py:147
  398.4 2.1 shard_map.80.refs_12_
  401.1 8.5 %collective-permute-done.90.refs_5_ = bf16[32,8192]{1,0:T(8,128)(2,1)S(1)} collective-permute-done((bf16[32,8192]{1,0:T(8,128)(2,1)S(1)}, bf16[32,8192]{1,0:T(8,128)(2,1)S(1)}, u32[]{:S(2)}, u32[]{:S(2)}) %collective-permute-start.90) | collective-permute-done | bytes 524320 | tf_op jit(solution)/shard_map/ppermute | solution.py:147
  409.6 10.9 %collective-permute-done.89.refs_4_ = bf16[32,8192]{1,0:T(8,128)(2,1)S(1)} collective-permute-done((bf16[32,8192]{1,0:T(8,128)(2,1)S(1)}, bf16[32,8192]{1,0:T(8,128)(2,1)S(1)}, u32[]{:S(2)}, u32[]{:S(2)}) %collective-permute-start.89) | collective-permute-done | bytes 524320 | tf_op jit(solution)/shard_map/ppermute | solution.py:147
  423.9 3.9 shard_map.81.refs_0_
  428.5 3.0 collective-permute-start.97
  431.5 3.1 collective-permute-start.101
  435.9 7.9 %collective-permute-done.97.refs_1_ = bf16[32,8192]{1,0:T(8,128)(2,1)S(1)} collective-permute-done((bf16[32,8192]{1,0:T(8,128)(2,1)S(1)}, bf16[32,8192]{1,0:T(8,128)(2,1)S(1)}, u32[]{:S(2)}, u32[]{:S(2)}) %collective-permute-start.97) | collective-permute-done | bytes 524320 | tf_op jit(solution)/shard_map/ppermute | solution.py:147
  444.6 2.1 shard_map.82.refs_12_
  447.3 8.5 %collective-permute-done.101.refs_5_ = bf16[32,8192]{1,0:T(8,128)(2,1)S(1)} collective-permute-done((bf16[32,8192]{1,0:T(8,128)(2,1)S(1)}, bf16[32,8192]{1,0:T(8,128)(2,1)S(1)}, u32[]{:S(2)}, u32[]{:S(2)}) %collective-permute-start.101) | collective-permute-done | bytes 524320 | tf_op jit(solution)/shard_map/ppermute | solution.py:147
  455.8 10.8 %collective-permute-done.100.refs_4_ = bf16[32,8192]{1,0:T(8,128)(2,1)S(1)} collective-permute-done((bf16[32,8192]{1,0:T(8,128)(2,1)S(1)}, bf16[32,8192]{1,0:T(8,128)(2,1)S(1)}, u32[]{:S(2)}, u32[]{:S(2)}) %collective-permute-start.100) | collective-permute-done | bytes 524320 | tf_op jit(solution)/shard_map/ppermute | solution.py:147
  470.1 4.7 shard_map.83
  (226 shorter events, 82.4 us)
Async XLA Ops:
  2.2 26.2 %collective-permute-start.6 = (bf16[32,64,256]{2,1,0:T(8,128)(2,1)S(1)}, bf16[32,64,256]{2,1,0:T(8,128)(2,1)S(1)}, u32[]{:S(2)}, u32[]{:S(2)}) collective-permute-start(bf16[32,64,256]{2,1,0:T(8,128)(2,1)S(1)} %get-tuple-element.88), channel_id=1, source_target_pairs={{0,8},{8,0},{16,24},{24,16},{1,9},{9,1},{17,25},{25,17},{2,10},{10... | collective-permute-start | bytes 3145736 | tf_op jit(solution)/shard_map/ppermute | solution.py:328
  5.2 24.6 %collective-permute-start.7 = (bf16[32,64,256]{2,1,0:T(8,128)(2,1)S(1)}, bf16[32,64,256]{2,1,0:T(8,128)(2,1)S(1)}, u32[]{:S(2)}, u32[]{:S(2)}) collective-permute-start(bf16[32,64,256]{2,1,0:T(8,128)(2,1)S(1)} %get-tuple-element.89), channel_id=1, source_target_pairs={{0,16},{8,24},{16,0},{24,8},{1,17},{9,25},{17,1},{25,9},{2,18},{10... | collective-permute-start | bytes 3145736 | tf_op jit(solution)/shard_map/ppermute | solution.py:328
  6.7 26.0 %collective-permute-start.3 = (bf16[32,8192]{1,0:T(8,128)(2,1)S(1)}, bf16[32,8192]{1,0:T(8,128)(2,1)S(1)}, u32[]{:S(2)}, u32[]{:S(2)}) collective-permute-start(bf16[32,8192]{1,0:T(8,128)(2,1)S(1)} %copy-done.7), channel_id=1, source_target_pairs={{0,2},{1,3},{2,0},{3,1},{4,6},{5,7},{6,4},{7,5},{8,10},{9,11},{10,... | collective-permute-start | bytes 1572872 | tf_op jit(solution)/shard_map/ppermute | solution.py:147
  8.3 26.1 %collective-permute-start.4 = (bf16[32,8192]{1,0:T(8,128)(2,1)S(1)}, bf16[32,8192]{1,0:T(8,128)(2,1)S(1)}, u32[]{:S(2)}, u32[]{:S(2)}) collective-permute-start(bf16[32,8192]{1,0:T(8,128)(2,1)S(1)} %copy-done.7), channel_id=1, source_target_pairs={{2,4},{3,5},{4,2},{5,3},{0,6},{1,7},{6,0},{7,1},{10,12},{11,13},{1... | collective-permute-start | bytes 1572872 | tf_op jit(solution)/shard_map/ppermute | solution.py:147
  30.6 23.8 %collective-permute-start.11 = (bf16[32,64,256]{2,1,0:T(8,128)(2,1)S(1)}, bf16[32,64,256]{2,1,0:T(8,128)(2,1)S(1)}, u32[]{:S(2)}, u32[]{:S(2)}) collective-permute-start(bf16[32,64,256]{2,1,0:T(8,128)(2,1)S(1)} %get-tuple-element.93), channel_id=1, source_target_pairs={{0,8},{8,0},{16,24},{24,16},{1,9},{9,1},{17,25},{25,17},{2,10},{10... | collective-permute-start | bytes 3145736 | tf_op jit(solution)/shard_map/ppermute | solution.py:328
  31.0 23.7 %collective-permute-start.12 = (bf16[32,64,256]{2,1,0:T(8,128)(2,1)S(1)}, bf16[32,64,256]{2,1,0:T(8,128)(2,1)S(1)}, u32[]{:S(2)}, u32[]{:S(2)}) collective-permute-start(bf16[32,64,256]{2,1,0:T(8,128)(2,1)S(1)} %get-tuple-element.94), channel_id=1, source_target_pairs={{0,16},{8,24},{16,0},{24,8},{1,17},{9,25},{17,1},{25,9},{2,18},{10... | collective-permute-start | bytes 3145736 | tf_op jit(solution)/shard_map/ppermute | solution.py:328
  56.8 23.4 %collective-permute-start.16 = (bf16[32,64,256]{2,1,0:T(8,128)(2,1)}, bf16[32,64,256]{2,1,0:T(8,128)(2,1)}, u32[]{:S(2)}, u32[]{:S(2)}) collective-permute-start(bf16[32,64,256]{2,1,0:T(8,128)(2,1)} %get-tuple-element.99), channel_id=1, source_target_pairs={{0,8},{8,0},{16,24},{24,16},{1,9},{9,1},{17,25},{25,17},{2,10},{10... | collective-permute-start | bytes 3145736 | tf_op jit(solution)/shard_map/ppermute | solution.py:328
  58.2 24.2 %collective-permute-start.17 = (bf16[32,64,256]{2,1,0:T(8,128)(2,1)}, bf16[32,64,256]{2,1,0:T(8,128)(2,1)S(1)}, u32[]{:S(2)}, u32[]{:S(2)}) collective-permute-start(bf16[32,64,256]{2,1,0:T(8,128)(2,1)} %get-tuple-element.100), channel_id=1, source_target_pairs={{0,16},{8,24},{16,0},{24,8},{1,17},{9,25},{17,1},{25,9},{2,18},{10... | collective-permute-start | bytes 3145736 | tf_op jit(solution)/shard_map/ppermute | solution.py:328
  62.0 25.2 %collective-permute-start.2 = (s32[2,512]{1,0:T(2,128)S(1)}, s32[2,512]{1,0:T(2,128)S(1)}, u32[]{:S(2)}, u32[]{:S(2)}) collective-permute-start(s32[2,512]{1,0:T(2,128)S(1)} %fusion.1), channel_id=1, source_target_pairs={{0,24},{8,16},{16,8},{24,0},{1,25},{9,17},{17,9},{25,1},{2,26},{10... | collective-permute-start | bytes 12296 | tf_op jit(solution)/shard_map/ppermute | solution.py:353
  62.6 25.2 %collective-permute-start.1 = (s32[2,512]{1,0:T(2,128)S(1)}, s32[2,512]{1,0:T(2,128)S(1)}, u32[]{:S(2)}, u32[]{:S(2)}) collective-permute-start(s32[2,512]{1,0:T(2,128)S(1)} %fusion.1), channel_id=1, source_target_pairs={{0,16},{8,24},{16,0},{24,8},{1,17},{9,25},{17,1},{25,9},{2,18},{10... | collective-permute-start | bytes 12296 | tf_op jit(solution)/shard_map/ppermute | solution.py:353
  64.1 25.2 %collective-permute-start = (s32[2,512]{1,0:T(2,128)S(1)}, s32[2,512]{1,0:T(2,128)S(1)}, u32[]{:S(2)}, u32[]{:S(2)}) collective-permute-start(s32[2,512]{1,0:T(2,128)S(1)} %fusion.1), channel_id=1, source_target_pairs={{0,8},{8,0},{16,24},{24,16},{1,9},{9,1},{17,25},{25,17},{2,10},{10... | collective-permute-start | bytes 12296 | tf_op jit(solution)/shard_map/ppermute | solution.py:353
  87.9 22.1 %collective-permute-start.18 = (bf16[32,64,256]{2,1,0:T(8,128)(2,1)S(1)}, bf16[32,64,256]{2,1,0:T(8,128)(2,1)S(1)}, u32[]{:S(2)}, u32[]{:S(2)}) collective-permute-start(bf16[32,64,256]{2,1,0:T(8,128)(2,1)S(1)} %get-tuple-element.104), channel_id=1, source_target_pairs={{0,8},{8,0},{16,24},{24,16},{1,9},{9,1},{17,25},{25,17},{2,10},{10... | collective-permute-start | bytes 3145736 | tf_op jit(solution)/shard_map/ppermute | solution.py:328
  89.3 20.7 %collective-permute-start.19 = (bf16[32,64,256]{2,1,0:T(8,128)(2,1)S(1)}, bf16[32,64,256]{2,1,0:T(8,128)(2,1)S(1)}, u32[]{:S(2)}, u32[]{:S(2)}) collective-permute-start(bf16[32,64,256]{2,1,0:T(8,128)(2,1)S(1)} %get-tuple-element.105), channel_id=1, source_target_pairs={{0,16},{8,24},{16,0},{24,8},{1,17},{9,25},{17,1},{25,9},{2,18},{10... | collective-permute-start | bytes 3145736 | tf_op jit(solution)/shard_map/ppermute | solution.py:328
  93.1 23.3 %collective-permute-start.13 = (bf16[32,8192]{1,0:T(8,128)(2,1)S(1)}, bf16[32,8192]{1,0:T(8,128)(2,1)S(1)}, u32[]{:S(2)}, u32[]{:S(2)}) collective-permute-start(bf16[32,8192]{1,0:T(8,128)(2,1)S(1)} %copy-done.14), channel_id=1, source_target_pairs={{0,1},{1,0},{2,3},{3,2},{4,5},{5,4},{6,7},{7,6},{8,9},{9,8},{10,11... | collective-permute-start | bytes 1572872 | tf_op jit(solution)/shard_map/ppermute | solution.py:151
  93.2 23.3 %collective-permute-start.14 = (bf16[32,8192]{1,0:T(8,128)(2,1)S(1)}, bf16[32,8192]{1,0:T(8,128)(2,1)S(1)}, u32[]{:S(2)}, u32[]{:S(2)}) collective-permute-start(bf16[32,8192]{1,0:T(8,128)(2,1)S(1)} %collective-permute-done.8.refs_3_), channel_id=1, source_target_pairs={{0,1},{1,0},{2,3},{3,2},{4,5},{5,4},{6,7},{7,6},{8,9},{9,8},{10,11... | collective-permute-start | bytes 1572872 | tf_op jit(solution)/shard_map/ppermute | solution.py:151
  110.7 22.6 %collective-permute-start.26 = (bf16[32,64,256]{2,1,0:T(8,128)(2,1)S(1)}, bf16[32,64,256]{2,1,0:T(8,128)(2,1)S(1)}, u32[]{:S(2)}, u32[]{:S(2)}) collective-permute-start(bf16[32,64,256]{2,1,0:T(8,128)(2,1)S(1)} %get-tuple-element.108), channel_id=1, source_target_pairs={{0,8},{8,0},{16,24},{24,16},{1,9},{9,1},{17,25},{25,17},{2,10},{10... | collective-permute-start | bytes 3145736 | tf_op jit(solution)/shard_map/ppermute | solution.py:328
  111.8 21.5 %collective-permute-start.27 = (bf16[32,64,256]{2,1,0:T(8,128)(2,1)S(1)}, bf16[32,64,256]{2,1,0:T(8,128)(2,1)S(1)}, u32[]{:S(2)}, u32[]{:S(2)}) collective-permute-start(bf16[32,64,256]{2,1,0:T(8,128)(2,1)S(1)} %get-tuple-element.109), channel_id=1, source_target_pairs={{0,16},{8,24},{16,0},{24,8},{1,17},{9,25},{17,1},{25,9},{2,18},{10... | collective-permute-start | bytes 3145736 | tf_op jit(solution)/shard_map/ppermute | solution.py:328
  122.1 26.1 %collective-permute-start.24 = (bf16[32,8192]{1,0:T(8,128)(2,1)S(1)}, bf16[32,8192]{1,0:T(8,128)(2,1)S(1)}, u32[]{:S(2)}, u32[]{:S(2)}) collective-permute-start(bf16[32,8192]{1,0:T(8,128)(2,1)S(1)} %shard_map.61.refs_0_), channel_id=1, source_target_pairs={{2,4},{3,5},{4,2},{5,3},{0,6},{1,7},{6,0},{7,1},{10,12},{11,13},{1... | collective-permute-start | bytes 1572872 | tf_op jit(solution)/shard_map/ppermute | solution.py:147
  134.1 20.0 %collective-permute-start.31 = (bf16[32,64,256]{2,1,0:T(8,128)(2,1)S(1)}, bf16[32,64,256]{2,1,0:T(8,128)(2,1)S(1)}, u32[]{:S(2)}, u32[]{:S(2)}) collective-permute-start(bf16[32,64,256]{2,1,0:T(8,128)(2,1)S(1)} %get-tuple-element.114), channel_id=1, source_target_pairs={{0,8},{8,0},{16,24},{24,16},{1,9},{9,1},{17,25},{25,17},{2,10},{10... | collective-permute-start | bytes 3145736 | tf_op jit(solution)/shard_map/ppermute | solution.py:328
  135.2 19.0 %collective-permute-start.32 = (bf16[32,64,256]{2,1,0:T(8,128)(2,1)S(1)}, bf16[32,64,256]{2,1,0:T(8,128)(2,1)S(1)}, u32[]{:S(2)}, u32[]{:S(2)}) collective-permute-start(bf16[32,64,256]{2,1,0:T(8,128)(2,1)S(1)} %get-tuple-element.115), channel_id=1, source_target_pairs={{0,16},{8,24},{16,0},{24,8},{1,17},{9,25},{17,1},{25,9},{2,18},{10... | collective-permute-start | bytes 3145736 | tf_op jit(solution)/shard_map/ppermute | solution.py:328
  150.2 21.0 %collective-permute-start.33 = (bf16[32,8192]{1,0:T(8,128)(2,1)S(1)}, bf16[32,8192]{1,0:T(8,128)(2,1)S(1)}, u32[]{:S(2)}, u32[]{:S(2)}) collective-permute-start(bf16[32,8192]{1,0:T(8,128)(2,1)S(1)} %collective-permute-done.24.refs_2_), channel_id=1, source_target_pairs={{0,1},{1,0},{2,3},{3,2},{4,5},{5,4},{6,7},{7,6},{8,9},{9,8},{10,11... | collective-permute-start | bytes 1572872 | tf_op jit(solution)/shard_map/ppermute | solution.py:151
  150.8 20.4 %collective-permute-start.34 = (bf16[32,8192]{1,0:T(8,128)(2,1)S(1)}, bf16[32,8192]{1,0:T(8,128)(2,1)S(1)}, u32[]{:S(2)}, u32[]{:S(2)}) collective-permute-start(bf16[32,8192]{1,0:T(8,128)(2,1)S(1)} %collective-permute-done.28.refs_3_), channel_id=1, source_target_pairs={{0,1},{1,0},{2,3},{3,2},{4,5},{5,4},{6,7},{7,6},{8,9},{9,8},{10,11... | collective-permute-start | bytes 1572872 | tf_op jit(solution)/shard_map/ppermute | solution.py:151
  168.5 25.9 %collective-permute-start.39 = (bf16[32,64,256]{2,1,0:T(8,128)(2,1)S(1)}, bf16[32,64,256]{2,1,0:T(8,128)(2,1)S(1)}, u32[]{:S(2)}, u32[]{:S(2)}) collective-permute-start(bf16[32,64,256]{2,1,0:T(8,128)(2,1)S(1)} %get-tuple-element.121), channel_id=1, source_target_pairs={{0,8},{8,0},{16,24},{24,16},{1,9},{9,1},{17,25},{25,17},{2,10},{10... | collective-permute-start | bytes 3145736 | tf_op jit(solution)/shard_map/ppermute | solution.py:328
  170.7 25.2 %collective-permute-start.40 = (bf16[32,64,256]{2,1,0:T(8,128)(2,1)S(1)}, bf16[32,64,256]{2,1,0:T(8,128)(2,1)S(1)}, u32[]{:S(2)}, u32[]{:S(2)}) collective-permute-start(bf16[32,64,256]{2,1,0:T(8,128)(2,1)S(1)} %get-tuple-element.122), channel_id=1, source_target_pairs={{0,16},{8,24},{16,0},{24,8},{1,17},{9,25},{17,1},{25,9},{2,18},{10... | collective-permute-start | bytes 3145736 | tf_op jit(solution)/shard_map/ppermute | solution.py:328
  175.2 25.6 %collective-permute-start.36 = (bf16[32,8192]{1,0:T(8,128)(2,1)S(1)}, bf16[32,8192]{1,0:T(8,128)(2,1)S(1)}, u32[]{:S(2)}, u32[]{:S(2)}) collective-permute-start(bf16[32,8192]{1,0:T(8,128)(2,1)S(1)} %shard_map.66.refs_0_), channel_id=1, source_target_pairs={{0,2},{1,3},{2,0},{3,1},{4,6},{5,7},{6,4},{7,5},{8,10},{9,11},{10,... | collective-permute-start | bytes 1572872 | tf_op jit(solution)/shard_map/ppermute | solution.py:147
  175.3 25.5 %collective-permute-start.37 = (bf16[32,8192]{1,0:T(8,128)(2,1)S(1)}, bf16[32,8192]{1,0:T(8,128)(2,1)S(1)}, u32[]{:S(2)}, u32[]{:S(2)}) collective-permute-start(bf16[32,8192]{1,0:T(8,128)(2,1)S(1)} %shard_map.66.refs_0_), channel_id=1, source_target_pairs={{2,4},{3,5},{4,2},{5,3},{0,6},{1,7},{6,0},{7,1},{10,12},{11,13},{1... | collective-permute-start | bytes 1572872 | tf_op jit(solution)/shard_map/ppermute | solution.py:147
  196.6 24.5 %collective-permute-start.44 = (bf16[32,64,256]{2,1,0:T(8,128)(2,1)S(1)}, bf16[32,64,256]{2,1,0:T(8,128)(2,1)S(1)}, u32[]{:S(2)}, u32[]{:S(2)}) collective-permute-start(bf16[32,64,256]{2,1,0:T(8,128)(2,1)S(1)} %get-tuple-element.130), channel_id=1, source_target_pairs={{0,8},{8,0},{16,24},{24,16},{1,9},{9,1},{17,25},{25,17},{2,10},{10... | collective-permute-start | bytes 3145736 | tf_op jit(solution)/shard_map/ppermute | solution.py:328
  197.0 24.4 %collective-permute-start.45 = (bf16[32,64,256]{2,1,0:T(8,128)(2,1)S(1)}, bf16[32,64,256]{2,1,0:T(8,128)(2,1)S(1)}, u32[]{:S(2)}, u32[]{:S(2)}) collective-permute-start(bf16[32,64,256]{2,1,0:T(8,128)(2,1)S(1)} %get-tuple-element.131), channel_id=1, source_target_pairs={{0,16},{8,24},{16,0},{24,8},{1,17},{9,25},{17,1},{25,9},{2,18},{10... | collective-permute-start | bytes 3145736 | tf_op jit(solution)/shard_map/ppermute | solution.py:328
  201.6 23.7 %collective-permute-start.42 = (bf16[32,8192]{1,0:T(8,128)(2,1)S(1)}, bf16[32,8192]{1,0:T(8,128)(2,1)S(1)}, u32[]{:S(2)}, u32[]{:S(2)}) collective-permute-start(bf16[32,8192]{1,0:T(8,128)(2,1)S(1)} %collective-permute-done.37.refs_2_), channel_id=1, source_target_pairs={{4,6},{5,7},{2,0},{3,1},{12,14},{13,15},{10,8},{11,9},{20,22},{21,... | collective-permute-start | bytes 1572872 | tf_op jit(solution)/shard_map/ppermute | solution.py:147
  202.9 23.5 %collective-permute-start.46 = (bf16[32,8192]{1,0:T(8,128)(2,1)S(1)}, bf16[32,8192]{1,0:T(8,128)(2,1)S(1)}, u32[]{:S(2)}, u32[]{:S(2)}) collective-permute-start(bf16[32,8192]{1,0:T(8,128)(2,1)S(1)} %collective-permute-done.37.refs_2_), channel_id=1, source_target_pairs={{0,1},{1,0},{2,3},{3,2},{4,5},{5,4},{6,7},{7,6},{8,9},{9,8},{10,11... | collective-permute-start | bytes 1572872 | tf_op jit(solution)/shard_map/ppermute | solution.py:151
  203.5 22.9 %collective-permute-start.47 = (bf16[32,8192]{1,0:T(8,128)(2,1)S(1)}, bf16[32,8192]{1,0:T(8,128)(2,1)S(1)}, u32[]{:S(2)}, u32[]{:S(2)}) collective-permute-start(bf16[32,8192]{1,0:T(8,128)(2,1)S(1)} %collective-permute-done.41.refs_3_), channel_id=1, source_target_pairs={{0,1},{1,0},{2,3},{3,2},{4,5},{5,4},{6,7},{7,6},{8,9},{9,8},{10,11... | collective-permute-start | bytes 1572872 | tf_op jit(solution)/shard_map/ppermute | solution.py:151
  225.4 25.6 %collective-permute-start.52 = (bf16[32,64,256]{2,1,0:T(8,128)(2,1)S(1)}, bf16[32,64,256]{2,1,0:T(8,128)(2,1)S(1)}, u32[]{:S(2)}, u32[]{:S(2)}) collective-permute-start(bf16[32,64,256]{2,1,0:T(8,128)(2,1)S(1)} %get-tuple-element.137), channel_id=1, source_target_pairs={{0,8},{8,0},{16,24},{24,16},{1,9},{9,1},{17,25},{25,17},{2,10},{10... | collective-permute-start | bytes 3145736 | tf_op jit(solution)/shard_map/ppermute | solution.py:328
  225.8 25.2 %collective-permute-start.53 = (bf16[32,64,256]{2,1,0:T(8,128)(2,1)S(1)}, bf16[32,64,256]{2,1,0:T(8,128)(2,1)S(1)}, u32[]{:S(2)}, u32[]{:S(2)}) collective-permute-start(bf16[32,64,256]{2,1,0:T(8,128)(2,1)S(1)} %get-tuple-element.138), channel_id=1, source_target_pairs={{0,16},{8,24},{16,0},{24,8},{1,17},{9,25},{17,1},{25,9},{2,18},{10... | collective-permute-start | bytes 3145736 | tf_op jit(solution)/shard_map/ppermute | solution.py:328
  231.2 19.9 %collective-permute-start.51 = (bf16[32,8192]{1,0:T(8,128)(2,1)S(1)}, bf16[32,8192]{1,0:T(8,128)(2,1)S(1)}, u32[]{:S(2)}, u32[]{:S(2)}) collective-permute-start(bf16[32,8192]{1,0:T(8,128)(2,1)S(1)} %shard_map.70.refs_0_), channel_id=1, source_target_pairs={{0,1},{1,0},{2,3},{3,2},{4,5},{5,4},{6,7},{7,6},{8,9},{9,8},{10,11... | collective-permute-start | bytes 1572872 | tf_op jit(solution)/shard_map/ppermute | solution.py:151
  231.4 25.5 %collective-permute-start.49 = (bf16[32,8192]{1,0:T(8,128)(2,1)S(1)}, bf16[32,8192]{1,0:T(8,128)(2,1)S(1)}, u32[]{:S(2)}, u32[]{:S(2)}) collective-permute-start(bf16[32,8192]{1,0:T(8,128)(2,1)S(1)} %shard_map.70.refs_0_), channel_id=1, source_target_pairs={{0,2},{1,3},{2,0},{3,1},{4,6},{5,7},{6,4},{7,5},{8,10},{9,11},{10,... | collective-permute-start | bytes 1572872 | tf_op jit(solution)/shard_map/ppermute | solution.py:147
  231.4 25.5 %collective-permute-start.50 = (bf16[32,8192]{1,0:T(8,128)(2,1)S(1)}, bf16[32,8192]{1,0:T(8,128)(2,1)S(1)}, u32[]{:S(2)}, u32[]{:S(2)}) collective-permute-start(bf16[32,8192]{1,0:T(8,128)(2,1)S(1)} %shard_map.70.refs_0_), channel_id=1, source_target_pairs={{2,4},{3,5},{4,2},{5,3},{0,6},{1,7},{6,0},{7,1},{10,12},{11,13},{1... | collective-permute-start | bytes 1572872 | tf_op jit(solution)/shard_map/ppermute | solution.py:147
  252.0 24.7 %collective-permute-start.57 = (bf16[32,64,256]{2,1,0:T(8,128)(2,1)S(1)}, bf16[32,64,256]{2,1,0:T(8,128)(2,1)S(1)}, u32[]{:S(2)}, u32[]{:S(2)}) collective-permute-start(bf16[32,64,256]{2,1,0:T(8,128)(2,1)S(1)} %get-tuple-element.146), channel_id=1, source_target_pairs={{0,8},{8,0},{16,24},{24,16},{1,9},{9,1},{17,25},{25,17},{2,10},{10... | collective-permute-start | bytes 3145736 | tf_op jit(solution)/shard_map/ppermute | solution.py:328
  253.7 24.1 %collective-permute-start.58 = (bf16[32,64,256]{2,1,0:T(8,128)(2,1)S(1)}, bf16[32,64,256]{2,1,0:T(8,128)(2,1)S(1)}, u32[]{:S(2)}, u32[]{:S(2)}) collective-permute-start(bf16[32,64,256]{2,1,0:T(8,128)(2,1)S(1)} %get-tuple-element.147), channel_id=1, source_target_pairs={{0,16},{8,24},{16,0},{24,8},{1,17},{9,25},{17,1},{25,9},{2,18},{10... | collective-permute-start | bytes 3145736 | tf_op jit(solution)/shard_map/ppermute | solution.py:328
  257.6 21.0 %collective-permute-start.55 = (bf16[32,8192]{1,0:T(8,128)(2,1)S(1)}, bf16[32,8192]{1,0:T(8,128)(2,1)S(1)}, u32[]{:S(2)}, u32[]{:S(2)}) collective-permute-start(bf16[32,8192]{1,0:T(8,128)(2,1)S(1)} %collective-permute-done.50.refs_2_), channel_id=1, source_target_pairs={{4,6},{5,7},{2,0},{3,1},{12,14},{13,15},{10,8},{11,9},{20,22},{21,... | collective-permute-start | bytes 1572872 | tf_op jit(solution)/shard_map/ppermute | solution.py:147
  261.0 18.7 %collective-permute-start.59 = (bf16[32,8192]{1,0:T(8,128)(2,1)S(1)}, bf16[32,8192]{1,0:T(8,128)(2,1)S(1)}, u32[]{:S(2)}, u32[]{:S(2)}) collective-permute-start(bf16[32,8192]{1,0:T(8,128)(2,1)S(1)} %collective-permute-done.50.refs_2_), channel_id=1, source_target_pairs={{0,1},{1,0},{2,3},{3,2},{4,5},{5,4},{6,7},{7,6},{8,9},{9,8},{10,11... | collective-permute-start | bytes 1572872 | tf_op jit(solution)/shard_map/ppermute | solution.py:151
  261.6 18.1 %collective-permute-start.60 = (bf16[32,8192]{1,0:T(8,128)(2,1)S(1)}, bf16[32,8192]{1,0:T(8,128)(2,1)S(1)}, u32[]{:S(2)}, u32[]{:S(2)}) collective-permute-start(bf16[32,8192]{1,0:T(8,128)(2,1)S(1)} %collective-permute-done.54.refs_3_), channel_id=1, source_target_pairs={{0,1},{1,0},{2,3},{3,2},{4,5},{5,4},{6,7},{7,6},{8,9},{9,8},{10,11... | collective-permute-start | bytes 1572872 | tf_op jit(solution)/shard_map/ppermute | solution.py:151
  278.7 25.6 %collective-permute-start.65 = (bf16[32,64,256]{2,1,0:T(8,128)(2,1)S(1)}, bf16[32,64,256]{2,1,0:T(8,128)(2,1)S(1)}, u32[]{:S(2)}, u32[]{:S(2)}) collective-permute-start(bf16[32,64,256]{2,1,0:T(8,128)(2,1)S(1)} %get-tuple-element.154), channel_id=1, source_target_pairs={{0,8},{8,0},{16,24},{24,16},{1,9},{9,1},{17,25},{25,17},{2,10},{10... | collective-permute-start | bytes 3145736 | tf_op jit(solution)/shard_map/ppermute | solution.py:328
  279.3 25.2 %collective-permute-start.66 = (bf16[32,64,256]{2,1,0:T(8,128)(2,1)S(1)}, bf16[32,64,256]{2,1,0:T(8,128)(2,1)S(1)}, u32[]{:S(2)}, u32[]{:S(2)}) collective-permute-start(bf16[32,64,256]{2,1,0:T(8,128)(2,1)S(1)} %get-tuple-element.155), channel_id=1, source_target_pairs={{0,16},{8,24},{16,0},{24,8},{1,17},{9,25},{17,1},{25,9},{2,18},{10... | collective-permute-start | bytes 3145736 | tf_op jit(solution)/shard_map/ppermute | solution.py:328
  284.5 20.1 %collective-permute-start.64 = (bf16[32,8192]{1,0:T(8,128)(2,1)S(1)}, bf16[32,8192]{1,0:T(8,128)(2,1)S(1)}, u32[]{:S(2)}, u32[]{:S(2)}) collective-permute-start(bf16[32,8192]{1,0:T(8,128)(2,1)S(1)} %shard_map.74.refs_0_), channel_id=1, source_target_pairs={{0,1},{1,0},{2,3},{3,2},{4,5},{5,4},{6,7},{7,6},{8,9},{9,8},{10,11... | collective-permute-start | bytes 1572872 | tf_op jit(solution)/shard_map/ppermute | solution.py:151
  284.7 25.4 %collective-permute-start.62 = (bf16[32,8192]{1,0:T(8,128)(2,1)S(1)}, bf16[32,8192]{1,0:T(8,128)(2,1)S(1)}, u32[]{:S(2)}, u32[]{:S(2)}) collective-permute-start(bf16[32,8192]{1,0:T(8,128)(2,1)S(1)} %shard_map.74.refs_0_), channel_id=1, source_target_pairs={{0,2},{1,3},{2,0},{3,1},{4,6},{5,7},{6,4},{7,5},{8,10},{9,11},{10,... | collective-permute-start | bytes 1572872 | tf_op jit(solution)/shard_map/ppermute | solution.py:147
  284.7 25.4 %collective-permute-start.63 = (bf16[32,8192]{1,0:T(8,128)(2,1)S(1)}, bf16[32,8192]{1,0:T(8,128)(2,1)S(1)}, u32[]{:S(2)}, u32[]{:S(2)}) collective-permute-start(bf16[32,8192]{1,0:T(8,128)(2,1)S(1)} %shard_map.74.refs_0_), channel_id=1, source_target_pairs={{2,4},{3,5},{4,2},{5,3},{0,6},{1,7},{6,0},{7,1},{10,12},{11,13},{1... | collective-permute-start | bytes 1572872 | tf_op jit(solution)/shard_map/ppermute | solution.py:147
  325.4 26.8 %collective-permute-start.77 = (bf16[32,64,256]{2,1,0:T(8,128)(2,1)S(1)}, bf16[32,64,256]{2,1,0:T(8,128)(2,1)S(1)}, u32[]{:S(2)}, u32[]{:S(2)}) collective-permute-start(bf16[32,64,256]{2,1,0:T(8,128)(2,1)S(1)} %get-tuple-element.161), channel_id=1, source_target_pairs={{0,8},{8,0},{16,24},{24,16},{1,9},{9,1},{17,25},{25,17},{2,10},{10... | collective-permute-start | bytes 3145736 | tf_op jit(solution)/shard_map/ppermute | solution.py:328
  326.3 26.0 %collective-permute-start.78 = (bf16[32,64,256]{2,1,0:T(8,128)(2,1)S(1)}, bf16[32,64,256]{2,1,0:T(8,128)(2,1)S(1)}, u32[]{:S(2)}, u32[]{:S(2)}) collective-permute-start(bf16[32,64,256]{2,1,0:T(8,128)(2,1)S(1)} %get-tuple-element.162), channel_id=1, source_target_pairs={{0,16},{8,24},{16,0},{24,8},{1,17},{9,25},{17,1},{25,9},{2,18},{10... | collective-permute-start | bytes 3145736 | tf_op jit(solution)/shard_map/ppermute | solution.py:328
  332.4 19.2 %collective-permute-start.73 = (bf16[32,8192]{1,0:T(8,128)(2,1)S(1)}, bf16[32,8192]{1,0:T(8,128)(2,1)S(1)}, u32[]{:S(2)}, u32[]{:S(2)}) collective-permute-start(bf16[32,8192]{1,0:T(8,128)(2,1)S(1)} %shard_map.77.refs_0_), channel_id=1, source_target_pairs={{0,2},{1,3},{2,0},{3,1},{4,6},{5,7},{6,4},{7,5},{8,10},{9,11},{10,... | collective-permute-start | bytes 1572872 | tf_op jit(solution)/shard_map/ppermute | solution.py:147
  339.2 24.1 %collective-permute-start.79 = (bf16[32,8192]{1,0:T(8,128)(2,1)S(1)}, bf16[32,8192]{1,0:T(8,128)(2,1)S(1)}, u32[]{:S(2)}, u32[]{:S(2)}) collective-permute-start(bf16[32,8192]{1,0:T(8,128)(2,1)S(1)} %shard_map.77.refs_0_), channel_id=1, source_target_pairs={{0,6},{1,7},{6,0},{7,1},{8,14},{9,15},{14,8},{15,9},{16,22},{17,23... | collective-permute-start | bytes 1572872 | tf_op jit(solution)/shard_map/ppermute | solution.py:147
  342.3 31.7 %collective-permute-start.76 = (bf16[32,8192]{1,0:T(8,128)(2,1)S(1)}, bf16[32,8192]{1,0:T(8,128)(2,1)S(1)}, u32[]{:S(2)}, u32[]{:S(2)}) collective-permute-start(bf16[32,8192]{1,0:T(8,128)(2,1)S(1)} %collective-permute-done.74.refs_2_), channel_id=1, source_target_pairs={{4,6},{5,7},{2,0},{3,1},{12,14},{13,15},{10,8},{11,9},{20,22},{21,... | collective-permute-start | bytes 1572872 | tf_op jit(solution)/shard_map/ppermute | solution.py:147
  351.6 22.4 %collective-permute-start.75 = (bf16[32,8192]{1,0:T(8,128)(2,1)S(1)}, bf16[32,8192]{1,0:T(8,128)(2,1)S(1)}, u32[]{:S(2)}, u32[]{:S(2)}) collective-permute-start(bf16[32,8192]{1,0:T(8,128)(2,1)S(1)} %collective-permute-done.73.refs_1_), channel_id=1, source_target_pairs={{2,4},{3,5},{4,2},{5,3},{10,12},{11,13},{12,10},{13,11},{18,20},{1... | collective-permute-start | bytes 1572872 | tf_op jit(solution)/shard_map/ppermute | solution.py:147
  352.3 22.2 %collective-permute-start.80 = (bf16[32,8192]{1,0:T(8,128)(2,1)S(1)}, bf16[32,8192]{1,0:T(8,128)(2,1)S(1)}, u32[]{:S(2)}, u32[]{:S(2)}) collective-permute-start(bf16[32,8192]{1,0:T(8,128)(2,1)S(1)} %shard_map.77.refs_0_), channel_id=1, source_target_pairs={{0,1},{1,0},{2,3},{3,2},{4,5},{5,4},{6,7},{7,6},{8,9},{9,8},{10,11... | collective-permute-start | bytes 1572872 | tf_op jit(solution)/shard_map/ppermute | solution.py:151
  354.5 20.1 %collective-permute-start.81 = (bf16[32,8192]{1,0:T(8,128)(2,1)S(1)}, bf16[32,8192]{1,0:T(8,128)(2,1)S(1)}, u32[]{:S(2)}, u32[]{:S(2)}) collective-permute-start(bf16[32,8192]{1,0:T(8,128)(2,1)S(1)} %collective-permute-done.73.refs_1_), channel_id=1, source_target_pairs={{0,1},{1,0},{2,3},{3,2},{4,5},{5,4},{6,7},{7,6},{8,9},{9,8},{10,11... | collective-permute-start | bytes 1572872 | tf_op jit(solution)/shard_map/ppermute | solution.py:151
  385.3 24.3 %collective-permute-start.90 = (bf16[32,8192]{1,0:T(8,128)(2,1)S(1)}, bf16[32,8192]{1,0:T(8,128)(2,1)S(1)}, u32[]{:S(2)}, u32[]{:S(2)}) collective-permute-start(bf16[32,8192]{1,0:T(8,128)(2,1)S(1)} %shard_map.79.refs_0_), channel_id=1, source_target_pairs={{0,6},{1,7},{6,0},{7,1},{8,14},{9,15},{14,8},{15,9},{16,22},{17,23... | collective-permute-start | bytes 1572872 | tf_op jit(solution)/shard_map/ppermute | solution.py:147
  388.4 32.1 %collective-permute-start.89 = (bf16[32,8192]{1,0:T(8,128)(2,1)S(1)}, bf16[32,8192]{1,0:T(8,128)(2,1)S(1)}, u32[]{:S(2)}, u32[]{:S(2)}) collective-permute-start(bf16[32,8192]{1,0:T(8,128)(2,1)S(1)} %collective-permute-done.87.refs_2_), channel_id=1, source_target_pairs={{4,6},{5,7},{2,0},{3,1},{12,14},{13,15},{10,8},{11,9},{20,22},{21,... | collective-permute-start | bytes 1572872 | tf_op jit(solution)/shard_map/ppermute | solution.py:147
  397.6 22.8 %collective-permute-start.88 = (bf16[32,8192]{1,0:T(8,128)(2,1)S(1)}, bf16[32,8192]{1,0:T(8,128)(2,1)S(1)}, u32[]{:S(2)}, u32[]{:S(2)}) collective-permute-start(bf16[32,8192]{1,0:T(8,128)(2,1)S(1)} %collective-permute-done.86.refs_1_), channel_id=1, source_target_pairs={{2,4},{3,5},{4,2},{5,3},{10,12},{11,13},{12,10},{13,11},{18,20},{1... | collective-permute-start | bytes 1572872 | tf_op jit(solution)/shard_map/ppermute | solution.py:147
  398.3 22.7 %collective-permute-start.91 = (bf16[32,8192]{1,0:T(8,128)(2,1)S(1)}, bf16[32,8192]{1,0:T(8,128)(2,1)S(1)}, u32[]{:S(2)}, u32[]{:S(2)}) collective-permute-start(bf16[32,8192]{1,0:T(8,128)(2,1)S(1)} %shard_map.79.refs_0_), channel_id=1, source_target_pairs={{0,1},{1,0},{2,3},{3,2},{4,5},{5,4},{6,7},{7,6},{8,9},{9,8},{10,11... | collective-permute-start | bytes 1572872 | tf_op jit(solution)/shard_map/ppermute | solution.py:151
  400.5 20.6 %collective-permute-start.92 = (bf16[32,8192]{1,0:T(8,128)(2,1)S(1)}, bf16[32,8192]{1,0:T(8,128)(2,1)S(1)}, u32[]{:S(2)}, u32[]{:S(2)}) collective-permute-start(bf16[32,8192]{1,0:T(8,128)(2,1)S(1)} %collective-permute-done.86.refs_1_), channel_id=1, source_target_pairs={{0,1},{1,0},{2,3},{3,2},{4,5},{5,4},{6,7},{7,6},{8,9},{9,8},{10,11... | collective-permute-start | bytes 1572872 | tf_op jit(solution)/shard_map/ppermute | solution.py:151
  431.5 24.3 %collective-permute-start.101 = (bf16[32,8192]{1,0:T(8,128)(2,1)S(1)}, bf16[32,8192]{1,0:T(8,128)(2,1)S(1)}, u32[]{:S(2)}, u32[]{:S(2)}) collective-permute-start(bf16[32,8192]{1,0:T(8,128)(2,1)S(1)} %shard_map.81.refs_0_), channel_id=1, source_target_pairs={{0,6},{1,7},{6,0},{7,1},{8,14},{9,15},{14,8},{15,9},{16,22},{17,23... | collective-permute-start | bytes 1572872 | tf_op jit(solution)/shard_map/ppermute | solution.py:147
  434.6 32.0 %collective-permute-start.100 = (bf16[32,8192]{1,0:T(8,128)(2,1)S(1)}, bf16[32,8192]{1,0:T(8,128)(2,1)S(1)}, u32[]{:S(2)}, u32[]{:S(2)}) collective-permute-start(bf16[32,8192]{1,0:T(8,128)(2,1)S(1)} %collective-permute-done.98.refs_2_), channel_id=1, source_target_pairs={{4,6},{5,7},{2,0},{3,1},{12,14},{13,15},{10,8},{11,9},{20,22},{21,... | collective-permute-start | bytes 1572872 | tf_op jit(solution)/shard_map/ppermute | solution.py:147
  443.9 22.8 %collective-permute-start.99 = (bf16[32,8192]{1,0:T(8,128)(2,1)S(1)}, bf16[32,8192]{1,0:T(8,128)(2,1)S(1)}, u32[]{:S(2)}, u32[]{:S(2)}) collective-permute-start(bf16[32,8192]{1,0:T(8,128)(2,1)S(1)} %collective-permute-done.97.refs_1_), channel_id=1, source_target_pairs={{2,4},{3,5},{4,2},{5,3},{10,12},{11,13},{12,10},{13,11},{18,20},{1... | collective-permute-start | bytes 1572872 | tf_op jit(solution)/shard_map/ppermute | solution.py:147
  444.6 22.6 %collective-permute-start.102 = (bf16[32,8192]{1,0:T(8,128)(2,1)S(1)}, bf16[32,8192]{1,0:T(8,128)(2,1)S(1)}, u32[]{:S(2)}, u32[]{:S(2)}) collective-permute-start(bf16[32,8192]{1,0:T(8,128)(2,1)S(1)} %shard_map.81.refs_0_), channel_id=1, source_target_pairs={{0,1},{1,0},{2,3},{3,2},{4,5},{5,4},{6,7},{7,6},{8,9},{9,8},{10,11... | collective-permute-start | bytes 1572872 | tf_op jit(solution)/shard_map/ppermute | solution.py:151
  446.7 20.5 %collective-permute-start.103 = (bf16[32,8192]{1,0:T(8,128)(2,1)S(1)}, bf16[32,8192]{1,0:T(8,128)(2,1)S(1)}, u32[]{:S(2)}, u32[]{:S(2)}) collective-permute-start(bf16[32,8192]{1,0:T(8,128)(2,1)S(1)} %collective-permute-done.97.refs_1_), channel_id=1, source_target_pairs={{0,1},{1,0},{2,3},{3,2},{4,5},{5,4},{6,7},{7,6},{8,9},{9,8},{10,11... | collective-permute-start | bytes 1572872 | tf_op jit(solution)/shard_map/ppermute | solution.py:151
  (62 other events, 530.5 us)

commit v4 on v3

--- a/solution.py
+++ b/solution.py
@@ -15,8 +15,10 @@
 CORES = 2
 WEIGHT_PARTS = 4
 STREAM_SEED = 486
+BUSY_LAYERS = (0, 1, 3, 4)
 LAYER_VMEM = 10 * 2**20
 SMALL_VMEM = 2 * 2**20
+BRIEF = pl.CostEstimate(flops=0, transcendentals=0, bytes_accessed=0)
 
 clamp_top = 32.0
 
@@ -114,6 +116,7 @@
         in_specs=[smem] + [pl.BlockSpec(memory_space=pl.ANY)] * len(weights),
         out_specs=pl.BlockSpec(memory_space=pltpu.VMEM),
         scratch_shapes=[pltpu.SemaphoreType.DMA((shape[0],))],
+        cost_estimate=BRIEF,
         compiler_params=pltpu.CompilerParams(vmem_limit_bytes=SMALL_VMEM),
     )(place, *pinned(weights, in_hbm))
 
@@ -127,7 +130,7 @@
     smem = pl.BlockSpec(memory_space=pltpu.SMEM)
     anywhere = pl.BlockSpec(memory_space=pl.ANY)
     vmem = pl.BlockSpec(memory_space=pltpu.VMEM)
-    kernel = functools.partial(layer_kernel, act_plan, 16)
+    kernel = functools.partial(layer_kernel, act_plan, 64)
     return pl.pallas_call(
         kernel,
         out_shape=jax.ShapeDtypeStruct((rows, neurons), jnp.bfloat16),
@@ -138,6 +141,7 @@
             pltpu.VMEM((2, rows, LANES), jnp.bfloat16),
             pltpu.SemaphoreType.DMA((slots,)),
         ],
+        cost_estimate=BRIEF,
         compiler_params=pltpu.CompilerParams(vmem_limit_bytes=LAYER_VMEM),
     )(codes, place, *acts, weights, bias)
 
@@ -161,13 +165,14 @@
     cross = along_line(x, inside if split else inside + ends)
     trade = [along_line(x, ends)] if split else []
     x_swapped = to_other_core(x)
-    near, cross = pause(x_swapped, [near, cross])
+    near, cross = pause([x_swapped], [near, cross])
     far = along_line(near, inside)
     outer = along_line(cross, [(2, 3), (1, 0)])
-    near_swapped = to_other_core(near)
-    (outer,) = pause(near_swapped, [outer])
-    rest = [cross, far, outer] + trade
-    return [x, near] + rest + [x_swapped, near_swapped] + [to_other_core(buf) for buf in rest]
+    near_swapped, cross_swapped = to_other_core(near), to_other_core(cross)
+    far, outer = pause([near_swapped, cross_swapped], [far, outer])
+    rest = [far, outer] + trade
+    swapped = [x_swapped, near_swapped, cross_swapped] + [to_other_core(buf) for buf in rest]
+    return [x, near, cross] + rest + swapped
 
 
 def line_plan(split):
@@ -260,6 +265,7 @@
         in_specs=[smem] + [pl.BlockSpec(memory_space=pl.ANY)] * len(operands),
         out_specs=[pl.BlockSpec(memory_space=pltpu.VMEM)] * len(choices),
         scratch_shapes=[pltpu.SemaphoreType.DMA((len(choices),))],
+        cost_estimate=BRIEF,
         compiler_params=pltpu.CompilerParams(vmem_limit_bytes=SMALL_VMEM),
     )(place, *pinned(operands, in_hbm))
 
@@ -277,6 +283,7 @@
         in_specs=[pl.BlockSpec(memory_space=pl.ANY)],
         out_specs=pl.BlockSpec(memory_space=pltpu.VMEM),
         scratch_shapes=[pltpu.SemaphoreType.DMA],
+        cost_estimate=BRIEF,
         compiler_params=pltpu.CompilerParams(vmem_limit_bytes=SMALL_VMEM),
     )(pltpu.with_memory_space_constraint(x, pltpu.HBM))
 
@@ -364,6 +371,13 @@
     pairs = neurons // LANES
     is_line = row_devs == 4 * CORES and lax.axis_size("pipe") == 4
 
+    z = my_row // CORES
+    is_middle = (z > 0) & (z < row_devs // CORES - 1)
+    place = jnp.stack([is_middle.astype(jnp.int32), lax.axis_index("pipe").astype(jnp.int32)])
+    if is_line:
+        stream = WeightStream(weights, place, 4, WEIGHT_PARTS)
+        layout, bias = stream.advance(through=[layout, bias])
+
     mine = lax.dynamic_slice_in_dim(layout, my_row * slot_count, slot_count, axis=1)
     owners, local = mine // blocks, mine % blocks
     table = line_slots(row_devs) if is_line else np.tile(np.arange(row_devs, dtype=np.int32), (row_devs, 1))
@@ -373,19 +387,20 @@
     codes = (((slots << bits_for(pairs)) | (local // 2)) << 1) | (local % 2)
 
     if is_line:
-        all_codes, all_bias = gather_square(codes), gather_square(bias)
+        base = 2 ** (bits_for(4 * CORES * pairs * 2) // 2)
+        sent = jnp.concatenate([bias, *(part.astype(jnp.bfloat16) for part in (codes // base, codes % base))], axis=1)
+        got = gather_square(sent)
+        high, low = (
+            got[:, neurons + n * slot_count : neurons + (n + 1) * slot_count].astype(jnp.int32) for n in range(2)
+        )
+        all_codes, all_bias = high * base + low, got[:, :neurons]
     else:
         all_codes = lax.all_gather(codes, "pipe", axis=0, tiled=True)
         all_bias = lax.all_gather(bias, "pipe", axis=0, tiled=True)
-    z = my_row // CORES
-    is_middle = (z > 0) & (z < row_devs // CORES - 1)
-    place = jnp.stack([is_middle.astype(jnp.int32), lax.axis_index("pipe").astype(jnp.int32)])
     layers = weights.shape[0] * lax.axis_size("pipe")
 
     current = features
     if is_line:
-        stream = WeightStream(weights, place, 4, WEIGHT_PARTS)
-        stream.advance()
         for layer in range(layers):
             step = 0
 
@@ -393,12 +408,12 @@
                 nonlocal step
                 step += 1
                 if layer == 0 and step == 1:
-                    stream.weights = load(after_all(weights, arrived))
+                    stream.weights = load(after_all(weights, *arrived))
                     stream.loaded = True
                 if step == 1:
-                    through = stream.advance([arrived] + ([all_codes, all_bias] if layer == 0 else []), through)
-                else:
-                    through = stream.advance([arrived], through)
+                    through = stream.advance(arrived + ([all_codes, all_bias] if layer == 0 else []), through)
+                elif layer in BUSY_LAYERS:
+                    through = stream.advance(arrived, through)
                 if step == 2 and stream.started >= stream.ready[layer]:
                     through, _ = lax.optimization_barrier((through, stream.gather(layer)))
                 return through

time: 476 us -> 472 us (level); the launches traced: 475 us -> 463 us
  Pallas kernels: 65.1 us -> 58.1 us
  starting transfers between devices: 97.7 us -> 91.8 us
    ppermute x35, waiting for transfers between devices: 137 us -> 156 us  [along_line(): return lax.ppermute(x, 'rows', moves)]
    ppermute x24, waiting for transfers between devices: 155 us -> 139 us  [advance(): lax.ppermute(array, 'pipe', [(p, p ^ side) for p in range(self.square)])]
    pallas_call x8, Pallas kernels: 32.1 us -> 26.4 us  [apply_layer(): pl.pallas_call(kernel, out_shape=jax.ShapeDtypeStruct((rows, neurons), jn...]
  transfers between devices with their start and end apart: 108 -> 105, of which waited for: 49 -> 59; matrix products, arithmetic and copies ran while one was open for 1% -> 0% of each run, Pallas kernels for 10% -> 9%
where the time goes in v4:
time: 472 us; the launch traced here: 463 us
  waiting for transfers between devices  308 us (65%)
  starting transfers between devices  91.8 us (19%)
  Pallas kernels  58.1 us (12%)
    ppermute x35, waiting for transfers between devices, along_line(): return lax.ppermute(x, 'rows', moves)  156 us
    ppermute x24, waiting for transfers between devices, advance(): lax.ppermute(array, 'pipe', [(p, p ^ side) for p in range(self.square)])  139 us
    ppermute x35, starting transfers between devices, along_line(): return lax.ppermute(x, 'rows', moves)  48.8 us
    ppermute x24, starting transfers between devices, advance(): lax.ppermute(array, 'pipe', [(p, p ^ side) for p in range(self.square)])  27.9 us
    pallas_call x8, Pallas kernels, apply_layer(): pl.pallas_call(kernel, out_shape=jax.ShapeDtypeStruct((rows, neurons), jn...  26.4 us
    pallas_call x8, Pallas kernels, gather_weights(): pl.pallas_call(functools.partial(gather_weights_kernel, plan), out_shape=...  17.2 us
    ppermute x43, waiting for transfers between devices, to_other_core(): lax.ppermute(x, 'rows', [(i, i ^ 1) for i in range(lax.axis_size('rows'))])  13.2 us
    pallas_call x12, Pallas kernels, pick(): pl.pallas_call(functools.partial(pick_kernel, choices, len(choices)), out...  11.1 us
  transfers between devices with their start and end apart: 105, of which 59 were waited for; matrix products, arithmetic and copies ran while one was open for 0% of the time, Pallas kernels for 9%

profile of v4, /device:TPU:0, one launch (start us, length us, event | category | flops | bytes accessed | tf_op | source)
XLA Modules:
  0.0 463.2 jit_solution(14789165585800513537)
XLA Ops:
  0.1 3.1 shard_map.55
  6.4 3.0 collective-permute-start
  11.0 1.9 collective-permute-start.6
  14.7 1.6 collective-permute-start.3
  16.3 3.6 collective-permute-start.4
  20.3 3.4 shard_map.56.refs_2_.refs_1_.refs_0_.refs_4_.refs_3_.refs_5_
  23.7 12.3 %collective-permute-done.6.refs_0_.refs_1_.refs_3_.refs_2_ = bf16[32,64,256]{2,1,0:T(8,128)(2,1)S(1)} collective-permute-done((bf16[32,64,256]{2,1,0:T(8,128)(2,1)}, bf16[32,64,256]{2,1,0:T(8,128)(2,1)S(1)}, u32[]{:S(2)}, u32[]{:S(2)}) %collective-permute-start.6) | collective-permute-done | bytes 1048608 | tf_op jit(solution)/shard_map/ppermute | solution.py:335
  40.0 2.4 collective-permute-done.4.refs_2_
  45.0 16.4 %collective-permute-done.12.refs_0_.refs_6_.refs_5_ = bf16[32,64,256]{2,1,0:T(8,128)(2,1)S(1)} collective-permute-done((bf16[32,64,256]{2,1,0:T(8,128)(2,1)S(1)}, bf16[32,64,256]{2,1,0:T(8,128)(2,1)S(1)}, u32[]{:S(2)}, u32[]{:S(2)}) %collective-permute-start.12) | collective-permute-done | bytes 1048608 | tf_op jit(solution)/shard_map/ppermute | solution.py:335
  65.5 19.4 %collective-permute-done.16.refs_2_.refs_7_ = bf16[32,64,256]{2,1,0:T(8,128)(2,1)S(1)} collective-permute-done((bf16[32,64,256]{2,1,0:T(8,128)(2,1)S(1)}, bf16[32,64,256]{2,1,0:T(8,128)(2,1)S(1)}, u32[]{:S(2)}, u32[]{:S(2)}) %collective-permute-start.16) | collective-permute-done | bytes 1048608 | tf_op jit(solution)/shard_map/ppermute | solution.py:335
  90.9 11.3 %collective-permute-done.9.refs_4_ = bf16[32,8192]{1,0:T(8,128)(2,1)S(1)} collective-permute-done((bf16[32,8192]{1,0:T(8,128)(2,1)S(1)}, bf16[32,8192]{1,0:T(8,128)(2,1)S(1)}, u32[]{:S(2)}, u32[]{:S(2)}) %collective-permute-start.9) | collective-permute-done | bytes 524320 | tf_op jit(solution)/shard_map/ppermute | solution.py:151
  102.7 5.4 %collective-permute-done.18.refs_7_.refs_0_.refs_1_.refs_3_ = bf16[32,64,256]{2,1,0:T(8,128)(2,1)S(1)} collective-permute-done((bf16[32,64,256]{2,1,0:T(8,128)(2,1)S(1)}, bf16[32,64,256]{2,1,0:T(8,128)(2,1)S(1)}, u32[]{:S(2)}, u32[]{:S(2)}) %collective-permute-start.18) | collective-permute-done | bytes 1048608 | tf_op jit(solution)/shard_map/ppermute | solution.py:335
  110.7 1.6 collective-permute-start.24
  112.4 2.1 shard_map.60.refs_10_
  114.5 3.2 shard_map.61.refs_0_
  119.2 2.5 collective-permute-start.21
  121.7 9.7 %collective-permute-done.23.refs_2_.refs_7_.refs_8_.refs_4_ = bf16[32,64,256]{2,1,0:T(8,128)(2,1)S(1)} collective-permute-done((bf16[32,64,256]{2,1,0:T(8,128)(2,1)S(1)}, bf16[32,64,256]{2,1,0:T(8,128)(2,1)S(1)}, u32[]{:S(2)}, u32[]{:S(2)}) %collective-permute-start.23) | collective-permute-done | bytes 1048608 | tf_op jit(solution)/shard_map/ppermute | solution.py:335
  134.0 1.7 collective-permute-start.30
  135.7 9.6 %collective-permute-done.21.refs_2_ = bf16[32,8192]{1,0:T(8,128)(2,1)S(1)} collective-permute-done((bf16[32,8192]{1,0:T(8,128)(2,1)S(1)}, bf16[32,8192]{1,0:T(8,128)(2,1)S(1)}, u32[]{:S(2)}, u32[]{:S(2)}) %collective-permute-start.21) | collective-permute-done | bytes 524320 | tf_op jit(solution)/shard_map/ppermute | solution.py:151
  148.5 3.8 collective-permute-done.29.refs_4_.refs_2_.refs_0_.refs_10_
  153.2 2.1 shard_map.65.refs_10_
  156.1 7.0 %collective-permute-done.26.refs_4_ = bf16[32,8192]{1,0:T(8,128)(2,1)S(1)} collective-permute-done((bf16[32,8192]{1,0:T(8,128)(2,1)S(1)}, bf16[32,8192]{1,0:T(8,128)(2,1)S(1)}, u32[]{:S(2)}, u32[]{:S(2)}) %collective-permute-start.26) | collective-permute-done | bytes 524320 | tf_op jit(solution)/shard_map/ppermute | solution.py:151
  163.6 1.7 collective-permute-start.36
  165.8 3.2 shard_map.66.refs_0_
  169.1 1.6 collective-permute-start.34
  170.9 17.7 %collective-permute-done.36.refs_2_.refs_3_.refs_8_.refs_5_ = bf16[32,64,256]{2,1,0:T(8,128)(2,1)S(1)} collective-permute-done((bf16[32,64,256]{2,1,0:T(8,128)(2,1)S(1)}, bf16[32,64,256]{2,1,0:T(8,128)(2,1)S(1)}, u32[]{:S(2)}, u32[]{:S(2)}) %collective-permute-start.36) | collective-permute-done | bytes 1048608 | tf_op jit(solution)/shard_map/ppermute | solution.py:335
  190.8 3.9 collective-permute-done.33.refs_1_
  196.7 2.3 shard_map.68.refs_10_
  199.5 1.6 collective-permute-start.47
  201.7 9.3 %collective-permute-done.39.refs_4_ = bf16[32,8192]{1,0:T(8,128)(2,1)S(1)} collective-permute-done((bf16[32,8192]{1,0:T(8,128)(2,1)S(1)}, bf16[32,8192]{1,0:T(8,128)(2,1)S(1)}, u32[]{:S(2)}, u32[]{:S(2)}) %collective-permute-start.39) | collective-permute-done | bytes 524320 | tf_op jit(solution)/shard_map/ppermute | solution.py:151
  213.6 3.2 shard_map.69.refs_0_
  217.0 1.9 collective-permute-start.44
  220.1 4.5 collective-permute-done.47.refs_1_.refs_5_.refs_7_.refs_4_
  228.7 2.7 collective-permute-done.44.refs_1_
  231.4 12.3 %collective-permute-done.45.refs_2_ = bf16[32,8192]{1,0:T(8,128)(2,1)S(1)} collective-permute-done((bf16[32,8192]{1,0:T(8,128)(2,1)S(1)}, bf16[32,8192]{1,0:T(8,128)(2,1)S(1)}, u32[]{:S(2)}, u32[]{:S(2)}) %collective-permute-start.45) | collective-permute-done | bytes 524320 | tf_op jit(solution)/shard_map/ppermute | solution.py:151
  246.8 3.9 collective-permute-done.53.refs_4_.refs_2_.refs_1_.refs_10_
  251.1 2.1 shard_map.72.refs_10_
  254.0 7.4 %collective-permute-done.50.refs_4_ = bf16[32,8192]{1,0:T(8,128)(2,1)S(1)} collective-permute-done((bf16[32,8192]{1,0:T(8,128)(2,1)S(1)}, bf16[32,8192]{1,0:T(8,128)(2,1)S(1)}, u32[]{:S(2)}, u32[]{:S(2)}) %collective-permute-start.50) | collective-permute-done | bytes 524320 | tf_op jit(solution)/shard_map/ppermute | solution.py:151
  264.1 3.2 shard_map.73.refs_0_
  268.2 1.8 collective-permute-start.58
  270.1 16.9 %collective-permute-done.60.refs_1_.refs_6_.refs_8_.refs_7_ = bf16[32,64,256]{2,1,0:T(8,128)(2,1)S(1)} collective-permute-done((bf16[32,64,256]{2,1,0:T(8,128)(2,1)S(1)}, bf16[32,64,256]{2,1,0:T(8,128)(2,1)S(1)}, u32[]{:S(2)}, u32[]{:S(2)}) %collective-permute-start.60) | collective-permute-done | bytes 1048608 | tf_op jit(solution)/shard_map/ppermute | solution.py:335
  291.1 2.8 collective-permute-done.58.refs_2_
  297.1 2.1 shard_map.76.refs_10_
  299.2 13.7 %collective-permute-done.66.refs_0_.refs_5_.refs_2_ = bf16[32,64,256]{2,1,0:T(8,128)(2,1)S(1)} collective-permute-done((bf16[32,64,256]{2,1,0:T(8,128)(2,1)S(1)}, bf16[32,64,256]{2,1,0:T(8,128)(2,1)S(1)}, u32[]{:S(2)}, u32[]{:S(2)}) %collective-permute-start.66) | collective-permute-done | bytes 1048608 | tf_op jit(solution)/shard_map/ppermute | solution.py:335
  316.7 3.4 shard_map.77.refs_0_
  322.1 4.4 collective-permute-start.77
  326.5 8.0 %collective-permute-done.70.refs_1_ = bf16[32,8192]{1,0:T(8,128)(2,1)S(1)} collective-permute-done((bf16[32,8192]{1,0:T(8,128)(2,1)S(1)}, bf16[32,8192]{1,0:T(8,128)(2,1)S(1)}, u32[]{:S(2)}, u32[]{:S(2)}) %collective-permute-start.70) | collective-permute-done | bytes 524320 | tf_op jit(solution)/shard_map/ppermute | solution.py:151
  336.5 3.3 collective-permute-done.75.refs_6_.refs_5_
  341.0 2.1 shard_map.78.refs_12_
  343.7 3.0 collective-permute-done.77.refs_5_
  346.7 15.3 %collective-permute-done.73.refs_4_ = bf16[32,8192]{1,0:T(8,128)(2,1)S(1)} collective-permute-done((bf16[32,8192]{1,0:T(8,128)(2,1)S(1)}, bf16[32,8192]{1,0:T(8,128)(2,1)S(1)}, u32[]{:S(2)}, u32[]{:S(2)}) %collective-permute-start.73) | collective-permute-done | bytes 524320 | tf_op jit(solution)/shard_map/ppermute | solution.py:151
  364.6 3.2 shard_map.79.refs_0_
  368.6 4.4 collective-permute-start.87
  373.1 8.8 %collective-permute-done.83.refs_1_ = bf16[32,8192]{1,0:T(8,128)(2,1)S(1)} collective-permute-done((bf16[32,8192]{1,0:T(8,128)(2,1)S(1)}, bf16[32,8192]{1,0:T(8,128)(2,1)S(1)}, u32[]{:S(2)}, u32[]{:S(2)}) %collective-permute-start.83) | collective-permute-done | bytes 524320 | tf_op jit(solution)/shard_map/ppermute | solution.py:151
  383.9 2.1 shard_map.80.refs_12_
  386.6 7.4 %collective-permute-done.87.refs_5_ = bf16[32,8192]{1,0:T(8,128)(2,1)S(1)} collective-permute-done((bf16[32,8192]{1,0:T(8,128)(2,1)S(1)}, bf16[32,8192]{1,0:T(8,128)(2,1)S(1)}, u32[]{:S(2)}, u32[]{:S(2)}) %collective-permute-start.87) | collective-permute-done | bytes 524320 | tf_op jit(solution)/shard_map/ppermute | solution.py:151
  394.5 14.5 %collective-permute-done.86.refs_4_ = bf16[32,8192]{1,0:T(8,128)(2,1)S(1)} collective-permute-done((bf16[32,8192]{1,0:T(8,128)(2,1)S(1)}, bf16[32,8192]{1,0:T(8,128)(2,1)S(1)}, u32[]{:S(2)}, u32[]{:S(2)}) %collective-permute-start.86) | collective-permute-done | bytes 524320 | tf_op jit(solution)/shard_map/ppermute | solution.py:151
  411.7 3.2 shard_map.81.refs_0_
  415.7 4.5 collective-permute-start.98
  420.2 8.8 %collective-permute-done.94.refs_1_ = bf16[32,8192]{1,0:T(8,128)(2,1)S(1)} collective-permute-done((bf16[32,8192]{1,0:T(8,128)(2,1)S(1)}, bf16[32,8192]{1,0:T(8,128)(2,1)S(1)}, u32[]{:S(2)}, u32[]{:S(2)}) %collective-permute-start.94) | collective-permute-done | bytes 524320 | tf_op jit(solution)/shard_map/ppermute | solution.py:151
  431.0 2.4 shard_map.82.refs_12_
  433.9 7.1 %collective-permute-done.98.refs_5_ = bf16[32,8192]{1,0:T(8,128)(2,1)S(1)} collective-permute-done((bf16[32,8192]{1,0:T(8,128)(2,1)S(1)}, bf16[32,8192]{1,0:T(8,128)(2,1)S(1)}, u32[]{:S(2)}, u32[]{:S(2)}) %collective-permute-start.98) | collective-permute-done | bytes 524320 | tf_op jit(solution)/shard_map/ppermute | solution.py:151
  441.6 14.5 %collective-permute-done.97.refs_4_ = bf16[32,8192]{1,0:T(8,128)(2,1)S(1)} collective-permute-done((bf16[32,8192]{1,0:T(8,128)(2,1)S(1)}, bf16[32,8192]{1,0:T(8,128)(2,1)S(1)}, u32[]{:S(2)}, u32[]{:S(2)}) %collective-permute-start.97) | collective-permute-done | bytes 524320 | tf_op jit(solution)/shard_map/ppermute | solution.py:151
  458.8 4.0 shard_map.83
  (197 shorter events, 90.8 us)
Async XLA Ops:
  11.0 25.1 %collective-permute-start.6 = (bf16[32,64,256]{2,1,0:T(8,128)(2,1)}, bf16[32,64,256]{2,1,0:T(8,128)(2,1)S(1)}, u32[]{:S(2)}, u32[]{:S(2)}) collective-permute-start(bf16[32,64,256]{2,1,0:T(8,128)(2,1)} %get-tuple-element.101), channel_id=1, source_target_pairs={{0,8},{8,0},{16,24},{24,16},{1,9},{9,1},{17,25},{25,17},{2,10},{10... | collective-permute-start | bytes 3145736 | tf_op jit(solution)/shard_map/ppermute | solution.py:335
  12.9 24.4 %collective-permute-start.7 = (bf16[32,64,256]{2,1,0:T(8,128)(2,1)}, bf16[32,64,256]{2,1,0:T(8,128)(2,1)S(1)}, u32[]{:S(2)}, u32[]{:S(2)}) collective-permute-start(bf16[32,64,256]{2,1,0:T(8,128)(2,1)} %copy-done.1), channel_id=1, source_target_pairs={{0,16},{8,24},{16,0},{24,8},{1,17},{9,25},{17,1},{25,9},{2,18},{10... | collective-permute-start | bytes 3145736 | tf_op jit(solution)/shard_map/ppermute | solution.py:335
  14.7 25.3 %collective-permute-start.3 = (bf16[32,8192]{1,0:T(8,128)(2,1)S(1)}, bf16[32,8192]{1,0:T(8,128)(2,1)S(1)}, u32[]{:S(2)}, u32[]{:S(2)}) collective-permute-start(bf16[32,8192]{1,0:T(8,128)(2,1)S(1)} %copy-done), channel_id=1, source_target_pairs={{0,2},{1,3},{2,0},{3,1},{4,6},{5,7},{6,4},{7,5},{8,10},{9,11},{10,... | collective-permute-start | bytes 1572872 | tf_op jit(solution)/shard_map/ppermute | solution.py:151
  16.3 26.1 %collective-permute-start.4 = (bf16[32,8192]{1,0:T(8,128)(2,1)S(1)}, bf16[32,8192]{1,0:T(8,128)(2,1)S(1)}, u32[]{:S(2)}, u32[]{:S(2)}) collective-permute-start(bf16[32,8192]{1,0:T(8,128)(2,1)S(1)} %copy-done), channel_id=1, source_target_pairs={{2,4},{3,5},{4,2},{5,3},{0,6},{1,7},{6,0},{7,1},{10,12},{11,13},{1... | collective-permute-start | bytes 1572872 | tf_op jit(solution)/shard_map/ppermute | solution.py:151
  38.1 23.3 %collective-permute-start.12 = (bf16[32,64,256]{2,1,0:T(8,128)(2,1)S(1)}, bf16[32,64,256]{2,1,0:T(8,128)(2,1)S(1)}, u32[]{:S(2)}, u32[]{:S(2)}) collective-permute-start(bf16[32,64,256]{2,1,0:T(8,128)(2,1)S(1)} %get-tuple-element.108), channel_id=1, source_target_pairs={{0,8},{8,0},{16,24},{24,16},{1,9},{9,1},{17,25},{25,17},{2,10},{10... | collective-permute-start | bytes 3145736 | tf_op jit(solution)/shard_map/ppermute | solution.py:335
  38.5 23.2 %collective-permute-start.13 = (bf16[32,64,256]{2,1,0:T(8,128)(2,1)S(1)}, bf16[32,64,256]{2,1,0:T(8,128)(2,1)S(1)}, u32[]{:S(2)}, u32[]{:S(2)}) collective-permute-start(bf16[32,64,256]{2,1,0:T(8,128)(2,1)S(1)} %get-tuple-element.109), channel_id=1, source_target_pairs={{0,16},{8,24},{16,0},{24,8},{1,17},{9,25},{17,1},{25,9},{2,18},{10... | collective-permute-start | bytes 3145736 | tf_op jit(solution)/shard_map/ppermute | solution.py:335
  62.5 22.4 %collective-permute-start.16 = (bf16[32,64,256]{2,1,0:T(8,128)(2,1)S(1)}, bf16[32,64,256]{2,1,0:T(8,128)(2,1)S(1)}, u32[]{:S(2)}, u32[]{:S(2)}) collective-permute-start(bf16[32,64,256]{2,1,0:T(8,128)(2,1)S(1)} %get-tuple-element.114), channel_id=1, source_target_pairs={{0,8},{8,0},{16,24},{24,16},{1,9},{9,1},{17,25},{25,17},{2,10},{10... | collective-permute-start | bytes 3145736 | tf_op jit(solution)/shard_map/ppermute | solution.py:335
  63.9 21.8 %collective-permute-start.17 = (bf16[32,64,256]{2,1,0:T(8,128)(2,1)S(1)}, bf16[32,64,256]{2,1,0:T(8,128)(2,1)S(1)}, u32[]{:S(2)}, u32[]{:S(2)}) collective-permute-start(bf16[32,64,256]{2,1,0:T(8,128)(2,1)S(1)} %get-tuple-element.115), channel_id=1, source_target_pairs={{0,16},{8,24},{16,0},{24,8},{1,17},{9,25},{17,1},{25,9},{2,18},{10... | collective-permute-start | bytes 3145736 | tf_op jit(solution)/shard_map/ppermute | solution.py:335
  86.4 21.7 %collective-permute-start.18 = (bf16[32,64,256]{2,1,0:T(8,128)(2,1)S(1)}, bf16[32,64,256]{2,1,0:T(8,128)(2,1)S(1)}, u32[]{:S(2)}, u32[]{:S(2)}) collective-permute-start(bf16[32,64,256]{2,1,0:T(8,128)(2,1)S(1)} %get-tuple-element.120), channel_id=1, source_target_pairs={{0,8},{8,0},{16,24},{24,16},{1,9},{9,1},{17,25},{25,17},{2,10},{10... | collective-permute-start | bytes 3145736 | tf_op jit(solution)/shard_map/ppermute | solution.py:335
  87.4 21.6 %collective-permute-start.19 = (bf16[32,64,256]{2,1,0:T(8,128)(2,1)S(1)}, bf16[32,64,256]{2,1,0:T(8,128)(2,1)S(1)}, u32[]{:S(2)}, u32[]{:S(2)}) collective-permute-start(bf16[32,64,256]{2,1,0:T(8,128)(2,1)S(1)} %get-tuple-element.121), channel_id=1, source_target_pairs={{0,16},{8,24},{16,0},{24,8},{1,17},{9,25},{17,1},{25,9},{2,18},{10... | collective-permute-start | bytes 3145736 | tf_op jit(solution)/shard_map/ppermute | solution.py:335
  109.7 21.6 %collective-permute-start.23 = (bf16[32,64,256]{2,1,0:T(8,128)(2,1)S(1)}, bf16[32,64,256]{2,1,0:T(8,128)(2,1)S(1)}, u32[]{:S(2)}, u32[]{:S(2)}) collective-permute-start(bf16[32,64,256]{2,1,0:T(8,128)(2,1)S(1)} %get-tuple-element.124), channel_id=1, source_target_pairs={{0,8},{8,0},{16,24},{24,16},{1,9},{9,1},{17,25},{25,17},{2,10},{10... | collective-permute-start | bytes 3145736 | tf_op jit(solution)/shard_map/ppermute | solution.py:335
  110.7 22.2 %collective-permute-start.24 = (bf16[32,64,256]{2,1,0:T(8,128)(2,1)S(1)}, bf16[32,64,256]{2,1,0:T(8,128)(2,1)S(1)}, u32[]{:S(2)}, u32[]{:S(2)}) collective-permute-start(bf16[32,64,256]{2,1,0:T(8,128)(2,1)S(1)} %get-tuple-element.125), channel_id=1, source_target_pairs={{0,16},{8,24},{16,0},{24,8},{1,17},{9,25},{17,1},{25,9},{2,18},{10... | collective-permute-start | bytes 3145736 | tf_op jit(solution)/shard_map/ppermute | solution.py:335
  117.7 17.9 %collective-permute-start.20 = (bf16[32,8192]{1,0:T(8,128)(2,1)S(1)}, bf16[32,8192]{1,0:T(8,128)(2,1)S(1)}, u32[]{:S(2)}, u32[]{:S(2)}) collective-permute-start(bf16[32,8192]{1,0:T(8,128)(2,1)S(1)} %shard_map.61.refs_0_), channel_id=1, source_target_pairs={{0,2},{1,3},{2,0},{3,1},{4,6},{5,7},{6,4},{7,5},{8,10},{9,11},{10,... | collective-permute-start | bytes 1572872 | tf_op jit(solution)/shard_map/ppermute | solution.py:151
  119.2 26.1 %collective-permute-start.21 = (bf16[32,8192]{1,0:T(8,128)(2,1)S(1)}, bf16[32,8192]{1,0:T(8,128)(2,1)S(1)}, u32[]{:S(2)}, u32[]{:S(2)}) collective-permute-start(bf16[32,8192]{1,0:T(8,128)(2,1)S(1)} %shard_map.61.refs_0_), channel_id=1, source_target_pairs={{2,4},{3,5},{4,2},{5,3},{0,6},{1,7},{6,0},{7,1},{10,12},{11,13},{1... | collective-permute-start | bytes 1572872 | tf_op jit(solution)/shard_map/ppermute | solution.py:151
  133.6 18.7 %collective-permute-start.29 = (bf16[32,64,256]{2,1,0:T(8,128)(2,1)S(1)}, bf16[32,64,256]{2,1,0:T(8,128)(2,1)S(1)}, u32[]{:S(2)}, u32[]{:S(2)}) collective-permute-start(bf16[32,64,256]{2,1,0:T(8,128)(2,1)S(1)} %get-tuple-element.130), channel_id=1, source_target_pairs={{0,8},{8,0},{16,24},{24,16},{1,9},{9,1},{17,25},{25,17},{2,10},{10... | collective-permute-start | bytes 3145736 | tf_op jit(solution)/shard_map/ppermute | solution.py:335
  134.0 19.2 %collective-permute-start.30 = (bf16[32,64,256]{2,1,0:T(8,128)(2,1)S(1)}, bf16[32,64,256]{2,1,0:T(8,128)(2,1)S(1)}, u32[]{:S(2)}, u32[]{:S(2)}) collective-permute-start(bf16[32,64,256]{2,1,0:T(8,128)(2,1)S(1)} %get-tuple-element.131), channel_id=1, source_target_pairs={{0,16},{8,24},{16,0},{24,8},{1,17},{9,25},{17,1},{25,9},{2,18},{10... | collective-permute-start | bytes 3145736 | tf_op jit(solution)/shard_map/ppermute | solution.py:335
  147.2 15.9 %collective-permute-start.26 = (bf16[32,8192]{1,0:T(8,128)(2,1)S(1)}, bf16[32,8192]{1,0:T(8,128)(2,1)S(1)}, u32[]{:S(2)}, u32[]{:S(2)}) collective-permute-start(bf16[32,8192]{1,0:T(8,128)(2,1)S(1)} %collective-permute-done.21.refs_2_), channel_id=1, source_target_pairs={{4,6},{5,7},{2,0},{3,1},{12,14},{13,15},{10,8},{11,9},{20,22},{21,... | collective-permute-start | bytes 1572872 | tf_op jit(solution)/shard_map/ppermute | solution.py:151
  163.6 25.1 %collective-permute-start.36 = (bf16[32,64,256]{2,1,0:T(8,128)(2,1)S(1)}, bf16[32,64,256]{2,1,0:T(8,128)(2,1)S(1)}, u32[]{:S(2)}, u32[]{:S(2)}) collective-permute-start(bf16[32,64,256]{2,1,0:T(8,128)(2,1)S(1)} %get-tuple-element.137), channel_id=1, source_target_pairs={{0,8},{8,0},{16,24},{24,16},{1,9},{9,1},{17,25},{25,17},{2,10},{10... | collective-permute-start | bytes 3145736 | tf_op jit(solution)/shard_map/ppermute | solution.py:335
  165.2 24.8 %collective-permute-start.37 = (bf16[32,64,256]{2,1,0:T(8,128)(2,1)S(1)}, bf16[32,64,256]{2,1,0:T(8,128)(2,1)S(1)}, u32[]{:S(2)}, u32[]{:S(2)}) collective-permute-start(bf16[32,64,256]{2,1,0:T(8,128)(2,1)S(1)} %get-tuple-element.138), channel_id=1, source_target_pairs={{0,16},{8,24},{16,0},{24,8},{1,17},{9,25},{17,1},{25,9},{2,18},{10... | collective-permute-start | bytes 3145736 | tf_op jit(solution)/shard_map/ppermute | solution.py:335
  169.1 25.5 %collective-permute-start.33 = (bf16[32,8192]{1,0:T(8,128)(2,1)S(1)}, bf16[32,8192]{1,0:T(8,128)(2,1)S(1)}, u32[]{:S(2)}, u32[]{:S(2)}) collective-permute-start(bf16[32,8192]{1,0:T(8,128)(2,1)S(1)} %shard_map.66.refs_0_), channel_id=1, source_target_pairs={{0,2},{1,3},{2,0},{3,1},{4,6},{5,7},{6,4},{7,5},{8,10},{9,11},{10,... | collective-permute-start | bytes 1572872 | tf_op jit(solution)/shard_map/ppermute | solution.py:151
  169.1 25.5 %collective-permute-start.34 = (bf16[32,8192]{1,0:T(8,128)(2,1)S(1)}, bf16[32,8192]{1,0:T(8,128)(2,1)S(1)}, u32[]{:S(2)}, u32[]{:S(2)}) collective-permute-start(bf16[32,8192]{1,0:T(8,128)(2,1)S(1)} %shard_map.66.refs_0_), channel_id=1, source_target_pairs={{2,4},{3,5},{4,2},{5,3},{0,6},{1,7},{6,0},{7,1},{10,12},{11,13},{1... | collective-permute-start | bytes 1572872 | tf_op jit(solution)/shard_map/ppermute | solution.py:151
  195.3 15.7 %collective-permute-start.39 = (bf16[32,8192]{1,0:T(8,128)(2,1)S(1)}, bf16[32,8192]{1,0:T(8,128)(2,1)S(1)}, u32[]{:S(2)}, u32[]{:S(2)}) collective-permute-start(bf16[32,8192]{1,0:T(8,128)(2,1)S(1)} %collective-permute-done.34.refs_2_), channel_id=1, source_target_pairs={{4,6},{5,7},{2,0},{3,1},{12,14},{13,15},{10,8},{11,9},{20,22},{21,... | collective-permute-start | bytes 1572872 | tf_op jit(solution)/shard_map/ppermute | solution.py:151
  196.6 14.4 %collective-permute-start.40 = (bf16[32,8192]{1,0:T(8,128)(2,1)S(1)}, bf16[32,8192]{1,0:T(8,128)(2,1)S(1)}, u32[]{:S(2)}, u32[]{:S(2)}) collective-permute-start(bf16[32,8192]{1,0:T(8,128)(2,1)S(1)} %collective-permute-done.33.refs_1_), channel_id=1, source_target_pairs={{0,1},{1,0},{2,3},{3,2},{4,5},{5,4},{6,7},{7,6},{8,9},{9,8},{10,11... | collective-permute-start | bytes 1572872 | tf_op jit(solution)/shard_map/ppermute | solution.py:155
  199.5 25.1 %collective-permute-start.47 = (bf16[32,64,256]{2,1,0:T(8,128)(2,1)S(1)}, bf16[32,64,256]{2,1,0:T(8,128)(2,1)S(1)}, u32[]{:S(2)}, u32[]{:S(2)}) collective-permute-start(bf16[32,64,256]{2,1,0:T(8,128)(2,1)S(1)} %get-tuple-element.148), channel_id=1, source_target_pairs={{0,8},{8,0},{16,24},{24,16},{1,9},{9,1},{17,25},{25,17},{2,10},{10... | collective-permute-start | bytes 3145736 | tf_op jit(solution)/shard_map/ppermute | solution.py:335
  201.1 24.9 %collective-permute-start.48 = (bf16[32,64,256]{2,1,0:T(8,128)(2,1)S(1)}, bf16[32,64,256]{2,1,0:T(8,128)(2,1)S(1)}, u32[]{:S(2)}, u32[]{:S(2)}) collective-permute-start(bf16[32,64,256]{2,1,0:T(8,128)(2,1)S(1)} %get-tuple-element.149), channel_id=1, source_target_pairs={{0,16},{8,24},{16,0},{24,8},{1,17},{9,25},{17,1},{25,9},{2,18},{10... | collective-permute-start | bytes 3145736 | tf_op jit(solution)/shard_map/ppermute | solution.py:335
  217.0 14.4 %collective-permute-start.44 = (bf16[32,8192]{1,0:T(8,128)(2,1)S(1)}, bf16[32,8192]{1,0:T(8,128)(2,1)S(1)}, u32[]{:S(2)}, u32[]{:S(2)}) collective-permute-start(bf16[32,8192]{1,0:T(8,128)(2,1)S(1)} %shard_map.69.refs_0_), channel_id=1, source_target_pairs={{0,2},{1,3},{2,0},{3,1},{4,6},{5,7},{6,4},{7,5},{8,10},{9,11},{10,... | collective-permute-start | bytes 1572872 | tf_op jit(solution)/shard_map/ppermute | solution.py:151
  218.9 24.7 %collective-permute-start.45 = (bf16[32,8192]{1,0:T(8,128)(2,1)S(1)}, bf16[32,8192]{1,0:T(8,128)(2,1)S(1)}, u32[]{:S(2)}, u32[]{:S(2)}) collective-permute-start(bf16[32,8192]{1,0:T(8,128)(2,1)S(1)} %shard_map.69.refs_0_), channel_id=1, source_target_pairs={{2,4},{3,5},{4,2},{5,3},{0,6},{1,7},{6,0},{7,1},{10,12},{11,13},{1... | collective-permute-start | bytes 1572872 | tf_op jit(solution)/shard_map/ppermute | solution.py:151
  226.7 24.0 %collective-permute-start.53 = (bf16[32,64,256]{2,1,0:T(8,128)(2,1)S(1)}, bf16[32,64,256]{2,1,0:T(8,128)(2,1)S(1)}, u32[]{:S(2)}, u32[]{:S(2)}) collective-permute-start(bf16[32,64,256]{2,1,0:T(8,128)(2,1)S(1)} %get-tuple-element.157), channel_id=1, source_target_pairs={{0,8},{8,0},{16,24},{24,16},{1,9},{9,1},{17,25},{25,17},{2,10},{10... | collective-permute-start | bytes 3145736 | tf_op jit(solution)/shard_map/ppermute | solution.py:335
  227.2 23.9 %collective-permute-start.54 = (bf16[32,64,256]{2,1,0:T(8,128)(2,1)S(1)}, bf16[32,64,256]{2,1,0:T(8,128)(2,1)S(1)}, u32[]{:S(2)}, u32[]{:S(2)}) collective-permute-start(bf16[32,64,256]{2,1,0:T(8,128)(2,1)S(1)} %get-tuple-element.158), channel_id=1, source_target_pairs={{0,16},{8,24},{16,0},{24,8},{1,17},{9,25},{17,1},{25,9},{2,18},{10... | collective-permute-start | bytes 3145736 | tf_op jit(solution)/shard_map/ppermute | solution.py:335
  245.5 15.8 %collective-permute-start.50 = (bf16[32,8192]{1,0:T(8,128)(2,1)S(1)}, bf16[32,8192]{1,0:T(8,128)(2,1)S(1)}, u32[]{:S(2)}, u32[]{:S(2)}) collective-permute-start(bf16[32,8192]{1,0:T(8,128)(2,1)S(1)} %collective-permute-done.45.refs_2_), channel_id=1, source_target_pairs={{4,6},{5,7},{2,0},{3,1},{12,14},{13,15},{10,8},{11,9},{20,22},{21,... | collective-permute-start | bytes 1572872 | tf_op jit(solution)/shard_map/ppermute | solution.py:151
  261.9 25.1 %collective-permute-start.60 = (bf16[32,64,256]{2,1,0:T(8,128)(2,1)S(1)}, bf16[32,64,256]{2,1,0:T(8,128)(2,1)S(1)}, u32[]{:S(2)}, u32[]{:S(2)}) collective-permute-start(bf16[32,64,256]{2,1,0:T(8,128)(2,1)S(1)} %get-tuple-element.166), channel_id=1, source_target_pairs={{0,8},{8,0},{16,24},{24,16},{1,9},{9,1},{17,25},{25,17},{2,10},{10... | collective-permute-start | bytes 3145736 | tf_op jit(solution)/shard_map/ppermute | solution.py:335
  263.4 24.8 %collective-permute-start.61 = (bf16[32,64,256]{2,1,0:T(8,128)(2,1)S(1)}, bf16[32,64,256]{2,1,0:T(8,128)(2,1)S(1)}, u32[]{:S(2)}, u32[]{:S(2)}) collective-permute-start(bf16[32,64,256]{2,1,0:T(8,128)(2,1)S(1)} %get-tuple-element.167), channel_id=1, source_target_pairs={{0,16},{8,24},{16,0},{24,8},{1,17},{9,25},{17,1},{25,9},{2,18},{10... | collective-permute-start | bytes 3145736 | tf_op jit(solution)/shard_map/ppermute | solution.py:335
  267.2 21.0 %collective-permute-start.59 = (bf16[32,8192]{1,0:T(8,128)(2,1)S(1)}, bf16[32,8192]{1,0:T(8,128)(2,1)S(1)}, u32[]{:S(2)}, u32[]{:S(2)}) collective-permute-start(bf16[32,8192]{1,0:T(8,128)(2,1)S(1)} %shard_map.73.refs_0_), channel_id=1, source_target_pairs={{0,1},{1,0},{2,3},{3,2},{4,5},{5,4},{6,7},{7,6},{8,9},{9,8},{10,11... | collective-permute-start | bytes 1572872 | tf_op jit(solution)/shard_map/ppermute | solution.py:155
  267.4 23.6 %collective-permute-start.57 = (bf16[32,8192]{1,0:T(8,128)(2,1)S(1)}, bf16[32,8192]{1,0:T(8,128)(2,1)S(1)}, u32[]{:S(2)}, u32[]{:S(2)}) collective-permute-start(bf16[32,8192]{1,0:T(8,128)(2,1)S(1)} %shard_map.73.refs_0_), channel_id=1, source_target_pairs={{0,2},{1,3},{2,0},{3,1},{4,6},{5,7},{6,4},{7,5},{8,10},{9,11},{10,... | collective-permute-start | bytes 1572872 | tf_op jit(solution)/shard_map/ppermute | solution.py:151
  268.2 25.6 %collective-permute-start.58 = (bf16[32,8192]{1,0:T(8,128)(2,1)S(1)}, bf16[32,8192]{1,0:T(8,128)(2,1)S(1)}, u32[]{:S(2)}, u32[]{:S(2)}) collective-permute-start(bf16[32,8192]{1,0:T(8,128)(2,1)S(1)} %shard_map.73.refs_0_), channel_id=1, source_target_pairs={{2,4},{3,5},{4,2},{5,3},{0,6},{1,7},{6,0},{7,1},{10,12},{11,13},{1... | collective-permute-start | bytes 1572872 | tf_op jit(solution)/shard_map/ppermute | solution.py:151
  289.0 24.0 %collective-permute-start.66 = (bf16[32,64,256]{2,1,0:T(8,128)(2,1)S(1)}, bf16[32,64,256]{2,1,0:T(8,128)(2,1)S(1)}, u32[]{:S(2)}, u32[]{:S(2)}) collective-permute-start(bf16[32,64,256]{2,1,0:T(8,128)(2,1)S(1)} %get-tuple-element.176), channel_id=1, source_target_pairs={{0,8},{8,0},{16,24},{24,16},{1,9},{9,1},{17,25},{25,17},{2,10},{10... | collective-permute-start | bytes 3145736 | tf_op jit(solution)/shard_map/ppermute | solution.py:335
  289.5 23.7 %collective-permute-start.67 = (bf16[32,64,256]{2,1,0:T(8,128)(2,1)S(1)}, bf16[32,64,256]{2,1,0:T(8,128)(2,1)S(1)}, u32[]{:S(2)}, u32[]{:S(2)}) collective-permute-start(bf16[32,64,256]{2,1,0:T(8,128)(2,1)S(1)} %get-tuple-element.177), channel_id=1, source_target_pairs={{0,16},{8,24},{16,0},{24,8},{1,17},{9,25},{17,1},{25,9},{2,18},{10... | collective-permute-start | bytes 3145736 | tf_op jit(solution)/shard_map/ppermute | solution.py:335
  294.4 19.6 %collective-permute-start.62 = (bf16[32,8192]{1,0:T(8,128)(2,1)S(1)}, bf16[32,8192]{1,0:T(8,128)(2,1)S(1)}, u32[]{:S(2)}, u32[]{:S(2)}) collective-permute-start(bf16[32,8192]{1,0:T(8,128)(2,1)S(1)} %collective-permute-done.57.refs_1_), channel_id=1, source_target_pairs={{2,4},{3,5},{4,2},{5,3},{10,12},{11,13},{12,10},{13,11},{18,20},{1... | collective-permute-start | bytes 1572872 | tf_op jit(solution)/shard_map/ppermute | solution.py:151
  295.8 18.2 %collective-permute-start.63 = (bf16[32,8192]{1,0:T(8,128)(2,1)S(1)}, bf16[32,8192]{1,0:T(8,128)(2,1)S(1)}, u32[]{:S(2)}, u32[]{:S(2)}) collective-permute-start(bf16[32,8192]{1,0:T(8,128)(2,1)S(1)} %collective-permute-done.58.refs_2_), channel_id=1, source_target_pairs={{4,6},{5,7},{2,0},{3,1},{12,14},{13,15},{10,8},{11,9},{20,22},{21,... | collective-permute-start | bytes 1572872 | tf_op jit(solution)/shard_map/ppermute | solution.py:151
  314.6 25.2 %collective-permute-start.75 = (bf16[32,64,256]{2,1,0:T(8,128)(2,1)S(1)}, bf16[32,64,256]{2,1,0:T(8,128)(2,1)S(1)}, u32[]{:S(2)}, u32[]{:S(2)}) collective-permute-start(bf16[32,64,256]{2,1,0:T(8,128)(2,1)S(1)} %get-tuple-element.183), channel_id=1, source_target_pairs={{0,8},{8,0},{16,24},{24,16},{1,9},{9,1},{17,25},{25,17},{2,10},{10... | collective-permute-start | bytes 3145736 | tf_op jit(solution)/shard_map/ppermute | solution.py:335
  316.1 24.9 %collective-permute-start.76 = (bf16[32,64,256]{2,1,0:T(8,128)(2,1)S(1)}, bf16[32,64,256]{2,1,0:T(8,128)(2,1)S(1)}, u32[]{:S(2)}, u32[]{:S(2)}) collective-permute-start(bf16[32,64,256]{2,1,0:T(8,128)(2,1)S(1)} %get-tuple-element.184), channel_id=1, source_target_pairs={{0,16},{8,24},{16,0},{24,8},{1,17},{9,25},{17,1},{25,9},{2,18},{10... | collective-permute-start | bytes 3145736 | tf_op jit(solution)/shard_map/ppermute | solution.py:335
  320.3 14.2 %collective-permute-start.70 = (bf16[32,8192]{1,0:T(8,128)(2,1)S(1)}, bf16[32,8192]{1,0:T(8,128)(2,1)S(1)}, u32[]{:S(2)}, u32[]{:S(2)}) collective-permute-start(bf16[32,8192]{1,0:T(8,128)(2,1)S(1)} %shard_map.77.refs_0_), channel_id=1, source_target_pairs={{0,2},{1,3},{2,0},{3,1},{4,6},{5,7},{6,4},{7,5},{8,10},{9,11},{10,... | collective-permute-start | bytes 1572872 | tf_op jit(solution)/shard_map/ppermute | solution.py:151
  321.3 13.9 %collective-permute-start.71 = (bf16[32,8192]{1,0:T(8,128)(2,1)S(1)}, bf16[32,8192]{1,0:T(8,128)(2,1)S(1)}, u32[]{:S(2)}, u32[]{:S(2)}) collective-permute-start(bf16[32,8192]{1,0:T(8,128)(2,1)S(1)} %shard_map.77.refs_0_), channel_id=1, source_target_pairs={{2,4},{3,5},{4,2},{5,3},{10,12},{11,13},{12,10},{13,11},{18,20},{1... | collective-permute-start | bytes 1572872 | tf_op jit(solution)/shard_map/ppermute | solution.py:151
  322.1 24.6 %collective-permute-start.77 = (bf16[32,8192]{1,0:T(8,128)(2,1)S(1)}, bf16[32,8192]{1,0:T(8,128)(2,1)S(1)}, u32[]{:S(2)}, u32[]{:S(2)}) collective-permute-start(bf16[32,8192]{1,0:T(8,128)(2,1)S(1)} %shard_map.77.refs_0_), channel_id=1, source_target_pairs={{0,6},{1,7},{6,0},{7,1},{8,14},{9,15},{14,8},{15,9},{16,22},{17,23... | collective-permute-start | bytes 1572872 | tf_op jit(solution)/shard_map/ppermute | solution.py:151
  335.2 26.8 %collective-permute-start.73 = (bf16[32,8192]{1,0:T(8,128)(2,1)S(1)}, bf16[32,8192]{1,0:T(8,128)(2,1)S(1)}, u32[]{:S(2)}, u32[]{:S(2)}) collective-permute-start(bf16[32,8192]{1,0:T(8,128)(2,1)S(1)} %collective-permute-done.71.refs_2_), channel_id=1, source_target_pairs={{4,6},{5,7},{2,0},{3,1},{12,14},{13,15},{10,8},{11,9},{20,22},{21,... | collective-permute-start | bytes 1572872 | tf_op jit(solution)/shard_map/ppermute | solution.py:151
  343.1 19.4 %collective-permute-start.78 = (bf16[32,8192]{1,0:T(8,128)(2,1)S(1)}, bf16[32,8192]{1,0:T(8,128)(2,1)S(1)}, u32[]{:S(2)}, u32[]{:S(2)}) collective-permute-start(bf16[32,8192]{1,0:T(8,128)(2,1)S(1)} %collective-permute-done.70.refs_1_), channel_id=1, source_target_pairs={{0,1},{1,0},{2,3},{3,2},{4,5},{5,4},{6,7},{7,6},{8,9},{9,8},{10,11... | collective-permute-start | bytes 1572872 | tf_op jit(solution)/shard_map/ppermute | solution.py:155
  343.2 19.3 %collective-permute-start.79 = (bf16[32,8192]{1,0:T(8,128)(2,1)S(1)}, bf16[32,8192]{1,0:T(8,128)(2,1)S(1)}, u32[]{:S(2)}, u32[]{:S(2)}) collective-permute-start(bf16[32,8192]{1,0:T(8,128)(2,1)S(1)} %collective-permute-done.71.refs_2_), channel_id=1, source_target_pairs={{0,1},{1,0},{2,3},{3,2},{4,5},{5,4},{6,7},{7,6},{8,9},{9,8},{10,11... | collective-permute-start | bytes 1572872 | tf_op jit(solution)/shard_map/ppermute | solution.py:155
  346.6 15.8 %collective-permute-start.82 = (bf16[32,8192]{1,0:T(8,128)(2,1)S(1)}, bf16[32,8192]{1,0:T(8,128)(2,1)S(1)}, u32[]{:S(2)}, u32[]{:S(2)}) collective-permute-start(bf16[32,8192]{1,0:T(8,128)(2,1)S(1)} %collective-permute-done.77.refs_5_), channel_id=1, source_target_pairs={{0,1},{1,0},{2,3},{3,2},{4,5},{5,4},{6,7},{7,6},{8,9},{9,8},{10,11... | collective-permute-start | bytes 1572872 | tf_op jit(solution)/shard_map/ppermute | solution.py:155
  367.8 14.0 %collective-permute-start.83 = (bf16[32,8192]{1,0:T(8,128)(2,1)S(1)}, bf16[32,8192]{1,0:T(8,128)(2,1)S(1)}, u32[]{:S(2)}, u32[]{:S(2)}) collective-permute-start(bf16[32,8192]{1,0:T(8,128)(2,1)S(1)} %shard_map.79.refs_0_), channel_id=1, source_target_pairs={{0,2},{1,3},{2,0},{3,1},{4,6},{5,7},{6,4},{7,5},{8,10},{9,11},{10,... | collective-permute-start | bytes 1572872 | tf_op jit(solution)/shard_map/ppermute | solution.py:151
  367.9 14.6 %collective-permute-start.84 = (bf16[32,8192]{1,0:T(8,128)(2,1)S(1)}, bf16[32,8192]{1,0:T(8,128)(2,1)S(1)}, u32[]{:S(2)}, u32[]{:S(2)}) collective-permute-start(bf16[32,8192]{1,0:T(8,128)(2,1)S(1)} %shard_map.79.refs_0_), channel_id=1, source_target_pairs={{2,4},{3,5},{4,2},{5,3},{10,12},{11,13},{12,10},{13,11},{18,20},{1... | collective-permute-start | bytes 1572872 | tf_op jit(solution)/shard_map/ppermute | solution.py:151
  368.6 25.4 %collective-permute-start.87 = (bf16[32,8192]{1,0:T(8,128)(2,1)S(1)}, bf16[32,8192]{1,0:T(8,128)(2,1)S(1)}, u32[]{:S(2)}, u32[]{:S(2)}) collective-permute-start(bf16[32,8192]{1,0:T(8,128)(2,1)S(1)} %shard_map.79.refs_0_), channel_id=1, source_target_pairs={{0,6},{1,7},{6,0},{7,1},{8,14},{9,15},{14,8},{15,9},{16,22},{17,23... | collective-permute-start | bytes 1572872 | tf_op jit(solution)/shard_map/ppermute | solution.py:151
  382.6 26.5 %collective-permute-start.86 = (bf16[32,8192]{1,0:T(8,128)(2,1)S(1)}, bf16[32,8192]{1,0:T(8,128)(2,1)S(1)}, u32[]{:S(2)}, u32[]{:S(2)}) collective-permute-start(bf16[32,8192]{1,0:T(8,128)(2,1)S(1)} %collective-permute-done.84.refs_2_), channel_id=1, source_target_pairs={{4,6},{5,7},{2,0},{3,1},{12,14},{13,15},{10,8},{11,9},{20,22},{21,... | collective-permute-start | bytes 1572872 | tf_op jit(solution)/shard_map/ppermute | solution.py:151
  383.9 25.2 %collective-permute-start.88 = (bf16[32,8192]{1,0:T(8,128)(2,1)S(1)}, bf16[32,8192]{1,0:T(8,128)(2,1)S(1)}, u32[]{:S(2)}, u32[]{:S(2)}) collective-permute-start(bf16[32,8192]{1,0:T(8,128)(2,1)S(1)} %shard_map.79.refs_0_), channel_id=1, source_target_pairs={{0,1},{1,0},{2,3},{3,2},{4,5},{5,4},{6,7},{7,6},{8,9},{9,8},{10,11... | collective-permute-start | bytes 1572872 | tf_op jit(solution)/shard_map/ppermute | solution.py:155
  386.0 23.6 %collective-permute-start.89 = (bf16[32,8192]{1,0:T(8,128)(2,1)S(1)}, bf16[32,8192]{1,0:T(8,128)(2,1)S(1)}, u32[]{:S(2)}, u32[]{:S(2)}) collective-permute-start(bf16[32,8192]{1,0:T(8,128)(2,1)S(1)} %collective-permute-done.83.refs_1_), channel_id=1, source_target_pairs={{0,1},{1,0},{2,3},{3,2},{4,5},{5,4},{6,7},{7,6},{8,9},{9,8},{10,11... | collective-permute-start | bytes 1572872 | tf_op jit(solution)/shard_map/ppermute | solution.py:155
  394.0 15.6 %collective-permute-start.90 = (bf16[32,8192]{1,0:T(8,128)(2,1)S(1)}, bf16[32,8192]{1,0:T(8,128)(2,1)S(1)}, u32[]{:S(2)}, u32[]{:S(2)}) collective-permute-start(bf16[32,8192]{1,0:T(8,128)(2,1)S(1)} %collective-permute-done.84.refs_2_), channel_id=1, source_target_pairs={{0,1},{1,0},{2,3},{3,2},{4,5},{5,4},{6,7},{7,6},{8,9},{9,8},{10,11... | collective-permute-start | bytes 1572872 | tf_op jit(solution)/shard_map/ppermute | solution.py:155
  394.0 15.6 %collective-permute-start.93 = (bf16[32,8192]{1,0:T(8,128)(2,1)S(1)}, bf16[32,8192]{1,0:T(8,128)(2,1)S(1)}, u32[]{:S(2)}, u32[]{:S(2)}) collective-permute-start(bf16[32,8192]{1,0:T(8,128)(2,1)S(1)} %collective-permute-done.87.refs_5_), channel_id=1, source_target_pairs={{0,1},{1,0},{2,3},{3,2},{4,5},{5,4},{6,7},{7,6},{8,9},{9,8},{10,11... | collective-permute-start | bytes 1572872 | tf_op jit(solution)/shard_map/ppermute | solution.py:155
  414.9 14.0 %collective-permute-start.94 = (bf16[32,8192]{1,0:T(8,128)(2,1)S(1)}, bf16[32,8192]{1,0:T(8,128)(2,1)S(1)}, u32[]{:S(2)}, u32[]{:S(2)}) collective-permute-start(bf16[32,8192]{1,0:T(8,128)(2,1)S(1)} %shard_map.81.refs_0_), channel_id=1, source_target_pairs={{0,2},{1,3},{2,0},{3,1},{4,6},{5,7},{6,4},{7,5},{8,10},{9,11},{10,... | collective-permute-start | bytes 1572872 | tf_op jit(solution)/shard_map/ppermute | solution.py:151
  415.0 14.6 %collective-permute-start.95 = (bf16[32,8192]{1,0:T(8,128)(2,1)S(1)}, bf16[32,8192]{1,0:T(8,128)(2,1)S(1)}, u32[]{:S(2)}, u32[]{:S(2)}) collective-permute-start(bf16[32,8192]{1,0:T(8,128)(2,1)S(1)} %shard_map.81.refs_0_), channel_id=1, source_target_pairs={{2,4},{3,5},{4,2},{5,3},{10,12},{11,13},{12,10},{13,11},{18,20},{1... | collective-permute-start | bytes 1572872 | tf_op jit(solution)/shard_map/ppermute | solution.py:151
  415.7 25.4 %collective-permute-start.98 = (bf16[32,8192]{1,0:T(8,128)(2,1)S(1)}, bf16[32,8192]{1,0:T(8,128)(2,1)S(1)}, u32[]{:S(2)}, u32[]{:S(2)}) collective-permute-start(bf16[32,8192]{1,0:T(8,128)(2,1)S(1)} %shard_map.81.refs_0_), channel_id=1, source_target_pairs={{0,6},{1,7},{6,0},{7,1},{8,14},{9,15},{14,8},{15,9},{16,22},{17,23... | collective-permute-start | bytes 1572872 | tf_op jit(solution)/shard_map/ppermute | solution.py:151
  429.6 26.5 %collective-permute-start.97 = (bf16[32,8192]{1,0:T(8,128)(2,1)S(1)}, bf16[32,8192]{1,0:T(8,128)(2,1)S(1)}, u32[]{:S(2)}, u32[]{:S(2)}) collective-permute-start(bf16[32,8192]{1,0:T(8,128)(2,1)S(1)} %collective-permute-done.95.refs_2_), channel_id=1, source_target_pairs={{4,6},{5,7},{2,0},{3,1},{12,14},{13,15},{10,8},{11,9},{20,22},{21,... | collective-permute-start | bytes 1572872 | tf_op jit(solution)/shard_map/ppermute | solution.py:151
  430.9 25.2 %collective-permute-start.99 = (bf16[32,8192]{1,0:T(8,128)(2,1)S(1)}, bf16[32,8192]{1,0:T(8,128)(2,1)S(1)}, u32[]{:S(2)}, u32[]{:S(2)}) collective-permute-start(bf16[32,8192]{1,0:T(8,128)(2,1)S(1)} %shard_map.81.refs_0_), channel_id=1, source_target_pairs={{0,1},{1,0},{2,3},{3,2},{4,5},{5,4},{6,7},{7,6},{8,9},{9,8},{10,11... | collective-permute-start | bytes 1572872 | tf_op jit(solution)/shard_map/ppermute | solution.py:155
  433.4 23.3 %collective-permute-start.100 = (bf16[32,8192]{1,0:T(8,128)(2,1)S(1)}, bf16[32,8192]{1,0:T(8,128)(2,1)S(1)}, u32[]{:S(2)}, u32[]{:S(2)}) collective-permute-start(bf16[32,8192]{1,0:T(8,128)(2,1)S(1)} %collective-permute-done.94.refs_1_), channel_id=1, source_target_pairs={{0,1},{1,0},{2,3},{3,2},{4,5},{5,4},{6,7},{7,6},{8,9},{9,8},{10,11... | collective-permute-start | bytes 1572872 | tf_op jit(solution)/shard_map/ppermute | solution.py:155
  441.1 15.6 %collective-permute-start.101 = (bf16[32,8192]{1,0:T(8,128)(2,1)S(1)}, bf16[32,8192]{1,0:T(8,128)(2,1)S(1)}, u32[]{:S(2)}, u32[]{:S(2)}) collective-permute-start(bf16[32,8192]{1,0:T(8,128)(2,1)S(1)} %collective-permute-done.95.refs_2_), channel_id=1, source_target_pairs={{0,1},{1,0},{2,3},{3,2},{4,5},{5,4},{6,7},{7,6},{8,9},{9,8},{10,11... | collective-permute-start | bytes 1572872 | tf_op jit(solution)/shard_map/ppermute | solution.py:155
  441.1 15.6 %collective-permute-start.104 = (bf16[32,8192]{1,0:T(8,128)(2,1)S(1)}, bf16[32,8192]{1,0:T(8,128)(2,1)S(1)}, u32[]{:S(2)}, u32[]{:S(2)}) collective-permute-start(bf16[32,8192]{1,0:T(8,128)(2,1)S(1)} %collective-permute-done.98.refs_5_), channel_id=1, source_target_pairs={{0,1},{1,0},{2,3},{3,2},{4,5},{5,4},{6,7},{7,6},{8,9},{9,8},{10,11... | collective-permute-start | bytes 1572872 | tf_op jit(solution)/shard_map/ppermute | solution.py:155
  (44 other events, 234.3 us)

commit v5 on v4

--- a/solution.py
+++ b/solution.py
@@ -130,7 +130,7 @@
     smem = pl.BlockSpec(memory_space=pltpu.SMEM)
     anywhere = pl.BlockSpec(memory_space=pl.ANY)
     vmem = pl.BlockSpec(memory_space=pltpu.VMEM)
-    kernel = functools.partial(layer_kernel, act_plan, 64)
+    kernel = functools.partial(layer_kernel, act_plan, 16)
     return pl.pallas_call(
         kernel,
         out_shape=jax.ShapeDtypeStruct((rows, neurons), jnp.bfloat16),

time: 472 us -> 469 us (level); the launches traced: 463 us -> 468 us
  Pallas kernels: 58.1 us -> 63.4 us
    ppermute x24, waiting for transfers between devices: 139 us -> 133 us  [advance(): lax.ppermute(array, 'pipe', [(p, p ^ side) for p in range(self.square)])]
    ppermute x35, waiting for transfers between devices: 156 us -> 162 us  [along_line(): return lax.ppermute(x, 'rows', moves)]
    pallas_call x8, Pallas kernels: 26.4 us -> 32.1 us  [apply_layer(): pl.pallas_call(kernel, out_shape=jax.ShapeDtypeStruct((rows, neurons), jn...]
  transfers between devices with their start and end apart: 105 -> 105, of which waited for: 59 -> 59; matrix products, arithmetic and copies ran while one was open for 0% -> 0% of each run, Pallas kernels for 9% -> 10%
where the time goes in v5:
time: 469 us; the launch traced here: 468 us
  waiting for transfers between devices  308 us (66%)
  starting transfers between devices  91.2 us (19%)
  Pallas kernels  63.4 us (14%)
    ppermute x35, waiting for transfers between devices, along_line(): return lax.ppermute(x, 'rows', moves)  162 us
    ppermute x24, waiting for transfers between devices, advance(): lax.ppermute(array, 'pipe', [(p, p ^ side) for p in range(self.square)])  133 us
    ppermute x35, starting transfers between devices, along_line(): return lax.ppermute(x, 'rows', moves)  48.3 us
    pallas_call x8, Pallas kernels, apply_layer(): pl.pallas_call(kernel, out_shape=jax.ShapeDtypeStruct((rows, neurons), jn...  32.1 us
    ppermute x24, starting transfers between devices, advance(): lax.ppermute(array, 'pipe', [(p, p ^ side) for p in range(self.square)])  27.9 us
    pallas_call x8, Pallas kernels, gather_weights(): pl.pallas_call(functools.partial(gather_weights_kernel, plan), out_shape=...  16.8 us
    ppermute x43, waiting for transfers between devices, to_other_core(): lax.ppermute(x, 'rows', [(i, i ^ 1) for i in range(lax.axis_size('rows'))])  13.9 us
    pallas_call x12, Pallas kernels, pick(): pl.pallas_call(functools.partial(pick_kernel, choices, len(choices)), out...  11.1 us
  transfers between devices with their start and end apart: 105, of which 59 were waited for; matrix products, arithmetic and copies ran while one was open for 0% of the time, Pallas kernels for 10%

profile of v5, /device:TPU:0, one launch (start us, length us, event | category | flops | bytes accessed | tf_op | source)
XLA Modules:
  0.0 467.9 jit_solution(16048370472815740264)
XLA Ops:
  0.1 3.1 shard_map.55
  6.4 3.0 collective-permute-start
  11.0 1.9 collective-permute-start.6
  14.7 1.6 collective-permute-start.3
  16.3 3.6 collective-permute-start.4
  20.3 3.4 shard_map.56.refs_2_.refs_1_.refs_0_.refs_4_.refs_3_.refs_5_
  23.7 12.3 %collective-permute-done.6.refs_0_.refs_1_.refs_3_.refs_2_ = bf16[32,64,256]{2,1,0:T(8,128)(2,1)S(1)} collective-permute-done((bf16[32,64,256]{2,1,0:T(8,128)(2,1)}, bf16[32,64,256]{2,1,0:T(8,128)(2,1)S(1)}, u32[]{:S(2)}, u32[]{:S(2)}) %collective-permute-start.6) | collective-permute-done | bytes 1048608 | tf_op jit(solution)/shard_map/ppermute | solution.py:335
  40.0 2.4 collective-permute-done.4.refs_2_
  45.0 16.4 %collective-permute-done.12.refs_0_.refs_6_.refs_5_ = bf16[32,64,256]{2,1,0:T(8,128)(2,1)S(1)} collective-permute-done((bf16[32,64,256]{2,1,0:T(8,128)(2,1)S(1)}, bf16[32,64,256]{2,1,0:T(8,128)(2,1)S(1)}, u32[]{:S(2)}, u32[]{:S(2)}) %collective-permute-start.12) | collective-permute-done | bytes 1048608 | tf_op jit(solution)/shard_map/ppermute | solution.py:335
  65.5 19.4 %collective-permute-done.16.refs_2_.refs_7_ = bf16[32,64,256]{2,1,0:T(8,128)(2,1)S(1)} collective-permute-done((bf16[32,64,256]{2,1,0:T(8,128)(2,1)S(1)}, bf16[32,64,256]{2,1,0:T(8,128)(2,1)S(1)}, u32[]{:S(2)}, u32[]{:S(2)}) %collective-permute-start.16) | collective-permute-done | bytes 1048608 | tf_op jit(solution)/shard_map/ppermute | solution.py:335
  90.9 11.3 %collective-permute-done.9.refs_4_ = bf16[32,8192]{1,0:T(8,128)(2,1)S(1)} collective-permute-done((bf16[32,8192]{1,0:T(8,128)(2,1)S(1)}, bf16[32,8192]{1,0:T(8,128)(2,1)S(1)}, u32[]{:S(2)}, u32[]{:S(2)}) %collective-permute-start.9) | collective-permute-done | bytes 524320 | tf_op jit(solution)/shard_map/ppermute | solution.py:151
  102.7 5.4 %collective-permute-done.18.refs_7_.refs_0_.refs_1_.refs_3_ = bf16[32,64,256]{2,1,0:T(8,128)(2,1)S(1)} collective-permute-done((bf16[32,64,256]{2,1,0:T(8,128)(2,1)S(1)}, bf16[32,64,256]{2,1,0:T(8,128)(2,1)S(1)}, u32[]{:S(2)}, u32[]{:S(2)}) %collective-permute-start.18) | collective-permute-done | bytes 1048608 | tf_op jit(solution)/shard_map/ppermute | solution.py:335
  110.7 1.6 collective-permute-start.24
  112.4 2.1 shard_map.60.refs_10_
  114.5 3.9 shard_map.61.refs_0_
  119.9 2.5 collective-permute-start.21
  122.4 9.0 %collective-permute-done.23.refs_2_.refs_7_.refs_8_.refs_4_ = bf16[32,64,256]{2,1,0:T(8,128)(2,1)S(1)} collective-permute-done((bf16[32,64,256]{2,1,0:T(8,128)(2,1)S(1)}, bf16[32,64,256]{2,1,0:T(8,128)(2,1)S(1)}, u32[]{:S(2)}, u32[]{:S(2)}) %collective-permute-start.23) | collective-permute-done | bytes 1048608 | tf_op jit(solution)/shard_map/ppermute | solution.py:335
  134.0 1.7 collective-permute-start.30
  135.7 10.3 %collective-permute-done.21.refs_2_ = bf16[32,8192]{1,0:T(8,128)(2,1)S(1)} collective-permute-done((bf16[32,8192]{1,0:T(8,128)(2,1)S(1)}, bf16[32,8192]{1,0:T(8,128)(2,1)S(1)}, u32[]{:S(2)}, u32[]{:S(2)}) %collective-permute-start.21) | collective-permute-done | bytes 524320 | tf_op jit(solution)/shard_map/ppermute | solution.py:151
  149.2 3.1 collective-permute-done.29.refs_4_.refs_2_.refs_0_.refs_10_
  153.2 2.1 shard_map.65.refs_10_
  156.1 7.7 %collective-permute-done.26.refs_4_ = bf16[32,8192]{1,0:T(8,128)(2,1)S(1)} collective-permute-done((bf16[32,8192]{1,0:T(8,128)(2,1)S(1)}, bf16[32,8192]{1,0:T(8,128)(2,1)S(1)}, u32[]{:S(2)}, u32[]{:S(2)}) %collective-permute-start.26) | collective-permute-done | bytes 524320 | tf_op jit(solution)/shard_map/ppermute | solution.py:151
  164.3 1.6 collective-permute-start.36
  166.5 3.9 shard_map.66.refs_0_
  170.6 1.6 collective-permute-start.34
  172.4 17.0 %collective-permute-done.36.refs_2_.refs_3_.refs_8_.refs_5_ = bf16[32,64,256]{2,1,0:T(8,128)(2,1)S(1)} collective-permute-done((bf16[32,64,256]{2,1,0:T(8,128)(2,1)S(1)}, bf16[32,64,256]{2,1,0:T(8,128)(2,1)S(1)}, u32[]{:S(2)}, u32[]{:S(2)}) %collective-permute-start.36) | collective-permute-done | bytes 1048608 | tf_op jit(solution)/shard_map/ppermute | solution.py:335
  191.5 4.6 collective-permute-done.33.refs_1_
  198.2 2.1 shard_map.68.refs_10_
  200.9 1.6 collective-permute-start.47
  203.0 9.5 %collective-permute-done.39.refs_4_ = bf16[32,8192]{1,0:T(8,128)(2,1)S(1)} collective-permute-done((bf16[32,8192]{1,0:T(8,128)(2,1)S(1)}, bf16[32,8192]{1,0:T(8,128)(2,1)S(1)}, u32[]{:S(2)}, u32[]{:S(2)}) %collective-permute-start.39) | collective-permute-done | bytes 524320 | tf_op jit(solution)/shard_map/ppermute | solution.py:151
  215.1 3.9 shard_map.69.refs_0_
  219.3 1.9 collective-permute-start.44
  222.4 3.6 collective-permute-done.47.refs_1_.refs_5_.refs_7_.refs_4_
  230.0 3.6 collective-permute-done.44.refs_1_
  233.6 12.2 %collective-permute-done.45.refs_2_ = bf16[32,8192]{1,0:T(8,128)(2,1)S(1)} collective-permute-done((bf16[32,8192]{1,0:T(8,128)(2,1)S(1)}, bf16[32,8192]{1,0:T(8,128)(2,1)S(1)}, u32[]{:S(2)}, u32[]{:S(2)}) %collective-permute-start.45) | collective-permute-done | bytes 524320 | tf_op jit(solution)/shard_map/ppermute | solution.py:151
  249.3 2.8 collective-permute-done.53.refs_4_.refs_2_.refs_1_.refs_10_
  252.4 2.1 shard_map.72.refs_10_
  255.3 8.4 %collective-permute-done.50.refs_4_ = bf16[32,8192]{1,0:T(8,128)(2,1)S(1)} collective-permute-done((bf16[32,8192]{1,0:T(8,128)(2,1)S(1)}, bf16[32,8192]{1,0:T(8,128)(2,1)S(1)}, u32[]{:S(2)}, u32[]{:S(2)}) %collective-permute-start.50) | collective-permute-done | bytes 524320 | tf_op jit(solution)/shard_map/ppermute | solution.py:151
  266.3 3.9 shard_map.73.refs_0_
  270.5 2.6 collective-permute-start.58
  273.0 16.2 %collective-permute-done.60.refs_1_.refs_6_.refs_8_.refs_7_ = bf16[32,64,256]{2,1,0:T(8,128)(2,1)S(1)} collective-permute-done((bf16[32,64,256]{2,1,0:T(8,128)(2,1)S(1)}, bf16[32,64,256]{2,1,0:T(8,128)(2,1)S(1)}, u32[]{:S(2)}, u32[]{:S(2)}) %collective-permute-start.60) | collective-permute-done | bytes 1048608 | tf_op jit(solution)/shard_map/ppermute | solution.py:335
  293.3 3.5 collective-permute-done.58.refs_2_
  300.0 2.1 shard_map.76.refs_10_
  302.1 13.0 %collective-permute-done.66.refs_0_.refs_5_.refs_2_ = bf16[32,64,256]{2,1,0:T(8,128)(2,1)S(1)} collective-permute-done((bf16[32,64,256]{2,1,0:T(8,128)(2,1)S(1)}, bf16[32,64,256]{2,1,0:T(8,128)(2,1)S(1)}, u32[]{:S(2)}, u32[]{:S(2)}) %collective-permute-start.66) | collective-permute-done | bytes 1048608 | tf_op jit(solution)/shard_map/ppermute | solution.py:335
  319.0 3.9 shard_map.77.refs_0_
  324.8 4.4 collective-permute-start.77
  329.3 8.0 %collective-permute-done.70.refs_1_ = bf16[32,8192]{1,0:T(8,128)(2,1)S(1)} collective-permute-done((bf16[32,8192]{1,0:T(8,128)(2,1)S(1)}, bf16[32,8192]{1,0:T(8,128)(2,1)S(1)}, u32[]{:S(2)}, u32[]{:S(2)}) %collective-permute-start.70) | collective-permute-done | bytes 524320 | tf_op jit(solution)/shard_map/ppermute | solution.py:151
  339.3 2.8 collective-permute-done.75.refs_6_.refs_5_
  343.2 2.1 shard_map.78.refs_12_
  345.9 3.5 collective-permute-done.77.refs_5_
  349.4 15.3 %collective-permute-done.73.refs_4_ = bf16[32,8192]{1,0:T(8,128)(2,1)S(1)} collective-permute-done((bf16[32,8192]{1,0:T(8,128)(2,1)S(1)}, bf16[32,8192]{1,0:T(8,128)(2,1)S(1)}, u32[]{:S(2)}, u32[]{:S(2)}) %collective-permute-start.73) | collective-permute-done | bytes 524320 | tf_op jit(solution)/shard_map/ppermute | solution.py:151
  367.4 3.9 shard_map.79.refs_0_
  372.1 4.4 collective-permute-start.87
  376.6 8.8 %collective-permute-done.83.refs_1_ = bf16[32,8192]{1,0:T(8,128)(2,1)S(1)} collective-permute-done((bf16[32,8192]{1,0:T(8,128)(2,1)S(1)}, bf16[32,8192]{1,0:T(8,128)(2,1)S(1)}, u32[]{:S(2)}, u32[]{:S(2)}) %collective-permute-start.83) | collective-permute-done | bytes 524320 | tf_op jit(solution)/shard_map/ppermute | solution.py:151
  387.4 2.1 shard_map.80.refs_12_
  390.1 7.4 %collective-permute-done.87.refs_5_ = bf16[32,8192]{1,0:T(8,128)(2,1)S(1)} collective-permute-done((bf16[32,8192]{1,0:T(8,128)(2,1)S(1)}, bf16[32,8192]{1,0:T(8,128)(2,1)S(1)}, u32[]{:S(2)}, u32[]{:S(2)}) %collective-permute-start.87) | collective-permute-done | bytes 524320 | tf_op jit(solution)/shard_map/ppermute | solution.py:151
  398.0 14.5 %collective-permute-done.86.refs_4_ = bf16[32,8192]{1,0:T(8,128)(2,1)S(1)} collective-permute-done((bf16[32,8192]{1,0:T(8,128)(2,1)S(1)}, bf16[32,8192]{1,0:T(8,128)(2,1)S(1)}, u32[]{:S(2)}, u32[]{:S(2)}) %collective-permute-start.86) | collective-permute-done | bytes 524320 | tf_op jit(solution)/shard_map/ppermute | solution.py:151
  415.2 3.9 shard_map.81.refs_0_
  419.9 4.5 collective-permute-start.98
  424.4 8.8 %collective-permute-done.94.refs_1_ = bf16[32,8192]{1,0:T(8,128)(2,1)S(1)} collective-permute-done((bf16[32,8192]{1,0:T(8,128)(2,1)S(1)}, bf16[32,8192]{1,0:T(8,128)(2,1)S(1)}, u32[]{:S(2)}, u32[]{:S(2)}) %collective-permute-start.94) | collective-permute-done | bytes 524320 | tf_op jit(solution)/shard_map/ppermute | solution.py:151
  435.3 2.1 shard_map.82.refs_12_
  437.9 7.4 %collective-permute-done.98.refs_5_ = bf16[32,8192]{1,0:T(8,128)(2,1)S(1)} collective-permute-done((bf16[32,8192]{1,0:T(8,128)(2,1)S(1)}, bf16[32,8192]{1,0:T(8,128)(2,1)S(1)}, u32[]{:S(2)}, u32[]{:S(2)}) %collective-permute-start.98) | collective-permute-done | bytes 524320 | tf_op jit(solution)/shard_map/ppermute | solution.py:151
  445.8 14.6 %collective-permute-done.97.refs_4_ = bf16[32,8192]{1,0:T(8,128)(2,1)S(1)} collective-permute-done((bf16[32,8192]{1,0:T(8,128)(2,1)S(1)}, bf16[32,8192]{1,0:T(8,128)(2,1)S(1)}, u32[]{:S(2)}, u32[]{:S(2)}) %collective-permute-start.97) | collective-permute-done | bytes 524320 | tf_op jit(solution)/shard_map/ppermute | solution.py:151
  463.0 4.7 %shard_map.83 = bf16[32,8192]{1,0:T(8,128)(2,1)} custom-call(s32[512]{0:T(512)S(1)} %bitcast.25, s32[2]{0:T(128)S(1)} %pad_add_fusion.place, bf16[32,8192]{1,0:T(8,128)(2,1)S(1)} %shard_map.81.refs_0_, bf16[32,8192]{1,0:T(8,128)(2,1)S(1)} %collective-permute-done.94.refs_1_, bf16[32,8192]{1,0:T(8,128)(2,1)S(1)} %collective-permute-done.95.refs_2_, ...), custom_call_target="tpu_custom_call" | custom-call | tf_op jit(solution)/shard_map/pallas_call | solution.py:134
  (197 shorter events, 90.2 us)
Async XLA Ops:
  11.0 25.1 %collective-permute-start.6 = (bf16[32,64,256]{2,1,0:T(8,128)(2,1)}, bf16[32,64,256]{2,1,0:T(8,128)(2,1)S(1)}, u32[]{:S(2)}, u32[]{:S(2)}) collective-permute-start(bf16[32,64,256]{2,1,0:T(8,128)(2,1)} %get-tuple-element.101), channel_id=1, source_target_pairs={{0,8},{8,0},{16,24},{24,16},{1,9},{9,1},{17,25},{25,17},{2,10},{10... | collective-permute-start | bytes 3145736 | tf_op jit(solution)/shard_map/ppermute | solution.py:335
  12.9 24.4 %collective-permute-start.7 = (bf16[32,64,256]{2,1,0:T(8,128)(2,1)}, bf16[32,64,256]{2,1,0:T(8,128)(2,1)S(1)}, u32[]{:S(2)}, u32[]{:S(2)}) collective-permute-start(bf16[32,64,256]{2,1,0:T(8,128)(2,1)} %copy-done.1), channel_id=1, source_target_pairs={{0,16},{8,24},{16,0},{24,8},{1,17},{9,25},{17,1},{25,9},{2,18},{10... | collective-permute-start | bytes 3145736 | tf_op jit(solution)/shard_map/ppermute | solution.py:335
  14.7 25.3 %collective-permute-start.3 = (bf16[32,8192]{1,0:T(8,128)(2,1)S(1)}, bf16[32,8192]{1,0:T(8,128)(2,1)S(1)}, u32[]{:S(2)}, u32[]{:S(2)}) collective-permute-start(bf16[32,8192]{1,0:T(8,128)(2,1)S(1)} %copy-done), channel_id=1, source_target_pairs={{0,2},{1,3},{2,0},{3,1},{4,6},{5,7},{6,4},{7,5},{8,10},{9,11},{10,... | collective-permute-start | bytes 1572872 | tf_op jit(solution)/shard_map/ppermute | solution.py:151
  16.3 26.1 %collective-permute-start.4 = (bf16[32,8192]{1,0:T(8,128)(2,1)S(1)}, bf16[32,8192]{1,0:T(8,128)(2,1)S(1)}, u32[]{:S(2)}, u32[]{:S(2)}) collective-permute-start(bf16[32,8192]{1,0:T(8,128)(2,1)S(1)} %copy-done), channel_id=1, source_target_pairs={{2,4},{3,5},{4,2},{5,3},{0,6},{1,7},{6,0},{7,1},{10,12},{11,13},{1... | collective-permute-start | bytes 1572872 | tf_op jit(solution)/shard_map/ppermute | solution.py:151
  38.1 23.3 %collective-permute-start.12 = (bf16[32,64,256]{2,1,0:T(8,128)(2,1)S(1)}, bf16[32,64,256]{2,1,0:T(8,128)(2,1)S(1)}, u32[]{:S(2)}, u32[]{:S(2)}) collective-permute-start(bf16[32,64,256]{2,1,0:T(8,128)(2,1)S(1)} %get-tuple-element.108), channel_id=1, source_target_pairs={{0,8},{8,0},{16,24},{24,16},{1,9},{9,1},{17,25},{25,17},{2,10},{10... | collective-permute-start | bytes 3145736 | tf_op jit(solution)/shard_map/ppermute | solution.py:335
  38.5 23.2 %collective-permute-start.13 = (bf16[32,64,256]{2,1,0:T(8,128)(2,1)S(1)}, bf16[32,64,256]{2,1,0:T(8,128)(2,1)S(1)}, u32[]{:S(2)}, u32[]{:S(2)}) collective-permute-start(bf16[32,64,256]{2,1,0:T(8,128)(2,1)S(1)} %get-tuple-element.109), channel_id=1, source_target_pairs={{0,16},{8,24},{16,0},{24,8},{1,17},{9,25},{17,1},{25,9},{2,18},{10... | collective-permute-start | bytes 3145736 | tf_op jit(solution)/shard_map/ppermute | solution.py:335
  62.5 22.4 %collective-permute-start.16 = (bf16[32,64,256]{2,1,0:T(8,128)(2,1)S(1)}, bf16[32,64,256]{2,1,0:T(8,128)(2,1)S(1)}, u32[]{:S(2)}, u32[]{:S(2)}) collective-permute-start(bf16[32,64,256]{2,1,0:T(8,128)(2,1)S(1)} %get-tuple-element.114), channel_id=1, source_target_pairs={{0,8},{8,0},{16,24},{24,16},{1,9},{9,1},{17,25},{25,17},{2,10},{10... | collective-permute-start | bytes 3145736 | tf_op jit(solution)/shard_map/ppermute | solution.py:335
  63.9 21.8 %collective-permute-start.17 = (bf16[32,64,256]{2,1,0:T(8,128)(2,1)S(1)}, bf16[32,64,256]{2,1,0:T(8,128)(2,1)S(1)}, u32[]{:S(2)}, u32[]{:S(2)}) collective-permute-start(bf16[32,64,256]{2,1,0:T(8,128)(2,1)S(1)} %get-tuple-element.115), channel_id=1, source_target_pairs={{0,16},{8,24},{16,0},{24,8},{1,17},{9,25},{17,1},{25,9},{2,18},{10... | collective-permute-start | bytes 3145736 | tf_op jit(solution)/shard_map/ppermute | solution.py:335
  86.4 21.7 %collective-permute-start.18 = (bf16[32,64,256]{2,1,0:T(8,128)(2,1)S(1)}, bf16[32,64,256]{2,1,0:T(8,128)(2,1)S(1)}, u32[]{:S(2)}, u32[]{:S(2)}) collective-permute-start(bf16[32,64,256]{2,1,0:T(8,128)(2,1)S(1)} %get-tuple-element.120), channel_id=1, source_target_pairs={{0,8},{8,0},{16,24},{24,16},{1,9},{9,1},{17,25},{25,17},{2,10},{10... | collective-permute-start | bytes 3145736 | tf_op jit(solution)/shard_map/ppermute | solution.py:335
  87.4 21.6 %collective-permute-start.19 = (bf16[32,64,256]{2,1,0:T(8,128)(2,1)S(1)}, bf16[32,64,256]{2,1,0:T(8,128)(2,1)S(1)}, u32[]{:S(2)}, u32[]{:S(2)}) collective-permute-start(bf16[32,64,256]{2,1,0:T(8,128)(2,1)S(1)} %get-tuple-element.121), channel_id=1, source_target_pairs={{0,16},{8,24},{16,0},{24,8},{1,17},{9,25},{17,1},{25,9},{2,18},{10... | collective-permute-start | bytes 3145736 | tf_op jit(solution)/shard_map/ppermute | solution.py:335
  109.7 21.6 %collective-permute-start.23 = (bf16[32,64,256]{2,1,0:T(8,128)(2,1)S(1)}, bf16[32,64,256]{2,1,0:T(8,128)(2,1)S(1)}, u32[]{:S(2)}, u32[]{:S(2)}) collective-permute-start(bf16[32,64,256]{2,1,0:T(8,128)(2,1)S(1)} %get-tuple-element.124), channel_id=1, source_target_pairs={{0,8},{8,0},{16,24},{24,16},{1,9},{9,1},{17,25},{25,17},{2,10},{10... | collective-permute-start | bytes 3145736 | tf_op jit(solution)/shard_map/ppermute | solution.py:335
  110.7 22.2 %collective-permute-start.24 = (bf16[32,64,256]{2,1,0:T(8,128)(2,1)S(1)}, bf16[32,64,256]{2,1,0:T(8,128)(2,1)S(1)}, u32[]{:S(2)}, u32[]{:S(2)}) collective-permute-start(bf16[32,64,256]{2,1,0:T(8,128)(2,1)S(1)} %get-tuple-element.125), channel_id=1, source_target_pairs={{0,16},{8,24},{16,0},{24,8},{1,17},{9,25},{17,1},{25,9},{2,18},{10... | collective-permute-start | bytes 3145736 | tf_op jit(solution)/shard_map/ppermute | solution.py:335
  118.5 17.2 %collective-permute-start.20 = (bf16[32,8192]{1,0:T(8,128)(2,1)S(1)}, bf16[32,8192]{1,0:T(8,128)(2,1)S(1)}, u32[]{:S(2)}, u32[]{:S(2)}) collective-permute-start(bf16[32,8192]{1,0:T(8,128)(2,1)S(1)} %shard_map.61.refs_0_), channel_id=1, source_target_pairs={{0,2},{1,3},{2,0},{3,1},{4,6},{5,7},{6,4},{7,5},{8,10},{9,11},{10,... | collective-permute-start | bytes 1572872 | tf_op jit(solution)/shard_map/ppermute | solution.py:151
  119.9 26.1 %collective-permute-start.21 = (bf16[32,8192]{1,0:T(8,128)(2,1)S(1)}, bf16[32,8192]{1,0:T(8,128)(2,1)S(1)}, u32[]{:S(2)}, u32[]{:S(2)}) collective-permute-start(bf16[32,8192]{1,0:T(8,128)(2,1)S(1)} %shard_map.61.refs_0_), channel_id=1, source_target_pairs={{2,4},{3,5},{4,2},{5,3},{0,6},{1,7},{6,0},{7,1},{10,12},{11,13},{1... | collective-permute-start | bytes 1572872 | tf_op jit(solution)/shard_map/ppermute | solution.py:151
  133.6 18.7 %collective-permute-start.29 = (bf16[32,64,256]{2,1,0:T(8,128)(2,1)S(1)}, bf16[32,64,256]{2,1,0:T(8,128)(2,1)S(1)}, u32[]{:S(2)}, u32[]{:S(2)}) collective-permute-start(bf16[32,64,256]{2,1,0:T(8,128)(2,1)S(1)} %get-tuple-element.130), channel_id=1, source_target_pairs={{0,8},{8,0},{16,24},{24,16},{1,9},{9,1},{17,25},{25,17},{2,10},{10... | collective-permute-start | bytes 3145736 | tf_op jit(solution)/shard_map/ppermute | solution.py:335
  134.0 19.2 %collective-permute-start.30 = (bf16[32,64,256]{2,1,0:T(8,128)(2,1)S(1)}, bf16[32,64,256]{2,1,0:T(8,128)(2,1)S(1)}, u32[]{:S(2)}, u32[]{:S(2)}) collective-permute-start(bf16[32,64,256]{2,1,0:T(8,128)(2,1)S(1)} %get-tuple-element.131), channel_id=1, source_target_pairs={{0,16},{8,24},{16,0},{24,8},{1,17},{9,25},{17,1},{25,9},{2,18},{10... | collective-permute-start | bytes 3145736 | tf_op jit(solution)/shard_map/ppermute | solution.py:335
  147.9 15.9 %collective-permute-start.26 = (bf16[32,8192]{1,0:T(8,128)(2,1)S(1)}, bf16[32,8192]{1,0:T(8,128)(2,1)S(1)}, u32[]{:S(2)}, u32[]{:S(2)}) collective-permute-start(bf16[32,8192]{1,0:T(8,128)(2,1)S(1)} %collective-permute-done.21.refs_2_), channel_id=1, source_target_pairs={{4,6},{5,7},{2,0},{3,1},{12,14},{13,15},{10,8},{11,9},{20,22},{21,... | collective-permute-start | bytes 1572872 | tf_op jit(solution)/shard_map/ppermute | solution.py:151
  164.3 25.1 %collective-permute-start.36 = (bf16[32,64,256]{2,1,0:T(8,128)(2,1)S(1)}, bf16[32,64,256]{2,1,0:T(8,128)(2,1)S(1)}, u32[]{:S(2)}, u32[]{:S(2)}) collective-permute-start(bf16[32,64,256]{2,1,0:T(8,128)(2,1)S(1)} %get-tuple-element.137), channel_id=1, source_target_pairs={{0,8},{8,0},{16,24},{24,16},{1,9},{9,1},{17,25},{25,17},{2,10},{10... | collective-permute-start | bytes 3145736 | tf_op jit(solution)/shard_map/ppermute | solution.py:335
  166.0 24.8 %collective-permute-start.37 = (bf16[32,64,256]{2,1,0:T(8,128)(2,1)S(1)}, bf16[32,64,256]{2,1,0:T(8,128)(2,1)S(1)}, u32[]{:S(2)}, u32[]{:S(2)}) collective-permute-start(bf16[32,64,256]{2,1,0:T(8,128)(2,1)S(1)} %get-tuple-element.138), channel_id=1, source_target_pairs={{0,16},{8,24},{16,0},{24,8},{1,17},{9,25},{17,1},{25,9},{2,18},{10... | collective-permute-start | bytes 3145736 | tf_op jit(solution)/shard_map/ppermute | solution.py:335
  170.6 25.5 %collective-permute-start.33 = (bf16[32,8192]{1,0:T(8,128)(2,1)S(1)}, bf16[32,8192]{1,0:T(8,128)(2,1)S(1)}, u32[]{:S(2)}, u32[]{:S(2)}) collective-permute-start(bf16[32,8192]{1,0:T(8,128)(2,1)S(1)} %shard_map.66.refs_0_), channel_id=1, source_target_pairs={{0,2},{1,3},{2,0},{3,1},{4,6},{5,7},{6,4},{7,5},{8,10},{9,11},{10,... | collective-permute-start | bytes 1572872 | tf_op jit(solution)/shard_map/ppermute | solution.py:151
  170.6 25.5 %collective-permute-start.34 = (bf16[32,8192]{1,0:T(8,128)(2,1)S(1)}, bf16[32,8192]{1,0:T(8,128)(2,1)S(1)}, u32[]{:S(2)}, u32[]{:S(2)}) collective-permute-start(bf16[32,8192]{1,0:T(8,128)(2,1)S(1)} %shard_map.66.refs_0_), channel_id=1, source_target_pairs={{2,4},{3,5},{4,2},{5,3},{0,6},{1,7},{6,0},{7,1},{10,12},{11,13},{1... | collective-permute-start | bytes 1572872 | tf_op jit(solution)/shard_map/ppermute | solution.py:151
  196.8 15.7 %collective-permute-start.39 = (bf16[32,8192]{1,0:T(8,128)(2,1)S(1)}, bf16[32,8192]{1,0:T(8,128)(2,1)S(1)}, u32[]{:S(2)}, u32[]{:S(2)}) collective-permute-start(bf16[32,8192]{1,0:T(8,128)(2,1)S(1)} %collective-permute-done.34.refs_2_), channel_id=1, source_target_pairs={{4,6},{5,7},{2,0},{3,1},{12,14},{13,15},{10,8},{11,9},{20,22},{21,... | collective-permute-start | bytes 1572872 | tf_op jit(solution)/shard_map/ppermute | solution.py:151
  198.1 14.4 %collective-permute-start.40 = (bf16[32,8192]{1,0:T(8,128)(2,1)S(1)}, bf16[32,8192]{1,0:T(8,128)(2,1)S(1)}, u32[]{:S(2)}, u32[]{:S(2)}) collective-permute-start(bf16[32,8192]{1,0:T(8,128)(2,1)S(1)} %collective-permute-done.33.refs_1_), channel_id=1, source_target_pairs={{0,1},{1,0},{2,3},{3,2},{4,5},{5,4},{6,7},{7,6},{8,9},{9,8},{10,11... | collective-permute-start | bytes 1572872 | tf_op jit(solution)/shard_map/ppermute | solution.py:155
  200.9 25.1 %collective-permute-start.47 = (bf16[32,64,256]{2,1,0:T(8,128)(2,1)S(1)}, bf16[32,64,256]{2,1,0:T(8,128)(2,1)S(1)}, u32[]{:S(2)}, u32[]{:S(2)}) collective-permute-start(bf16[32,64,256]{2,1,0:T(8,128)(2,1)S(1)} %get-tuple-element.148), channel_id=1, source_target_pairs={{0,8},{8,0},{16,24},{24,16},{1,9},{9,1},{17,25},{25,17},{2,10},{10... | collective-permute-start | bytes 3145736 | tf_op jit(solution)/shard_map/ppermute | solution.py:335
  202.4 24.9 %collective-permute-start.48 = (bf16[32,64,256]{2,1,0:T(8,128)(2,1)S(1)}, bf16[32,64,256]{2,1,0:T(8,128)(2,1)S(1)}, u32[]{:S(2)}, u32[]{:S(2)}) collective-permute-start(bf16[32,64,256]{2,1,0:T(8,128)(2,1)S(1)} %get-tuple-element.149), channel_id=1, source_target_pairs={{0,16},{8,24},{16,0},{24,8},{1,17},{9,25},{17,1},{25,9},{2,18},{10... | collective-permute-start | bytes 3145736 | tf_op jit(solution)/shard_map/ppermute | solution.py:335
  219.3 14.4 %collective-permute-start.44 = (bf16[32,8192]{1,0:T(8,128)(2,1)S(1)}, bf16[32,8192]{1,0:T(8,128)(2,1)S(1)}, u32[]{:S(2)}, u32[]{:S(2)}) collective-permute-start(bf16[32,8192]{1,0:T(8,128)(2,1)S(1)} %shard_map.69.refs_0_), channel_id=1, source_target_pairs={{0,2},{1,3},{2,0},{3,1},{4,6},{5,7},{6,4},{7,5},{8,10},{9,11},{10,... | collective-permute-start | bytes 1572872 | tf_op jit(solution)/shard_map/ppermute | solution.py:151
  221.2 24.7 %collective-permute-start.45 = (bf16[32,8192]{1,0:T(8,128)(2,1)S(1)}, bf16[32,8192]{1,0:T(8,128)(2,1)S(1)}, u32[]{:S(2)}, u32[]{:S(2)}) collective-permute-start(bf16[32,8192]{1,0:T(8,128)(2,1)S(1)} %shard_map.69.refs_0_), channel_id=1, source_target_pairs={{2,4},{3,5},{4,2},{5,3},{0,6},{1,7},{6,0},{7,1},{10,12},{11,13},{1... | collective-permute-start | bytes 1572872 | tf_op jit(solution)/shard_map/ppermute | solution.py:151
  228.0 24.0 %collective-permute-start.53 = (bf16[32,64,256]{2,1,0:T(8,128)(2,1)S(1)}, bf16[32,64,256]{2,1,0:T(8,128)(2,1)S(1)}, u32[]{:S(2)}, u32[]{:S(2)}) collective-permute-start(bf16[32,64,256]{2,1,0:T(8,128)(2,1)S(1)} %get-tuple-element.157), channel_id=1, source_target_pairs={{0,8},{8,0},{16,24},{24,16},{1,9},{9,1},{17,25},{25,17},{2,10},{10... | collective-permute-start | bytes 3145736 | tf_op jit(solution)/shard_map/ppermute | solution.py:335
  228.6 23.9 %collective-permute-start.54 = (bf16[32,64,256]{2,1,0:T(8,128)(2,1)S(1)}, bf16[32,64,256]{2,1,0:T(8,128)(2,1)S(1)}, u32[]{:S(2)}, u32[]{:S(2)}) collective-permute-start(bf16[32,64,256]{2,1,0:T(8,128)(2,1)S(1)} %get-tuple-element.158), channel_id=1, source_target_pairs={{0,16},{8,24},{16,0},{24,8},{1,17},{9,25},{17,1},{25,9},{2,18},{10... | collective-permute-start | bytes 3145736 | tf_op jit(solution)/shard_map/ppermute | solution.py:335
  247.8 15.8 %collective-permute-start.50 = (bf16[32,8192]{1,0:T(8,128)(2,1)S(1)}, bf16[32,8192]{1,0:T(8,128)(2,1)S(1)}, u32[]{:S(2)}, u32[]{:S(2)}) collective-permute-start(bf16[32,8192]{1,0:T(8,128)(2,1)S(1)} %collective-permute-done.45.refs_2_), channel_id=1, source_target_pairs={{4,6},{5,7},{2,0},{3,1},{12,14},{13,15},{10,8},{11,9},{20,22},{21,... | collective-permute-start | bytes 1572872 | tf_op jit(solution)/shard_map/ppermute | solution.py:151
  264.1 25.1 %collective-permute-start.60 = (bf16[32,64,256]{2,1,0:T(8,128)(2,1)S(1)}, bf16[32,64,256]{2,1,0:T(8,128)(2,1)S(1)}, u32[]{:S(2)}, u32[]{:S(2)}) collective-permute-start(bf16[32,64,256]{2,1,0:T(8,128)(2,1)S(1)} %get-tuple-element.166), channel_id=1, source_target_pairs={{0,8},{8,0},{16,24},{24,16},{1,9},{9,1},{17,25},{25,17},{2,10},{10... | collective-permute-start | bytes 3145736 | tf_op jit(solution)/shard_map/ppermute | solution.py:335
  265.7 24.8 %collective-permute-start.61 = (bf16[32,64,256]{2,1,0:T(8,128)(2,1)S(1)}, bf16[32,64,256]{2,1,0:T(8,128)(2,1)S(1)}, u32[]{:S(2)}, u32[]{:S(2)}) collective-permute-start(bf16[32,64,256]{2,1,0:T(8,128)(2,1)S(1)} %get-tuple-element.167), channel_id=1, source_target_pairs={{0,16},{8,24},{16,0},{24,8},{1,17},{9,25},{17,1},{25,9},{2,18},{10... | collective-permute-start | bytes 3145736 | tf_op jit(solution)/shard_map/ppermute | solution.py:335
  270.2 20.3 %collective-permute-start.59 = (bf16[32,8192]{1,0:T(8,128)(2,1)S(1)}, bf16[32,8192]{1,0:T(8,128)(2,1)S(1)}, u32[]{:S(2)}, u32[]{:S(2)}) collective-permute-start(bf16[32,8192]{1,0:T(8,128)(2,1)S(1)} %shard_map.73.refs_0_), channel_id=1, source_target_pairs={{0,1},{1,0},{2,3},{3,2},{4,5},{5,4},{6,7},{7,6},{8,9},{9,8},{10,11... | collective-permute-start | bytes 1572872 | tf_op jit(solution)/shard_map/ppermute | solution.py:155
  270.4 22.9 %collective-permute-start.57 = (bf16[32,8192]{1,0:T(8,128)(2,1)S(1)}, bf16[32,8192]{1,0:T(8,128)(2,1)S(1)}, u32[]{:S(2)}, u32[]{:S(2)}) collective-permute-start(bf16[32,8192]{1,0:T(8,128)(2,1)S(1)} %shard_map.73.refs_0_), channel_id=1, source_target_pairs={{0,2},{1,3},{2,0},{3,1},{4,6},{5,7},{6,4},{7,5},{8,10},{9,11},{10,... | collective-permute-start | bytes 1572872 | tf_op jit(solution)/shard_map/ppermute | solution.py:151
  270.5 26.3 %collective-permute-start.58 = (bf16[32,8192]{1,0:T(8,128)(2,1)S(1)}, bf16[32,8192]{1,0:T(8,128)(2,1)S(1)}, u32[]{:S(2)}, u32[]{:S(2)}) collective-permute-start(bf16[32,8192]{1,0:T(8,128)(2,1)S(1)} %shard_map.73.refs_0_), channel_id=1, source_target_pairs={{2,4},{3,5},{4,2},{5,3},{0,6},{1,7},{6,0},{7,1},{10,12},{11,13},{1... | collective-permute-start | bytes 1572872 | tf_op jit(solution)/shard_map/ppermute | solution.py:151
  291.2 24.0 %collective-permute-start.66 = (bf16[32,64,256]{2,1,0:T(8,128)(2,1)S(1)}, bf16[32,64,256]{2,1,0:T(8,128)(2,1)S(1)}, u32[]{:S(2)}, u32[]{:S(2)}) collective-permute-start(bf16[32,64,256]{2,1,0:T(8,128)(2,1)S(1)} %get-tuple-element.176), channel_id=1, source_target_pairs={{0,8},{8,0},{16,24},{24,16},{1,9},{9,1},{17,25},{25,17},{2,10},{10... | collective-permute-start | bytes 3145736 | tf_op jit(solution)/shard_map/ppermute | solution.py:335
  291.8 23.7 %collective-permute-start.67 = (bf16[32,64,256]{2,1,0:T(8,128)(2,1)S(1)}, bf16[32,64,256]{2,1,0:T(8,128)(2,1)S(1)}, u32[]{:S(2)}, u32[]{:S(2)}) collective-permute-start(bf16[32,64,256]{2,1,0:T(8,128)(2,1)S(1)} %get-tuple-element.177), channel_id=1, source_target_pairs={{0,16},{8,24},{16,0},{24,8},{1,17},{9,25},{17,1},{25,9},{2,18},{10... | collective-permute-start | bytes 3145736 | tf_op jit(solution)/shard_map/ppermute | solution.py:335
  297.3 18.9 %collective-permute-start.62 = (bf16[32,8192]{1,0:T(8,128)(2,1)S(1)}, bf16[32,8192]{1,0:T(8,128)(2,1)S(1)}, u32[]{:S(2)}, u32[]{:S(2)}) collective-permute-start(bf16[32,8192]{1,0:T(8,128)(2,1)S(1)} %collective-permute-done.57.refs_1_), channel_id=1, source_target_pairs={{2,4},{3,5},{4,2},{5,3},{10,12},{11,13},{12,10},{13,11},{18,20},{1... | collective-permute-start | bytes 1572872 | tf_op jit(solution)/shard_map/ppermute | solution.py:151
  298.7 17.5 %collective-permute-start.63 = (bf16[32,8192]{1,0:T(8,128)(2,1)S(1)}, bf16[32,8192]{1,0:T(8,128)(2,1)S(1)}, u32[]{:S(2)}, u32[]{:S(2)}) collective-permute-start(bf16[32,8192]{1,0:T(8,128)(2,1)S(1)} %collective-permute-done.58.refs_2_), channel_id=1, source_target_pairs={{4,6},{5,7},{2,0},{3,1},{12,14},{13,15},{10,8},{11,9},{20,22},{21,... | collective-permute-start | bytes 1572872 | tf_op jit(solution)/shard_map/ppermute | solution.py:151
  316.9 25.2 %collective-permute-start.75 = (bf16[32,64,256]{2,1,0:T(8,128)(2,1)S(1)}, bf16[32,64,256]{2,1,0:T(8,128)(2,1)S(1)}, u32[]{:S(2)}, u32[]{:S(2)}) collective-permute-start(bf16[32,64,256]{2,1,0:T(8,128)(2,1)S(1)} %get-tuple-element.183), channel_id=1, source_target_pairs={{0,8},{8,0},{16,24},{24,16},{1,9},{9,1},{17,25},{25,17},{2,10},{10... | collective-permute-start | bytes 3145736 | tf_op jit(solution)/shard_map/ppermute | solution.py:335
  318.4 24.9 %collective-permute-start.76 = (bf16[32,64,256]{2,1,0:T(8,128)(2,1)S(1)}, bf16[32,64,256]{2,1,0:T(8,128)(2,1)S(1)}, u32[]{:S(2)}, u32[]{:S(2)}) collective-permute-start(bf16[32,64,256]{2,1,0:T(8,128)(2,1)S(1)} %get-tuple-element.184), channel_id=1, source_target_pairs={{0,16},{8,24},{16,0},{24,8},{1,17},{9,25},{17,1},{25,9},{2,18},{10... | collective-permute-start | bytes 3145736 | tf_op jit(solution)/shard_map/ppermute | solution.py:335
  323.1 14.2 %collective-permute-start.70 = (bf16[32,8192]{1,0:T(8,128)(2,1)S(1)}, bf16[32,8192]{1,0:T(8,128)(2,1)S(1)}, u32[]{:S(2)}, u32[]{:S(2)}) collective-permute-start(bf16[32,8192]{1,0:T(8,128)(2,1)S(1)} %shard_map.77.refs_0_), channel_id=1, source_target_pairs={{0,2},{1,3},{2,0},{3,1},{4,6},{5,7},{6,4},{7,5},{8,10},{9,11},{10,... | collective-permute-start | bytes 1572872 | tf_op jit(solution)/shard_map/ppermute | solution.py:151
  323.3 14.6 %collective-permute-start.71 = (bf16[32,8192]{1,0:T(8,128)(2,1)S(1)}, bf16[32,8192]{1,0:T(8,128)(2,1)S(1)}, u32[]{:S(2)}, u32[]{:S(2)}) collective-permute-start(bf16[32,8192]{1,0:T(8,128)(2,1)S(1)} %shard_map.77.refs_0_), channel_id=1, source_target_pairs={{2,4},{3,5},{4,2},{5,3},{10,12},{11,13},{12,10},{13,11},{18,20},{1... | collective-permute-start | bytes 1572872 | tf_op jit(solution)/shard_map/ppermute | solution.py:151
  324.8 24.6 %collective-permute-start.77 = (bf16[32,8192]{1,0:T(8,128)(2,1)S(1)}, bf16[32,8192]{1,0:T(8,128)(2,1)S(1)}, u32[]{:S(2)}, u32[]{:S(2)}) collective-permute-start(bf16[32,8192]{1,0:T(8,128)(2,1)S(1)} %shard_map.77.refs_0_), channel_id=1, source_target_pairs={{0,6},{1,7},{6,0},{7,1},{8,14},{9,15},{14,8},{15,9},{16,22},{17,23... | collective-permute-start | bytes 1572872 | tf_op jit(solution)/shard_map/ppermute | solution.py:151
  338.0 26.8 %collective-permute-start.73 = (bf16[32,8192]{1,0:T(8,128)(2,1)S(1)}, bf16[32,8192]{1,0:T(8,128)(2,1)S(1)}, u32[]{:S(2)}, u32[]{:S(2)}) collective-permute-start(bf16[32,8192]{1,0:T(8,128)(2,1)S(1)} %collective-permute-done.71.refs_2_), channel_id=1, source_target_pairs={{4,6},{5,7},{2,0},{3,1},{12,14},{13,15},{10,8},{11,9},{20,22},{21,... | collective-permute-start | bytes 1572872 | tf_op jit(solution)/shard_map/ppermute | solution.py:151
  345.3 19.9 %collective-permute-start.78 = (bf16[32,8192]{1,0:T(8,128)(2,1)S(1)}, bf16[32,8192]{1,0:T(8,128)(2,1)S(1)}, u32[]{:S(2)}, u32[]{:S(2)}) collective-permute-start(bf16[32,8192]{1,0:T(8,128)(2,1)S(1)} %collective-permute-done.70.refs_1_), channel_id=1, source_target_pairs={{0,1},{1,0},{2,3},{3,2},{4,5},{5,4},{6,7},{7,6},{8,9},{9,8},{10,11... | collective-permute-start | bytes 1572872 | tf_op jit(solution)/shard_map/ppermute | solution.py:155
  345.4 19.8 %collective-permute-start.79 = (bf16[32,8192]{1,0:T(8,128)(2,1)S(1)}, bf16[32,8192]{1,0:T(8,128)(2,1)S(1)}, u32[]{:S(2)}, u32[]{:S(2)}) collective-permute-start(bf16[32,8192]{1,0:T(8,128)(2,1)S(1)} %collective-permute-done.71.refs_2_), channel_id=1, source_target_pairs={{0,1},{1,0},{2,3},{3,2},{4,5},{5,4},{6,7},{7,6},{8,9},{9,8},{10,11... | collective-permute-start | bytes 1572872 | tf_op jit(solution)/shard_map/ppermute | solution.py:155
  349.4 15.8 %collective-permute-start.82 = (bf16[32,8192]{1,0:T(8,128)(2,1)S(1)}, bf16[32,8192]{1,0:T(8,128)(2,1)S(1)}, u32[]{:S(2)}, u32[]{:S(2)}) collective-permute-start(bf16[32,8192]{1,0:T(8,128)(2,1)S(1)} %collective-permute-done.77.refs_5_), channel_id=1, source_target_pairs={{0,1},{1,0},{2,3},{3,2},{4,5},{5,4},{6,7},{7,6},{8,9},{9,8},{10,11... | collective-permute-start | bytes 1572872 | tf_op jit(solution)/shard_map/ppermute | solution.py:155
  371.3 14.0 %collective-permute-start.83 = (bf16[32,8192]{1,0:T(8,128)(2,1)S(1)}, bf16[32,8192]{1,0:T(8,128)(2,1)S(1)}, u32[]{:S(2)}, u32[]{:S(2)}) collective-permute-start(bf16[32,8192]{1,0:T(8,128)(2,1)S(1)} %shard_map.79.refs_0_), channel_id=1, source_target_pairs={{0,2},{1,3},{2,0},{3,1},{4,6},{5,7},{6,4},{7,5},{8,10},{9,11},{10,... | collective-permute-start | bytes 1572872 | tf_op jit(solution)/shard_map/ppermute | solution.py:151
  371.4 14.6 %collective-permute-start.84 = (bf16[32,8192]{1,0:T(8,128)(2,1)S(1)}, bf16[32,8192]{1,0:T(8,128)(2,1)S(1)}, u32[]{:S(2)}, u32[]{:S(2)}) collective-permute-start(bf16[32,8192]{1,0:T(8,128)(2,1)S(1)} %shard_map.79.refs_0_), channel_id=1, source_target_pairs={{2,4},{3,5},{4,2},{5,3},{10,12},{11,13},{12,10},{13,11},{18,20},{1... | collective-permute-start | bytes 1572872 | tf_op jit(solution)/shard_map/ppermute | solution.py:151
  372.1 25.4 %collective-permute-start.87 = (bf16[32,8192]{1,0:T(8,128)(2,1)S(1)}, bf16[32,8192]{1,0:T(8,128)(2,1)S(1)}, u32[]{:S(2)}, u32[]{:S(2)}) collective-permute-start(bf16[32,8192]{1,0:T(8,128)(2,1)S(1)} %shard_map.79.refs_0_), channel_id=1, source_target_pairs={{0,6},{1,7},{6,0},{7,1},{8,14},{9,15},{14,8},{15,9},{16,22},{17,23... | collective-permute-start | bytes 1572872 | tf_op jit(solution)/shard_map/ppermute | solution.py:151
  386.1 26.5 %collective-permute-start.86 = (bf16[32,8192]{1,0:T(8,128)(2,1)S(1)}, bf16[32,8192]{1,0:T(8,128)(2,1)S(1)}, u32[]{:S(2)}, u32[]{:S(2)}) collective-permute-start(bf16[32,8192]{1,0:T(8,128)(2,1)S(1)} %collective-permute-done.84.refs_2_), channel_id=1, source_target_pairs={{4,6},{5,7},{2,0},{3,1},{12,14},{13,15},{10,8},{11,9},{20,22},{21,... | collective-permute-start | bytes 1572872 | tf_op jit(solution)/shard_map/ppermute | solution.py:151
  387.4 25.2 %collective-permute-start.88 = (bf16[32,8192]{1,0:T(8,128)(2,1)S(1)}, bf16[32,8192]{1,0:T(8,128)(2,1)S(1)}, u32[]{:S(2)}, u32[]{:S(2)}) collective-permute-start(bf16[32,8192]{1,0:T(8,128)(2,1)S(1)} %shard_map.79.refs_0_), channel_id=1, source_target_pairs={{0,1},{1,0},{2,3},{3,2},{4,5},{5,4},{6,7},{7,6},{8,9},{9,8},{10,11... | collective-permute-start | bytes 1572872 | tf_op jit(solution)/shard_map/ppermute | solution.py:155
  389.5 23.6 %collective-permute-start.89 = (bf16[32,8192]{1,0:T(8,128)(2,1)S(1)}, bf16[32,8192]{1,0:T(8,128)(2,1)S(1)}, u32[]{:S(2)}, u32[]{:S(2)}) collective-permute-start(bf16[32,8192]{1,0:T(8,128)(2,1)S(1)} %collective-permute-done.83.refs_1_), channel_id=1, source_target_pairs={{0,1},{1,0},{2,3},{3,2},{4,5},{5,4},{6,7},{7,6},{8,9},{9,8},{10,11... | collective-permute-start | bytes 1572872 | tf_op jit(solution)/shard_map/ppermute | solution.py:155
  397.5 15.6 %collective-permute-start.90 = (bf16[32,8192]{1,0:T(8,128)(2,1)S(1)}, bf16[32,8192]{1,0:T(8,128)(2,1)S(1)}, u32[]{:S(2)}, u32[]{:S(2)}) collective-permute-start(bf16[32,8192]{1,0:T(8,128)(2,1)S(1)} %collective-permute-done.84.refs_2_), channel_id=1, source_target_pairs={{0,1},{1,0},{2,3},{3,2},{4,5},{5,4},{6,7},{7,6},{8,9},{9,8},{10,11... | collective-permute-start | bytes 1572872 | tf_op jit(solution)/shard_map/ppermute | solution.py:155
  397.5 15.6 %collective-permute-start.93 = (bf16[32,8192]{1,0:T(8,128)(2,1)S(1)}, bf16[32,8192]{1,0:T(8,128)(2,1)S(1)}, u32[]{:S(2)}, u32[]{:S(2)}) collective-permute-start(bf16[32,8192]{1,0:T(8,128)(2,1)S(1)} %collective-permute-done.87.refs_5_), channel_id=1, source_target_pairs={{0,1},{1,0},{2,3},{3,2},{4,5},{5,4},{6,7},{7,6},{8,9},{9,8},{10,11... | collective-permute-start | bytes 1572872 | tf_op jit(solution)/shard_map/ppermute | solution.py:155
  419.1 14.0 %collective-permute-start.94 = (bf16[32,8192]{1,0:T(8,128)(2,1)S(1)}, bf16[32,8192]{1,0:T(8,128)(2,1)S(1)}, u32[]{:S(2)}, u32[]{:S(2)}) collective-permute-start(bf16[32,8192]{1,0:T(8,128)(2,1)S(1)} %shard_map.81.refs_0_), channel_id=1, source_target_pairs={{0,2},{1,3},{2,0},{3,1},{4,6},{5,7},{6,4},{7,5},{8,10},{9,11},{10,... | collective-permute-start | bytes 1572872 | tf_op jit(solution)/shard_map/ppermute | solution.py:151
  419.2 14.6 %collective-permute-start.95 = (bf16[32,8192]{1,0:T(8,128)(2,1)S(1)}, bf16[32,8192]{1,0:T(8,128)(2,1)S(1)}, u32[]{:S(2)}, u32[]{:S(2)}) collective-permute-start(bf16[32,8192]{1,0:T(8,128)(2,1)S(1)} %shard_map.81.refs_0_), channel_id=1, source_target_pairs={{2,4},{3,5},{4,2},{5,3},{10,12},{11,13},{12,10},{13,11},{18,20},{1... | collective-permute-start | bytes 1572872 | tf_op jit(solution)/shard_map/ppermute | solution.py:151
  419.9 25.4 %collective-permute-start.98 = (bf16[32,8192]{1,0:T(8,128)(2,1)S(1)}, bf16[32,8192]{1,0:T(8,128)(2,1)S(1)}, u32[]{:S(2)}, u32[]{:S(2)}) collective-permute-start(bf16[32,8192]{1,0:T(8,128)(2,1)S(1)} %shard_map.81.refs_0_), channel_id=1, source_target_pairs={{0,6},{1,7},{6,0},{7,1},{8,14},{9,15},{14,8},{15,9},{16,22},{17,23... | collective-permute-start | bytes 1572872 | tf_op jit(solution)/shard_map/ppermute | solution.py:151
  433.9 26.5 %collective-permute-start.97 = (bf16[32,8192]{1,0:T(8,128)(2,1)S(1)}, bf16[32,8192]{1,0:T(8,128)(2,1)S(1)}, u32[]{:S(2)}, u32[]{:S(2)}) collective-permute-start(bf16[32,8192]{1,0:T(8,128)(2,1)S(1)} %collective-permute-done.95.refs_2_), channel_id=1, source_target_pairs={{4,6},{5,7},{2,0},{3,1},{12,14},{13,15},{10,8},{11,9},{20,22},{21,... | collective-permute-start | bytes 1572872 | tf_op jit(solution)/shard_map/ppermute | solution.py:151
  435.2 25.2 %collective-permute-start.99 = (bf16[32,8192]{1,0:T(8,128)(2,1)S(1)}, bf16[32,8192]{1,0:T(8,128)(2,1)S(1)}, u32[]{:S(2)}, u32[]{:S(2)}) collective-permute-start(bf16[32,8192]{1,0:T(8,128)(2,1)S(1)} %shard_map.81.refs_0_), channel_id=1, source_target_pairs={{0,1},{1,0},{2,3},{3,2},{4,5},{5,4},{6,7},{7,6},{8,9},{9,8},{10,11... | collective-permute-start | bytes 1572872 | tf_op jit(solution)/shard_map/ppermute | solution.py:155
  437.4 23.5 %collective-permute-start.100 = (bf16[32,8192]{1,0:T(8,128)(2,1)S(1)}, bf16[32,8192]{1,0:T(8,128)(2,1)S(1)}, u32[]{:S(2)}, u32[]{:S(2)}) collective-permute-start(bf16[32,8192]{1,0:T(8,128)(2,1)S(1)} %collective-permute-done.94.refs_1_), channel_id=1, source_target_pairs={{0,1},{1,0},{2,3},{3,2},{4,5},{5,4},{6,7},{7,6},{8,9},{9,8},{10,11... | collective-permute-start | bytes 1572872 | tf_op jit(solution)/shard_map/ppermute | solution.py:155
  445.3 15.6 %collective-permute-start.101 = (bf16[32,8192]{1,0:T(8,128)(2,1)S(1)}, bf16[32,8192]{1,0:T(8,128)(2,1)S(1)}, u32[]{:S(2)}, u32[]{:S(2)}) collective-permute-start(bf16[32,8192]{1,0:T(8,128)(2,1)S(1)} %collective-permute-done.95.refs_2_), channel_id=1, source_target_pairs={{0,1},{1,0},{2,3},{3,2},{4,5},{5,4},{6,7},{7,6},{8,9},{9,8},{10,11... | collective-permute-start | bytes 1572872 | tf_op jit(solution)/shard_map/ppermute | solution.py:155
  445.3 15.6 %collective-permute-start.104 = (bf16[32,8192]{1,0:T(8,128)(2,1)S(1)}, bf16[32,8192]{1,0:T(8,128)(2,1)S(1)}, u32[]{:S(2)}, u32[]{:S(2)}) collective-permute-start(bf16[32,8192]{1,0:T(8,128)(2,1)S(1)} %collective-permute-done.98.refs_5_), channel_id=1, source_target_pairs={{0,1},{1,0},{2,3},{3,2},{4,5},{5,4},{6,7},{7,6},{8,9},{9,8},{10,11... | collective-permute-start | bytes 1572872 | tf_op jit(solution)/shard_map/ppermute | solution.py:155
  (44 other events, 231.9 us)

commit v6 on v5

--- a/solution.py
+++ b/solution.py
@@ -169,7 +169,7 @@
     far = along_line(near, inside)
     outer = along_line(cross, [(2, 3), (1, 0)])
     near_swapped, cross_swapped = to_other_core(near), to_other_core(cross)
-    far, outer = pause([near_swapped, cross_swapped], [far, outer])
+    (outer,) = pause([near_swapped], [outer])
     rest = [far, outer] + trade
     swapped = [x_swapped, near_swapped, cross_swapped] + [to_other_core(buf) for buf in rest]
     return [x, near, cross] + rest + swapped

time: 469 us -> 467 us (level)
  waiting for transfers between devices: 308 us -> 297 us
  starting transfers between devices: 91.2 us -> 101 us
    ppermute x35, waiting for transfers between devices: 162 us -> 144 us  [along_line(): return lax.ppermute(x, 'rows', moves)]
    ppermute x35, starting transfers between devices: 48.3 us -> 60.5 us  [along_line(): return lax.ppermute(x, 'rows', moves)]
    ppermute x24, waiting for transfers between devices: 133 us -> 141 us  [advance(): lax.ppermute(array, 'pipe', [(p, p ^ side) for p in range(self.square)])]
  transfers between devices with their start and end apart: 105 -> 105, of which waited for: 59 -> 54; matrix products, arithmetic and copies ran while one was open for 0% -> 0% of each run, Pallas kernels for 10% -> 10%
where the time goes in v6:
time: 467 us
  waiting for transfers between devices  297 us (64%)
  starting transfers between devices  101 us (22%)
  Pallas kernels  63.4 us (14%)
    ppermute x35, waiting for transfers between devices, along_line(): return lax.ppermute(x, 'rows', moves)  144 us
    ppermute x24, waiting for transfers between devices, advance(): lax.ppermute(array, 'pipe', [(p, p ^ side) for p in range(self.square)])  141 us
    ppermute x35, starting transfers between devices, along_line(): return lax.ppermute(x, 'rows', moves)  60.5 us
    pallas_call x8, Pallas kernels, apply_layer(): pl.pallas_call(kernel, out_shape=jax.ShapeDtypeStruct((rows, neurons), jn...  32.1 us
    ppermute x24, starting transfers between devices, advance(): lax.ppermute(array, 'pipe', [(p, p ^ side) for p in range(self.square)])  28.8 us
    pallas_call x8, Pallas kernels, gather_weights(): pl.pallas_call(functools.partial(gather_weights_kernel, plan), out_shape=...  16.8 us
    ppermute x43, waiting for transfers between devices, to_other_core(): lax.ppermute(x, 'rows', [(i, i ^ 1) for i in range(lax.axis_size('rows'))])  11.8 us
    pallas_call x12, Pallas kernels, pick(): pl.pallas_call(functools.partial(pick_kernel, choices, len(choices)), out...  11.1 us
  transfers between devices with their start and end apart: 105, of which 54 were waited for; matrix products, arithmetic and copies ran while one was open for 0% of the time, Pallas kernels for 10%

profile of v6, /device:TPU:0, one launch (start us, length us, event | category | flops | bytes accessed | tf_op | source)
XLA Modules:
  0.0 466.7 jit_solution(11658406746721748638)
XLA Ops:
  0.1 3.1 shard_map.55
  6.4 3.0 collective-permute-start
  11.0 1.9 collective-permute-start.6
  16.3 3.6 collective-permute-start.4
  20.3 3.4 shard_map.56.refs_2_.refs_1_.refs_0_.refs_4_.refs_3_.refs_5_
  23.7 12.3 %collective-permute-done.6.refs_0_.refs_1_.refs_3_.refs_2_ = bf16[32,64,256]{2,1,0:T(8,128)(2,1)S(1)} collective-permute-done((bf16[32,64,256]{2,1,0:T(8,128)(2,1)}, bf16[32,64,256]{2,1,0:T(8,128)(2,1)S(1)}, u32[]{:S(2)}, u32[]{:S(2)}) %collective-permute-start.6) | collective-permute-done | bytes 1048608 | tf_op jit(solution)/shard_map/ppermute | solution.py:335
  40.0 2.4 collective-permute-done.4.refs_2_
  42.4 1.9 collective-permute-done.10.refs_6_
  44.3 17.1 %collective-permute-done.11.refs_0_.refs_6_.refs_5_ = bf16[32,64,256]{2,1,0:T(8,128)(2,1)S(1)} collective-permute-done((bf16[32,64,256]{2,1,0:T(8,128)(2,1)S(1)}, bf16[32,64,256]{2,1,0:T(8,128)(2,1)S(1)}, u32[]{:S(2)}, u32[]{:S(2)}) %collective-permute-start.11) | collective-permute-done | bytes 1048608 | tf_op jit(solution)/shard_map/ppermute | solution.py:335
  65.5 19.4 %collective-permute-done.16.refs_2_.refs_7_ = bf16[32,64,256]{2,1,0:T(8,128)(2,1)S(1)} collective-permute-done((bf16[32,64,256]{2,1,0:T(8,128)(2,1)S(1)}, bf16[32,64,256]{2,1,0:T(8,128)(2,1)S(1)}, u32[]{:S(2)}, u32[]{:S(2)}) %collective-permute-start.16) | collective-permute-done | bytes 1048608 | tf_op jit(solution)/shard_map/ppermute | solution.py:335
  91.5 10.7 %collective-permute-done.9.refs_4_ = bf16[32,8192]{1,0:T(8,128)(2,1)S(1)} collective-permute-done((bf16[32,8192]{1,0:T(8,128)(2,1)S(1)}, bf16[32,8192]{1,0:T(8,128)(2,1)S(1)}, u32[]{:S(2)}, u32[]{:S(2)}) %collective-permute-start.9) | collective-permute-done | bytes 524320 | tf_op jit(solution)/shard_map/ppermute | solution.py:151
  102.2 5.9 %collective-permute-done.18.refs_7_.refs_0_.refs_1_.refs_3_ = bf16[32,64,256]{2,1,0:T(8,128)(2,1)S(1)} collective-permute-done((bf16[32,64,256]{2,1,0:T(8,128)(2,1)S(1)}, bf16[32,64,256]{2,1,0:T(8,128)(2,1)S(1)}, u32[]{:S(2)}, u32[]{:S(2)}) %collective-permute-start.18) | collective-permute-done | bytes 1048608 | tf_op jit(solution)/shard_map/ppermute | solution.py:335
  112.4 2.1 shard_map.60.refs_10_
  114.5 3.9 shard_map.61.refs_0_
  119.9 2.5 collective-permute-start.21
  122.4 8.9 %collective-permute-done.23.refs_2_.refs_7_.refs_8_.refs_4_ = bf16[32,64,256]{2,1,0:T(8,128)(2,1)S(1)} collective-permute-done((bf16[32,64,256]{2,1,0:T(8,128)(2,1)S(1)}, bf16[32,64,256]{2,1,0:T(8,128)(2,1)S(1)}, u32[]{:S(2)}, u32[]{:S(2)}) %collective-permute-start.23) | collective-permute-done | bytes 1048608 | tf_op jit(solution)/shard_map/ppermute | solution.py:335
  134.0 1.7 collective-permute-start.29
  135.7 10.3 %collective-permute-done.21.refs_2_ = bf16[32,8192]{1,0:T(8,128)(2,1)S(1)} collective-permute-done((bf16[32,8192]{1,0:T(8,128)(2,1)S(1)}, bf16[32,8192]{1,0:T(8,128)(2,1)S(1)}, u32[]{:S(2)}, u32[]{:S(2)}) %collective-permute-start.21) | collective-permute-done | bytes 524320 | tf_op jit(solution)/shard_map/ppermute | solution.py:151
  148.7 3.6 collective-permute-done.28.refs_4_.refs_2_.refs_0_.refs_10_
  153.2 2.1 shard_map.65.refs_10_
  156.1 7.7 %collective-permute-done.26.refs_4_ = bf16[32,8192]{1,0:T(8,128)(2,1)S(1)} collective-permute-done((bf16[32,8192]{1,0:T(8,128)(2,1)S(1)}, bf16[32,8192]{1,0:T(8,128)(2,1)S(1)}, u32[]{:S(2)}, u32[]{:S(2)}) %collective-permute-start.26) | collective-permute-done | bytes 524320 | tf_op jit(solution)/shard_map/ppermute | solution.py:151
  166.0 3.9 shard_map.66.refs_0_
  170.0 2.5 collective-permute-start.33
  172.5 2.6 collective-permute-start.34
  175.1 14.2 %collective-permute-done.36.refs_2_.refs_3_.refs_8_.refs_5_ = bf16[32,64,256]{2,1,0:T(8,128)(2,1)S(1)} collective-permute-done((bf16[32,64,256]{2,1,0:T(8,128)(2,1)S(1)}, bf16[32,64,256]{2,1,0:T(8,128)(2,1)S(1)}, u32[]{:S(2)}, u32[]{:S(2)}) %collective-permute-start.36) | collective-permute-done | bytes 1048608 | tf_op jit(solution)/shard_map/ppermute | solution.py:335
  191.5 7.1 %collective-permute-done.34.refs_2_ = bf16[32,8192]{1,0:T(8,128)(2,1)S(1)} collective-permute-done((bf16[32,8192]{1,0:T(8,128)(2,1)S(1)}, bf16[32,8192]{1,0:T(8,128)(2,1)S(1)}, u32[]{:S(2)}, u32[]{:S(2)}) %collective-permute-start.34) | collective-permute-done | bytes 524320 | tf_op jit(solution)/shard_map/ppermute | solution.py:151
  200.7 2.1 shard_map.68.refs_10_
  204.3 9.7 %collective-permute-done.39.refs_4_ = bf16[32,8192]{1,0:T(8,128)(2,1)S(1)} collective-permute-done((bf16[32,8192]{1,0:T(8,128)(2,1)S(1)}, bf16[32,8192]{1,0:T(8,128)(2,1)S(1)}, u32[]{:S(2)}, u32[]{:S(2)}) %collective-permute-start.39) | collective-permute-done | bytes 524320 | tf_op jit(solution)/shard_map/ppermute | solution.py:151
  218.1 3.9 shard_map.69.refs_0_
  222.2 2.2 collective-permute-start.44
  225.7 2.8 collective-permute-done.47.refs_1_.refs_5_.refs_7_.refs_4_
  228.5 9.3 %collective-permute-done.48.refs_2_.refs_3_.refs_0_.refs_1_ = bf16[32,64,256]{2,1,0:T(8,128)(2,1)S(1)} collective-permute-done((bf16[32,64,256]{2,1,0:T(8,128)(2,1)S(1)}, bf16[32,64,256]{2,1,0:T(8,128)(2,1)S(1)}, u32[]{:S(2)}, u32[]{:S(2)}) %collective-permute-start.48) | collective-permute-done | bytes 1048608 | tf_op jit(solution)/shard_map/ppermute | solution.py:335
  238.8 1.7 collective-permute-start.53
  240.5 8.7 %collective-permute-done.45.refs_2_ = bf16[32,8192]{1,0:T(8,128)(2,1)S(1)} collective-permute-done((bf16[32,8192]{1,0:T(8,128)(2,1)S(1)}, bf16[32,8192]{1,0:T(8,128)(2,1)S(1)}, u32[]{:S(2)}, u32[]{:S(2)}) %collective-permute-start.45) | collective-permute-done | bytes 524320 | tf_op jit(solution)/shard_map/ppermute | solution.py:151
  252.1 9.5 %collective-permute-done.52.refs_4_.refs_2_.refs_1_.refs_10_ = bf16[32,64,256]{2,1,0:T(8,128)(2,1)S(1)} collective-permute-done((bf16[32,64,256]{2,1,0:T(8,128)(2,1)S(1)}, bf16[32,64,256]{2,1,0:T(8,128)(2,1)S(1)}, u32[]{:S(2)}, u32[]{:S(2)}) %collective-permute-start.52) | collective-permute-done | bytes 1048608 | tf_op jit(solution)/shard_map/ppermute | solution.py:335
  261.6 2.1 shard_map.72.refs_10_
  264.5 1.7 collective-permute-done.50.refs_4_
  268.1 3.9 shard_map.73.refs_0_
  272.2 3.3 collective-permute-start.57
  276.6 15.1 %collective-permute-done.60.refs_1_.refs_6_.refs_8_.refs_7_ = bf16[32,64,256]{2,1,0:T(8,128)(2,1)S(1)} collective-permute-done((bf16[32,64,256]{2,1,0:T(8,128)(2,1)S(1)}, bf16[32,64,256]{2,1,0:T(8,128)(2,1)S(1)}, u32[]{:S(2)}, u32[]{:S(2)}) %collective-permute-start.60) | collective-permute-done | bytes 1048608 | tf_op jit(solution)/shard_map/ppermute | solution.py:335
  295.8 4.5 collective-permute-done.58.refs_2_
  302.2 2.1 shard_map.76.refs_10_
  305.0 12.3 %collective-permute-done.65.refs_0_.refs_5_.refs_2_ = bf16[32,64,256]{2,1,0:T(8,128)(2,1)S(1)} collective-permute-done((bf16[32,64,256]{2,1,0:T(8,128)(2,1)S(1)}, bf16[32,64,256]{2,1,0:T(8,128)(2,1)S(1)}, u32[]{:S(2)}, u32[]{:S(2)}) %collective-permute-start.65) | collective-permute-done | bytes 1048608 | tf_op jit(solution)/shard_map/ppermute | solution.py:335
  321.5 3.9 shard_map.77.refs_0_
  326.2 4.1 collective-permute-start.70
  330.3 4.5 collective-permute-start.77
  336.1 6.4 %collective-permute-done.70.refs_1_ = bf16[32,8192]{1,0:T(8,128)(2,1)S(1)} collective-permute-done((bf16[32,8192]{1,0:T(8,128)(2,1)S(1)}, bf16[32,8192]{1,0:T(8,128)(2,1)S(1)}, u32[]{:S(2)}, u32[]{:S(2)}) %collective-permute-start.70) | collective-permute-done | bytes 524320 | tf_op jit(solution)/shard_map/ppermute | solution.py:151
  343.2 1.7 collective-permute-done.75.refs_6_.refs_5_
  345.3 2.1 shard_map.78.refs_12_
  348.0 8.3 %collective-permute-done.77.refs_5_ = bf16[32,8192]{1,0:T(8,128)(2,1)S(1)} collective-permute-done((bf16[32,8192]{1,0:T(8,128)(2,1)S(1)}, bf16[32,8192]{1,0:T(8,128)(2,1)S(1)}, u32[]{:S(2)}, u32[]{:S(2)}) %collective-permute-start.77) | collective-permute-done | bytes 524320 | tf_op jit(solution)/shard_map/ppermute | solution.py:151
  356.3 11.0 %collective-permute-done.73.refs_4_ = bf16[32,8192]{1,0:T(8,128)(2,1)S(1)} collective-permute-done((bf16[32,8192]{1,0:T(8,128)(2,1)S(1)}, bf16[32,8192]{1,0:T(8,128)(2,1)S(1)}, u32[]{:S(2)}, u32[]{:S(2)}) %collective-permute-start.73) | collective-permute-done | bytes 524320 | tf_op jit(solution)/shard_map/ppermute | solution.py:151
  370.0 3.9 shard_map.79.refs_0_
  376.1 4.5 collective-permute-start.87
  382.0 6.7 %collective-permute-done.83.refs_1_ = bf16[32,8192]{1,0:T(8,128)(2,1)S(1)} collective-permute-done((bf16[32,8192]{1,0:T(8,128)(2,1)S(1)}, bf16[32,8192]{1,0:T(8,128)(2,1)S(1)}, u32[]{:S(2)}, u32[]{:S(2)}) %collective-permute-start.83) | collective-permute-done | bytes 524320 | tf_op jit(solution)/shard_map/ppermute | solution.py:151
  389.4 2.1 shard_map.80.refs_12_
  391.6 10.2 %collective-permute-done.87.refs_5_ = bf16[32,8192]{1,0:T(8,128)(2,1)S(1)} collective-permute-done((bf16[32,8192]{1,0:T(8,128)(2,1)S(1)}, bf16[32,8192]{1,0:T(8,128)(2,1)S(1)}, u32[]{:S(2)}, u32[]{:S(2)}) %collective-permute-start.87) | collective-permute-done | bytes 524320 | tf_op jit(solution)/shard_map/ppermute | solution.py:151
  401.8 10.8 %collective-permute-done.86.refs_4_ = bf16[32,8192]{1,0:T(8,128)(2,1)S(1)} collective-permute-done((bf16[32,8192]{1,0:T(8,128)(2,1)S(1)}, bf16[32,8192]{1,0:T(8,128)(2,1)S(1)}, u32[]{:S(2)}, u32[]{:S(2)}) %collective-permute-start.86) | collective-permute-done | bytes 524320 | tf_op jit(solution)/shard_map/ppermute | solution.py:151
  416.1 3.9 shard_map.81.refs_0_
  421.8 4.5 collective-permute-start.98
  427.7 7.0 %collective-permute-done.94.refs_1_ = bf16[32,8192]{1,0:T(8,128)(2,1)S(1)} collective-permute-done((bf16[32,8192]{1,0:T(8,128)(2,1)S(1)}, bf16[32,8192]{1,0:T(8,128)(2,1)S(1)}, u32[]{:S(2)}, u32[]{:S(2)}) %collective-permute-start.94) | collective-permute-done | bytes 524320 | tf_op jit(solution)/shard_map/ppermute | solution.py:151
  435.4 2.1 shard_map.82.refs_12_
  437.6 10.0 %collective-permute-done.98.refs_5_ = bf16[32,8192]{1,0:T(8,128)(2,1)S(1)} collective-permute-done((bf16[32,8192]{1,0:T(8,128)(2,1)S(1)}, bf16[32,8192]{1,0:T(8,128)(2,1)S(1)}, u32[]{:S(2)}, u32[]{:S(2)}) %collective-permute-start.98) | collective-permute-done | bytes 524320 | tf_op jit(solution)/shard_map/ppermute | solution.py:151
  447.6 10.8 %collective-permute-done.97.refs_4_ = bf16[32,8192]{1,0:T(8,128)(2,1)S(1)} collective-permute-done((bf16[32,8192]{1,0:T(8,128)(2,1)S(1)}, bf16[32,8192]{1,0:T(8,128)(2,1)S(1)}, u32[]{:S(2)}, u32[]{:S(2)}) %collective-permute-start.97) | collective-permute-done | bytes 524320 | tf_op jit(solution)/shard_map/ppermute | solution.py:151
  461.8 4.7 %shard_map.83 = bf16[32,8192]{1,0:T(8,128)(2,1)} custom-call(s32[512]{0:T(512)S(1)} %bitcast.25, s32[2]{0:T(128)S(1)} %pad_add_fusion.place, bf16[32,8192]{1,0:T(8,128)(2,1)S(1)} %shard_map.81.refs_0_, bf16[32,8192]{1,0:T(8,128)(2,1)S(1)} %collective-permute-done.94.refs_1_, bf16[32,8192]{1,0:T(8,128)(2,1)S(1)} %collective-permute-done.95.refs_2_, ...), custom_call_target="tpu_custom_call" | custom-call | tf_op jit(solution)/shard_map/pallas_call | solution.py:134
  (197 shorter events, 89.3 us)
Async XLA Ops:
  11.0 25.1 %collective-permute-start.6 = (bf16[32,64,256]{2,1,0:T(8,128)(2,1)}, bf16[32,64,256]{2,1,0:T(8,128)(2,1)S(1)}, u32[]{:S(2)}, u32[]{:S(2)}) collective-permute-start(bf16[32,64,256]{2,1,0:T(8,128)(2,1)} %get-tuple-element.90), channel_id=1, source_target_pairs={{0,8},{8,0},{16,24},{24,16},{1,9},{9,1},{17,25},{25,17},{2,10},{10... | collective-permute-start | bytes 3145736 | tf_op jit(solution)/shard_map/ppermute | solution.py:335
  12.9 24.4 %collective-permute-start.7 = (bf16[32,64,256]{2,1,0:T(8,128)(2,1)}, bf16[32,64,256]{2,1,0:T(8,128)(2,1)S(1)}, u32[]{:S(2)}, u32[]{:S(2)}) collective-permute-start(bf16[32,64,256]{2,1,0:T(8,128)(2,1)} %copy-done.1), channel_id=1, source_target_pairs={{0,16},{8,24},{16,0},{24,8},{1,17},{9,25},{17,1},{25,9},{2,18},{10... | collective-permute-start | bytes 3145736 | tf_op jit(solution)/shard_map/ppermute | solution.py:335
  14.7 25.3 %collective-permute-start.3 = (bf16[32,8192]{1,0:T(8,128)(2,1)S(1)}, bf16[32,8192]{1,0:T(8,128)(2,1)S(1)}, u32[]{:S(2)}, u32[]{:S(2)}) collective-permute-start(bf16[32,8192]{1,0:T(8,128)(2,1)S(1)} %copy-done), channel_id=1, source_target_pairs={{0,2},{1,3},{2,0},{3,1},{4,6},{5,7},{6,4},{7,5},{8,10},{9,11},{10,... | collective-permute-start | bytes 1572872 | tf_op jit(solution)/shard_map/ppermute | solution.py:151
  16.3 26.1 %collective-permute-start.4 = (bf16[32,8192]{1,0:T(8,128)(2,1)S(1)}, bf16[32,8192]{1,0:T(8,128)(2,1)S(1)}, u32[]{:S(2)}, u32[]{:S(2)}) collective-permute-start(bf16[32,8192]{1,0:T(8,128)(2,1)S(1)} %copy-done), channel_id=1, source_target_pairs={{2,4},{3,5},{4,2},{5,3},{0,6},{1,7},{6,0},{7,1},{10,12},{11,13},{1... | collective-permute-start | bytes 1572872 | tf_op jit(solution)/shard_map/ppermute | solution.py:151
  38.1 23.3 %collective-permute-start.11 = (bf16[32,64,256]{2,1,0:T(8,128)(2,1)S(1)}, bf16[32,64,256]{2,1,0:T(8,128)(2,1)S(1)}, u32[]{:S(2)}, u32[]{:S(2)}) collective-permute-start(bf16[32,64,256]{2,1,0:T(8,128)(2,1)S(1)} %get-tuple-element.97), channel_id=1, source_target_pairs={{0,8},{8,0},{16,24},{24,16},{1,9},{9,1},{17,25},{25,17},{2,10},{10... | collective-permute-start | bytes 3145736 | tf_op jit(solution)/shard_map/ppermute | solution.py:335
  38.5 23.2 %collective-permute-start.12 = (bf16[32,64,256]{2,1,0:T(8,128)(2,1)S(1)}, bf16[32,64,256]{2,1,0:T(8,128)(2,1)S(1)}, u32[]{:S(2)}, u32[]{:S(2)}) collective-permute-start(bf16[32,64,256]{2,1,0:T(8,128)(2,1)S(1)} %get-tuple-element.98), channel_id=1, source_target_pairs={{0,16},{8,24},{16,0},{24,8},{1,17},{9,25},{17,1},{25,9},{2,18},{10... | collective-permute-start | bytes 3145736 | tf_op jit(solution)/shard_map/ppermute | solution.py:335
  62.5 22.4 %collective-permute-start.16 = (bf16[32,64,256]{2,1,0:T(8,128)(2,1)S(1)}, bf16[32,64,256]{2,1,0:T(8,128)(2,1)S(1)}, u32[]{:S(2)}, u32[]{:S(2)}) collective-permute-start(bf16[32,64,256]{2,1,0:T(8,128)(2,1)S(1)} %get-tuple-element.103), channel_id=1, source_target_pairs={{0,8},{8,0},{16,24},{24,16},{1,9},{9,1},{17,25},{25,17},{2,10},{10... | collective-permute-start | bytes 3145736 | tf_op jit(solution)/shard_map/ppermute | solution.py:335
  63.9 21.8 %collective-permute-start.17 = (bf16[32,64,256]{2,1,0:T(8,128)(2,1)S(1)}, bf16[32,64,256]{2,1,0:T(8,128)(2,1)S(1)}, u32[]{:S(2)}, u32[]{:S(2)}) collective-permute-start(bf16[32,64,256]{2,1,0:T(8,128)(2,1)S(1)} %get-tuple-element.104), channel_id=1, source_target_pairs={{0,16},{8,24},{16,0},{24,8},{1,17},{9,25},{17,1},{25,9},{2,18},{10... | collective-permute-start | bytes 3145736 | tf_op jit(solution)/shard_map/ppermute | solution.py:335
  86.4 21.7 %collective-permute-start.18 = (bf16[32,64,256]{2,1,0:T(8,128)(2,1)S(1)}, bf16[32,64,256]{2,1,0:T(8,128)(2,1)S(1)}, u32[]{:S(2)}, u32[]{:S(2)}) collective-permute-start(bf16[32,64,256]{2,1,0:T(8,128)(2,1)S(1)} %get-tuple-element.108), channel_id=1, source_target_pairs={{0,8},{8,0},{16,24},{24,16},{1,9},{9,1},{17,25},{25,17},{2,10},{10... | collective-permute-start | bytes 3145736 | tf_op jit(solution)/shard_map/ppermute | solution.py:335
  87.4 21.6 %collective-permute-start.19 = (bf16[32,64,256]{2,1,0:T(8,128)(2,1)S(1)}, bf16[32,64,256]{2,1,0:T(8,128)(2,1)S(1)}, u32[]{:S(2)}, u32[]{:S(2)}) collective-permute-start(bf16[32,64,256]{2,1,0:T(8,128)(2,1)S(1)} %get-tuple-element.109), channel_id=1, source_target_pairs={{0,16},{8,24},{16,0},{24,8},{1,17},{9,25},{17,1},{25,9},{2,18},{10... | collective-permute-start | bytes 3145736 | tf_op jit(solution)/shard_map/ppermute | solution.py:335
  90.9 23.6 %collective-permute-start.13 = (bf16[32,8192]{1,0:T(8,128)(2,1)S(1)}, bf16[32,8192]{1,0:T(8,128)(2,1)S(1)}, u32[]{:S(2)}, u32[]{:S(2)}) collective-permute-start(bf16[32,8192]{1,0:T(8,128)(2,1)S(1)} %collective-permute-done.4.refs_2_), channel_id=1, source_target_pairs={{0,1},{1,0},{2,3},{3,2},{4,5},{5,4},{6,7},{7,6},{8,9},{9,8},{10,11... | collective-permute-start | bytes 1572872 | tf_op jit(solution)/shard_map/ppermute | solution.py:155
  91.0 23.5 %collective-permute-start.14 = (bf16[32,8192]{1,0:T(8,128)(2,1)S(1)}, bf16[32,8192]{1,0:T(8,128)(2,1)S(1)}, u32[]{:S(2)}, u32[]{:S(2)}) collective-permute-start(bf16[32,8192]{1,0:T(8,128)(2,1)S(1)} %collective-permute-done.8.refs_3_), channel_id=1, source_target_pairs={{0,1},{1,0},{2,3},{3,2},{4,5},{5,4},{6,7},{7,6},{8,9},{9,8},{10,11... | collective-permute-start | bytes 1572872 | tf_op jit(solution)/shard_map/ppermute | solution.py:155
  109.7 21.6 %collective-permute-start.23 = (bf16[32,64,256]{2,1,0:T(8,128)(2,1)S(1)}, bf16[32,64,256]{2,1,0:T(8,128)(2,1)S(1)}, u32[]{:S(2)}, u32[]{:S(2)}) collective-permute-start(bf16[32,64,256]{2,1,0:T(8,128)(2,1)S(1)} %get-tuple-element.112), channel_id=1, source_target_pairs={{0,8},{8,0},{16,24},{24,16},{1,9},{9,1},{17,25},{25,17},{2,10},{10... | collective-permute-start | bytes 3145736 | tf_op jit(solution)/shard_map/ppermute | solution.py:335
  110.7 22.2 %collective-permute-start.24 = (bf16[32,64,256]{2,1,0:T(8,128)(2,1)S(1)}, bf16[32,64,256]{2,1,0:T(8,128)(2,1)S(1)}, u32[]{:S(2)}, u32[]{:S(2)}) collective-permute-start(bf16[32,64,256]{2,1,0:T(8,128)(2,1)S(1)} %get-tuple-element.113), channel_id=1, source_target_pairs={{0,16},{8,24},{16,0},{24,8},{1,17},{9,25},{17,1},{25,9},{2,18},{10... | collective-permute-start | bytes 3145736 | tf_op jit(solution)/shard_map/ppermute | solution.py:335
  118.5 17.2 %collective-permute-start.20 = (bf16[32,8192]{1,0:T(8,128)(2,1)S(1)}, bf16[32,8192]{1,0:T(8,128)(2,1)S(1)}, u32[]{:S(2)}, u32[]{:S(2)}) collective-permute-start(bf16[32,8192]{1,0:T(8,128)(2,1)S(1)} %shard_map.61.refs_0_), channel_id=1, source_target_pairs={{0,2},{1,3},{2,0},{3,1},{4,6},{5,7},{6,4},{7,5},{8,10},{9,11},{10,... | collective-permute-start | bytes 1572872 | tf_op jit(solution)/shard_map/ppermute | solution.py:151
  119.9 26.1 %collective-permute-start.21 = (bf16[32,8192]{1,0:T(8,128)(2,1)S(1)}, bf16[32,8192]{1,0:T(8,128)(2,1)S(1)}, u32[]{:S(2)}, u32[]{:S(2)}) collective-permute-start(bf16[32,8192]{1,0:T(8,128)(2,1)S(1)} %shard_map.61.refs_0_), channel_id=1, source_target_pairs={{2,4},{3,5},{4,2},{5,3},{0,6},{1,7},{6,0},{7,1},{10,12},{11,13},{1... | collective-permute-start | bytes 1572872 | tf_op jit(solution)/shard_map/ppermute | solution.py:151
  133.6 18.7 %collective-permute-start.28 = (bf16[32,64,256]{2,1,0:T(8,128)(2,1)S(1)}, bf16[32,64,256]{2,1,0:T(8,128)(2,1)S(1)}, u32[]{:S(2)}, u32[]{:S(2)}) collective-permute-start(bf16[32,64,256]{2,1,0:T(8,128)(2,1)S(1)} %get-tuple-element.118), channel_id=1, source_target_pairs={{0,8},{8,0},{16,24},{24,16},{1,9},{9,1},{17,25},{25,17},{2,10},{10... | collective-permute-start | bytes 3145736 | tf_op jit(solution)/shard_map/ppermute | solution.py:335
  134.0 19.2 %collective-permute-start.29 = (bf16[32,64,256]{2,1,0:T(8,128)(2,1)S(1)}, bf16[32,64,256]{2,1,0:T(8,128)(2,1)S(1)}, u32[]{:S(2)}, u32[]{:S(2)}) collective-permute-start(bf16[32,64,256]{2,1,0:T(8,128)(2,1)S(1)} %get-tuple-element.119), channel_id=1, source_target_pairs={{0,16},{8,24},{16,0},{24,8},{1,17},{9,25},{17,1},{25,9},{2,18},{10... | collective-permute-start | bytes 3145736 | tf_op jit(solution)/shard_map/ppermute | solution.py:335
  146.7 17.1 %collective-permute-start.26 = (bf16[32,8192]{1,0:T(8,128)(2,1)S(1)}, bf16[32,8192]{1,0:T(8,128)(2,1)S(1)}, u32[]{:S(2)}, u32[]{:S(2)}) collective-permute-start(bf16[32,8192]{1,0:T(8,128)(2,1)S(1)} %collective-permute-done.21.refs_2_), channel_id=1, source_target_pairs={{4,6},{5,7},{2,0},{3,1},{12,14},{13,15},{10,8},{11,9},{20,22},{21,... | collective-permute-start | bytes 1572872 | tf_op jit(solution)/shard_map/ppermute | solution.py:151
  148.0 18.0 %collective-permute-start.30 = (bf16[32,8192]{1,0:T(8,128)(2,1)S(1)}, bf16[32,8192]{1,0:T(8,128)(2,1)S(1)}, u32[]{:S(2)}, u32[]{:S(2)}) collective-permute-start(bf16[32,8192]{1,0:T(8,128)(2,1)S(1)} %collective-permute-done.21.refs_2_), channel_id=1, source_target_pairs={{0,1},{1,0},{2,3},{3,2},{4,5},{5,4},{6,7},{7,6},{8,9},{9,8},{10,11... | collective-permute-start | bytes 1572872 | tf_op jit(solution)/shard_map/ppermute | solution.py:155
  148.6 17.5 %collective-permute-start.31 = (bf16[32,8192]{1,0:T(8,128)(2,1)S(1)}, bf16[32,8192]{1,0:T(8,128)(2,1)S(1)}, u32[]{:S(2)}, u32[]{:S(2)}) collective-permute-start(bf16[32,8192]{1,0:T(8,128)(2,1)S(1)} %collective-permute-done.25.refs_3_), channel_id=1, source_target_pairs={{0,1},{1,0},{2,3},{3,2},{4,5},{5,4},{6,7},{7,6},{8,9},{9,8},{10,11... | collective-permute-start | bytes 1572872 | tf_op jit(solution)/shard_map/ppermute | solution.py:155
  163.8 25.6 %collective-permute-start.36 = (bf16[32,64,256]{2,1,0:T(8,128)(2,1)S(1)}, bf16[32,64,256]{2,1,0:T(8,128)(2,1)S(1)}, u32[]{:S(2)}, u32[]{:S(2)}) collective-permute-start(bf16[32,64,256]{2,1,0:T(8,128)(2,1)S(1)} %get-tuple-element.125), channel_id=1, source_target_pairs={{0,8},{8,0},{16,24},{24,16},{1,9},{9,1},{17,25},{25,17},{2,10},{10... | collective-permute-start | bytes 3145736 | tf_op jit(solution)/shard_map/ppermute | solution.py:335
  165.5 25.3 %collective-permute-start.37 = (bf16[32,64,256]{2,1,0:T(8,128)(2,1)S(1)}, bf16[32,64,256]{2,1,0:T(8,128)(2,1)S(1)}, u32[]{:S(2)}, u32[]{:S(2)}) collective-permute-start(bf16[32,64,256]{2,1,0:T(8,128)(2,1)S(1)} %get-tuple-element.126), channel_id=1, source_target_pairs={{0,16},{8,24},{16,0},{24,8},{1,17},{9,25},{17,1},{25,9},{2,18},{10... | collective-permute-start | bytes 3145736 | tf_op jit(solution)/shard_map/ppermute | solution.py:335
  170.0 21.5 %collective-permute-start.33 = (bf16[32,8192]{1,0:T(8,128)(2,1)S(1)}, bf16[32,8192]{1,0:T(8,128)(2,1)S(1)}, u32[]{:S(2)}, u32[]{:S(2)}) collective-permute-start(bf16[32,8192]{1,0:T(8,128)(2,1)S(1)} %shard_map.66.refs_0_), channel_id=1, source_target_pairs={{0,2},{1,3},{2,0},{3,1},{4,6},{5,7},{6,4},{7,5},{8,10},{9,11},{10,... | collective-permute-start | bytes 1572872 | tf_op jit(solution)/shard_map/ppermute | solution.py:151
  172.5 26.1 %collective-permute-start.34 = (bf16[32,8192]{1,0:T(8,128)(2,1)S(1)}, bf16[32,8192]{1,0:T(8,128)(2,1)S(1)}, u32[]{:S(2)}, u32[]{:S(2)}) collective-permute-start(bf16[32,8192]{1,0:T(8,128)(2,1)S(1)} %shard_map.66.refs_0_), channel_id=1, source_target_pairs={{2,4},{3,5},{4,2},{5,3},{0,6},{1,7},{6,0},{7,1},{10,12},{11,13},{1... | collective-permute-start | bytes 1572872 | tf_op jit(solution)/shard_map/ppermute | solution.py:151
  199.9 15.6 %collective-permute-start.38 = (bf16[32,8192]{1,0:T(8,128)(2,1)S(1)}, bf16[32,8192]{1,0:T(8,128)(2,1)S(1)}, u32[]{:S(2)}, u32[]{:S(2)}) collective-permute-start(bf16[32,8192]{1,0:T(8,128)(2,1)S(1)} %collective-permute-done.33.refs_1_), channel_id=1, source_target_pairs={{2,4},{3,5},{4,2},{5,3},{10,12},{11,13},{12,10},{13,11},{18,20},{1... | collective-permute-start | bytes 1572872 | tf_op jit(solution)/shard_map/ppermute | solution.py:151
  203.4 25.1 %collective-permute-start.47 = (bf16[32,64,256]{2,1,0:T(8,128)(2,1)S(1)}, bf16[32,64,256]{2,1,0:T(8,128)(2,1)S(1)}, u32[]{:S(2)}, u32[]{:S(2)}) collective-permute-start(bf16[32,64,256]{2,1,0:T(8,128)(2,1)S(1)} %get-tuple-element.134), channel_id=1, source_target_pairs={{0,8},{8,0},{16,24},{24,16},{1,9},{9,1},{17,25},{25,17},{2,10},{10... | collective-permute-start | bytes 3145736 | tf_op jit(solution)/shard_map/ppermute | solution.py:335
  214.0 23.8 %collective-permute-start.48 = (bf16[32,64,256]{2,1,0:T(8,128)(2,1)S(1)}, bf16[32,64,256]{2,1,0:T(8,128)(2,1)S(1)}, u32[]{:S(2)}, u32[]{:S(2)}) collective-permute-start(bf16[32,64,256]{2,1,0:T(8,128)(2,1)S(1)} %get-tuple-element.135), channel_id=1, source_target_pairs={{0,16},{8,24},{16,0},{24,8},{1,17},{9,25},{17,1},{25,9},{2,18},{10... | collective-permute-start | bytes 3145736 | tf_op jit(solution)/shard_map/ppermute | solution.py:335
  222.0 15.8 %collective-permute-start.46 = (bf16[32,8192]{1,0:T(8,128)(2,1)S(1)}, bf16[32,8192]{1,0:T(8,128)(2,1)S(1)}, u32[]{:S(2)}, u32[]{:S(2)}) collective-permute-start(bf16[32,8192]{1,0:T(8,128)(2,1)S(1)} %shard_map.69.refs_0_), channel_id=1, source_target_pairs={{0,1},{1,0},{2,3},{3,2},{4,5},{5,4},{6,7},{7,6},{8,9},{9,8},{10,11... | collective-permute-start | bytes 1572872 | tf_op jit(solution)/shard_map/ppermute | solution.py:155
  222.2 18.3 %collective-permute-start.44 = (bf16[32,8192]{1,0:T(8,128)(2,1)S(1)}, bf16[32,8192]{1,0:T(8,128)(2,1)S(1)}, u32[]{:S(2)}, u32[]{:S(2)}) collective-permute-start(bf16[32,8192]{1,0:T(8,128)(2,1)S(1)} %shard_map.69.refs_0_), channel_id=1, source_target_pairs={{0,2},{1,3},{2,0},{3,1},{4,6},{5,7},{6,4},{7,5},{8,10},{9,11},{10,... | collective-permute-start | bytes 1572872 | tf_op jit(solution)/shard_map/ppermute | solution.py:151
  224.5 24.7 %collective-permute-start.45 = (bf16[32,8192]{1,0:T(8,128)(2,1)S(1)}, bf16[32,8192]{1,0:T(8,128)(2,1)S(1)}, u32[]{:S(2)}, u32[]{:S(2)}) collective-permute-start(bf16[32,8192]{1,0:T(8,128)(2,1)S(1)} %shard_map.69.refs_0_), channel_id=1, source_target_pairs={{2,4},{3,5},{4,2},{5,3},{0,6},{1,7},{6,0},{7,1},{10,12},{11,13},{1... | collective-permute-start | bytes 1572872 | tf_op jit(solution)/shard_map/ppermute | solution.py:151
  238.6 23.0 %collective-permute-start.52 = (bf16[32,64,256]{2,1,0:T(8,128)(2,1)S(1)}, bf16[32,64,256]{2,1,0:T(8,128)(2,1)S(1)}, u32[]{:S(2)}, u32[]{:S(2)}) collective-permute-start(bf16[32,64,256]{2,1,0:T(8,128)(2,1)S(1)} %get-tuple-element.142), channel_id=1, source_target_pairs={{0,8},{8,0},{16,24},{24,16},{1,9},{9,1},{17,25},{25,17},{2,10},{10... | collective-permute-start | bytes 3145736 | tf_op jit(solution)/shard_map/ppermute | solution.py:335
  238.8 22.8 %collective-permute-start.53 = (bf16[32,64,256]{2,1,0:T(8,128)(2,1)S(1)}, bf16[32,64,256]{2,1,0:T(8,128)(2,1)S(1)}, u32[]{:S(2)}, u32[]{:S(2)}) collective-permute-start(bf16[32,64,256]{2,1,0:T(8,128)(2,1)S(1)} %get-tuple-element.143), channel_id=1, source_target_pairs={{0,16},{8,24},{16,0},{24,8},{1,17},{9,25},{17,1},{25,9},{2,18},{10... | collective-permute-start | bytes 3145736 | tf_op jit(solution)/shard_map/ppermute | solution.py:335
  249.9 16.2 %collective-permute-start.50 = (bf16[32,8192]{1,0:T(8,128)(2,1)S(1)}, bf16[32,8192]{1,0:T(8,128)(2,1)S(1)}, u32[]{:S(2)}, u32[]{:S(2)}) collective-permute-start(bf16[32,8192]{1,0:T(8,128)(2,1)S(1)} %collective-permute-done.45.refs_2_), channel_id=1, source_target_pairs={{4,6},{5,7},{2,0},{3,1},{12,14},{13,15},{10,8},{11,9},{20,22},{21,... | collective-permute-start | bytes 1572872 | tf_op jit(solution)/shard_map/ppermute | solution.py:151
  251.4 16.6 %collective-permute-start.54 = (bf16[32,8192]{1,0:T(8,128)(2,1)S(1)}, bf16[32,8192]{1,0:T(8,128)(2,1)S(1)}, u32[]{:S(2)}, u32[]{:S(2)}) collective-permute-start(bf16[32,8192]{1,0:T(8,128)(2,1)S(1)} %collective-permute-done.45.refs_2_), channel_id=1, source_target_pairs={{0,1},{1,0},{2,3},{3,2},{4,5},{5,4},{6,7},{7,6},{8,9},{9,8},{10,11... | collective-permute-start | bytes 1572872 | tf_op jit(solution)/shard_map/ppermute | solution.py:155
  252.0 16.0 %collective-permute-start.55 = (bf16[32,8192]{1,0:T(8,128)(2,1)S(1)}, bf16[32,8192]{1,0:T(8,128)(2,1)S(1)}, u32[]{:S(2)}, u32[]{:S(2)}) collective-permute-start(bf16[32,8192]{1,0:T(8,128)(2,1)S(1)} %collective-permute-done.49.refs_3_), channel_id=1, source_target_pairs={{0,1},{1,0},{2,3},{3,2},{4,5},{5,4},{6,7},{7,6},{8,9},{9,8},{10,11... | collective-permute-start | bytes 1572872 | tf_op jit(solution)/shard_map/ppermute | solution.py:155
  266.1 25.6 %collective-permute-start.60 = (bf16[32,64,256]{2,1,0:T(8,128)(2,1)S(1)}, bf16[32,64,256]{2,1,0:T(8,128)(2,1)S(1)}, u32[]{:S(2)}, u32[]{:S(2)}) collective-permute-start(bf16[32,64,256]{2,1,0:T(8,128)(2,1)S(1)} %get-tuple-element.151), channel_id=1, source_target_pairs={{0,8},{8,0},{16,24},{24,16},{1,9},{9,1},{17,25},{25,17},{2,10},{10... | collective-permute-start | bytes 3145736 | tf_op jit(solution)/shard_map/ppermute | solution.py:335
  266.8 25.3 %collective-permute-start.61 = (bf16[32,64,256]{2,1,0:T(8,128)(2,1)S(1)}, bf16[32,64,256]{2,1,0:T(8,128)(2,1)S(1)}, u32[]{:S(2)}, u32[]{:S(2)}) collective-permute-start(bf16[32,64,256]{2,1,0:T(8,128)(2,1)S(1)} %get-tuple-element.152), channel_id=1, source_target_pairs={{0,16},{8,24},{16,0},{24,8},{1,17},{9,25},{17,1},{25,9},{2,18},{10... | collective-permute-start | bytes 3145736 | tf_op jit(solution)/shard_map/ppermute | solution.py:335
  272.0 20.1 %collective-permute-start.59 = (bf16[32,8192]{1,0:T(8,128)(2,1)S(1)}, bf16[32,8192]{1,0:T(8,128)(2,1)S(1)}, u32[]{:S(2)}, u32[]{:S(2)}) collective-permute-start(bf16[32,8192]{1,0:T(8,128)(2,1)S(1)} %shard_map.73.refs_0_), channel_id=1, source_target_pairs={{0,1},{1,0},{2,3},{3,2},{4,5},{5,4},{6,7},{7,6},{8,9},{9,8},{10,11... | collective-permute-start | bytes 1572872 | tf_op jit(solution)/shard_map/ppermute | solution.py:155
  272.2 23.6 %collective-permute-start.57 = (bf16[32,8192]{1,0:T(8,128)(2,1)S(1)}, bf16[32,8192]{1,0:T(8,128)(2,1)S(1)}, u32[]{:S(2)}, u32[]{:S(2)}) collective-permute-start(bf16[32,8192]{1,0:T(8,128)(2,1)S(1)} %shard_map.73.refs_0_), channel_id=1, source_target_pairs={{0,2},{1,3},{2,0},{3,1},{4,6},{5,7},{6,4},{7,5},{8,10},{9,11},{10,... | collective-permute-start | bytes 1572872 | tf_op jit(solution)/shard_map/ppermute | solution.py:151
  275.5 24.8 %collective-permute-start.58 = (bf16[32,8192]{1,0:T(8,128)(2,1)S(1)}, bf16[32,8192]{1,0:T(8,128)(2,1)S(1)}, u32[]{:S(2)}, u32[]{:S(2)}) collective-permute-start(bf16[32,8192]{1,0:T(8,128)(2,1)S(1)} %shard_map.73.refs_0_), channel_id=1, source_target_pairs={{2,4},{3,5},{4,2},{5,3},{0,6},{1,7},{6,0},{7,1},{10,12},{11,13},{1... | collective-permute-start | bytes 1572872 | tf_op jit(solution)/shard_map/ppermute | solution.py:151
  292.8 24.5 %collective-permute-start.65 = (bf16[32,64,256]{2,1,0:T(8,128)(2,1)S(1)}, bf16[32,64,256]{2,1,0:T(8,128)(2,1)S(1)}, u32[]{:S(2)}, u32[]{:S(2)}) collective-permute-start(bf16[32,64,256]{2,1,0:T(8,128)(2,1)S(1)} %get-tuple-element.159), channel_id=1, source_target_pairs={{0,8},{8,0},{16,24},{24,16},{1,9},{9,1},{17,25},{25,17},{2,10},{10... | collective-permute-start | bytes 3145736 | tf_op jit(solution)/shard_map/ppermute | solution.py:335
  294.3 24.2 %collective-permute-start.66 = (bf16[32,64,256]{2,1,0:T(8,128)(2,1)S(1)}, bf16[32,64,256]{2,1,0:T(8,128)(2,1)S(1)}, u32[]{:S(2)}, u32[]{:S(2)}) collective-permute-start(bf16[32,64,256]{2,1,0:T(8,128)(2,1)S(1)} %get-tuple-element.160), channel_id=1, source_target_pairs={{0,16},{8,24},{16,0},{24,8},{1,17},{9,25},{17,1},{25,9},{2,18},{10... | collective-permute-start | bytes 3145736 | tf_op jit(solution)/shard_map/ppermute | solution.py:335
  300.9 18.3 %collective-permute-start.63 = (bf16[32,8192]{1,0:T(8,128)(2,1)S(1)}, bf16[32,8192]{1,0:T(8,128)(2,1)S(1)}, u32[]{:S(2)}, u32[]{:S(2)}) collective-permute-start(bf16[32,8192]{1,0:T(8,128)(2,1)S(1)} %collective-permute-done.58.refs_2_), channel_id=1, source_target_pairs={{4,6},{5,7},{2,0},{3,1},{12,14},{13,15},{10,8},{11,9},{20,22},{21,... | collective-permute-start | bytes 1572872 | tf_op jit(solution)/shard_map/ppermute | solution.py:151
  304.4 17.1 %collective-permute-start.67 = (bf16[32,8192]{1,0:T(8,128)(2,1)S(1)}, bf16[32,8192]{1,0:T(8,128)(2,1)S(1)}, u32[]{:S(2)}, u32[]{:S(2)}) collective-permute-start(bf16[32,8192]{1,0:T(8,128)(2,1)S(1)} %collective-permute-done.58.refs_2_), channel_id=1, source_target_pairs={{0,1},{1,0},{2,3},{3,2},{4,5},{5,4},{6,7},{7,6},{8,9},{9,8},{10,11... | collective-permute-start | bytes 1572872 | tf_op jit(solution)/shard_map/ppermute | solution.py:155
  304.9 16.6 %collective-permute-start.68 = (bf16[32,8192]{1,0:T(8,128)(2,1)S(1)}, bf16[32,8192]{1,0:T(8,128)(2,1)S(1)}, u32[]{:S(2)}, u32[]{:S(2)}) collective-permute-start(bf16[32,8192]{1,0:T(8,128)(2,1)S(1)} %collective-permute-done.62.refs_3_), channel_id=1, source_target_pairs={{0,1},{1,0},{2,3},{3,2},{4,5},{5,4},{6,7},{7,6},{8,9},{9,8},{10,11... | collective-permute-start | bytes 1572872 | tf_op jit(solution)/shard_map/ppermute | solution.py:155
  319.4 25.6 %collective-permute-start.75 = (bf16[32,64,256]{2,1,0:T(8,128)(2,1)S(1)}, bf16[32,64,256]{2,1,0:T(8,128)(2,1)S(1)}, u32[]{:S(2)}, u32[]{:S(2)}) collective-permute-start(bf16[32,64,256]{2,1,0:T(8,128)(2,1)S(1)} %get-tuple-element.166), channel_id=1, source_target_pairs={{0,8},{8,0},{16,24},{24,16},{1,9},{9,1},{17,25},{25,17},{2,10},{10... | collective-permute-start | bytes 3145736 | tf_op jit(solution)/shard_map/ppermute | solution.py:335
  320.0 25.3 %collective-permute-start.76 = (bf16[32,64,256]{2,1,0:T(8,128)(2,1)S(1)}, bf16[32,64,256]{2,1,0:T(8,128)(2,1)S(1)}, u32[]{:S(2)}, u32[]{:S(2)}) collective-permute-start(bf16[32,64,256]{2,1,0:T(8,128)(2,1)S(1)} %get-tuple-element.167), channel_id=1, source_target_pairs={{0,16},{8,24},{16,0},{24,8},{1,17},{9,25},{17,1},{25,9},{2,18},{10... | collective-permute-start | bytes 3145736 | tf_op jit(solution)/shard_map/ppermute | solution.py:335
  326.2 16.3 %collective-permute-start.70 = (bf16[32,8192]{1,0:T(8,128)(2,1)S(1)}, bf16[32,8192]{1,0:T(8,128)(2,1)S(1)}, u32[]{:S(2)}, u32[]{:S(2)}) collective-permute-start(bf16[32,8192]{1,0:T(8,128)(2,1)S(1)} %shard_map.77.refs_0_), channel_id=1, source_target_pairs={{0,2},{1,3},{2,0},{3,1},{4,6},{5,7},{6,4},{7,5},{8,10},{9,11},{10,... | collective-permute-start | bytes 1572872 | tf_op jit(solution)/shard_map/ppermute | solution.py:151
  330.3 26.1 %collective-permute-start.77 = (bf16[32,8192]{1,0:T(8,128)(2,1)S(1)}, bf16[32,8192]{1,0:T(8,128)(2,1)S(1)}, u32[]{:S(2)}, u32[]{:S(2)}) collective-permute-start(bf16[32,8192]{1,0:T(8,128)(2,1)S(1)} %shard_map.77.refs_0_), channel_id=1, source_target_pairs={{0,6},{1,7},{6,0},{7,1},{8,14},{9,15},{14,8},{15,9},{16,22},{17,23... | collective-permute-start | bytes 1572872 | tf_op jit(solution)/shard_map/ppermute | solution.py:151
  334.8 32.6 %collective-permute-start.73 = (bf16[32,8192]{1,0:T(8,128)(2,1)S(1)}, bf16[32,8192]{1,0:T(8,128)(2,1)S(1)}, u32[]{:S(2)}, u32[]{:S(2)}) collective-permute-start(bf16[32,8192]{1,0:T(8,128)(2,1)S(1)} %collective-permute-done.71.refs_2_), channel_id=1, source_target_pairs={{4,6},{5,7},{2,0},{3,1},{12,14},{13,15},{10,8},{11,9},{20,22},{21,... | collective-permute-start | bytes 1572872 | tf_op jit(solution)/shard_map/ppermute | solution.py:151
  342.5 24.8 %collective-permute-start.72 = (bf16[32,8192]{1,0:T(8,128)(2,1)S(1)}, bf16[32,8192]{1,0:T(8,128)(2,1)S(1)}, u32[]{:S(2)}, u32[]{:S(2)}) collective-permute-start(bf16[32,8192]{1,0:T(8,128)(2,1)S(1)} %collective-permute-done.70.refs_1_), channel_id=1, source_target_pairs={{2,4},{3,5},{4,2},{5,3},{10,12},{11,13},{12,10},{13,11},{18,20},{1... | collective-permute-start | bytes 1572872 | tf_op jit(solution)/shard_map/ppermute | solution.py:151
  347.4 20.5 %collective-permute-start.78 = (bf16[32,8192]{1,0:T(8,128)(2,1)S(1)}, bf16[32,8192]{1,0:T(8,128)(2,1)S(1)}, u32[]{:S(2)}, u32[]{:S(2)}) collective-permute-start(bf16[32,8192]{1,0:T(8,128)(2,1)S(1)} %collective-permute-done.70.refs_1_), channel_id=1, source_target_pairs={{0,1},{1,0},{2,3},{3,2},{4,5},{5,4},{6,7},{7,6},{8,9},{9,8},{10,11... | collective-permute-start | bytes 1572872 | tf_op jit(solution)/shard_map/ppermute | solution.py:155
  347.5 20.4 %collective-permute-start.79 = (bf16[32,8192]{1,0:T(8,128)(2,1)S(1)}, bf16[32,8192]{1,0:T(8,128)(2,1)S(1)}, u32[]{:S(2)}, u32[]{:S(2)}) collective-permute-start(bf16[32,8192]{1,0:T(8,128)(2,1)S(1)} %collective-permute-done.71.refs_2_), channel_id=1, source_target_pairs={{0,1},{1,0},{2,3},{3,2},{4,5},{5,4},{6,7},{7,6},{8,9},{9,8},{10,11... | collective-permute-start | bytes 1572872 | tf_op jit(solution)/shard_map/ppermute | solution.py:155
  376.1 25.7 %collective-permute-start.87 = (bf16[32,8192]{1,0:T(8,128)(2,1)S(1)}, bf16[32,8192]{1,0:T(8,128)(2,1)S(1)}, u32[]{:S(2)}, u32[]{:S(2)}) collective-permute-start(bf16[32,8192]{1,0:T(8,128)(2,1)S(1)} %shard_map.79.refs_0_), channel_id=1, source_target_pairs={{0,6},{1,7},{6,0},{7,1},{8,14},{9,15},{14,8},{15,9},{16,22},{17,23... | collective-permute-start | bytes 1572872 | tf_op jit(solution)/shard_map/ppermute | solution.py:151
  380.6 32.0 %collective-permute-start.86 = (bf16[32,8192]{1,0:T(8,128)(2,1)S(1)}, bf16[32,8192]{1,0:T(8,128)(2,1)S(1)}, u32[]{:S(2)}, u32[]{:S(2)}) collective-permute-start(bf16[32,8192]{1,0:T(8,128)(2,1)S(1)} %collective-permute-done.84.refs_2_), channel_id=1, source_target_pairs={{4,6},{5,7},{2,0},{3,1},{12,14},{13,15},{10,8},{11,9},{20,22},{21,... | collective-permute-start | bytes 1572872 | tf_op jit(solution)/shard_map/ppermute | solution.py:151
  381.9 30.7 %collective-permute-start.88 = (bf16[32,8192]{1,0:T(8,128)(2,1)S(1)}, bf16[32,8192]{1,0:T(8,128)(2,1)S(1)}, u32[]{:S(2)}, u32[]{:S(2)}) collective-permute-start(bf16[32,8192]{1,0:T(8,128)(2,1)S(1)} %shard_map.79.refs_0_), channel_id=1, source_target_pairs={{0,1},{1,0},{2,3},{3,2},{4,5},{5,4},{6,7},{7,6},{8,9},{9,8},{10,11... | collective-permute-start | bytes 1572872 | tf_op jit(solution)/shard_map/ppermute | solution.py:155
  388.7 24.5 %collective-permute-start.85 = (bf16[32,8192]{1,0:T(8,128)(2,1)S(1)}, bf16[32,8192]{1,0:T(8,128)(2,1)S(1)}, u32[]{:S(2)}, u32[]{:S(2)}) collective-permute-start(bf16[32,8192]{1,0:T(8,128)(2,1)S(1)} %collective-permute-done.83.refs_1_), channel_id=1, source_target_pairs={{2,4},{3,5},{4,2},{5,3},{10,12},{11,13},{12,10},{13,11},{18,20},{1... | collective-permute-start | bytes 1572872 | tf_op jit(solution)/shard_map/ppermute | solution.py:151
  391.5 21.8 %collective-permute-start.89 = (bf16[32,8192]{1,0:T(8,128)(2,1)S(1)}, bf16[32,8192]{1,0:T(8,128)(2,1)S(1)}, u32[]{:S(2)}, u32[]{:S(2)}) collective-permute-start(bf16[32,8192]{1,0:T(8,128)(2,1)S(1)} %collective-permute-done.83.refs_1_), channel_id=1, source_target_pairs={{0,1},{1,0},{2,3},{3,2},{4,5},{5,4},{6,7},{7,6},{8,9},{9,8},{10,11... | collective-permute-start | bytes 1572872 | tf_op jit(solution)/shard_map/ppermute | solution.py:155
  421.8 25.7 %collective-permute-start.98 = (bf16[32,8192]{1,0:T(8,128)(2,1)S(1)}, bf16[32,8192]{1,0:T(8,128)(2,1)S(1)}, u32[]{:S(2)}, u32[]{:S(2)}) collective-permute-start(bf16[32,8192]{1,0:T(8,128)(2,1)S(1)} %shard_map.81.refs_0_), channel_id=1, source_target_pairs={{0,6},{1,7},{6,0},{7,1},{8,14},{9,15},{14,8},{15,9},{16,22},{17,23... | collective-permute-start | bytes 1572872 | tf_op jit(solution)/shard_map/ppermute | solution.py:151
  426.4 32.0 %collective-permute-start.97 = (bf16[32,8192]{1,0:T(8,128)(2,1)S(1)}, bf16[32,8192]{1,0:T(8,128)(2,1)S(1)}, u32[]{:S(2)}, u32[]{:S(2)}) collective-permute-start(bf16[32,8192]{1,0:T(8,128)(2,1)S(1)} %collective-permute-done.95.refs_2_), channel_id=1, source_target_pairs={{4,6},{5,7},{2,0},{3,1},{12,14},{13,15},{10,8},{11,9},{20,22},{21,... | collective-permute-start | bytes 1572872 | tf_op jit(solution)/shard_map/ppermute | solution.py:151
  427.7 30.8 %collective-permute-start.99 = (bf16[32,8192]{1,0:T(8,128)(2,1)S(1)}, bf16[32,8192]{1,0:T(8,128)(2,1)S(1)}, u32[]{:S(2)}, u32[]{:S(2)}) collective-permute-start(bf16[32,8192]{1,0:T(8,128)(2,1)S(1)} %shard_map.81.refs_0_), channel_id=1, source_target_pairs={{0,1},{1,0},{2,3},{3,2},{4,5},{5,4},{6,7},{7,6},{8,9},{9,8},{10,11... | collective-permute-start | bytes 1572872 | tf_op jit(solution)/shard_map/ppermute | solution.py:155
  434.7 24.2 %collective-permute-start.96 = (bf16[32,8192]{1,0:T(8,128)(2,1)S(1)}, bf16[32,8192]{1,0:T(8,128)(2,1)S(1)}, u32[]{:S(2)}, u32[]{:S(2)}) collective-permute-start(bf16[32,8192]{1,0:T(8,128)(2,1)S(1)} %collective-permute-done.94.refs_1_), channel_id=1, source_target_pairs={{2,4},{3,5},{4,2},{5,3},{10,12},{11,13},{12,10},{13,11},{18,20},{1... | collective-permute-start | bytes 1572872 | tf_op jit(solution)/shard_map/ppermute | solution.py:151
  437.5 21.5 %collective-permute-start.100 = (bf16[32,8192]{1,0:T(8,128)(2,1)S(1)}, bf16[32,8192]{1,0:T(8,128)(2,1)S(1)}, u32[]{:S(2)}, u32[]{:S(2)}) collective-permute-start(bf16[32,8192]{1,0:T(8,128)(2,1)S(1)} %collective-permute-done.94.refs_1_), channel_id=1, source_target_pairs={{0,1},{1,0},{2,3},{3,2},{4,5},{5,4},{6,7},{7,6},{8,9},{9,8},{10,11... | collective-permute-start | bytes 1572872 | tf_op jit(solution)/shard_map/ppermute | solution.py:155
  (44 other events, 266.1 us)

commit v7 on v6

--- a/solution.py
+++ b/solution.py
@@ -130,7 +130,7 @@
     smem = pl.BlockSpec(memory_space=pltpu.SMEM)
     anywhere = pl.BlockSpec(memory_space=pl.ANY)
     vmem = pl.BlockSpec(memory_space=pltpu.VMEM)
-    kernel = functools.partial(layer_kernel, act_plan, 16)
+    kernel = functools.partial(layer_kernel, act_plan, 32)
     return pl.pallas_call(
         kernel,
         out_shape=jax.ShapeDtypeStruct((rows, neurons), jnp.bfloat16),

time: 467 us -> 465 us (level)
  transfers between devices with their start and end apart: 105 -> 105, of which waited for: 54 -> 53; matrix products, arithmetic and copies ran while one was open for 0% -> 0% of each run, Pallas kernels for 10% -> 10%
where the time goes in v7:
time: 465 us
  waiting for transfers between devices  298 us (64%)
  starting transfers between devices  101 us (22%)
  Pallas kernels  60.8 us (13%)
    ppermute x24, waiting for transfers between devices, advance(): lax.ppermute(array, 'pipe', [(p, p ^ side) for p in range(self.square)])  144 us
    ppermute x35, waiting for transfers between devices, along_line(): return lax.ppermute(x, 'rows', moves)  142 us
    ppermute x35, starting transfers between devices, along_line(): return lax.ppermute(x, 'rows', moves)  60.6 us
    pallas_call x8, Pallas kernels, apply_layer(): pl.pallas_call(kernel, out_shape=jax.ShapeDtypeStruct((rows, neurons), jn...  29.5 us
    ppermute x24, starting transfers between devices, advance(): lax.ppermute(array, 'pipe', [(p, p ^ side) for p in range(self.square)])  28.9 us
    pallas_call x8, Pallas kernels, gather_weights(): pl.pallas_call(functools.partial(gather_weights_kernel, plan), out_shape=...  16.8 us
    ppermute x43, waiting for transfers between devices, to_other_core(): lax.ppermute(x, 'rows', [(i, i ^ 1) for i in range(lax.axis_size('rows'))])  11.8 us
    pallas_call x12, Pallas kernels, pick(): pl.pallas_call(functools.partial(pick_kernel, choices, len(choices)), out...  11.1 us
  transfers between devices with their start and end apart: 105, of which 53 were waited for; matrix products, arithmetic and copies ran while one was open for 0% of the time, Pallas kernels for 10%

profile of v7, /device:TPU:0, one launch (start us, length us, event | category | flops | bytes accessed | tf_op | source)
XLA Modules:
  0.0 464.6 jit_solution(4123664920285029781)
XLA Ops:
  0.1 3.1 shard_map.55
  6.4 3.0 collective-permute-start
  11.0 1.9 collective-permute-start.6
  14.7 1.6 collective-permute-start.3
  16.3 3.6 collective-permute-start.4
  20.3 3.4 shard_map.56.refs_2_.refs_1_.refs_0_.refs_4_.refs_3_.refs_5_
  23.7 12.3 %collective-permute-done.6.refs_0_.refs_1_.refs_3_.refs_2_ = bf16[32,64,256]{2,1,0:T(8,128)(2,1)S(1)} collective-permute-done((bf16[32,64,256]{2,1,0:T(8,128)(2,1)}, bf16[32,64,256]{2,1,0:T(8,128)(2,1)S(1)}, u32[]{:S(2)}, u32[]{:S(2)}) %collective-permute-start.6) | collective-permute-done | bytes 1048608 | tf_op jit(solution)/shard_map/ppermute | solution.py:335
  40.0 2.4 collective-permute-done.4.refs_2_
  42.4 1.9 collective-permute-done.10.refs_6_
  44.3 17.1 %collective-permute-done.11.refs_0_.refs_6_.refs_5_ = bf16[32,64,256]{2,1,0:T(8,128)(2,1)S(1)} collective-permute-done((bf16[32,64,256]{2,1,0:T(8,128)(2,1)S(1)}, bf16[32,64,256]{2,1,0:T(8,128)(2,1)S(1)}, u32[]{:S(2)}, u32[]{:S(2)}) %collective-permute-start.11) | collective-permute-done | bytes 1048608 | tf_op jit(solution)/shard_map/ppermute | solution.py:335
  65.5 19.4 %collective-permute-done.16.refs_2_.refs_7_ = bf16[32,64,256]{2,1,0:T(8,128)(2,1)S(1)} collective-permute-done((bf16[32,64,256]{2,1,0:T(8,128)(2,1)S(1)}, bf16[32,64,256]{2,1,0:T(8,128)(2,1)S(1)}, u32[]{:S(2)}, u32[]{:S(2)}) %collective-permute-start.16) | collective-permute-done | bytes 1048608 | tf_op jit(solution)/shard_map/ppermute | solution.py:335
  91.5 10.7 %collective-permute-done.9.refs_4_ = bf16[32,8192]{1,0:T(8,128)(2,1)S(1)} collective-permute-done((bf16[32,8192]{1,0:T(8,128)(2,1)S(1)}, bf16[32,8192]{1,0:T(8,128)(2,1)S(1)}, u32[]{:S(2)}, u32[]{:S(2)}) %collective-permute-start.9) | collective-permute-done | bytes 524320 | tf_op jit(solution)/shard_map/ppermute | solution.py:151
  102.2 5.9 %collective-permute-done.18.refs_7_.refs_0_.refs_1_.refs_3_ = bf16[32,64,256]{2,1,0:T(8,128)(2,1)S(1)} collective-permute-done((bf16[32,64,256]{2,1,0:T(8,128)(2,1)S(1)}, bf16[32,64,256]{2,1,0:T(8,128)(2,1)S(1)}, u32[]{:S(2)}, u32[]{:S(2)}) %collective-permute-start.18) | collective-permute-done | bytes 1048608 | tf_op jit(solution)/shard_map/ppermute | solution.py:335
  112.4 2.1 shard_map.60.refs_10_
  114.5 3.6 shard_map.61.refs_0_
  119.6 2.5 collective-permute-start.21
  122.1 9.3 %collective-permute-done.23.refs_2_.refs_7_.refs_8_.refs_4_ = bf16[32,64,256]{2,1,0:T(8,128)(2,1)S(1)} collective-permute-done((bf16[32,64,256]{2,1,0:T(8,128)(2,1)S(1)}, bf16[32,64,256]{2,1,0:T(8,128)(2,1)S(1)}, u32[]{:S(2)}, u32[]{:S(2)}) %collective-permute-start.23) | collective-permute-done | bytes 1048608 | tf_op jit(solution)/shard_map/ppermute | solution.py:335
  134.0 1.7 collective-permute-start.29
  135.7 10.0 %collective-permute-done.21.refs_2_ = bf16[32,8192]{1,0:T(8,128)(2,1)S(1)} collective-permute-done((bf16[32,8192]{1,0:T(8,128)(2,1)S(1)}, bf16[32,8192]{1,0:T(8,128)(2,1)S(1)}, u32[]{:S(2)}, u32[]{:S(2)}) %collective-permute-start.21) | collective-permute-done | bytes 524320 | tf_op jit(solution)/shard_map/ppermute | solution.py:151
  148.3 4.0 collective-permute-done.28.refs_4_.refs_2_.refs_0_.refs_10_
  153.2 2.1 shard_map.65.refs_10_
  156.1 7.4 %collective-permute-done.26.refs_4_ = bf16[32,8192]{1,0:T(8,128)(2,1)S(1)} collective-permute-done((bf16[32,8192]{1,0:T(8,128)(2,1)S(1)}, bf16[32,8192]{1,0:T(8,128)(2,1)S(1)}, u32[]{:S(2)}, u32[]{:S(2)}) %collective-permute-start.26) | collective-permute-done | bytes 524320 | tf_op jit(solution)/shard_map/ppermute | solution.py:151
  163.5 1.7 collective-permute-start.36
  165.7 3.6 shard_map.66.refs_0_
  169.3 2.5 collective-permute-start.33
  171.8 2.6 collective-permute-start.34
  174.5 14.6 %collective-permute-done.36.refs_2_.refs_3_.refs_8_.refs_5_ = bf16[32,64,256]{2,1,0:T(8,128)(2,1)S(1)} collective-permute-done((bf16[32,64,256]{2,1,0:T(8,128)(2,1)S(1)}, bf16[32,64,256]{2,1,0:T(8,128)(2,1)S(1)}, u32[]{:S(2)}, u32[]{:S(2)}) %collective-permute-start.36) | collective-permute-done | bytes 1048608 | tf_op jit(solution)/shard_map/ppermute | solution.py:335
  191.2 6.8 %collective-permute-done.34.refs_2_ = bf16[32,8192]{1,0:T(8,128)(2,1)S(1)} collective-permute-done((bf16[32,8192]{1,0:T(8,128)(2,1)S(1)}, bf16[32,8192]{1,0:T(8,128)(2,1)S(1)}, u32[]{:S(2)}, u32[]{:S(2)}) %collective-permute-start.34) | collective-permute-done | bytes 524320 | tf_op jit(solution)/shard_map/ppermute | solution.py:151
  200.0 2.1 shard_map.68.refs_10_
  203.6 9.7 %collective-permute-done.39.refs_4_ = bf16[32,8192]{1,0:T(8,128)(2,1)S(1)} collective-permute-done((bf16[32,8192]{1,0:T(8,128)(2,1)S(1)}, bf16[32,8192]{1,0:T(8,128)(2,1)S(1)}, u32[]{:S(2)}, u32[]{:S(2)}) %collective-permute-start.39) | collective-permute-done | bytes 524320 | tf_op jit(solution)/shard_map/ppermute | solution.py:151
  217.5 3.7 shard_map.69.refs_0_
  221.4 2.2 collective-permute-start.44
  224.9 3.0 collective-permute-done.47.refs_1_.refs_5_.refs_7_.refs_4_
  227.8 9.3 %collective-permute-done.48.refs_2_.refs_3_.refs_0_.refs_1_ = bf16[32,64,256]{2,1,0:T(8,128)(2,1)S(1)} collective-permute-done((bf16[32,64,256]{2,1,0:T(8,128)(2,1)S(1)}, bf16[32,64,256]{2,1,0:T(8,128)(2,1)S(1)}, u32[]{:S(2)}, u32[]{:S(2)}) %collective-permute-start.48) | collective-permute-done | bytes 1048608 | tf_op jit(solution)/shard_map/ppermute | solution.py:335
  239.8 8.5 %collective-permute-done.45.refs_2_ = bf16[32,8192]{1,0:T(8,128)(2,1)S(1)} collective-permute-done((bf16[32,8192]{1,0:T(8,128)(2,1)S(1)}, bf16[32,8192]{1,0:T(8,128)(2,1)S(1)}, u32[]{:S(2)}, u32[]{:S(2)}) %collective-permute-start.45) | collective-permute-done | bytes 524320 | tf_op jit(solution)/shard_map/ppermute | solution.py:151
  251.0 9.8 %collective-permute-done.52.refs_4_.refs_2_.refs_1_.refs_10_ = bf16[32,64,256]{2,1,0:T(8,128)(2,1)S(1)} collective-permute-done((bf16[32,64,256]{2,1,0:T(8,128)(2,1)S(1)}, bf16[32,64,256]{2,1,0:T(8,128)(2,1)S(1)}, u32[]{:S(2)}, u32[]{:S(2)}) %collective-permute-start.52) | collective-permute-done | bytes 1048608 | tf_op jit(solution)/shard_map/ppermute | solution.py:335
  261.0 2.1 shard_map.72.refs_10_
  267.2 3.6 shard_map.73.refs_0_
  271.0 3.3 collective-permute-start.57
  275.5 15.4 %collective-permute-done.60.refs_1_.refs_6_.refs_8_.refs_7_ = bf16[32,64,256]{2,1,0:T(8,128)(2,1)S(1)} collective-permute-done((bf16[32,64,256]{2,1,0:T(8,128)(2,1)S(1)}, bf16[32,64,256]{2,1,0:T(8,128)(2,1)S(1)}, u32[]{:S(2)}, u32[]{:S(2)}) %collective-permute-start.60) | collective-permute-done | bytes 1048608 | tf_op jit(solution)/shard_map/ppermute | solution.py:335
  294.9 4.2 collective-permute-done.58.refs_2_
  301.1 2.1 shard_map.76.refs_10_
  303.9 12.6 %collective-permute-done.65.refs_0_.refs_5_.refs_2_ = bf16[32,64,256]{2,1,0:T(8,128)(2,1)S(1)} collective-permute-done((bf16[32,64,256]{2,1,0:T(8,128)(2,1)S(1)}, bf16[32,64,256]{2,1,0:T(8,128)(2,1)S(1)}, u32[]{:S(2)}, u32[]{:S(2)}) %collective-permute-start.65) | collective-permute-done | bytes 1048608 | tf_op jit(solution)/shard_map/ppermute | solution.py:335
  320.7 3.6 shard_map.77.refs_0_
  325.0 4.1 collective-permute-start.70
  329.1 4.5 collective-permute-start.77
  334.9 6.4 %collective-permute-done.70.refs_1_ = bf16[32,8192]{1,0:T(8,128)(2,1)S(1)} collective-permute-done((bf16[32,8192]{1,0:T(8,128)(2,1)S(1)}, bf16[32,8192]{1,0:T(8,128)(2,1)S(1)}, u32[]{:S(2)}, u32[]{:S(2)}) %collective-permute-start.70) | collective-permute-done | bytes 524320 | tf_op jit(solution)/shard_map/ppermute | solution.py:151
  342.1 2.0 collective-permute-done.75.refs_6_.refs_5_
  344.4 2.1 shard_map.78.refs_12_
  347.1 8.0 %collective-permute-done.77.refs_5_ = bf16[32,8192]{1,0:T(8,128)(2,1)S(1)} collective-permute-done((bf16[32,8192]{1,0:T(8,128)(2,1)S(1)}, bf16[32,8192]{1,0:T(8,128)(2,1)S(1)}, u32[]{:S(2)}, u32[]{:S(2)}) %collective-permute-start.77) | collective-permute-done | bytes 524320 | tf_op jit(solution)/shard_map/ppermute | solution.py:151
  355.2 11.0 %collective-permute-done.73.refs_4_ = bf16[32,8192]{1,0:T(8,128)(2,1)S(1)} collective-permute-done((bf16[32,8192]{1,0:T(8,128)(2,1)S(1)}, bf16[32,8192]{1,0:T(8,128)(2,1)S(1)}, u32[]{:S(2)}, u32[]{:S(2)}) %collective-permute-start.73) | collective-permute-done | bytes 524320 | tf_op jit(solution)/shard_map/ppermute | solution.py:151
  368.9 3.6 shard_map.79.refs_0_
  374.8 4.5 collective-permute-start.87
  380.7 6.7 %collective-permute-done.83.refs_1_ = bf16[32,8192]{1,0:T(8,128)(2,1)S(1)} collective-permute-done((bf16[32,8192]{1,0:T(8,128)(2,1)S(1)}, bf16[32,8192]{1,0:T(8,128)(2,1)S(1)}, u32[]{:S(2)}, u32[]{:S(2)}) %collective-permute-start.83) | collective-permute-done | bytes 524320 | tf_op jit(solution)/shard_map/ppermute | solution.py:151
  388.1 2.1 shard_map.80.refs_12_
  390.3 10.2 %collective-permute-done.87.refs_5_ = bf16[32,8192]{1,0:T(8,128)(2,1)S(1)} collective-permute-done((bf16[32,8192]{1,0:T(8,128)(2,1)S(1)}, bf16[32,8192]{1,0:T(8,128)(2,1)S(1)}, u32[]{:S(2)}, u32[]{:S(2)}) %collective-permute-start.87) | collective-permute-done | bytes 524320 | tf_op jit(solution)/shard_map/ppermute | solution.py:151
  400.5 10.7 %collective-permute-done.86.refs_4_ = bf16[32,8192]{1,0:T(8,128)(2,1)S(1)} collective-permute-done((bf16[32,8192]{1,0:T(8,128)(2,1)S(1)}, bf16[32,8192]{1,0:T(8,128)(2,1)S(1)}, u32[]{:S(2)}, u32[]{:S(2)}) %collective-permute-start.86) | collective-permute-done | bytes 524320 | tf_op jit(solution)/shard_map/ppermute | solution.py:151
  414.7 3.6 shard_map.81.refs_0_
  420.1 4.5 collective-permute-start.98
  426.0 7.0 %collective-permute-done.94.refs_1_ = bf16[32,8192]{1,0:T(8,128)(2,1)S(1)} collective-permute-done((bf16[32,8192]{1,0:T(8,128)(2,1)S(1)}, bf16[32,8192]{1,0:T(8,128)(2,1)S(1)}, u32[]{:S(2)}, u32[]{:S(2)}) %collective-permute-start.94) | collective-permute-done | bytes 524320 | tf_op jit(solution)/shard_map/ppermute | solution.py:151
  433.7 2.1 shard_map.82.refs_12_
  435.9 9.9 %collective-permute-done.98.refs_5_ = bf16[32,8192]{1,0:T(8,128)(2,1)S(1)} collective-permute-done((bf16[32,8192]{1,0:T(8,128)(2,1)S(1)}, bf16[32,8192]{1,0:T(8,128)(2,1)S(1)}, u32[]{:S(2)}, u32[]{:S(2)}) %collective-permute-start.98) | collective-permute-done | bytes 524320 | tf_op jit(solution)/shard_map/ppermute | solution.py:151
  445.8 10.8 %collective-permute-done.97.refs_4_ = bf16[32,8192]{1,0:T(8,128)(2,1)S(1)} collective-permute-done((bf16[32,8192]{1,0:T(8,128)(2,1)S(1)}, bf16[32,8192]{1,0:T(8,128)(2,1)S(1)}, u32[]{:S(2)}, u32[]{:S(2)}) %collective-permute-start.97) | collective-permute-done | bytes 524320 | tf_op jit(solution)/shard_map/ppermute | solution.py:151
  460.1 4.4 shard_map.83
  (197 shorter events, 89.2 us)
Async XLA Ops:
  11.0 25.1 %collective-permute-start.6 = (bf16[32,64,256]{2,1,0:T(8,128)(2,1)}, bf16[32,64,256]{2,1,0:T(8,128)(2,1)S(1)}, u32[]{:S(2)}, u32[]{:S(2)}) collective-permute-start(bf16[32,64,256]{2,1,0:T(8,128)(2,1)} %get-tuple-element.90), channel_id=1, source_target_pairs={{0,8},{8,0},{16,24},{24,16},{1,9},{9,1},{17,25},{25,17},{2,10},{10... | collective-permute-start | bytes 3145736 | tf_op jit(solution)/shard_map/ppermute | solution.py:335
  12.9 24.4 %collective-permute-start.7 = (bf16[32,64,256]{2,1,0:T(8,128)(2,1)}, bf16[32,64,256]{2,1,0:T(8,128)(2,1)S(1)}, u32[]{:S(2)}, u32[]{:S(2)}) collective-permute-start(bf16[32,64,256]{2,1,0:T(8,128)(2,1)} %copy-done.1), channel_id=1, source_target_pairs={{0,16},{8,24},{16,0},{24,8},{1,17},{9,25},{17,1},{25,9},{2,18},{10... | collective-permute-start | bytes 3145736 | tf_op jit(solution)/shard_map/ppermute | solution.py:335
  14.7 25.3 %collective-permute-start.3 = (bf16[32,8192]{1,0:T(8,128)(2,1)S(1)}, bf16[32,8192]{1,0:T(8,128)(2,1)S(1)}, u32[]{:S(2)}, u32[]{:S(2)}) collective-permute-start(bf16[32,8192]{1,0:T(8,128)(2,1)S(1)} %copy-done), channel_id=1, source_target_pairs={{0,2},{1,3},{2,0},{3,1},{4,6},{5,7},{6,4},{7,5},{8,10},{9,11},{10,... | collective-permute-start | bytes 1572872 | tf_op jit(solution)/shard_map/ppermute | solution.py:151
  16.3 26.1 %collective-permute-start.4 = (bf16[32,8192]{1,0:T(8,128)(2,1)S(1)}, bf16[32,8192]{1,0:T(8,128)(2,1)S(1)}, u32[]{:S(2)}, u32[]{:S(2)}) collective-permute-start(bf16[32,8192]{1,0:T(8,128)(2,1)S(1)} %copy-done), channel_id=1, source_target_pairs={{2,4},{3,5},{4,2},{5,3},{0,6},{1,7},{6,0},{7,1},{10,12},{11,13},{1... | collective-permute-start | bytes 1572872 | tf_op jit(solution)/shard_map/ppermute | solution.py:151
  38.1 23.3 %collective-permute-start.11 = (bf16[32,64,256]{2,1,0:T(8,128)(2,1)S(1)}, bf16[32,64,256]{2,1,0:T(8,128)(2,1)S(1)}, u32[]{:S(2)}, u32[]{:S(2)}) collective-permute-start(bf16[32,64,256]{2,1,0:T(8,128)(2,1)S(1)} %get-tuple-element.97), channel_id=1, source_target_pairs={{0,8},{8,0},{16,24},{24,16},{1,9},{9,1},{17,25},{25,17},{2,10},{10... | collective-permute-start | bytes 3145736 | tf_op jit(solution)/shard_map/ppermute | solution.py:335
  38.5 23.2 %collective-permute-start.12 = (bf16[32,64,256]{2,1,0:T(8,128)(2,1)S(1)}, bf16[32,64,256]{2,1,0:T(8,128)(2,1)S(1)}, u32[]{:S(2)}, u32[]{:S(2)}) collective-permute-start(bf16[32,64,256]{2,1,0:T(8,128)(2,1)S(1)} %get-tuple-element.98), channel_id=1, source_target_pairs={{0,16},{8,24},{16,0},{24,8},{1,17},{9,25},{17,1},{25,9},{2,18},{10... | collective-permute-start | bytes 3145736 | tf_op jit(solution)/shard_map/ppermute | solution.py:335
  62.5 22.4 %collective-permute-start.16 = (bf16[32,64,256]{2,1,0:T(8,128)(2,1)S(1)}, bf16[32,64,256]{2,1,0:T(8,128)(2,1)S(1)}, u32[]{:S(2)}, u32[]{:S(2)}) collective-permute-start(bf16[32,64,256]{2,1,0:T(8,128)(2,1)S(1)} %get-tuple-element.103), channel_id=1, source_target_pairs={{0,8},{8,0},{16,24},{24,16},{1,9},{9,1},{17,25},{25,17},{2,10},{10... | collective-permute-start | bytes 3145736 | tf_op jit(solution)/shard_map/ppermute | solution.py:335
  63.9 21.8 %collective-permute-start.17 = (bf16[32,64,256]{2,1,0:T(8,128)(2,1)S(1)}, bf16[32,64,256]{2,1,0:T(8,128)(2,1)S(1)}, u32[]{:S(2)}, u32[]{:S(2)}) collective-permute-start(bf16[32,64,256]{2,1,0:T(8,128)(2,1)S(1)} %get-tuple-element.104), channel_id=1, source_target_pairs={{0,16},{8,24},{16,0},{24,8},{1,17},{9,25},{17,1},{25,9},{2,18},{10... | collective-permute-start | bytes 3145736 | tf_op jit(solution)/shard_map/ppermute | solution.py:335
  86.4 21.7 %collective-permute-start.18 = (bf16[32,64,256]{2,1,0:T(8,128)(2,1)S(1)}, bf16[32,64,256]{2,1,0:T(8,128)(2,1)S(1)}, u32[]{:S(2)}, u32[]{:S(2)}) collective-permute-start(bf16[32,64,256]{2,1,0:T(8,128)(2,1)S(1)} %get-tuple-element.108), channel_id=1, source_target_pairs={{0,8},{8,0},{16,24},{24,16},{1,9},{9,1},{17,25},{25,17},{2,10},{10... | collective-permute-start | bytes 3145736 | tf_op jit(solution)/shard_map/ppermute | solution.py:335
  87.4 21.6 %collective-permute-start.19 = (bf16[32,64,256]{2,1,0:T(8,128)(2,1)S(1)}, bf16[32,64,256]{2,1,0:T(8,128)(2,1)S(1)}, u32[]{:S(2)}, u32[]{:S(2)}) collective-permute-start(bf16[32,64,256]{2,1,0:T(8,128)(2,1)S(1)} %get-tuple-element.109), channel_id=1, source_target_pairs={{0,16},{8,24},{16,0},{24,8},{1,17},{9,25},{17,1},{25,9},{2,18},{10... | collective-permute-start | bytes 3145736 | tf_op jit(solution)/shard_map/ppermute | solution.py:335
  90.9 23.6 %collective-permute-start.13 = (bf16[32,8192]{1,0:T(8,128)(2,1)S(1)}, bf16[32,8192]{1,0:T(8,128)(2,1)S(1)}, u32[]{:S(2)}, u32[]{:S(2)}) collective-permute-start(bf16[32,8192]{1,0:T(8,128)(2,1)S(1)} %collective-permute-done.4.refs_2_), channel_id=1, source_target_pairs={{0,1},{1,0},{2,3},{3,2},{4,5},{5,4},{6,7},{7,6},{8,9},{9,8},{10,11... | collective-permute-start | bytes 1572872 | tf_op jit(solution)/shard_map/ppermute | solution.py:155
  91.0 23.5 %collective-permute-start.14 = (bf16[32,8192]{1,0:T(8,128)(2,1)S(1)}, bf16[32,8192]{1,0:T(8,128)(2,1)S(1)}, u32[]{:S(2)}, u32[]{:S(2)}) collective-permute-start(bf16[32,8192]{1,0:T(8,128)(2,1)S(1)} %collective-permute-done.8.refs_3_), channel_id=1, source_target_pairs={{0,1},{1,0},{2,3},{3,2},{4,5},{5,4},{6,7},{7,6},{8,9},{9,8},{10,11... | collective-permute-start | bytes 1572872 | tf_op jit(solution)/shard_map/ppermute | solution.py:155
  109.7 21.6 %collective-permute-start.23 = (bf16[32,64,256]{2,1,0:T(8,128)(2,1)S(1)}, bf16[32,64,256]{2,1,0:T(8,128)(2,1)S(1)}, u32[]{:S(2)}, u32[]{:S(2)}) collective-permute-start(bf16[32,64,256]{2,1,0:T(8,128)(2,1)S(1)} %get-tuple-element.112), channel_id=1, source_target_pairs={{0,8},{8,0},{16,24},{24,16},{1,9},{9,1},{17,25},{25,17},{2,10},{10... | collective-permute-start | bytes 3145736 | tf_op jit(solution)/shard_map/ppermute | solution.py:335
  110.7 22.2 %collective-permute-start.24 = (bf16[32,64,256]{2,1,0:T(8,128)(2,1)S(1)}, bf16[32,64,256]{2,1,0:T(8,128)(2,1)S(1)}, u32[]{:S(2)}, u32[]{:S(2)}) collective-permute-start(bf16[32,64,256]{2,1,0:T(8,128)(2,1)S(1)} %get-tuple-element.113), channel_id=1, source_target_pairs={{0,16},{8,24},{16,0},{24,8},{1,17},{9,25},{17,1},{25,9},{2,18},{10... | collective-permute-start | bytes 3145736 | tf_op jit(solution)/shard_map/ppermute | solution.py:335
  118.1 17.5 %collective-permute-start.20 = (bf16[32,8192]{1,0:T(8,128)(2,1)S(1)}, bf16[32,8192]{1,0:T(8,128)(2,1)S(1)}, u32[]{:S(2)}, u32[]{:S(2)}) collective-permute-start(bf16[32,8192]{1,0:T(8,128)(2,1)S(1)} %shard_map.61.refs_0_), channel_id=1, source_target_pairs={{0,2},{1,3},{2,0},{3,1},{4,6},{5,7},{6,4},{7,5},{8,10},{9,11},{10,... | collective-permute-start | bytes 1572872 | tf_op jit(solution)/shard_map/ppermute | solution.py:151
  119.6 26.1 %collective-permute-start.21 = (bf16[32,8192]{1,0:T(8,128)(2,1)S(1)}, bf16[32,8192]{1,0:T(8,128)(2,1)S(1)}, u32[]{:S(2)}, u32[]{:S(2)}) collective-permute-start(bf16[32,8192]{1,0:T(8,128)(2,1)S(1)} %shard_map.61.refs_0_), channel_id=1, source_target_pairs={{2,4},{3,5},{4,2},{5,3},{0,6},{1,7},{6,0},{7,1},{10,12},{11,13},{1... | collective-permute-start | bytes 1572872 | tf_op jit(solution)/shard_map/ppermute | solution.py:151
  133.6 18.7 %collective-permute-start.28 = (bf16[32,64,256]{2,1,0:T(8,128)(2,1)S(1)}, bf16[32,64,256]{2,1,0:T(8,128)(2,1)S(1)}, u32[]{:S(2)}, u32[]{:S(2)}) collective-permute-start(bf16[32,64,256]{2,1,0:T(8,128)(2,1)S(1)} %get-tuple-element.118), channel_id=1, source_target_pairs={{0,8},{8,0},{16,24},{24,16},{1,9},{9,1},{17,25},{25,17},{2,10},{10... | collective-permute-start | bytes 3145736 | tf_op jit(solution)/shard_map/ppermute | solution.py:335
  134.0 19.2 %collective-permute-start.29 = (bf16[32,64,256]{2,1,0:T(8,128)(2,1)S(1)}, bf16[32,64,256]{2,1,0:T(8,128)(2,1)S(1)}, u32[]{:S(2)}, u32[]{:S(2)}) collective-permute-start(bf16[32,64,256]{2,1,0:T(8,128)(2,1)S(1)} %get-tuple-element.119), channel_id=1, source_target_pairs={{0,16},{8,24},{16,0},{24,8},{1,17},{9,25},{17,1},{25,9},{2,18},{10... | collective-permute-start | bytes 3145736 | tf_op jit(solution)/shard_map/ppermute | solution.py:335
  146.4 17.1 %collective-permute-start.26 = (bf16[32,8192]{1,0:T(8,128)(2,1)S(1)}, bf16[32,8192]{1,0:T(8,128)(2,1)S(1)}, u32[]{:S(2)}, u32[]{:S(2)}) collective-permute-start(bf16[32,8192]{1,0:T(8,128)(2,1)S(1)} %collective-permute-done.21.refs_2_), channel_id=1, source_target_pairs={{4,6},{5,7},{2,0},{3,1},{12,14},{13,15},{10,8},{11,9},{20,22},{21,... | collective-permute-start | bytes 1572872 | tf_op jit(solution)/shard_map/ppermute | solution.py:151
  147.7 18.0 %collective-permute-start.30 = (bf16[32,8192]{1,0:T(8,128)(2,1)S(1)}, bf16[32,8192]{1,0:T(8,128)(2,1)S(1)}, u32[]{:S(2)}, u32[]{:S(2)}) collective-permute-start(bf16[32,8192]{1,0:T(8,128)(2,1)S(1)} %collective-permute-done.21.refs_2_), channel_id=1, source_target_pairs={{0,1},{1,0},{2,3},{3,2},{4,5},{5,4},{6,7},{7,6},{8,9},{9,8},{10,11... | collective-permute-start | bytes 1572872 | tf_op jit(solution)/shard_map/ppermute | solution.py:155
  148.2 17.4 %collective-permute-start.31 = (bf16[32,8192]{1,0:T(8,128)(2,1)S(1)}, bf16[32,8192]{1,0:T(8,128)(2,1)S(1)}, u32[]{:S(2)}, u32[]{:S(2)}) collective-permute-start(bf16[32,8192]{1,0:T(8,128)(2,1)S(1)} %collective-permute-done.25.refs_3_), channel_id=1, source_target_pairs={{0,1},{1,0},{2,3},{3,2},{4,5},{5,4},{6,7},{7,6},{8,9},{9,8},{10,11... | collective-permute-start | bytes 1572872 | tf_op jit(solution)/shard_map/ppermute | solution.py:155
  163.5 25.6 %collective-permute-start.36 = (bf16[32,64,256]{2,1,0:T(8,128)(2,1)S(1)}, bf16[32,64,256]{2,1,0:T(8,128)(2,1)S(1)}, u32[]{:S(2)}, u32[]{:S(2)}) collective-permute-start(bf16[32,64,256]{2,1,0:T(8,128)(2,1)S(1)} %get-tuple-element.125), channel_id=1, source_target_pairs={{0,8},{8,0},{16,24},{24,16},{1,9},{9,1},{17,25},{25,17},{2,10},{10... | collective-permute-start | bytes 3145736 | tf_op jit(solution)/shard_map/ppermute | solution.py:335
  165.1 25.3 %collective-permute-start.37 = (bf16[32,64,256]{2,1,0:T(8,128)(2,1)S(1)}, bf16[32,64,256]{2,1,0:T(8,128)(2,1)S(1)}, u32[]{:S(2)}, u32[]{:S(2)}) collective-permute-start(bf16[32,64,256]{2,1,0:T(8,128)(2,1)S(1)} %get-tuple-element.126), channel_id=1, source_target_pairs={{0,16},{8,24},{16,0},{24,8},{1,17},{9,25},{17,1},{25,9},{2,18},{10... | collective-permute-start | bytes 3145736 | tf_op jit(solution)/shard_map/ppermute | solution.py:335
  169.3 21.8 %collective-permute-start.33 = (bf16[32,8192]{1,0:T(8,128)(2,1)S(1)}, bf16[32,8192]{1,0:T(8,128)(2,1)S(1)}, u32[]{:S(2)}, u32[]{:S(2)}) collective-permute-start(bf16[32,8192]{1,0:T(8,128)(2,1)S(1)} %shard_map.66.refs_0_), channel_id=1, source_target_pairs={{0,2},{1,3},{2,0},{3,1},{4,6},{5,7},{6,4},{7,5},{8,10},{9,11},{10,... | collective-permute-start | bytes 1572872 | tf_op jit(solution)/shard_map/ppermute | solution.py:151
  171.8 26.1 %collective-permute-start.34 = (bf16[32,8192]{1,0:T(8,128)(2,1)S(1)}, bf16[32,8192]{1,0:T(8,128)(2,1)S(1)}, u32[]{:S(2)}, u32[]{:S(2)}) collective-permute-start(bf16[32,8192]{1,0:T(8,128)(2,1)S(1)} %shard_map.66.refs_0_), channel_id=1, source_target_pairs={{2,4},{3,5},{4,2},{5,3},{0,6},{1,7},{6,0},{7,1},{10,12},{11,13},{1... | collective-permute-start | bytes 1572872 | tf_op jit(solution)/shard_map/ppermute | solution.py:151
  199.2 15.6 %collective-permute-start.38 = (bf16[32,8192]{1,0:T(8,128)(2,1)S(1)}, bf16[32,8192]{1,0:T(8,128)(2,1)S(1)}, u32[]{:S(2)}, u32[]{:S(2)}) collective-permute-start(bf16[32,8192]{1,0:T(8,128)(2,1)S(1)} %collective-permute-done.33.refs_1_), channel_id=1, source_target_pairs={{2,4},{3,5},{4,2},{5,3},{10,12},{11,13},{12,10},{13,11},{18,20},{1... | collective-permute-start | bytes 1572872 | tf_op jit(solution)/shard_map/ppermute | solution.py:151
  202.7 25.1 %collective-permute-start.47 = (bf16[32,64,256]{2,1,0:T(8,128)(2,1)S(1)}, bf16[32,64,256]{2,1,0:T(8,128)(2,1)S(1)}, u32[]{:S(2)}, u32[]{:S(2)}) collective-permute-start(bf16[32,64,256]{2,1,0:T(8,128)(2,1)S(1)} %get-tuple-element.134), channel_id=1, source_target_pairs={{0,8},{8,0},{16,24},{24,16},{1,9},{9,1},{17,25},{25,17},{2,10},{10... | collective-permute-start | bytes 3145736 | tf_op jit(solution)/shard_map/ppermute | solution.py:335
  213.3 23.8 %collective-permute-start.48 = (bf16[32,64,256]{2,1,0:T(8,128)(2,1)S(1)}, bf16[32,64,256]{2,1,0:T(8,128)(2,1)S(1)}, u32[]{:S(2)}, u32[]{:S(2)}) collective-permute-start(bf16[32,64,256]{2,1,0:T(8,128)(2,1)S(1)} %get-tuple-element.135), channel_id=1, source_target_pairs={{0,16},{8,24},{16,0},{24,8},{1,17},{9,25},{17,1},{25,9},{2,18},{10... | collective-permute-start | bytes 3145736 | tf_op jit(solution)/shard_map/ppermute | solution.py:335
  221.2 16.0 %collective-permute-start.46 = (bf16[32,8192]{1,0:T(8,128)(2,1)S(1)}, bf16[32,8192]{1,0:T(8,128)(2,1)S(1)}, u32[]{:S(2)}, u32[]{:S(2)}) collective-permute-start(bf16[32,8192]{1,0:T(8,128)(2,1)S(1)} %shard_map.69.refs_0_), channel_id=1, source_target_pairs={{0,1},{1,0},{2,3},{3,2},{4,5},{5,4},{6,7},{7,6},{8,9},{9,8},{10,11... | collective-permute-start | bytes 1572872 | tf_op jit(solution)/shard_map/ppermute | solution.py:155
  221.4 18.4 %collective-permute-start.44 = (bf16[32,8192]{1,0:T(8,128)(2,1)S(1)}, bf16[32,8192]{1,0:T(8,128)(2,1)S(1)}, u32[]{:S(2)}, u32[]{:S(2)}) collective-permute-start(bf16[32,8192]{1,0:T(8,128)(2,1)S(1)} %shard_map.69.refs_0_), channel_id=1, source_target_pairs={{0,2},{1,3},{2,0},{3,1},{4,6},{5,7},{6,4},{7,5},{8,10},{9,11},{10,... | collective-permute-start | bytes 1572872 | tf_op jit(solution)/shard_map/ppermute | solution.py:151
  223.6 24.7 %collective-permute-start.45 = (bf16[32,8192]{1,0:T(8,128)(2,1)S(1)}, bf16[32,8192]{1,0:T(8,128)(2,1)S(1)}, u32[]{:S(2)}, u32[]{:S(2)}) collective-permute-start(bf16[32,8192]{1,0:T(8,128)(2,1)S(1)} %shard_map.69.refs_0_), channel_id=1, source_target_pairs={{2,4},{3,5},{4,2},{5,3},{0,6},{1,7},{6,0},{7,1},{10,12},{11,13},{1... | collective-permute-start | bytes 1572872 | tf_op jit(solution)/shard_map/ppermute | solution.py:151
  237.9 23.0 %collective-permute-start.52 = (bf16[32,64,256]{2,1,0:T(8,128)(2,1)S(1)}, bf16[32,64,256]{2,1,0:T(8,128)(2,1)S(1)}, u32[]{:S(2)}, u32[]{:S(2)}) collective-permute-start(bf16[32,64,256]{2,1,0:T(8,128)(2,1)S(1)} %get-tuple-element.142), channel_id=1, source_target_pairs={{0,8},{8,0},{16,24},{24,16},{1,9},{9,1},{17,25},{25,17},{2,10},{10... | collective-permute-start | bytes 3145736 | tf_op jit(solution)/shard_map/ppermute | solution.py:335
  238.2 22.8 %collective-permute-start.53 = (bf16[32,64,256]{2,1,0:T(8,128)(2,1)S(1)}, bf16[32,64,256]{2,1,0:T(8,128)(2,1)S(1)}, u32[]{:S(2)}, u32[]{:S(2)}) collective-permute-start(bf16[32,64,256]{2,1,0:T(8,128)(2,1)S(1)} %get-tuple-element.143), channel_id=1, source_target_pairs={{0,16},{8,24},{16,0},{24,8},{1,17},{9,25},{17,1},{25,9},{2,18},{10... | collective-permute-start | bytes 3145736 | tf_op jit(solution)/shard_map/ppermute | solution.py:335
  249.1 16.2 %collective-permute-start.50 = (bf16[32,8192]{1,0:T(8,128)(2,1)S(1)}, bf16[32,8192]{1,0:T(8,128)(2,1)S(1)}, u32[]{:S(2)}, u32[]{:S(2)}) collective-permute-start(bf16[32,8192]{1,0:T(8,128)(2,1)S(1)} %collective-permute-done.45.refs_2_), channel_id=1, source_target_pairs={{4,6},{5,7},{2,0},{3,1},{12,14},{13,15},{10,8},{11,9},{20,22},{21,... | collective-permute-start | bytes 1572872 | tf_op jit(solution)/shard_map/ppermute | solution.py:151
  250.4 16.8 %collective-permute-start.54 = (bf16[32,8192]{1,0:T(8,128)(2,1)S(1)}, bf16[32,8192]{1,0:T(8,128)(2,1)S(1)}, u32[]{:S(2)}, u32[]{:S(2)}) collective-permute-start(bf16[32,8192]{1,0:T(8,128)(2,1)S(1)} %collective-permute-done.45.refs_2_), channel_id=1, source_target_pairs={{0,1},{1,0},{2,3},{3,2},{4,5},{5,4},{6,7},{7,6},{8,9},{9,8},{10,11... | collective-permute-start | bytes 1572872 | tf_op jit(solution)/shard_map/ppermute | solution.py:155
  250.9 16.2 %collective-permute-start.55 = (bf16[32,8192]{1,0:T(8,128)(2,1)S(1)}, bf16[32,8192]{1,0:T(8,128)(2,1)S(1)}, u32[]{:S(2)}, u32[]{:S(2)}) collective-permute-start(bf16[32,8192]{1,0:T(8,128)(2,1)S(1)} %collective-permute-done.49.refs_3_), channel_id=1, source_target_pairs={{0,1},{1,0},{2,3},{3,2},{4,5},{5,4},{6,7},{7,6},{8,9},{9,8},{10,11... | collective-permute-start | bytes 1572872 | tf_op jit(solution)/shard_map/ppermute | solution.py:155
  265.3 25.6 %collective-permute-start.60 = (bf16[32,64,256]{2,1,0:T(8,128)(2,1)S(1)}, bf16[32,64,256]{2,1,0:T(8,128)(2,1)S(1)}, u32[]{:S(2)}, u32[]{:S(2)}) collective-permute-start(bf16[32,64,256]{2,1,0:T(8,128)(2,1)S(1)} %get-tuple-element.151), channel_id=1, source_target_pairs={{0,8},{8,0},{16,24},{24,16},{1,9},{9,1},{17,25},{25,17},{2,10},{10... | collective-permute-start | bytes 3145736 | tf_op jit(solution)/shard_map/ppermute | solution.py:335
  265.9 25.3 %collective-permute-start.61 = (bf16[32,64,256]{2,1,0:T(8,128)(2,1)S(1)}, bf16[32,64,256]{2,1,0:T(8,128)(2,1)S(1)}, u32[]{:S(2)}, u32[]{:S(2)}) collective-permute-start(bf16[32,64,256]{2,1,0:T(8,128)(2,1)S(1)} %get-tuple-element.152), channel_id=1, source_target_pairs={{0,16},{8,24},{16,0},{24,8},{1,17},{9,25},{17,1},{25,9},{2,18},{10... | collective-permute-start | bytes 3145736 | tf_op jit(solution)/shard_map/ppermute | solution.py:335
  270.8 20.4 %collective-permute-start.59 = (bf16[32,8192]{1,0:T(8,128)(2,1)S(1)}, bf16[32,8192]{1,0:T(8,128)(2,1)S(1)}, u32[]{:S(2)}, u32[]{:S(2)}) collective-permute-start(bf16[32,8192]{1,0:T(8,128)(2,1)S(1)} %shard_map.73.refs_0_), channel_id=1, source_target_pairs={{0,1},{1,0},{2,3},{3,2},{4,5},{5,4},{6,7},{7,6},{8,9},{9,8},{10,11... | collective-permute-start | bytes 1572872 | tf_op jit(solution)/shard_map/ppermute | solution.py:155
  271.0 23.9 %collective-permute-start.57 = (bf16[32,8192]{1,0:T(8,128)(2,1)S(1)}, bf16[32,8192]{1,0:T(8,128)(2,1)S(1)}, u32[]{:S(2)}, u32[]{:S(2)}) collective-permute-start(bf16[32,8192]{1,0:T(8,128)(2,1)S(1)} %shard_map.73.refs_0_), channel_id=1, source_target_pairs={{0,2},{1,3},{2,0},{3,1},{4,6},{5,7},{6,4},{7,5},{8,10},{9,11},{10,... | collective-permute-start | bytes 1572872 | tf_op jit(solution)/shard_map/ppermute | solution.py:151
  274.3 24.8 %collective-permute-start.58 = (bf16[32,8192]{1,0:T(8,128)(2,1)S(1)}, bf16[32,8192]{1,0:T(8,128)(2,1)S(1)}, u32[]{:S(2)}, u32[]{:S(2)}) collective-permute-start(bf16[32,8192]{1,0:T(8,128)(2,1)S(1)} %shard_map.73.refs_0_), channel_id=1, source_target_pairs={{2,4},{3,5},{4,2},{5,3},{0,6},{1,7},{6,0},{7,1},{10,12},{11,13},{1... | collective-permute-start | bytes 1572872 | tf_op jit(solution)/shard_map/ppermute | solution.py:151
  291.9 24.6 %collective-permute-start.65 = (bf16[32,64,256]{2,1,0:T(8,128)(2,1)S(1)}, bf16[32,64,256]{2,1,0:T(8,128)(2,1)S(1)}, u32[]{:S(2)}, u32[]{:S(2)}) collective-permute-start(bf16[32,64,256]{2,1,0:T(8,128)(2,1)S(1)} %get-tuple-element.159), channel_id=1, source_target_pairs={{0,8},{8,0},{16,24},{24,16},{1,9},{9,1},{17,25},{25,17},{2,10},{10... | collective-permute-start | bytes 3145736 | tf_op jit(solution)/shard_map/ppermute | solution.py:335
  293.4 24.2 %collective-permute-start.66 = (bf16[32,64,256]{2,1,0:T(8,128)(2,1)S(1)}, bf16[32,64,256]{2,1,0:T(8,128)(2,1)S(1)}, u32[]{:S(2)}, u32[]{:S(2)}) collective-permute-start(bf16[32,64,256]{2,1,0:T(8,128)(2,1)S(1)} %get-tuple-element.160), channel_id=1, source_target_pairs={{0,16},{8,24},{16,0},{24,8},{1,17},{9,25},{17,1},{25,9},{2,18},{10... | collective-permute-start | bytes 3145736 | tf_op jit(solution)/shard_map/ppermute | solution.py:335
  299.8 18.6 %collective-permute-start.63 = (bf16[32,8192]{1,0:T(8,128)(2,1)S(1)}, bf16[32,8192]{1,0:T(8,128)(2,1)S(1)}, u32[]{:S(2)}, u32[]{:S(2)}) collective-permute-start(bf16[32,8192]{1,0:T(8,128)(2,1)S(1)} %collective-permute-done.58.refs_2_), channel_id=1, source_target_pairs={{4,6},{5,7},{2,0},{3,1},{12,14},{13,15},{10,8},{11,9},{20,22},{21,... | collective-permute-start | bytes 1572872 | tf_op jit(solution)/shard_map/ppermute | solution.py:151
  303.2 17.4 %collective-permute-start.67 = (bf16[32,8192]{1,0:T(8,128)(2,1)S(1)}, bf16[32,8192]{1,0:T(8,128)(2,1)S(1)}, u32[]{:S(2)}, u32[]{:S(2)}) collective-permute-start(bf16[32,8192]{1,0:T(8,128)(2,1)S(1)} %collective-permute-done.58.refs_2_), channel_id=1, source_target_pairs={{0,1},{1,0},{2,3},{3,2},{4,5},{5,4},{6,7},{7,6},{8,9},{9,8},{10,11... | collective-permute-start | bytes 1572872 | tf_op jit(solution)/shard_map/ppermute | solution.py:155
  303.8 16.9 %collective-permute-start.68 = (bf16[32,8192]{1,0:T(8,128)(2,1)S(1)}, bf16[32,8192]{1,0:T(8,128)(2,1)S(1)}, u32[]{:S(2)}, u32[]{:S(2)}) collective-permute-start(bf16[32,8192]{1,0:T(8,128)(2,1)S(1)} %collective-permute-done.62.refs_3_), channel_id=1, source_target_pairs={{0,1},{1,0},{2,3},{3,2},{4,5},{5,4},{6,7},{7,6},{8,9},{9,8},{10,11... | collective-permute-start | bytes 1572872 | tf_op jit(solution)/shard_map/ppermute | solution.py:155
  318.5 25.6 %collective-permute-start.75 = (bf16[32,64,256]{2,1,0:T(8,128)(2,1)S(1)}, bf16[32,64,256]{2,1,0:T(8,128)(2,1)S(1)}, u32[]{:S(2)}, u32[]{:S(2)}) collective-permute-start(bf16[32,64,256]{2,1,0:T(8,128)(2,1)S(1)} %get-tuple-element.166), channel_id=1, source_target_pairs={{0,8},{8,0},{16,24},{24,16},{1,9},{9,1},{17,25},{25,17},{2,10},{10... | collective-permute-start | bytes 3145736 | tf_op jit(solution)/shard_map/ppermute | solution.py:335
  319.2 25.3 %collective-permute-start.76 = (bf16[32,64,256]{2,1,0:T(8,128)(2,1)S(1)}, bf16[32,64,256]{2,1,0:T(8,128)(2,1)S(1)}, u32[]{:S(2)}, u32[]{:S(2)}) collective-permute-start(bf16[32,64,256]{2,1,0:T(8,128)(2,1)S(1)} %get-tuple-element.167), channel_id=1, source_target_pairs={{0,16},{8,24},{16,0},{24,8},{1,17},{9,25},{17,1},{25,9},{2,18},{10... | collective-permute-start | bytes 3145736 | tf_op jit(solution)/shard_map/ppermute | solution.py:335
  325.0 16.4 %collective-permute-start.70 = (bf16[32,8192]{1,0:T(8,128)(2,1)S(1)}, bf16[32,8192]{1,0:T(8,128)(2,1)S(1)}, u32[]{:S(2)}, u32[]{:S(2)}) collective-permute-start(bf16[32,8192]{1,0:T(8,128)(2,1)S(1)} %shard_map.77.refs_0_), channel_id=1, source_target_pairs={{0,2},{1,3},{2,0},{3,1},{4,6},{5,7},{6,4},{7,5},{8,10},{9,11},{10,... | collective-permute-start | bytes 1572872 | tf_op jit(solution)/shard_map/ppermute | solution.py:151
  329.1 26.1 %collective-permute-start.77 = (bf16[32,8192]{1,0:T(8,128)(2,1)S(1)}, bf16[32,8192]{1,0:T(8,128)(2,1)S(1)}, u32[]{:S(2)}, u32[]{:S(2)}) collective-permute-start(bf16[32,8192]{1,0:T(8,128)(2,1)S(1)} %shard_map.77.refs_0_), channel_id=1, source_target_pairs={{0,6},{1,7},{6,0},{7,1},{8,14},{9,15},{14,8},{15,9},{16,22},{17,23... | collective-permute-start | bytes 1572872 | tf_op jit(solution)/shard_map/ppermute | solution.py:151
  333.6 32.6 %collective-permute-start.73 = (bf16[32,8192]{1,0:T(8,128)(2,1)S(1)}, bf16[32,8192]{1,0:T(8,128)(2,1)S(1)}, u32[]{:S(2)}, u32[]{:S(2)}) collective-permute-start(bf16[32,8192]{1,0:T(8,128)(2,1)S(1)} %collective-permute-done.71.refs_2_), channel_id=1, source_target_pairs={{4,6},{5,7},{2,0},{3,1},{12,14},{13,15},{10,8},{11,9},{20,22},{21,... | collective-permute-start | bytes 1572872 | tf_op jit(solution)/shard_map/ppermute | solution.py:151
  341.4 24.8 %collective-permute-start.72 = (bf16[32,8192]{1,0:T(8,128)(2,1)S(1)}, bf16[32,8192]{1,0:T(8,128)(2,1)S(1)}, u32[]{:S(2)}, u32[]{:S(2)}) collective-permute-start(bf16[32,8192]{1,0:T(8,128)(2,1)S(1)} %collective-permute-done.70.refs_1_), channel_id=1, source_target_pairs={{2,4},{3,5},{4,2},{5,3},{10,12},{11,13},{12,10},{13,11},{18,20},{1... | collective-permute-start | bytes 1572872 | tf_op jit(solution)/shard_map/ppermute | solution.py:151
  346.6 20.2 %collective-permute-start.78 = (bf16[32,8192]{1,0:T(8,128)(2,1)S(1)}, bf16[32,8192]{1,0:T(8,128)(2,1)S(1)}, u32[]{:S(2)}, u32[]{:S(2)}) collective-permute-start(bf16[32,8192]{1,0:T(8,128)(2,1)S(1)} %collective-permute-done.70.refs_1_), channel_id=1, source_target_pairs={{0,1},{1,0},{2,3},{3,2},{4,5},{5,4},{6,7},{7,6},{8,9},{9,8},{10,11... | collective-permute-start | bytes 1572872 | tf_op jit(solution)/shard_map/ppermute | solution.py:155
  346.6 20.1 %collective-permute-start.79 = (bf16[32,8192]{1,0:T(8,128)(2,1)S(1)}, bf16[32,8192]{1,0:T(8,128)(2,1)S(1)}, u32[]{:S(2)}, u32[]{:S(2)}) collective-permute-start(bf16[32,8192]{1,0:T(8,128)(2,1)S(1)} %collective-permute-done.71.refs_2_), channel_id=1, source_target_pairs={{0,1},{1,0},{2,3},{3,2},{4,5},{5,4},{6,7},{7,6},{8,9},{9,8},{10,11... | collective-permute-start | bytes 1572872 | tf_op jit(solution)/shard_map/ppermute | solution.py:155
  374.8 25.7 %collective-permute-start.87 = (bf16[32,8192]{1,0:T(8,128)(2,1)S(1)}, bf16[32,8192]{1,0:T(8,128)(2,1)S(1)}, u32[]{:S(2)}, u32[]{:S(2)}) collective-permute-start(bf16[32,8192]{1,0:T(8,128)(2,1)S(1)} %shard_map.79.refs_0_), channel_id=1, source_target_pairs={{0,6},{1,7},{6,0},{7,1},{8,14},{9,15},{14,8},{15,9},{16,22},{17,23... | collective-permute-start | bytes 1572872 | tf_op jit(solution)/shard_map/ppermute | solution.py:151
  379.3 31.9 %collective-permute-start.86 = (bf16[32,8192]{1,0:T(8,128)(2,1)S(1)}, bf16[32,8192]{1,0:T(8,128)(2,1)S(1)}, u32[]{:S(2)}, u32[]{:S(2)}) collective-permute-start(bf16[32,8192]{1,0:T(8,128)(2,1)S(1)} %collective-permute-done.84.refs_2_), channel_id=1, source_target_pairs={{4,6},{5,7},{2,0},{3,1},{12,14},{13,15},{10,8},{11,9},{20,22},{21,... | collective-permute-start | bytes 1572872 | tf_op jit(solution)/shard_map/ppermute | solution.py:151
  380.6 30.6 %collective-permute-start.88 = (bf16[32,8192]{1,0:T(8,128)(2,1)S(1)}, bf16[32,8192]{1,0:T(8,128)(2,1)S(1)}, u32[]{:S(2)}, u32[]{:S(2)}) collective-permute-start(bf16[32,8192]{1,0:T(8,128)(2,1)S(1)} %shard_map.79.refs_0_), channel_id=1, source_target_pairs={{0,1},{1,0},{2,3},{3,2},{4,5},{5,4},{6,7},{7,6},{8,9},{9,8},{10,11... | collective-permute-start | bytes 1572872 | tf_op jit(solution)/shard_map/ppermute | solution.py:155
  387.4 24.4 %collective-permute-start.85 = (bf16[32,8192]{1,0:T(8,128)(2,1)S(1)}, bf16[32,8192]{1,0:T(8,128)(2,1)S(1)}, u32[]{:S(2)}, u32[]{:S(2)}) collective-permute-start(bf16[32,8192]{1,0:T(8,128)(2,1)S(1)} %collective-permute-done.83.refs_1_), channel_id=1, source_target_pairs={{2,4},{3,5},{4,2},{5,3},{10,12},{11,13},{12,10},{13,11},{18,20},{1... | collective-permute-start | bytes 1572872 | tf_op jit(solution)/shard_map/ppermute | solution.py:151
  390.2 21.7 %collective-permute-start.89 = (bf16[32,8192]{1,0:T(8,128)(2,1)S(1)}, bf16[32,8192]{1,0:T(8,128)(2,1)S(1)}, u32[]{:S(2)}, u32[]{:S(2)}) collective-permute-start(bf16[32,8192]{1,0:T(8,128)(2,1)S(1)} %collective-permute-done.83.refs_1_), channel_id=1, source_target_pairs={{0,1},{1,0},{2,3},{3,2},{4,5},{5,4},{6,7},{7,6},{8,9},{9,8},{10,11... | collective-permute-start | bytes 1572872 | tf_op jit(solution)/shard_map/ppermute | solution.py:155
  420.1 25.7 %collective-permute-start.98 = (bf16[32,8192]{1,0:T(8,128)(2,1)S(1)}, bf16[32,8192]{1,0:T(8,128)(2,1)S(1)}, u32[]{:S(2)}, u32[]{:S(2)}) collective-permute-start(bf16[32,8192]{1,0:T(8,128)(2,1)S(1)} %shard_map.81.refs_0_), channel_id=1, source_target_pairs={{0,6},{1,7},{6,0},{7,1},{8,14},{9,15},{14,8},{15,9},{16,22},{17,23... | collective-permute-start | bytes 1572872 | tf_op jit(solution)/shard_map/ppermute | solution.py:151
  424.6 32.0 %collective-permute-start.97 = (bf16[32,8192]{1,0:T(8,128)(2,1)S(1)}, bf16[32,8192]{1,0:T(8,128)(2,1)S(1)}, u32[]{:S(2)}, u32[]{:S(2)}) collective-permute-start(bf16[32,8192]{1,0:T(8,128)(2,1)S(1)} %collective-permute-done.95.refs_2_), channel_id=1, source_target_pairs={{4,6},{5,7},{2,0},{3,1},{12,14},{13,15},{10,8},{11,9},{20,22},{21,... | collective-permute-start | bytes 1572872 | tf_op jit(solution)/shard_map/ppermute | solution.py:151
  425.9 30.7 %collective-permute-start.99 = (bf16[32,8192]{1,0:T(8,128)(2,1)S(1)}, bf16[32,8192]{1,0:T(8,128)(2,1)S(1)}, u32[]{:S(2)}, u32[]{:S(2)}) collective-permute-start(bf16[32,8192]{1,0:T(8,128)(2,1)S(1)} %shard_map.81.refs_0_), channel_id=1, source_target_pairs={{0,1},{1,0},{2,3},{3,2},{4,5},{5,4},{6,7},{7,6},{8,9},{9,8},{10,11... | collective-permute-start | bytes 1572872 | tf_op jit(solution)/shard_map/ppermute | solution.py:155
  433.0 24.2 %collective-permute-start.96 = (bf16[32,8192]{1,0:T(8,128)(2,1)S(1)}, bf16[32,8192]{1,0:T(8,128)(2,1)S(1)}, u32[]{:S(2)}, u32[]{:S(2)}) collective-permute-start(bf16[32,8192]{1,0:T(8,128)(2,1)S(1)} %collective-permute-done.94.refs_1_), channel_id=1, source_target_pairs={{2,4},{3,5},{4,2},{5,3},{10,12},{11,13},{12,10},{13,11},{18,20},{1... | collective-permute-start | bytes 1572872 | tf_op jit(solution)/shard_map/ppermute | solution.py:151
  435.8 21.4 %collective-permute-start.100 = (bf16[32,8192]{1,0:T(8,128)(2,1)S(1)}, bf16[32,8192]{1,0:T(8,128)(2,1)S(1)}, u32[]{:S(2)}, u32[]{:S(2)}) collective-permute-start(bf16[32,8192]{1,0:T(8,128)(2,1)S(1)} %collective-permute-done.94.refs_1_), channel_id=1, source_target_pairs={{0,1},{1,0},{2,3},{3,2},{4,5},{5,4},{6,7},{7,6},{8,9},{9,8},{10,11... | collective-permute-start | bytes 1572872 | tf_op jit(solution)/shard_map/ppermute | solution.py:155
  (44 other events, 265.9 us)
